TPU v7x, 32 devices: a whole 2x2x4 slice. The times are simulated.
32 devices in a mesh: chan: 8 (over y, x, core), tm: 4 (over z).
Axes of the slice: x: 2, y: 2, z: 4, core: 2. Of those that a mesh axis runs over, the one named last changes fastest.
Arguments:
- voltages: bfloat16 [2, 2048, 131072], P(None, 'chan', 'tm'), may hold values from -6 to 6
- filter_taps: float32 [16, 64], replicated, may hold values from -1.5 to 1.5
- antenna_flags: int32 [2048], P('chan'), may hold values 0 or 1
Outputs:
- visibility: float32 [2048, 2, 8, 2048], P('tm', None, 'chan')
All inputs are finite; a program needn't handle non-finite values. No bound on the sum of `antenna_flags` on one device may be relied on, other than what follows from the above.
Results may differ from a plain program's by a relative error of at most 0.0028.
Values may be sent and summed in bfloat16 or wider, within the bound.
No kernel may reach another device: no remote copies, remote signals or barrier semaphores. Data moves between devices by JAX's collectives and lax.ppermute only.
A program may use at most 320 MiB of HBM per device.

v0:
```python
import math

import jax
import jax.numpy as jnp
from jax import lax
from jax.sharding import PartitionSpec as P


def passed_along(value, axis, by):
    count = lax.axis_size(axis)
    pairs = [(i, i + by) for i in range(count) if 0 <= i + by < count]
    return lax.ppermute(value, axis, pairs)


def dft_tables(signal_length, count):
    index_n = jnp.arange(signal_length, dtype=jnp.int32)
    index_c = jnp.arange(count, dtype=jnp.int32)
    phase = index_n[:, None] * index_c[None, :] % signal_length
    angle = phase.astype(jnp.float32) * (2.0 * math.pi / signal_length)
    return (jnp.cos(angle), jnp.sin(angle))


def on_device(voltages, filter_taps, antenna_flags):
    tap_count, signal_length = filter_taps.shape
    local_antennas = voltages.shape[1]
    frames_per_shard = voltages.shape[2] // signal_length
    tail = voltages[:, :, voltages.shape[2] - (tap_count - 1) * signal_length :]
    previous = passed_along(tail, "tm", 1)
    joined = jnp.concatenate([previous, voltages], axis=2).reshape(
        2, local_antennas, frames_per_shard + tap_count - 1, signal_length
    )
    filter_output = jnp.zeros((2, local_antennas, frames_per_shard, signal_length), jnp.float32)
    for tap_index in range(tap_count):
        begin = tap_count - 1 - tap_index
        filter_output = filter_output + filter_taps[tap_index][None, None, None, :] * joined[
            :, :, begin : begin + frames_per_shard, :
        ].astype(jnp.float32)
    channels = lax.axis_size("chan")
    cosine, sine_table = dft_tables(signal_length, channels)
    cos_part = jnp.einsum("pafn,nc->pcaf", filter_output, cosine, precision=lax.Precision.HIGHEST)
    sin_part = jnp.einsum(
        "pafn,nc->pcaf", filter_output, sine_table, precision=lax.Precision.HIGHEST
    )
    scale = antenna_flags.astype(jnp.float32)[None, :, None] / math.sqrt(signal_length)
    real_part = (cos_part[0] + sin_part[1]) * scale
    imag_part = (cos_part[1] - sin_part[0]) * scale
    spectra = jnp.stack([real_part, imag_part]).astype(jnp.bfloat16)
    turned_spectra = lax.all_to_all(spectra, "chan", split_axis=1, concat_axis=2, tiled=True)
    slices = lax.axis_size("tm")
    weight = 1.0 / (frames_per_shard * slices)
    block = turned_spectra.shape[2] // slices
    row_start = lax.axis_index("tm") * block
    piece = lax.all_gather(turned_spectra, "tm", axis=3, tiled=True)
    own_rows = lax.dynamic_slice_in_dim(piece, row_start, block, 2)
    visibility_real = jnp.einsum(
        "dox,dpx->odp", own_rows[0], piece[0], preferred_element_type=jnp.float32
    )
    visibility_real = visibility_real + jnp.einsum(
        "dox,dpx->odp", own_rows[1], piece[1], preferred_element_type=jnp.float32
    )
    visibility_imaginary = jnp.einsum(
        "dox,dpx->odp", own_rows[1], piece[0], preferred_element_type=jnp.float32
    )
    visibility_imaginary = visibility_imaginary - jnp.einsum(
        "dox,dpx->odp", own_rows[0], piece[1], preferred_element_type=jnp.float32
    )
    return jnp.stack([visibility_real, visibility_imaginary], axis=1) * weight


def solution(mesh):
    placed = (P(None, "chan", "tm"), P(), P("chan"))
    return jax.shard_map(
        on_device,
        mesh=mesh,
        in_specs=placed,
        out_specs=P("tm", None, "chan", None),
        check_vma=False,
    )
```

profile of v0, /device:TPU:0, one launch (start us, length us, event | category | flops | bytes accessed | tf_op | source)
XLA Modules:
  0.0 859.4 jit_solution(3323569740717605277)
XLA Ops:
  6.5 0.0 all-gather.2.cloned.1.call-start
  6.5 41.9 %copy.27 = bf16[2,256,32768]{1,2,0:T(8,128)(2,1)} copy(bf16[2,256,32768]{2,1,0:T(8,128)(2,1)} %param.3) | data formatting | bytes 67108864 | tf_op args[0]
  48.4 1.3 slice.168
  49.7 5.0 collective-permute-start
  54.7 0.0 copy-done.2
  54.7 0.6 convert_multiply_fusion
  55.3 0.0 copy-done
  55.3 20.3 %collective-permute-done = bf16[2,256,960]{1,2,0:T(8,128)(2,1)S(1)} collective-permute-done((bf16[2,256,960]{1,2,0:T(8,128)(2,1)S(1)}, bf16[2,256,960]{1,2,0:T(8,128)(2,1)S(1)}, u32[]{:S(2)}, u32[]{:S(2)}) %collective-permute-start) | collective-permute-done | bytes 983072 | tf_op jit(solution)/shard_map/ppermute | solution.py:12
  75.6 23.9 %pad_maximum_fusion = bf16[2,256,33728]{1,2,0:T(8,128)(2,1)} fusion(bf16[2,256,32768]{1,2,0:T(8,128)(2,1)} %copy.27, bf16[2,256,960]{1,2,0:T(8,128)(2,1)S(1)} %collective-permute-done), kind=kLoop, calls=%fused_computation.1 | loop fusion | flops 69074944 | bytes 69074944 | tf_op jit(solution)/shard_map/concatenate | solution.py:29
  99.6 204.7 %multiply_add_fusion = f32[2,256,512,64]{1,3,2,0:T(8,128)} fusion(bf16[2,256,527,64]{1,3,2,0:T(8,128)(2,1)} %bitcast.90, f32[64]{0:T(128)S(1)} %get-tuple-element.21, f32[64]{0:T(128)S(1)} %get-tuple-element.22, f32[64]{0:T(128)S(1)} %get-tuple-element.8, f32[64]{0:T(128)S(1)} %get-tuple-element.9, f32[64]{0:T(128)S(1)} %get-tuple-element.10, ...), kind=kLoop, calls=%fused_computation | loop fusion | flops 788529152 | bytes 603983872 | tf_op jit(solution)/shard_map/add | solution.py:35
  304.3 68.0 %copy.29 = f32[2,256,512,64]{2,3,1,0:T(8,128)} copy(f32[2,256,512,64]{1,3,2,0:T(8,128)} %multiply_add_fusion) | data formatting | bytes 134217728 | tf_op jit(solution)/shard_map/add | solution.py:35
  372.3 35.9 %convolution_bitcast_fusion = f32[2,8,256,512]{3,1,2,0:T(8,128)S(1)} fusion(f32[2,256,512,64]{2,3,1,0:T(8,128)} %copy.29), kind=kOutput, calls=%fused_computation.18 | convolution fusion | flops 1610619904 | bytes 75497472 | tf_op jit(solution)/shard_map/pafn,nc->pcaf/dot_general | solution.py:41
  408.2 0.0 copy-start.1
  408.2 36.0 %convolution_bitcast_fusion.1 = f32[2,8,256,512]{3,1,2,0:T(8,128)S(1)} fusion(f32[2,256,512,64]{2,3,1,0:T(8,128)} %copy.29), kind=kOutput, calls=%fused_computation.19 | convolution fusion | flops 1610619904 | bytes 75497472 | tf_op jit(solution)/shard_map/pafn,nc->pcaf/dot_general | solution.py:40
  444.3 0.0 copy-done.1
  444.3 1.1 fusion.7
  445.4 0.4 pad_maximum_fusion.1
  445.8 1.4 copy.31
  447.2 52.6 %all_to_all.12 = bf16[2,8,256,512]{3,2,0,1:T(8,128)(2,1)S(1)} all-to-all(bf16[2,8,256,512]{3,2,0,1:T(8,128)(2,1)S(1)} %copy.31), channel_id=1, replica_groups=mesh['chan'=8,'tm'=4] {'chan'}, dimensions={1} | all-to-all | bytes 8388608 | tf_op jit(solution)/shard_map/all_to_all | solution.py:48
  499.8 2.4 copy.32
  502.3 0.0 all-gather.2.cloned.1.call-update
  502.3 287.2 %all-gather.2.cloned.1.call-done = bf16[2,1,2048,2048]{3,2,0,1:T(8,128)(2,1)} async-done(((bf16[2,1,2048,512]{3,2,0,1:T(8,128)(2,1)}), bf16[2,1,2048,2048]{3,2,0,1:T(8,128)(2,1)}) %all-gather.2.cloned.1.call-update) | async-done | bytes 16777232 | tf_op jit(solution)/shard_map/all_gather | solution.py:53
  789.5 10.7 %fusion.1 = f32[2048,512]{1,0:T(8,128)} fusion(bf16[2,1,2048,2048]{3,2,0,1:T(8,128)(2,1)} %all-gather.2.cloned.1.call-done, s32[]{:T(128)S(6)} %select_n.13), kind=kOutput, calls=%fused_computation.6 | convolution fusion | flops 4294967296 | bytes 14680068 | tf_op jit(solution)/shard_map/dox,dpx->odp/dot_general | solution.py:55
  800.2 10.7 %fusion = f32[2048,512]{1,0:T(8,128)} fusion(bf16[2,1,2048,2048]{3,2,0,1:T(8,128)(2,1)} %all-gather.2.cloned.1.call-done, s32[]{:T(128)S(6)} %add.90, s32[]{:T(128)S(6)} %select_n.13), kind=kOutput, calls=%fused_computation.5 | convolution fusion | flops 4294967296 | bytes 14680072 | tf_op jit(solution)/shard_map/dox,dpx->odp/dot_general | solution.py:61
  810.9 0.0 slice-done
  810.9 0.0 slice-done.1
  810.9 0.0 slice-done.2
  810.9 0.0 slice-done.3
  810.9 6.7 add_bitcast_fusion
  817.6 10.2 %subtract_bitcast_fusion = f32[512,1,1,2048]{0,3,2,1:T(8,128)S(1)} fusion(f32[2048,512]{1,0:T(8,128)} %fusion, bf16[2,1,2048,2048]{3,2,0,1:T(8,128)(2,1)} %all-gather.2.cloned.1.call-done, s32[]{:T(128)S(6)} %select_n.13), kind=kOutput, calls=%fused_computation.16 | convolution fusion | flops 4296015872 | bytes 18874372 | tf_op jit(solution)/shard_map/dox,dpx->odp/dot_general | solution.py:64
  827.8 4.3 maximum_multiply_fusion
  832.0 20.5 %copy.33 = f32[512,2,1,2048]{3,2,1,0:T(1,128)} copy(f32[512,2,1,2048]{0,3,2,1:T(8,128)} %maximum_multiply_fusion) | data formatting | bytes 16777216 | tf_op jit(solution)/shard_map/mul | solution.py:67
  (8 shorter events, 0.0 us)
Async XLA Ops:
  6.5 48.2 %copy-start.2 = (s32[256]{0:T(256)S(1)}, s32[256]{0:T(256)}, u32[]{:S(2)}) copy-start(s32[256]{0:T(256)} %param.5) | copy-start | bytes 3076
  6.5 48.7 %copy-start = (f32[16,64]{1,0:T(8,128)S(1)}, f32[16,64]{1,0:T(8,128)}, u32[]{:S(2)}) copy-start(f32[16,64]{1,0:T(8,128)} %param.4) | copy-start | bytes 12292
  6.5 783.0 %all-gather.2.cloned.1.call-start = ((), (), s32[]{:S(2)}) async-start(), calls=%async_computation.1 | async-start | bytes 20971520 | tf_op jit(solution)/shard_map/all_gather | solution.py:53
  49.7 25.9 %collective-permute-start = (bf16[2,256,960]{1,2,0:T(8,128)(2,1)S(1)}, bf16[2,256,960]{1,2,0:T(8,128)(2,1)S(1)}, u32[]{:S(2)}, u32[]{:S(2)}) collective-permute-start(bf16[2,256,960]{1,2,0:T(8,128)(2,1)S(1)} %slice.168), channel_id=1, source_target_pairs={{0,1},{1,2},{2,3},{4,5},{5,6},{6,7},{8,9},{9,10},{10,11},{12,13},{... | collective-permute-start | bytes 2949128 | tf_op jit(solution)/shard_map/ppermute | solution.py:12
  408.2 36.0 %copy-start.1 = (f32[256]{0:T(256)S(1)}, f32[256]{0:T(256)}, u32[]{:S(2)}) copy-start(f32[256]{0:T(256)} %convert_multiply_fusion) | copy-start | bytes 3076
  789.5 21.4 %slice-start = ((s8[16777216]{0:T(1024)(128)(4,1)}), s8[4194304]{0:T(1024)(128)(4,1)S(1)}, s32[]{:S(2)}) async-start(s8[16777216]{0:T(1024)(128)(4,1)} %bitcast.92), calls=%async_computation.2 | async-start | bytes 8388608
  789.5 21.4 %slice-start.1 = ((s8[16777216]{0:T(1024)(128)(4,1)}), s8[4194304]{0:T(1024)(128)(4,1)S(1)}, s32[]{:S(2)}) async-start(s8[16777216]{0:T(1024)(128)(4,1)} %bitcast.92), calls=%async_computation.3 | async-start | bytes 8388608
  800.2 10.7 %slice-start.2 = ((s8[16777216]{0:T(1024)(128)(4,1)}), s8[4194304]{0:T(1024)(128)(4,1)S(1)}, s32[]{:S(2)}) async-start(s8[16777216]{0:T(1024)(128)(4,1)} %bitcast.92), calls=%async_computation.4 | async-start | bytes 8388608
  800.2 10.7 %slice-start.3 = ((s8[16777216]{0:T(1024)(128)(4,1)}), s8[4194304]{0:T(1024)(128)(4,1)S(1)}, s32[]{:S(2)}) async-start(s8[16777216]{0:T(1024)(128)(4,1)} %bitcast.92), calls=%async_computation.5 | async-start | bytes 8388608
Sparse Core Ops, SparseCore 0:
  502.4 287.0 all-gather.1
where the time goes:
time: 862 us; the launch traced here: 859 us
  waiting for transfers between devices  308 us (36%)
  other arithmetic  235 us (27%)
  local copies, waits for them, and re-layouts  136 us (16%)
  matrix products  110 us (13%)
  blocking collectives  52.6 us (6%)
  between operations  13.5 us (2%)
    all_gather x1, waiting for transfers between devices, on_device(): piece = lax.all_gather(turned_spectra, 'tm', axis=3, tiled=True)  287 us
    add x1, other arithmetic, on_device(): filter_output + filter_taps[tap_index][None, None, None, :] * joined[:, :...  205 us
    add x1, local copies, waits for them, and re-layouts, on_device(): filter_output + filter_taps[tap_index][None, None, None, :] * joined[:, :...  68 us
    all_to_all x1, blocking collectives, on_device(): lax.all_to_all(spectra, 'chan', split_axis=1, concat_axis=2, tiled=True)  52.6 us
    unnamed x15, local copies, waits for them, and re-layouts  41.9 us
    dot_general x1, matrix products, on_device(): jnp.einsum('pafn,nc->pcaf', filter_output, cosine, precision=lax.Precisio...  36 us
    dot_general x1, matrix products, on_device(): jnp.einsum('pafn,nc->pcaf', filter_output, sine_table, precision=lax.Prec...  35.9 us
    concatenate x1, other arithmetic, on_device(): jnp.concatenate([previous, voltages], axis=2)  23.9 us
  transfers between devices with their start and end apart: 2, of which 2 were waited for; matrix products, arithmetic and copies ran while one was open for 0% of the time, Pallas kernels for 0%

commit v1 on v0

v1 whole, which is shorter than its diff:
```python
import functools
import math

import jax
import jax.numpy as jnp
import numpy as np
from jax import lax
from jax.experimental import pallas as pl
from jax.experimental.pallas import tpu as pltpu
from jax.sharding import PartitionSpec as P

F32, BF16 = jnp.float32, jnp.bfloat16
GROUP = 8
VMEM_LIMIT = 48 * 1024 * 1024


def params(**more):
    return pltpu.CompilerParams(vmem_limit_bytes=VMEM_LIMIT, **more)


def filterbank_weights(filter_taps, channels):
    taps, length = filter_taps.shape
    phase = np.arange(length)[None, :] * np.arange(channels)[:, None] % length
    angle = phase * (2.0 * math.pi / length)
    trig = np.stack([np.cos(angle), np.sin(angle)]).reshape(2 * channels, length)
    trig = np.tile(trig, (1, taps)).astype(np.float32)
    base = filter_taps[::-1].reshape(1, taps * length) * trig
    wide = (taps + GROUP) * length
    rows = [
        jnp.pad(base, ((0, 0), ((f + 1) * length, wide - (f + 1 + taps) * length)))
        for f in range(GROUP)
    ]
    weights = jnp.stack(rows, axis=1).reshape(2 * channels * GROUP, wide)
    high = lax.reduce_precision(weights, 8, 7)
    return jnp.concatenate([high, weights - high], axis=0).astype(BF16)


def filterbank_kernel(channels, length, head_ref, v_ref, w_ref, s_ref, out_ref, window):
    step = pl.program_id(0)
    _, part, lanes = v_ref.shape
    head = head_ref.shape[2]
    wide = w_ref.shape[1]

    @pl.when(step == 0)
    def _():
        window[:, :head] = head_ref[...].reshape(2 * part, head)

    @pl.when(step > 0)
    def _():
        window[:, :head] = window[:, lanes:]

    window[:, head:] = v_ref[...].reshape(2 * part, lanes)
    scale = s_ref[...]
    half = channels * GROUP
    groups = lanes // (length * GROUP)

    def one(g):
        x = window[:, g * GROUP * length : g * GROUP * length + wide]
        r = lax.dot_general(w_ref[...], x, (((1,), (1,)), ((), ())), preferred_element_type=F32)
        r = r[: 2 * half] + r[2 * half :]
        cos, sin = r[:half], r[half:]
        real = (cos[:, :part] + sin[:, part:]) * scale
        imag = (cos[:, part:] - sin[:, :part]) * scale
        return real, imag

    for g in range(0, groups, 2):
        first, second = one(g), one(g + 1)
        for c in range(channels):
            rows = slice(c * GROUP, (c + 1) * GROUP)
            for ri in range(2):
                both = jnp.concatenate([first[ri][rows], second[ri][rows]], axis=0)
                out_ref[c, ri, g * GROUP : (g + 2) * GROUP, :] = both.astype(BF16)


def filterbank(voltages, halo, weights, scale, length, channels, part, h, t, frames):
    block = min(frames, 32)
    lanes = block * length
    head = halo.shape[2]
    first = t * frames * length
    if t == 0:
        before, head_map = halo, lambda s: (0, h, 0)
    else:
        before, head_map = voltages, lambda s: (0, h, first // head - 1)
    return pl.pallas_call(
        functools.partial(filterbank_kernel, channels, length),
        grid=(frames // block,),
        in_specs=[
            pl.BlockSpec((2, part, head), head_map),
            pl.BlockSpec((2, part, lanes), lambda s: (0, h, first // lanes + s)),
            pl.BlockSpec(weights.shape, lambda s: (0, 0)),
            pl.BlockSpec((1, part), lambda s: (0, h)),
        ],
        out_specs=pl.BlockSpec((channels, 2, block, part), lambda s: (0, 0, s, 0)),
        out_shape=jax.ShapeDtypeStruct((channels, 2, frames, part), BF16),
        scratch_shapes=[pltpu.VMEM((2 * part, head + lanes), BF16)],
        compiler_params=params(),
        cost_estimate=pl.CostEstimate(
            flops=2 * weights.size * 2 * part * frames // GROUP,
            bytes_accessed=2 * 2 * part * frames * length,
            transcendentals=0,
        ),
        name=f"filterbank_h{h}_t{t}",
    )(before, voltages, weights, scale)


def correlate_kernel(times, span, weight, fresh, same, tab, *refs):
    xs, ys = refs[:times], refs[times : 2 * times]
    out_ref = refs[2 * times] if fresh else refs[2 * times + 1]
    pair = pl.program_id(0)
    i, j = tab[0, pair], tab[1, pair]

    def side(ref, at, ri):
        return jnp.concatenate([ref[at * span + d, ri] for d in range(span)], axis=1)

    def product(x, y):
        return lax.dot_general(x, y, (((0,), (0,)), ((), ())), preferred_element_type=F32)

    real = imag = None
    for x_ref, y_ref in zip(xs, ys):
        xr, xi = side(x_ref, i, 0), side(x_ref, i, 1)
        yr, yi = side(y_ref, j, 0), side(y_ref, j, 1)
        re = product(xr, yr) + product(xi, yi)
        im = product(xi, yr) - product(xr, yi)
        real = re if real is None else real + re
        imag = im if imag is None else imag + im
    real, imag = real * weight, imag * weight
    if not same:
        out_ref[0] = real
        out_ref[1] = imag
        return

    @pl.when(i != j)
    def _():
        out_ref[0] = real
        out_ref[1] = imag

    @pl.when(i == j)
    def _():
        row = lax.broadcasted_iota(jnp.int32, real.shape, 0)
        col = lax.broadcasted_iota(jnp.int32, real.shape, 1)
        out_ref[0] = jnp.where(row >= col, real, imag)


def correlate(partial, total, pairs, first, xs, ys, span, weight, same):
    times = len(xs)
    size = span * xs[0].shape[3]
    table = np.asarray(pairs, np.int32).T
    whole = [pl.BlockSpec(a.shape, lambda p, tab: (0, 0, 0, 0)) for a in xs + ys]
    out_block = pl.BlockSpec((2, size, size), lambda p, tab: (first + p, 0, 0))
    shape = jax.ShapeDtypeStruct((total, size, size), F32)
    store = jax.ShapeDtypeStruct((total, size, size), BF16)
    fresh = partial is None
    anywhere = pl.BlockSpec(memory_space=pl.ANY)
    return pl.pallas_call(
        functools.partial(correlate_kernel, times, span, weight, fresh, same),
        grid_spec=pltpu.PrefetchScalarGridSpec(
            num_scalar_prefetch=1,
            grid=(len(pairs),),
            in_specs=whole + ([] if fresh else [anywhere]),
            out_specs=[out_block, anywhere, anywhere] if fresh else [out_block],
        ),
        out_shape=[shape, store, store] if fresh else [shape],
        input_output_aliases={} if fresh else {1 + 2 * times: 0},
        compiler_params=params(),
        cost_estimate=pl.CostEstimate(
            flops=len(pairs) * 8 * size * size * times * xs[0].shape[2],
            bytes_accessed=len(pairs) * 8 * size * size,
            transcendentals=0,
        ),
        name="correlate",
    )(jnp.asarray(table), *xs, *ys, *([] if fresh else [partial]))


class Plan:
    def __init__(self, slices, parts, count):
        self.slices, self.parts, self.count = slices, parts, count
        self.calls = []
        self.pair_at = {}
        for h in range(parts):
            for k in range(h, -1, -1):
                pairs = [
                    (i, j) for i in range(slices) for j in range(slices) if k < h or j <= i
                ]
                self.calls.append((h, k, pairs, len(self.pair_at)))
                for i, j in pairs:
                    self.pair_at[h, i, k, j] = len(self.pair_at)
        self.spare = 2 * len(self.pair_at)
        self.total = self.spare + 2
        self.right = self.messages(lambda i, j: max(i, j))
        self.left = self.messages(lambda i, j: slices - 1 - min(i, j))
        self.steps = 0
        for index in range(2 * (len(self.right) + len(self.left)) + 4 * slices):
            if self.senders(self.right, index) or self.senders(self.left, index):
                self.steps = index + 1

    def squares(self, h, i, k, j):
        at = 2 * self.pair_at[h, i, k, j]
        return (at, at) if (h, i) == (k, j) else (at, at + 1)

    def messages(self, reach):
        queues, last = [[] for _ in range(self.parts)], []
        for (h, i, k, j) in self.pair_at:
            far = reach(i, j)
            if far:
                for square in sorted(set(self.squares(h, i, k, j))):
                    (queues[h] if far > 1 else last).append((-far, square))
        if self.slices == 2:
            queues, last = [sorted(last)], []
        found = []
        for queue in [sorted(q) for q in queues] + [sorted(last)]:
            for at in range(0, len(queue), self.count):
                some = queue[at : at + self.count]
                ids = [square for _, square in some]
                ids += [self.spare] * (self.count - len(ids))
                found.append((ids, max(-far for far, _ in some)))
        return found

    def senders(self, messages, step):
        places = []
        for place in range(self.slices - 1):
            k = step - 2 * place
            if 0 <= k < len(messages) and messages[k][1] > place:
                places.append(place)
        return places

    def table(self):
        rows = np.full((self.slices, self.steps + 2, 2 * self.count), self.spare, np.int32)
        for z in range(self.slices):
            for step in range(self.steps + 2):
                for side, (messages, place) in enumerate(
                    ((self.right, z), (self.left, self.slices - 1 - z))
                ):
                    k = step - 2 * place
                    if 0 <= k < len(messages):
                        rows[z, step, side * self.count : (side + 1) * self.count] = messages[k][0]
        return rows

    def last_part(self, step):
        need = 0
        for messages in (self.right, self.left):
            for place in range(self.slices):
                k = step - 2 * place
                if 0 <= k < len(messages):
                    for square in messages[k][0]:
                        for (h, i, c, j), at in self.pair_at.items():
                            if at == square // 2:
                                need = max(need, h)
        return need

    def outputs(self):
        z_n, h_n = self.slices, self.parts
        ids = np.zeros((z_n, h_n, z_n, h_n, 2), np.int32)
        modes = np.zeros((z_n, h_n, z_n, h_n), np.int32)
        for z in range(z_n):
            for h in range(h_n):
                for j in range(z_n):
                    for k in range(h_n):
                        if (h, z, k, j) in self.pair_at:
                            ids[z, h, j, k] = self.squares(h, z, k, j)
                            modes[z, h, j, k] = 2 if (h, z) == (k, j) else 0
                        else:
                            ids[z, h, j, k] = self.squares(k, j, h, z)
                            modes[z, h, j, k] = 1
        return ids, modes


def hop_kernel(receives, sends, tab, *refs):
    refs = list(refs)
    p_right, p_left = refs[0], refs[1]
    at = 2
    if receives:
        in_right, in_left = refs[2], refs[3]
        at = 6
    outs = refs[at:]
    if receives:
        keep_right, keep_left = outs[0], outs[1]
        outs = outs[2:]
        keep_right[...] = in_right[...]
        keep_left[...] = in_left[...]
        if sends:
            outs[0][...] = (p_right[...] + in_right[...].astype(F32)).astype(BF16)
            outs[1][...] = (p_left[...] + in_left[...].astype(F32)).astype(BF16)
    else:
        outs[0][...] = p_right[...].astype(BF16)
        outs[1][...] = p_left[...].astype(BF16)


def hop(table, step, count, partial, received, kept, sends):
    size = partial.shape[1]
    block = (1, size, size)
    right = pl.BlockSpec(block, lambda b, tab: (tab[step, b], 0, 0))
    left = pl.BlockSpec(block, lambda b, tab: (tab[step, count + b], 0, 0))
    plain = pl.BlockSpec(block, lambda b, tab: (b, 0, 0))
    anywhere = pl.BlockSpec(memory_space=pl.ANY)
    receives = received is not None
    message = jax.ShapeDtypeStruct((count, size, size), BF16)
    in_specs, operands = [right, left], [partial, partial]
    out_specs, out_shape, aliases = [], [], {}
    if receives:
        in_specs += [plain, plain, anywhere, anywhere]
        operands += [*received, *kept]
        out_specs += [right, left]
        out_shape += [jax.ShapeDtypeStruct(k.shape, k.dtype) for k in kept]
        aliases = {5: 0, 6: 1}
    if sends:
        out_specs += [plain, plain]
        out_shape += [message, message]
    found = pl.pallas_call(
        functools.partial(hop_kernel, receives, sends),
        grid_spec=pltpu.PrefetchScalarGridSpec(
            num_scalar_prefetch=1, grid=(count,), in_specs=in_specs, out_specs=out_specs
        ),
        out_shape=out_shape,
        input_output_aliases=aliases,
        compiler_params=params(),
        cost_estimate=pl.CostEstimate(
            flops=4 * count * size * size, bytes_accessed=20 * count * size * size, transcendentals=0
        ),
        name="hop",
    )(table, *operands)
    if receives:
        kept, found = found[:2], found[2:]
    return kept, (found if sends else None)


def rows_kernel(slices, parts, span, part, stride, local, tab, mode, ends, *refs):
    n = slices * parts * 2
    own, right, left = refs[:n], refs[n : 2 * n], refs[2 * n : 3 * n]
    out_ref = refs[3 * n]
    h, d = pl.program_id(0), pl.program_id(1)
    has_right, has_left = ends[0] > 0, ends[1] > 0
    size = span * part
    rows = pl.ds(pl.multiple_of(d * part, part), part)

    def plain(at):
        r = jnp.where(has_right, right[at][0, rows, :].astype(F32), 0.0)
        l = jnp.where(has_left, left[at][0, rows, :].astype(F32), 0.0)
        return own[at][0, rows, :] + r + l

    def turned(at):
        r = jnp.where(has_right, right[at][0, :, rows].astype(F32), 0.0)
        l = jnp.where(has_left, left[at][0, :, rows].astype(F32), 0.0)
        return (own[at][0, :, rows] + r + l).T

    for j in range(slices):
        for k in range(parts):
            at = 2 * (j * parts + k)
            kind = mode[(h * slices + j) * parts + k]

            def put(ri, value, j=j, k=k):
                for e in range(span):
                    tile = ((j * span + e) * local + k * part) // 128
                    out_ref[pl.ds(ri * (stride // 2) + tile, part, stride=stride), :] = value[
                        :, e * part : (e + 1) * part
                    ]

            @pl.when(kind == 0)
            def _():
                put(0, plain(at))
                put(1, plain(at + 1))

            @pl.when(kind == 1)
            def _():
                put(0, turned(at))
                put(1, -turned(at + 1))

            @pl.when(kind == 2)
            def _():
                direct, mirror = plain(at), turned(at)
                row = lax.broadcasted_iota(jnp.int32, (part, size), 0) + d * part
                col = lax.broadcasted_iota(jnp.int32, (part, size), 1)
                put(0, jnp.where(row >= col, direct, mirror))
                put(1, jnp.where(row < col, direct, jnp.where(row == col, 0.0, -mirror)))


def visibility_rows(plan, partial, kept, span, part, antennas):
    slices, parts = plan.slices, plan.parts
    size = span * part
    local = parts * part
    ids, modes = plan.outputs()
    z = lax.axis_index("tm")
    table = jnp.asarray(ids.reshape(slices, -1))[z]
    mode = jnp.asarray(modes.reshape(slices, -1))[z]
    ends = jnp.stack([z, slices - 1 - z]).astype(jnp.int32)
    per_h = slices * parts * 2

    def spec(at):
        return pl.BlockSpec(
            (1, size, size), lambda h, d, tab, mode, ends: (tab[h * per_h + at], 0, 0)
        )

    stride = 2 * antennas // 128
    out = pl.pallas_call(
        functools.partial(rows_kernel, slices, parts, span, part, stride, local),
        grid_spec=pltpu.PrefetchScalarGridSpec(
            num_scalar_prefetch=3,
            grid=(parts, span),
            in_specs=[spec(at) for _ in range(3) for at in range(per_h)],
            out_specs=pl.BlockSpec(
                (part * stride, 128), lambda h, d, tab, mode, ends: (d * parts + h, 0)
            ),
        ),
        out_shape=jax.ShapeDtypeStruct((span * local * stride, 128), F32),
        compiler_params=params(),
        name="visibility_rows",
    )(table, mode, ends, *([partial] * per_h), *([kept[0]] * per_h), *([kept[1]] * per_h))
    return out.reshape(span * local, 2, 1, antennas)


def on_device(voltages, filter_taps, antenna_flags):
    taps, length = filter_taps.shape
    channels, slices = lax.axis_size("chan"), lax.axis_size("tm")
    local = voltages.shape[1]
    samples = voltages.shape[2]
    frames = samples // length
    part = 128
    parts = local // part
    span = channels // slices
    times = 2
    chunk = frames // times

    head = taps * length
    tail = voltages[:, :, samples - head :]
    halo = lax.ppermute(tail, "tm", [(i, i + 1) for i in range(slices - 1)])
    weights = filterbank_weights(filter_taps, channels)
    scale = (antenna_flags.astype(F32) / math.sqrt(length)).reshape(1, local)

    spectra = []
    for h in range(parts):
        found = {}
        for t in reversed(range(times)):
            own = filterbank(
                voltages, halo, weights, scale, length, channels, part, h, t, chunk
            )
            found[t] = lax.all_to_all(own, "chan", split_axis=0, concat_axis=0, tiled=True)
        spectra.append([found[t] for t in range(times)])

    plan = Plan(slices, parts, 4)
    table = jnp.asarray(plan.table())[lax.axis_index("tm")]
    weight = 1.0 / (frames * slices)
    partial, kept = None, None
    calls = list(plan.calls)

    def extend(partial, kept, upto):
        while calls and calls[0][0] <= upto:
            h, k, pairs, first = calls.pop(0)
            made = correlate(
                partial, plan.total, pairs, first, spectra[h], spectra[k], span, weight, h == k
            )
            partial = made[0]
            if kept is None:
                kept = made[1:]
        return partial, kept

    arrived = {}
    for step in range(plan.steps + 2):
        partial, kept = extend(partial, kept, plan.last_part(step))
        sends = step < plan.steps
        received = arrived.pop(step - 2, None)
        kept, outgoing = hop(table, step, plan.count, partial, received, kept, sends)
        if sends:
            right = [(p, p + 1) for p in plan.senders(plan.right, step)]
            end = slices - 1
            left = [(end - p, end - p - 1) for p in plan.senders(plan.left, step)]
            arrived[step] = [
                lax.ppermute(outgoing[0], "tm", right),
                lax.ppermute(outgoing[1], "tm", left),
            ]
    partial, kept = extend(partial, kept, parts)
    return visibility_rows(plan, partial, kept, span, part, channels * local)


def solution(mesh):
    placed = (P(None, "chan", "tm"), P(), P("chan"))
    return jax.shard_map(
        on_device,
        mesh=mesh,
        in_specs=placed,
        out_specs=P("tm", None, "chan", None),
        check_vma=False,
    )
```

time: 862 us -> 316 us (0.37)
  waiting for transfers between devices: 308 us -> 25.2 us
  other arithmetic: 235 us -> 1.75 us
  Pallas kernels: 0 us -> 160 us
  local copies, waits for them, and re-layouts: 136 us -> 17.5 us
  matrix products: 110 us -> 0 us
  starting transfers between devices: 4.99 us -> 107 us
  blocking collectives: 52.6 us -> 0 us
  between operations: 13.5 us -> 0.61 us
    all_gather x1 -> x0, waiting for transfers between devices: 287 us -> none  [on_device(): piece = lax.all_gather(turned_spectra, 'tm', axis=3, tiled=True)]
    add x1 -> x0, other arithmetic: 205 us -> none  [on_device(): filter_output + filter_taps[tap_index][None, None, None, :] * joined[:, :...]
    pallas_call x0 -> x25, Pallas kernels: none -> 160 us  [the longest x17 72.3 us: hop(): pl.pallas_call(functools.partial(hop_kernel, receives, sends), grid_spec=...]
    dot_general x6 -> x0, matrix products: 110 us -> none  [the longest x1 36 us: on_device(): jnp.einsum('pafn,nc->pcaf', filter_output, cosine, precision=lax.Precisio...]
    ppermute x1 -> x31, starting transfers between devices: 4.99 us -> 90.7 us  [the longest x15 70.2 us: on_device(): lax.ppermute(outgoing[0], 'tm', right)]
    add x1 -> x0, local copies, waits for them, and re-layouts: 68 us -> none  [on_device(): filter_output + filter_taps[tap_index][None, None, None, :] * joined[:, :...]
    all_to_all x1 -> x0, blocking collectives: 52.6 us -> none  [on_device(): lax.all_to_all(spectra, 'chan', split_axis=1, concat_axis=2, tiled=True)]
    unnamed x15 -> x24, local copies, waits for them, and re-layouts: 41.9 us -> 10.1 us
  transfers between devices with their start and end apart: 2 -> 35, of which waited for: 2 -> 16; matrix products, arithmetic and copies ran while one was open for 0% -> 1% of each run, Pallas kernels for 0% -> 41%
where the time goes in v1:
time: 316 us; the launch traced here: 313 us
  Pallas kernels  160 us (51%)
  starting transfers between devices  107 us (34%)
  waiting for transfers between devices  25.2 us (8%)
  local copies, waits for them, and re-layouts  17.5 us (6%)
    pallas_call x17, Pallas kernels, hop(): pl.pallas_call(functools.partial(hop_kernel, receives, sends), grid_spec=...  72.3 us
    ppermute x15, starting transfers between devices, on_device(): lax.ppermute(outgoing[0], 'tm', right)  70.2 us
    pallas_call x4, Pallas kernels, filterbank(): pl.pallas_call(functools.partial(filterbank_kernel, channels, length), gr...  43.8 us
    pallas_call x3, Pallas kernels, correlate(): pl.pallas_call(functools.partial(correlate_kernel, times, span, weight, f...  26.5 us
    pallas_call x1, Pallas kernels, visibility_rows(): pl.pallas_call(functools.partial(rows_kernel, slices, parts, span, part,...  17.6 us
    ppermute x15, starting transfers between devices, on_device(): lax.ppermute(outgoing[1], 'tm', left)  17 us
    all_to_all x4, starting transfers between devices, on_device(): lax.all_to_all(own, 'chan', split_axis=0, concat_axis=0, tiled=True)  16.8 us
    ppermute x15, waiting for transfers between devices, on_device(): lax.ppermute(outgoing[0], 'tm', right)  14.3 us
  transfers between devices with their start and end apart: 35, of which 16 were waited for; matrix products, arithmetic and copies ran while one was open for 1% of the time, Pallas kernels for 41%

profile of v1, /device:TPU:0, one launch (start us, length us, event | category | flops | bytes accessed | tf_op | source)
XLA Modules:
  0.0 312.7 jit_solution(16056324649870769894)
XLA Ops:
  4.8 11.3 %filterbank_h0_t1.1 = bf16[8,2,256,128]{3,2,1,0:T(8,128)(2,1)} custom-call(bf16[2,256,32768]{2,1,0:T(8,128)(2,1)} %v_ref.7, bf16[2,256,32768]{2,1,0:T(8,128)(2,1)} %v_ref.7, bf16[256,1536]{1,0:T(8,128)(2,1)S(1)} %pad_maximum_fusion.w_ref, f32[1,256]{1,0:T(1,128)S(1)} %bitcast.27), custom_call_target="tpu_custom_call" | custom-call | flops 6442450944 | bytes 8388608 | tf_op jit(solution)/shard_map/filterbank_h0_t1/pallas_call | solution.py:84
  16.1 5.2 %all-to-all-start.3 = ((bf16[8,2,256,128]{3,2,1,0:T(8,128)(2,1)}), bf16[8,2,256,128]{3,2,1,0:T(8,128)(2,1)S(1)}, u32[]{:S(2)}, u32[]{:S(2)}) async-start(bf16[8,2,256,128]{3,2,1,0:T(8,128)(2,1)} %filterbank_h0_t1.1), calls=%async_computation.3 | async-start | bytes 2097152 | tf_op jit(solution)/shard_map/all_to_all | solution.py:435
  27.1 11.3 %filterbank_h1_t1.1 = bf16[8,2,256,128]{3,2,1,0:T(8,128)(2,1)} custom-call(bf16[2,256,32768]{2,1,0:T(8,128)(2,1)} %v_ref.7, bf16[2,256,32768]{2,1,0:T(8,128)(2,1)} %v_ref.7, bf16[256,1536]{1,0:T(8,128)(2,1)S(1)} %pad_maximum_fusion.w_ref, f32[1,256]{1,0:T(1,128)S(1)} %bitcast.28), custom_call_target="tpu_custom_call" | custom-call | flops 6442450944 | bytes 8388608 | tf_op jit(solution)/shard_map/filterbank_h1_t1/pallas_call | solution.py:84
  43.6 6.8 %collective-permute-done.head_ref = bf16[2,256,1024]{2,1,0:T(8,128)(2,1)S(1)} collective-permute-done((bf16[2,256,1024]{2,1,0:T(8,128)(2,1)}, bf16[2,256,1024]{2,1,0:T(8,128)(2,1)S(1)}, u32[]{:S(2)}, u32[]{:S(2)}) %collective-permute-start) | collective-permute-done | bytes 1048608 | tf_op jit(solution)/shard_map/ppermute | solution.py:424
  50.4 10.8 %filterbank_h0_t0.1 = bf16[8,2,256,128]{3,2,1,0:T(8,128)(2,1)S(1)} custom-call(bf16[2,256,1024]{2,1,0:T(8,128)(2,1)S(1)} %collective-permute-done.head_ref, bf16[2,256,32768]{2,1,0:T(8,128)(2,1)} %v_ref.7, bf16[256,1536]{1,0:T(8,128)(2,1)S(1)} %pad_maximum_fusion.w_ref, f32[1,256]{1,0:T(1,128)S(1)} %bitcast.29), custom_call_target="tpu_custom_call" | custom-call | flops 6442450944 | bytes 8388608 | tf_op jit(solution)/shard_map/filterbank_h0_t0/pallas_call | solution.py:84
  67.3 10.4 %filterbank_h1_t0.1 = bf16[8,2,256,128]{3,2,1,0:T(8,128)(2,1)S(1)} custom-call(bf16[2,256,1024]{2,1,0:T(8,128)(2,1)S(1)} %copy-done.9, bf16[2,256,32768]{2,1,0:T(8,128)(2,1)} %v_ref.7, bf16[256,1536]{1,0:T(8,128)(2,1)S(1)} %pad_maximum_fusion.w_ref, f32[1,256]{1,0:T(1,128)S(1)} %bitcast.30), custom_call_target="tpu_custom_call" | custom-call | flops 6442450944 | bytes 8388608 | tf_op jit(solution)/shard_map/filterbank_h1_t0/pallas_call | solution.py:84
  89.2 7.6 %correlate.3 = (f32[74,256,256]{2,1,0:T(8,128)}, bf16[74,256,256]{2,1,0:T(8,128)(2,1)}, bf16[74,256,256]{2,1,0:T(8,128)(2,1)}) custom-call(s32[2,10]{1,0:T(2,128)S(1)} %copy-done.11, bf16[8,2,256,128]{3,2,1,0:T(8,128)(2,1)S(1)} %copy-done.4, bf16[8,2,256,128]{3,2,1,0:T(8,128)(2,1)S(1)} %copy-done.1, bf16[8,2,256,128]{3,2,1,0:T(8,128)(2,1)S(1)} %copy-done.4, ...), custom_call_target="tpu_custom_call" | custom-call | flops 2684354560 | bytes 5242880 | tf_op jit(solution)/shard_map/correlate/pallas_call | solution.py:154
  110.9 4.5 %collective-permute-done.1.refs_2_ = bf16[4,256,256]{2,1,0:T(8,128)(2,1)S(1)} collective-permute-done((bf16[4,256,256]{2,1,0:T(8,128)(2,1)S(1)}, bf16[4,256,256]{2,1,0:T(8,128)(2,1)S(1)}, u32[]{:S(2)}, u32[]{:S(2)}) %collective-permute-start.1) | collective-permute-done | bytes 524320 | tf_op jit(solution)/shard_map/ppermute | solution.py:466
  115.4 4.5 %hop.18 = (bf16[74,256,256]{2,1,0:T(8,128)(2,1)}, bf16[74,256,256]{2,1,0:T(8,128)(2,1)}, bf16[4,256,256]{2,1,0:T(8,128)(2,1)}, bf16[4,256,256]{2,1,0:T(8,128)(2,1)}) custom-call(s32[17,8]{1,0:T(8,128)S(1)} %dynamic-slice_bitcast_fusion.tab, f32[74,256,256]{2,1,0:T(8,128)} %get-tuple-element.68.refs_4_.refs_0_.refs_1_, ...), custom_call_target="tpu_custom_call", output_to_operand_aliasing={{0}: (5, {}), {1}: (6, {})} | custom-call | flops 1048576 | bytes 5242880 | tf_op jit(solution)/shard_map/hop/pallas_call | solution.py:308
  119.9 4.4 %collective-permute-start.3 = (bf16[4,256,256]{2,1,0:T(8,128)(2,1)}, bf16[4,256,256]{2,1,0:T(8,128)(2,1)S(1)}, u32[]{:S(2)}, u32[]{:S(2)}) collective-permute-start(bf16[4,256,256]{2,1,0:T(8,128)(2,1)} %get-tuple-element.73), channel_id=1, source_target_pairs={{0,1},{1,2},{4,5},{5,6},{8,9},{9,10},{12,13},{13,14},{16,17},{17,1... | collective-permute-start | bytes 1572872 | tf_op jit(solution)/shard_map/ppermute | solution.py:466
  125.8 7.6 %correlate.4.refs_4_ = f32[74,256,256]{2,1,0:T(8,128)} custom-call(s32[2,10]{1,0:T(2,128)S(1)} %copy-done.11, bf16[8,2,256,128]{3,2,1,0:T(8,128)(2,1)S(1)} %all-to-all-done.refs_0_.refs_2_, bf16[8,2,256,128]{3,2,1,0:T(8,128)(2,1)S(1)} %all-to-all-done.1.refs_1_.refs_3_, ...), custom_call_target="tpu_custom_call", output_to_operand_aliasing={{}: (5, {})} | custom-call | flops 2684354560 | bytes 5242880 | tf_op jit(solution)/shard_map/correlate/pallas_call | solution.py:154
  135.9 11.3 %correlate.5.refs_0_.refs_1_.refs_2_.refs_3_.refs_4_.refs_5_.refs_6_.refs_7_.refs_8_.refs_9_.refs_10_.refs_11_.refs_12_.refs_13_.refs_14_.refs_15_ = f32[74,256,256]{2,1,0:T(8,128)} custom-call(s32[2,16]{1,0:T(2,128)S(1)} %copy-done.10, bf16[8,2,256,128]{3,2,1,0:T(8,128)(2,1)S(1)} %all-to-all-done.refs_0_.refs_2_, ...), custom_call_target="tpu_custom_call", output_to_operand_aliasing={{}: (5, {})} | custom-call | flops 4294967296 | bytes 8388608 | tf_op jit(solution)/shard_map/correlate/pallas_call | solution.py:154
  152.2 4.5 %collective-permute-start.9 = (bf16[4,256,256]{2,1,0:T(8,128)(2,1)S(1)}, bf16[4,256,256]{2,1,0:T(8,128)(2,1)S(1)}, u32[]{:S(2)}, u32[]{:S(2)}) collective-permute-start(bf16[4,256,256]{2,1,0:T(8,128)(2,1)S(1)} %get-tuple-element.83), channel_id=1, source_target_pairs={{0,1},{1,2},{4,5},{5,6},{8,9},{9,10},{12,13},{13,14},{16,17},{17,1... | collective-permute-start | bytes 1572872 | tf_op jit(solution)/shard_map/ppermute | solution.py:466
  161.1 5.4 %collective-permute-start.7 = (bf16[4,256,256]{2,1,0:T(8,128)(2,1)S(1)}, bf16[4,256,256]{2,1,0:T(8,128)(2,1)S(1)}, u32[]{:S(2)}, u32[]{:S(2)}) collective-permute-start(bf16[4,256,256]{2,1,0:T(8,128)(2,1)S(1)} %get-tuple-element.81), channel_id=1, source_target_pairs={{0,1},{1,2},{2,3},{4,5},{5,6},{6,7},{8,9},{9,10},{10,11},{12,13},{... | collective-permute-start | bytes 1572872 | tf_op jit(solution)/shard_map/ppermute | solution.py:466
  173.3 5.4 %collective-permute-start.13 = (bf16[4,256,256]{2,1,0:T(8,128)(2,1)S(1)}, bf16[4,256,256]{2,1,0:T(8,128)(2,1)S(1)}, u32[]{:S(2)}, u32[]{:S(2)}) collective-permute-start(bf16[4,256,256]{2,1,0:T(8,128)(2,1)S(1)} %get-tuple-element.91), channel_id=1, source_target_pairs={{0,1},{1,2},{2,3},{4,5},{5,6},{6,7},{8,9},{9,10},{10,11},{12,13},{... | collective-permute-start | bytes 1572872 | tf_op jit(solution)/shard_map/ppermute | solution.py:466
  181.5 4.4 %hop.23 = (bf16[74,256,256]{2,1,0:T(8,128)(2,1)}, bf16[74,256,256]{2,1,0:T(8,128)(2,1)}, bf16[4,256,256]{2,1,0:T(8,128)(2,1)S(1)}, bf16[4,256,256]{2,1,0:T(8,128)(2,1)S(1)}) custom-call(s32[17,8]{1,0:T(8,128)S(1)} %dynamic-slice_bitcast_fusion.tab, ...), custom_call_target="tpu_custom_call", output_to_operand_aliasing={{0}: (5, {}), {1}: (6, {})} | custom-call | flops 1048576 | bytes 5242880 | tf_op jit(solution)/shard_map/hop/pallas_call | solution.py:308
  191.6 4.4 %hop.24 = (bf16[74,256,256]{2,1,0:T(8,128)(2,1)}, bf16[74,256,256]{2,1,0:T(8,128)(2,1)}, bf16[4,256,256]{2,1,0:T(8,128)(2,1)S(1)}, bf16[4,256,256]{2,1,0:T(8,128)(2,1)S(1)}) custom-call(s32[17,8]{1,0:T(8,128)S(1)} %dynamic-slice_bitcast_fusion.tab, ...), custom_call_target="tpu_custom_call", output_to_operand_aliasing={{0}: (5, {}), {1}: (6, {})} | custom-call | flops 1048576 | bytes 5242880 | tf_op jit(solution)/shard_map/hop/pallas_call | solution.py:308
  196.0 5.2 %collective-permute-start.17 = (bf16[4,256,256]{2,1,0:T(8,128)(2,1)S(1)}, bf16[4,256,256]{2,1,0:T(8,128)(2,1)S(1)}, u32[]{:S(2)}, u32[]{:S(2)}) collective-permute-start(bf16[4,256,256]{2,1,0:T(8,128)(2,1)S(1)} %get-tuple-element.99), channel_id=1, source_target_pairs={{0,1},{1,2},{2,3},{4,5},{5,6},{6,7},{8,9},{9,10},{10,11},{12,13},{... | collective-permute-start | bytes 1572872 | tf_op jit(solution)/shard_map/ppermute | solution.py:466
  207.1 5.2 %collective-permute-start.15 = (bf16[4,256,256]{2,1,0:T(8,128)(2,1)S(1)}, bf16[4,256,256]{2,1,0:T(8,128)(2,1)S(1)}, u32[]{:S(2)}, u32[]{:S(2)}) collective-permute-start(bf16[4,256,256]{2,1,0:T(8,128)(2,1)S(1)} %get-tuple-element.97), channel_id=1, source_target_pairs={{0,1},{1,2},{2,3},{4,5},{5,6},{6,7},{8,9},{9,10},{10,11},{12,13},{... | collective-permute-start | bytes 1572872 | tf_op jit(solution)/shard_map/ppermute | solution.py:466
  214.0 4.4 %hop.26 = (bf16[74,256,256]{2,1,0:T(8,128)(2,1)}, bf16[74,256,256]{2,1,0:T(8,128)(2,1)}, bf16[4,256,256]{2,1,0:T(8,128)(2,1)S(1)}, bf16[4,256,256]{2,1,0:T(8,128)(2,1)S(1)}) custom-call(s32[17,8]{1,0:T(8,128)S(1)} %dynamic-slice_bitcast_fusion.tab, ...), custom_call_target="tpu_custom_call", output_to_operand_aliasing={{0}: (5, {}), {1}: (6, {})} | custom-call | flops 1048576 | bytes 5242880 | tf_op jit(solution)/shard_map/hop/pallas_call | solution.py:308
  218.4 5.2 %collective-permute-start.21 = (bf16[4,256,256]{2,1,0:T(8,128)(2,1)S(1)}, bf16[4,256,256]{2,1,0:T(8,128)(2,1)S(1)}, u32[]{:S(2)}, u32[]{:S(2)}) collective-permute-start(bf16[4,256,256]{2,1,0:T(8,128)(2,1)S(1)} %get-tuple-element.107), channel_id=1, source_target_pairs={{0,1},{1,2},{2,3},{4,5},{5,6},{6,7},{8,9},{9,10},{10,11},{12,13},{... | collective-permute-start | bytes 1572872 | tf_op jit(solution)/shard_map/ppermute | solution.py:466
  229.6 5.2 %collective-permute-start.19 = (bf16[4,256,256]{2,1,0:T(8,128)(2,1)S(1)}, bf16[4,256,256]{2,1,0:T(8,128)(2,1)S(1)}, u32[]{:S(2)}, u32[]{:S(2)}) collective-permute-start(bf16[4,256,256]{2,1,0:T(8,128)(2,1)S(1)} %get-tuple-element.105), channel_id=1, source_target_pairs={{0,1},{1,2},{2,3},{4,5},{5,6},{6,7},{8,9},{9,10},{10,11},{12,13},{... | collective-permute-start | bytes 1572872 | tf_op jit(solution)/shard_map/ppermute | solution.py:466
  236.5 4.4 %hop.28 = (bf16[74,256,256]{2,1,0:T(8,128)(2,1)}, bf16[74,256,256]{2,1,0:T(8,128)(2,1)}, bf16[4,256,256]{2,1,0:T(8,128)(2,1)S(1)}, bf16[4,256,256]{2,1,0:T(8,128)(2,1)S(1)}) custom-call(s32[17,8]{1,0:T(8,128)S(1)} %dynamic-slice_bitcast_fusion.tab, ...), custom_call_target="tpu_custom_call", output_to_operand_aliasing={{0}: (5, {}), {1}: (6, {})} | custom-call | flops 1048576 | bytes 5242880 | tf_op jit(solution)/shard_map/hop/pallas_call | solution.py:308
  240.9 5.2 %collective-permute-start.25 = (bf16[4,256,256]{2,1,0:T(8,128)(2,1)S(1)}, bf16[4,256,256]{2,1,0:T(8,128)(2,1)S(1)}, u32[]{:S(2)}, u32[]{:S(2)}) collective-permute-start(bf16[4,256,256]{2,1,0:T(8,128)(2,1)S(1)} %get-tuple-element.115), channel_id=1, source_target_pairs={{0,1},{1,2},{2,3},{4,5},{5,6},{6,7},{8,9},{9,10},{10,11},{12,13},{... | collective-permute-start | bytes 1572872 | tf_op jit(solution)/shard_map/ppermute | solution.py:466
  247.7 4.4 %hop.29 = (bf16[74,256,256]{2,1,0:T(8,128)(2,1)}, bf16[74,256,256]{2,1,0:T(8,128)(2,1)}, bf16[4,256,256]{2,1,0:T(8,128)(2,1)S(1)}, bf16[4,256,256]{2,1,0:T(8,128)(2,1)S(1)}) custom-call(s32[17,8]{1,0:T(8,128)S(1)} %dynamic-slice_bitcast_fusion.tab, ...), custom_call_target="tpu_custom_call", output_to_operand_aliasing={{0}: (5, {}), {1}: (6, {})} | custom-call | flops 1048576 | bytes 5242880 | tf_op jit(solution)/shard_map/hop/pallas_call | solution.py:308
  252.1 5.2 %collective-permute-start.23 = (bf16[4,256,256]{2,1,0:T(8,128)(2,1)S(1)}, bf16[4,256,256]{2,1,0:T(8,128)(2,1)S(1)}, u32[]{:S(2)}, u32[]{:S(2)}) collective-permute-start(bf16[4,256,256]{2,1,0:T(8,128)(2,1)S(1)} %get-tuple-element.113), channel_id=1, source_target_pairs={{0,1},{1,2},{2,3},{4,5},{5,6},{6,7},{8,9},{9,10},{10,11},{12,13},{... | collective-permute-start | bytes 1572872 | tf_op jit(solution)/shard_map/ppermute | solution.py:466
  258.9 4.4 %hop.30 = (bf16[74,256,256]{2,1,0:T(8,128)(2,1)}, bf16[74,256,256]{2,1,0:T(8,128)(2,1)}, bf16[4,256,256]{2,1,0:T(8,128)(2,1)S(1)}, bf16[4,256,256]{2,1,0:T(8,128)(2,1)S(1)}) custom-call(s32[17,8]{1,0:T(8,128)S(1)} %dynamic-slice_bitcast_fusion.tab, ...), custom_call_target="tpu_custom_call", output_to_operand_aliasing={{0}: (5, {}), {1}: (6, {})} | custom-call | flops 1048576 | bytes 5242880 | tf_op jit(solution)/shard_map/hop/pallas_call | solution.py:308
  263.3 5.2 %collective-permute-start.29 = (bf16[4,256,256]{2,1,0:T(8,128)(2,1)S(1)}, bf16[4,256,256]{2,1,0:T(8,128)(2,1)S(1)}, u32[]{:S(2)}, u32[]{:S(2)}) collective-permute-start(bf16[4,256,256]{2,1,0:T(8,128)(2,1)S(1)} %get-tuple-element.123), channel_id=1, source_target_pairs={{0,1},{1,2},{4,5},{5,6},{8,9},{9,10},{12,13},{13,14},{16,17},{17,1... | collective-permute-start | bytes 1572872 | tf_op jit(solution)/shard_map/ppermute | solution.py:466
  270.2 4.5 %hop.31 = (bf16[74,256,256]{2,1,0:T(8,128)(2,1)}, bf16[74,256,256]{2,1,0:T(8,128)(2,1)}, bf16[4,256,256]{2,1,0:T(8,128)(2,1)}, bf16[4,256,256]{2,1,0:T(8,128)(2,1)}) custom-call(s32[17,8]{1,0:T(8,128)S(1)} %dynamic-slice_bitcast_fusion.tab, ...), custom_call_target="tpu_custom_call", output_to_operand_aliasing={{0}: (5, {}), {1}: (6, {})} | custom-call | flops 1048576 | bytes 5242880 | tf_op jit(solution)/shard_map/hop/pallas_call | solution.py:308
  274.7 5.2 %collective-permute-start.27 = (bf16[4,256,256]{2,1,0:T(8,128)(2,1)}, bf16[4,256,256]{2,1,0:T(8,128)(2,1)S(1)}, u32[]{:S(2)}, u32[]{:S(2)}) collective-permute-start(bf16[4,256,256]{2,1,0:T(8,128)(2,1)} %get-tuple-element.121), channel_id=1, source_target_pairs={{0,1},{4,5},{8,9},{12,13},{16,17},{20,21},{24,25},{28,29}} | collective-permute-start | bytes 1572872 | tf_op jit(solution)/shard_map/ppermute | solution.py:466
  286.3 4.5 %collective-permute-done.27.refs_2_ = bf16[4,256,256]{2,1,0:T(8,128)(2,1)S(1)} collective-permute-done((bf16[4,256,256]{2,1,0:T(8,128)(2,1)}, bf16[4,256,256]{2,1,0:T(8,128)(2,1)S(1)}, u32[]{:S(2)}, u32[]{:S(2)}) %collective-permute-start.27) | collective-permute-done | bytes 524320 | tf_op jit(solution)/shard_map/ppermute | solution.py:466
  294.9 17.6 %visibility_rows.1 = f32[16384,128]{1,0:T(8,128)} custom-call(s32[32]{0:T(128)S(1)} %fusion.1.tab, s32[16]{0:T(128)S(1)} %fusion.2.mode, s32[2]{0:T(128)S(1)} %pad_add_fusion.ends, f32[74,256,256]{2,1,0:T(8,128)} %correlate.5.refs_0_.refs_1_.refs_2_.refs_3_.refs_4_.refs_5_.refs_6_.refs_7_.refs_8_.refs_9_.refs_10_.refs_11_.refs_12_.refs_13_.refs_14_.refs_15_, ...), custom_call_target="tpu_custom_call" | custom-call | tf_op jit(solution)/shard_map/visibility_rows/pallas_call | solution.py:393
  (108 shorter events, 106.5 us)
Async XLA Ops:
  16.1 22.3 %all-to-all-start.3 = ((bf16[8,2,256,128]{3,2,1,0:T(8,128)(2,1)}), bf16[8,2,256,128]{3,2,1,0:T(8,128)(2,1)S(1)}, u32[]{:S(2)}, u32[]{:S(2)}) async-start(bf16[8,2,256,128]{3,2,1,0:T(8,128)(2,1)} %filterbank_h0_t1.1), calls=%async_computation.3 | async-start | bytes 2097152 | tf_op jit(solution)/shard_map/all_to_all | solution.py:435
  23.6 26.9 %collective-permute-start = (bf16[2,256,1024]{2,1,0:T(8,128)(2,1)}, bf16[2,256,1024]{2,1,0:T(8,128)(2,1)S(1)}, u32[]{:S(2)}, u32[]{:S(2)}) collective-permute-start(bf16[2,256,1024]{2,1,0:T(8,128)(2,1)} %slice.3), channel_id=1, source_target_pairs={{0,1},{1,2},{2,3},{4,5},{5,6},{6,7},{8,9},{9,10},{10,11},{12,13},{... | collective-permute-start | bytes 3145736 | tf_op jit(solution)/shard_map/ppermute | solution.py:424
  39.4 22.8 %all-to-all-start.1 = ((bf16[8,2,256,128]{3,2,1,0:T(8,128)(2,1)}), bf16[8,2,256,128]{3,2,1,0:T(8,128)(2,1)S(1)}, u32[]{:S(2)}, u32[]{:S(2)}) async-start(bf16[8,2,256,128]{3,2,1,0:T(8,128)(2,1)} %filterbank_h1_t1.1), calls=%async_computation.1 | async-start | bytes 2097152 | tf_op jit(solution)/shard_map/all_to_all | solution.py:435
  62.2 19.3 %all-to-all-start.2 = ((bf16[8,2,256,128]{3,2,1,0:T(8,128)(2,1)}), bf16[8,2,256,128]{3,2,1,0:T(8,128)(2,1)S(1)}, u32[]{:S(2)}, u32[]{:S(2)}) async-start(bf16[8,2,256,128]{3,2,1,0:T(8,128)(2,1)} %copy-done.7), calls=%async_computation.2 | async-start | bytes 2097152 | tf_op jit(solution)/shard_map/all_to_all | solution.py:435
  82.5 43.3 %all-to-all-start = ((bf16[8,2,256,128]{3,2,1,0:T(8,128)(2,1)}), bf16[8,2,256,128]{3,2,1,0:T(8,128)(2,1)S(1)}, u32[]{:S(2)}, u32[]{:S(2)}) async-start(bf16[8,2,256,128]{3,2,1,0:T(8,128)(2,1)} %copy-done.6), calls=%async_computation | async-start | bytes 2097152 | tf_op jit(solution)/shard_map/all_to_all | solution.py:435
  99.8 15.6 %collective-permute-start.1 = (bf16[4,256,256]{2,1,0:T(8,128)(2,1)S(1)}, bf16[4,256,256]{2,1,0:T(8,128)(2,1)S(1)}, u32[]{:S(2)}, u32[]{:S(2)}) collective-permute-start(bf16[4,256,256]{2,1,0:T(8,128)(2,1)S(1)} %get-tuple-element.69), channel_id=1, source_target_pairs={{0,1},{4,5},{8,9},{12,13},{16,17},{20,21},{24,25},{28,29}} | collective-permute-start | bytes 1572872 | tf_op jit(solution)/shard_map/ppermute | solution.py:466
  108.1 39.0 %collective-permute-start.5 = (bf16[4,256,256]{2,1,0:T(8,128)(2,1)}, bf16[4,256,256]{2,1,0:T(8,128)(2,1)S(1)}, u32[]{:S(2)}, u32[]{:S(2)}) collective-permute-start(bf16[4,256,256]{2,1,0:T(8,128)(2,1)} %get-tuple-element.75), channel_id=1, source_target_pairs={{0,1},{4,5},{8,9},{12,13},{16,17},{20,21},{24,25},{28,29}} | collective-permute-start | bytes 1572872 | tf_op jit(solution)/shard_map/ppermute | solution.py:466
  109.4 37.7 %collective-permute-start.6 = (bf16[4,256,256]{2,1,0:T(8,128)(2,1)}, bf16[4,256,256]{2,1,0:T(8,128)(2,1)}, u32[]{:S(2)}, u32[]{:S(2)}) collective-permute-start(bf16[4,256,256]{2,1,0:T(8,128)(2,1)} %get-tuple-element.76), channel_id=1, source_target_pairs={{3,2},{7,6},{11,10},{15,14},{19,18},{23,22},{27,26},{31,30}} | collective-permute-start | bytes 1572872 | tf_op jit(solution)/shard_map/ppermute | solution.py:467
  119.9 36.9 %collective-permute-start.3 = (bf16[4,256,256]{2,1,0:T(8,128)(2,1)}, bf16[4,256,256]{2,1,0:T(8,128)(2,1)S(1)}, u32[]{:S(2)}, u32[]{:S(2)}) collective-permute-start(bf16[4,256,256]{2,1,0:T(8,128)(2,1)} %get-tuple-element.73), channel_id=1, source_target_pairs={{0,1},{1,2},{4,5},{5,6},{8,9},{9,10},{12,13},{13,14},{16,17},{17,1... | collective-permute-start | bytes 1572872 | tf_op jit(solution)/shard_map/ppermute | solution.py:466
  124.3 32.5 %collective-permute-start.4 = (bf16[4,256,256]{2,1,0:T(8,128)(2,1)}, bf16[4,256,256]{2,1,0:T(8,128)(2,1)}, u32[]{:S(2)}, u32[]{:S(2)}) collective-permute-start(bf16[4,256,256]{2,1,0:T(8,128)(2,1)} %get-tuple-element.74), channel_id=1, source_target_pairs={{3,2},{2,1},{7,6},{6,5},{11,10},{10,9},{15,14},{14,13},{19,18},{18... | collective-permute-start | bytes 1572872 | tf_op jit(solution)/shard_map/ppermute | solution.py:467
  151.5 16.2 %collective-permute-start.10 = (bf16[4,256,256]{2,1,0:T(8,128)(2,1)S(1)}, bf16[4,256,256]{2,1,0:T(8,128)(2,1)S(1)}, u32[]{:S(2)}, u32[]{:S(2)}) collective-permute-start(bf16[4,256,256]{2,1,0:T(8,128)(2,1)S(1)} %get-tuple-element.84), channel_id=1, source_target_pairs={{3,2},{2,1},{7,6},{6,5},{11,10},{10,9},{15,14},{14,13},{19,18},{18... | collective-permute-start | bytes 1572872 | tf_op jit(solution)/shard_map/ppermute | solution.py:467
  152.2 16.9 %collective-permute-start.9 = (bf16[4,256,256]{2,1,0:T(8,128)(2,1)S(1)}, bf16[4,256,256]{2,1,0:T(8,128)(2,1)S(1)}, u32[]{:S(2)}, u32[]{:S(2)}) collective-permute-start(bf16[4,256,256]{2,1,0:T(8,128)(2,1)S(1)} %get-tuple-element.83), channel_id=1, source_target_pairs={{0,1},{1,2},{4,5},{5,6},{8,9},{9,10},{12,13},{13,14},{16,17},{17,1... | collective-permute-start | bytes 1572872 | tf_op jit(solution)/shard_map/ppermute | solution.py:466
  161.1 19.2 %collective-permute-start.7 = (bf16[4,256,256]{2,1,0:T(8,128)(2,1)S(1)}, bf16[4,256,256]{2,1,0:T(8,128)(2,1)S(1)}, u32[]{:S(2)}, u32[]{:S(2)}) collective-permute-start(bf16[4,256,256]{2,1,0:T(8,128)(2,1)S(1)} %get-tuple-element.81), channel_id=1, source_target_pairs={{0,1},{1,2},{2,3},{4,5},{5,6},{6,7},{8,9},{9,10},{10,11},{12,13},{... | collective-permute-start | bytes 1572872 | tf_op jit(solution)/shard_map/ppermute | solution.py:466
  166.4 15.1 %collective-permute-start.8 = (bf16[4,256,256]{2,1,0:T(8,128)(2,1)S(1)}, bf16[4,256,256]{2,1,0:T(8,128)(2,1)S(1)}, u32[]{:S(2)}, u32[]{:S(2)}) collective-permute-start(bf16[4,256,256]{2,1,0:T(8,128)(2,1)S(1)} %get-tuple-element.82), channel_id=1, source_target_pairs={{3,2},{2,1},{1,0},{7,6},{6,5},{5,4},{11,10},{10,9},{9,8},{15,14},{... | collective-permute-start | bytes 1572872 | tf_op jit(solution)/shard_map/ppermute | solution.py:467
  173.3 18.3 %collective-permute-start.13 = (bf16[4,256,256]{2,1,0:T(8,128)(2,1)S(1)}, bf16[4,256,256]{2,1,0:T(8,128)(2,1)S(1)}, u32[]{:S(2)}, u32[]{:S(2)}) collective-permute-start(bf16[4,256,256]{2,1,0:T(8,128)(2,1)S(1)} %get-tuple-element.91), channel_id=1, source_target_pairs={{0,1},{1,2},{2,3},{4,5},{5,6},{6,7},{8,9},{9,10},{10,11},{12,13},{... | collective-permute-start | bytes 1572872 | tf_op jit(solution)/shard_map/ppermute | solution.py:466
  178.7 12.9 %collective-permute-start.14 = (bf16[4,256,256]{2,1,0:T(8,128)(2,1)S(1)}, bf16[4,256,256]{2,1,0:T(8,128)(2,1)S(1)}, u32[]{:S(2)}, u32[]{:S(2)}) collective-permute-start(bf16[4,256,256]{2,1,0:T(8,128)(2,1)S(1)} %get-tuple-element.92), channel_id=1, source_target_pairs={{3,2},{2,1},{1,0},{7,6},{6,5},{5,4},{11,10},{10,9},{9,8},{15,14},{... | collective-permute-start | bytes 1572872 | tf_op jit(solution)/shard_map/ppermute | solution.py:467
  185.9 16.9 %collective-permute-start.11 = (bf16[4,256,256]{2,1,0:T(8,128)(2,1)S(1)}, bf16[4,256,256]{2,1,0:T(8,128)(2,1)S(1)}, u32[]{:S(2)}, u32[]{:S(2)}) collective-permute-start(bf16[4,256,256]{2,1,0:T(8,128)(2,1)S(1)} %get-tuple-element.89), channel_id=1, source_target_pairs={{0,1},{1,2},{4,5},{5,6},{8,9},{9,10},{12,13},{13,14},{16,17},{17,1... | collective-permute-start | bytes 1572872 | tf_op jit(solution)/shard_map/ppermute | solution.py:466
  196.0 18.0 %collective-permute-start.17 = (bf16[4,256,256]{2,1,0:T(8,128)(2,1)S(1)}, bf16[4,256,256]{2,1,0:T(8,128)(2,1)S(1)}, u32[]{:S(2)}, u32[]{:S(2)}) collective-permute-start(bf16[4,256,256]{2,1,0:T(8,128)(2,1)S(1)} %get-tuple-element.99), channel_id=1, source_target_pairs={{0,1},{1,2},{2,3},{4,5},{5,6},{6,7},{8,9},{9,10},{10,11},{12,13},{... | collective-permute-start | bytes 1572872 | tf_op jit(solution)/shard_map/ppermute | solution.py:466
  201.1 12.9 %collective-permute-start.18 = (bf16[4,256,256]{2,1,0:T(8,128)(2,1)S(1)}, bf16[4,256,256]{2,1,0:T(8,128)(2,1)S(1)}, u32[]{:S(2)}, u32[]{:S(2)}) collective-permute-start(bf16[4,256,256]{2,1,0:T(8,128)(2,1)S(1)} %get-tuple-element.100), channel_id=1, source_target_pairs={{3,2},{2,1},{1,0},{7,6},{6,5},{5,4},{11,10},{10,9},{9,8},{15,14},{... | collective-permute-start | bytes 1572872 | tf_op jit(solution)/shard_map/ppermute | solution.py:467
  207.1 18.1 %collective-permute-start.15 = (bf16[4,256,256]{2,1,0:T(8,128)(2,1)S(1)}, bf16[4,256,256]{2,1,0:T(8,128)(2,1)S(1)}, u32[]{:S(2)}, u32[]{:S(2)}) collective-permute-start(bf16[4,256,256]{2,1,0:T(8,128)(2,1)S(1)} %get-tuple-element.97), channel_id=1, source_target_pairs={{0,1},{1,2},{2,3},{4,5},{5,6},{6,7},{8,9},{9,10},{10,11},{12,13},{... | collective-permute-start | bytes 1572872 | tf_op jit(solution)/shard_map/ppermute | solution.py:466
  212.4 12.9 %collective-permute-start.16 = (bf16[4,256,256]{2,1,0:T(8,128)(2,1)S(1)}, bf16[4,256,256]{2,1,0:T(8,128)(2,1)S(1)}, u32[]{:S(2)}, u32[]{:S(2)}) collective-permute-start(bf16[4,256,256]{2,1,0:T(8,128)(2,1)S(1)} %get-tuple-element.98), channel_id=1, source_target_pairs={{3,2},{2,1},{1,0},{7,6},{6,5},{5,4},{11,10},{10,9},{9,8},{15,14},{... | collective-permute-start | bytes 1572872 | tf_op jit(solution)/shard_map/ppermute | solution.py:467
  218.4 18.1 %collective-permute-start.21 = (bf16[4,256,256]{2,1,0:T(8,128)(2,1)S(1)}, bf16[4,256,256]{2,1,0:T(8,128)(2,1)S(1)}, u32[]{:S(2)}, u32[]{:S(2)}) collective-permute-start(bf16[4,256,256]{2,1,0:T(8,128)(2,1)S(1)} %get-tuple-element.107), channel_id=1, source_target_pairs={{0,1},{1,2},{2,3},{4,5},{5,6},{6,7},{8,9},{9,10},{10,11},{12,13},{... | collective-permute-start | bytes 1572872 | tf_op jit(solution)/shard_map/ppermute | solution.py:466
  223.6 12.9 %collective-permute-start.22 = (bf16[4,256,256]{2,1,0:T(8,128)(2,1)S(1)}, bf16[4,256,256]{2,1,0:T(8,128)(2,1)S(1)}, u32[]{:S(2)}, u32[]{:S(2)}) collective-permute-start(bf16[4,256,256]{2,1,0:T(8,128)(2,1)S(1)} %get-tuple-element.108), channel_id=1, source_target_pairs={{3,2},{2,1},{1,0},{7,6},{6,5},{5,4},{11,10},{10,9},{9,8},{15,14},{... | collective-permute-start | bytes 1572872 | tf_op jit(solution)/shard_map/ppermute | solution.py:467
  229.6 18.1 %collective-permute-start.19 = (bf16[4,256,256]{2,1,0:T(8,128)(2,1)S(1)}, bf16[4,256,256]{2,1,0:T(8,128)(2,1)S(1)}, u32[]{:S(2)}, u32[]{:S(2)}) collective-permute-start(bf16[4,256,256]{2,1,0:T(8,128)(2,1)S(1)} %get-tuple-element.105), channel_id=1, source_target_pairs={{0,1},{1,2},{2,3},{4,5},{5,6},{6,7},{8,9},{9,10},{10,11},{12,13},{... | collective-permute-start | bytes 1572872 | tf_op jit(solution)/shard_map/ppermute | solution.py:466
  234.9 12.9 %collective-permute-start.20 = (bf16[4,256,256]{2,1,0:T(8,128)(2,1)S(1)}, bf16[4,256,256]{2,1,0:T(8,128)(2,1)S(1)}, u32[]{:S(2)}, u32[]{:S(2)}) collective-permute-start(bf16[4,256,256]{2,1,0:T(8,128)(2,1)S(1)} %get-tuple-element.106), channel_id=1, source_target_pairs={{3,2},{2,1},{1,0},{7,6},{6,5},{5,4},{11,10},{10,9},{9,8},{15,14},{... | collective-permute-start | bytes 1572872 | tf_op jit(solution)/shard_map/ppermute | solution.py:467
  240.9 18.1 %collective-permute-start.25 = (bf16[4,256,256]{2,1,0:T(8,128)(2,1)S(1)}, bf16[4,256,256]{2,1,0:T(8,128)(2,1)S(1)}, u32[]{:S(2)}, u32[]{:S(2)}) collective-permute-start(bf16[4,256,256]{2,1,0:T(8,128)(2,1)S(1)} %get-tuple-element.115), channel_id=1, source_target_pairs={{0,1},{1,2},{2,3},{4,5},{5,6},{6,7},{8,9},{9,10},{10,11},{12,13},{... | collective-permute-start | bytes 1572872 | tf_op jit(solution)/shard_map/ppermute | solution.py:466
  246.1 12.9 %collective-permute-start.26 = (bf16[4,256,256]{2,1,0:T(8,128)(2,1)S(1)}, bf16[4,256,256]{2,1,0:T(8,128)(2,1)S(1)}, u32[]{:S(2)}, u32[]{:S(2)}) collective-permute-start(bf16[4,256,256]{2,1,0:T(8,128)(2,1)S(1)} %get-tuple-element.116), channel_id=1, source_target_pairs={{3,2},{2,1},{1,0},{7,6},{6,5},{5,4},{11,10},{10,9},{9,8},{15,14},{... | collective-permute-start | bytes 1572872 | tf_op jit(solution)/shard_map/ppermute | solution.py:467
  252.1 18.1 %collective-permute-start.23 = (bf16[4,256,256]{2,1,0:T(8,128)(2,1)S(1)}, bf16[4,256,256]{2,1,0:T(8,128)(2,1)S(1)}, u32[]{:S(2)}, u32[]{:S(2)}) collective-permute-start(bf16[4,256,256]{2,1,0:T(8,128)(2,1)S(1)} %get-tuple-element.113), channel_id=1, source_target_pairs={{0,1},{1,2},{2,3},{4,5},{5,6},{6,7},{8,9},{9,10},{10,11},{12,13},{... | collective-permute-start | bytes 1572872 | tf_op jit(solution)/shard_map/ppermute | solution.py:466
  257.3 12.9 %collective-permute-start.24 = (bf16[4,256,256]{2,1,0:T(8,128)(2,1)S(1)}, bf16[4,256,256]{2,1,0:T(8,128)(2,1)S(1)}, u32[]{:S(2)}, u32[]{:S(2)}) collective-permute-start(bf16[4,256,256]{2,1,0:T(8,128)(2,1)S(1)} %get-tuple-element.114), channel_id=1, source_target_pairs={{3,2},{2,1},{1,0},{7,6},{6,5},{5,4},{11,10},{10,9},{9,8},{15,14},{... | collective-permute-start | bytes 1572872 | tf_op jit(solution)/shard_map/ppermute | solution.py:467
  263.3 18.8 %collective-permute-start.29 = (bf16[4,256,256]{2,1,0:T(8,128)(2,1)S(1)}, bf16[4,256,256]{2,1,0:T(8,128)(2,1)S(1)}, u32[]{:S(2)}, u32[]{:S(2)}) collective-permute-start(bf16[4,256,256]{2,1,0:T(8,128)(2,1)S(1)} %get-tuple-element.123), channel_id=1, source_target_pairs={{0,1},{1,2},{4,5},{5,6},{8,9},{9,10},{12,13},{13,14},{16,17},{17,1... | collective-permute-start | bytes 1572872 | tf_op jit(solution)/shard_map/ppermute | solution.py:466
  268.5 13.6 %collective-permute-start.30 = (bf16[4,256,256]{2,1,0:T(8,128)(2,1)S(1)}, bf16[4,256,256]{2,1,0:T(8,128)(2,1)S(1)}, u32[]{:S(2)}, u32[]{:S(2)}) collective-permute-start(bf16[4,256,256]{2,1,0:T(8,128)(2,1)S(1)} %get-tuple-element.124), channel_id=1, source_target_pairs={{3,2},{2,1},{7,6},{6,5},{11,10},{10,9},{15,14},{14,13},{19,18},{18... | collective-permute-start | bytes 1572872 | tf_op jit(solution)/shard_map/ppermute | solution.py:467
  274.7 16.1 %collective-permute-start.27 = (bf16[4,256,256]{2,1,0:T(8,128)(2,1)}, bf16[4,256,256]{2,1,0:T(8,128)(2,1)S(1)}, u32[]{:S(2)}, u32[]{:S(2)}) collective-permute-start(bf16[4,256,256]{2,1,0:T(8,128)(2,1)} %get-tuple-element.121), channel_id=1, source_target_pairs={{0,1},{4,5},{8,9},{12,13},{16,17},{20,21},{24,25},{28,29}} | collective-permute-start | bytes 1572872 | tf_op jit(solution)/shard_map/ppermute | solution.py:466
  (15 other events, 85.4 us)

commit v2 on v1

v2 whole, which is shorter than its diff:
```python
import functools
import math

import jax
import jax.numpy as jnp
import numpy as np
from jax import lax
from jax.experimental import pallas as pl
from jax.experimental.pallas import tpu as pltpu
from jax.sharding import PartitionSpec as P

F32, BF16 = jnp.float32, jnp.bfloat16
GROUP = 8
LANES = 128
VMEM_LIMIT = 52 * 1024 * 1024


def params(limit=VMEM_LIMIT):
    return pltpu.CompilerParams(vmem_limit_bytes=limit)


def weights_kernel(taps_ref, trig_ref, out_ref, wide):
    taps, length = taps_ref.shape
    rows = trig_ref.shape[0]
    size = GROUP * length
    flat = jnp.concatenate([taps_ref[taps - 1 - k : taps - k, :] for k in range(taps)], axis=1)
    base = flat * jnp.concatenate([trig_ref[...]] * taps, axis=1)
    for f in range(GROUP):
        before = jnp.zeros((rows, (f + 1) * length), F32)
        moved = [before, base]
        if f < GROUP - 1:
            moved.append(jnp.zeros((rows, (GROUP - 1 - f) * length), F32))
        moved = jnp.concatenate(moved, axis=1)
        for t in range(wide.shape[0]):
            wide[t, pl.ds(f, rows, stride=GROUP), :] = moved[:, t * LANES : (t + 1) * LANES]
    n = rows * GROUP
    each = size // LANES
    for t in range(wide.shape[0]):
        full = wide[t]
        high = full.astype(BF16)
        low = (full - high.astype(F32)).astype(BF16)
        m, lanes = t // each, slice(t % each * LANES, (t % each + 1) * LANES)
        out_ref[2 * m * n : (2 * m + 1) * n, lanes] = high
        out_ref[(2 * m + 1) * n : (2 * m + 2) * n, lanes] = low


def filterbank_weights(filter_taps, channels):
    taps, length = filter_taps.shape
    phase = np.arange(length)[None, :] * np.arange(channels)[:, None] % length
    angle = phase * (2.0 * math.pi / length)
    trig = np.stack([np.cos(angle), np.sin(angle)]).reshape(2 * channels, length)
    rows = 2 * channels * GROUP
    blocks = taps // GROUP + 1
    return pl.pallas_call(
        weights_kernel,
        out_shape=jax.ShapeDtypeStruct((blocks * 2 * rows, GROUP * length), BF16),
        scratch_shapes=[pltpu.VMEM((blocks * GROUP * length // LANES, rows, LANES), F32)],
        compiler_params=params(),
        name="weights",
    )(filter_taps, jnp.asarray(trig.astype(np.float32)))


def filterbank_kernel(channels, length, head_ref, v_ref, w_ref, s_ref, after_ref, out_ref, token_ref, carry):
    del after_ref, token_ref
    step = pl.program_id(0)
    _, part, lanes = v_ref.shape
    size = GROUP * length
    half = channels * GROUP
    rows = 2 * half
    blocks = w_ref.shape[0] // (2 * rows)
    scale = s_ref[...]

    def advance(ref, at):
        x = ref[:, :, at * size : (at + 1) * size].reshape(2 * part, size)
        r = lax.dot_general(w_ref[...], x, (((1,), (1,)), ((), ())), preferred_element_type=F32)
        third = [
            r[2 * m * rows : (2 * m + 1) * rows] + r[(2 * m + 1) * rows : (2 * m + 2) * rows]
            for m in range(blocks)
        ]
        done = carry[blocks - 2] + third[blocks - 1]
        for m in range(blocks - 2, 0, -1):
            carry[m] = carry[m - 1] + third[m]
        carry[0] = third[0]
        return done

    @pl.when(step == 0)
    def _():
        carry[...] = jnp.zeros_like(carry)
        for b in range(head_ref.shape[2] // size):
            advance(head_ref, b)

    def one(b):
        done = advance(v_ref, b)
        cos, sin = done[:half], done[half:]
        real = (cos[:, :part] + sin[:, part:]) * scale
        imag = (cos[:, part:] - sin[:, :part]) * scale
        return real, imag

    for b in range(0, lanes // size, 2):
        first, second = one(b), one(b + 1)
        for c in range(channels):
            take = slice(c * GROUP, (c + 1) * GROUP)
            for ri in range(2):
                both = jnp.concatenate([first[ri][take], second[ri][take]], axis=0)
                out_ref[c, ri, b * GROUP : (b + 2) * GROUP, :] = both.astype(BF16)


def filterbank(voltages, halo, weights, scale, length, channels, part, h, start, frames, after):
    block = min(frames, 64)
    lanes = block * length
    head = halo.shape[2]
    first = start * length
    if start == 0:
        before, head_map = halo, lambda s: (0, 0, 0)
    else:
        before, head_map = voltages, lambda s: (0, h, first // head - 1)
    blocks = head // (GROUP * length)
    return pl.pallas_call(
        functools.partial(filterbank_kernel, channels, length),
        grid=(frames // block,),
        in_specs=[
            pl.BlockSpec((2, part, head), head_map),
            pl.BlockSpec((2, part, lanes), lambda s: (0, h, first // lanes + s)),
            pl.BlockSpec(weights.shape, lambda s: (0, 0)),
            pl.BlockSpec((1, part), lambda s: (0, h)),
            pl.BlockSpec(memory_space=pl.ANY),
        ],
        out_specs=[
            pl.BlockSpec((channels, 2, block, part), lambda s: (0, 0, s, 0)),
            pl.BlockSpec(memory_space=pl.ANY),
        ],
        out_shape=[
            jax.ShapeDtypeStruct((channels, 2, frames, part), BF16),
            jax.ShapeDtypeStruct((8, LANES), F32),
        ],
        scratch_shapes=[pltpu.VMEM((blocks, 2 * channels * GROUP, 2 * part), F32)],
        compiler_params=params(),
        cost_estimate=pl.CostEstimate(
            flops=2 * weights.size * 2 * part * frames // GROUP,
            bytes_accessed=2 * 2 * part * frames * length,
            transcendentals=0,
        ),
        name=f"filterbank_h{h}_f{start}",
    )(before, voltages, weights, scale, after)


def correlate_kernel(nx, ny, span, weight, fresh, same, low, *refs):
    xs = refs[:nx]
    ys = xs if same else refs[nx : nx + ny]
    at = nx if same else nx + ny
    out_ref = refs[at] if fresh else refs[at + 1]
    i = pl.program_id(0) + low
    part = xs[0].shape[3]
    size = span * part
    count = ys[0].shape[0] // span

    def side(some, first, many, ri):
        wide = [
            jnp.concatenate([ref[first + d, ri] for d in range(many)], axis=1) for ref in some
        ]
        return wide[0] if len(wide) == 1 else jnp.concatenate(wide, axis=0)

    real, imag = side(xs, i * span, span, 0).T, side(xs, i * span, span, 1).T
    on_real = jnp.concatenate([real, imag], axis=0)
    on_imag = jnp.concatenate([imag, -real], axis=0)
    group = 2 if count % 2 == 0 else 1

    def columns_from(first):
        both = jnp.dot(on_real, side(ys, first * span, group * span, 0), preferred_element_type=F32)
        both = both + jnp.dot(
            on_imag, side(ys, first * span, group * span, 1), preferred_element_type=F32
        )
        both = both * weight
        for n in range(group):
            columns = slice(n * size, (n + 1) * size)
            out_ref[2 * (first + n)] = both[:size, columns]
            out_ref[2 * (first + n) + 1] = both[size:, columns]
            if same:

                @pl.when(i == first + n)
                def _():
                    row = lax.broadcasted_iota(jnp.int32, (size, size), 0)
                    col = lax.broadcasted_iota(jnp.int32, (size, size), 1)
                    out_ref[2 * (first + n)] = jnp.where(
                        row >= col, both[:size, columns], both[size:, columns]
                    )

    for first in range(0, count, group):
        if same and first > 0:
            pl.when(i >= first)(functools.partial(columns_from, first))
        else:
            columns_from(first)


def correlate(partial, total, slices, call, xs, ys, span, weight, same, low, high):
    size = span * xs[0].shape[3]
    frames = sum(x.shape[2] for x in xs)
    spectra = xs if same else xs + ys
    whole = [pl.BlockSpec(a.shape, lambda i: (0, 0, 0, 0)) for a in spectra]
    out_block = pl.BlockSpec((2 * slices, size, size), lambda i: (call * slices + low + i, 0, 0))
    shape = jax.ShapeDtypeStruct((total, size, size), F32)
    store = jax.ShapeDtypeStruct((total, size, size), BF16)
    fresh = partial is None
    anywhere = pl.BlockSpec(memory_space=pl.ANY)
    return pl.pallas_call(
        functools.partial(correlate_kernel, len(xs), len(ys), span, weight, fresh, same, low),
        grid=(high - low,),
        in_specs=whole + ([] if fresh else [anywhere]),
        out_specs=[out_block, anywhere, anywhere] if fresh else [out_block],
        out_shape=[shape, store, store] if fresh else [shape],
        input_output_aliases={} if fresh else {len(whole): 0},
        compiler_params=params(),
        cost_estimate=pl.CostEstimate(
            flops=8 * (high - low) * slices * size * size * frames,
            bytes_accessed=8 * (high - low) * slices * size * size,
            transcendentals=0,
        ),
        name="correlate",
    )(*spectra, *([] if fresh else [partial]))


class Plan:
    def __init__(self, slices, parts, count):
        self.slices, self.parts, self.count = slices, parts, count
        self.calls = []
        self.pair_at = {}
        for h in range(parts):
            for k in range(h, -1, -1):
                first = len(self.calls) * slices * slices
                self.calls.append((h, k))
                for i in range(slices):
                    for j in range(slices):
                        if k < h or j <= i:
                            self.pair_at[h, i, k, j] = first + i * slices + j
        self.spare = 2 * len(self.calls) * slices * slices
        self.total = self.spare + 2 * count
        self.right = self.messages(lambda i, j: max(i, j))
        self.left = self.messages(lambda i, j: slices - 1 - min(i, j))
        self.steps = 0
        for index in range(2 * (len(self.right) + len(self.left)) + 4 * slices):
            if self.senders(self.right, index) or self.senders(self.left, index):
                self.steps = index + 1

    def squares(self, h, i, k, j):
        at = 2 * self.pair_at[h, i, k, j]
        return (at, at) if (h, i) == (k, j) else (at, at + 1)

    def messages(self, reach):
        queues, last = [[] for _ in self.calls], []
        for (h, i, k, j) in self.pair_at:
            far = reach(i, j)
            if far:
                late = self.late(i, j) and self.late(j, i)
                for square in sorted(set(self.squares(h, i, k, j))):
                    (queues[self.call_of(h, k)] if far > 1 else last).append((-far, late, square))
        if self.slices == 2:
            queues, last = [last], []
        found = []
        for queue in [sorted(q) for q in queues] + [sorted(last)]:
            for at in range(0, len(queue), self.count):
                some = queue[at : at + self.count]
                ids = [square for _, _, square in some]
                found.append((ids, max(-far for far, _, _ in some)))
        return found

    def late(self, z, j):
        return (2 * z < self.slices) == (2 * j < self.slices)

    def first_ready(self):
        ready = 0
        ids, _ = self.outputs()
        for z in range(self.slices):
            for messages, place in ((self.right, z), (self.left, self.slices - 1 - z)):
                if place == 0:
                    continue
                for k, (squares, _) in enumerate(messages):
                    for j in range(self.slices):
                        if not self.late(z, j) and set(ids[z, :, j].ravel()) & set(squares):
                            ready = max(ready, k + 2 * place)
        return ready

    def senders(self, messages, step):
        places = []
        for place in range(self.slices - 1):
            k = step - 2 * place
            if 0 <= k < len(messages) and messages[k][1] > place:
                places.append(place)
        return places

    def table(self):
        rows = np.tile(
            self.spare + np.arange(2 * self.count, dtype=np.int32), (self.slices, self.steps + 2, 1)
        )
        for z in range(self.slices):
            for step in range(self.steps + 2):
                for side, (messages, place) in enumerate(
                    ((self.right, z), (self.left, self.slices - 1 - z))
                ):
                    k = step - 2 * place
                    if 0 <= k < len(messages):
                        for b, square in enumerate(messages[k][0]):
                            rows[z, step, side * self.count + b] = square
        return rows.reshape(-1)

    def call_of(self, h, k):
        return self.calls.index((h, k))

    def last_call(self, step):
        need = 0
        for messages in (self.right, self.left):
            for place in range(self.slices):
                k = step - 2 * place
                if 0 <= k < len(messages):
                    for square in messages[k][0]:
                        for (h, i, c, j), at in self.pair_at.items():
                            if at == square // 2:
                                need = max(need, self.call_of(h, c))
        return need

    def outputs(self):
        z_n, h_n = self.slices, self.parts
        ids = np.zeros((z_n, h_n, z_n, h_n, 2), np.int32)
        modes = np.zeros((z_n, h_n, z_n, h_n), np.int32)
        for z in range(z_n):
            for h in range(h_n):
                for j in range(z_n):
                    for k in range(h_n):
                        if (h, z, k, j) in self.pair_at:
                            ids[z, h, j, k] = self.squares(h, z, k, j)
                            modes[z, h, j, k] = 2 if (h, z) == (k, j) else 0
                        else:
                            ids[z, h, j, k] = self.squares(k, j, h, z)
                            modes[z, h, j, k] = 1
        return ids, modes


def hop_kernel(receives, sends, held, count, steps, step, tab, place, *refs):
    refs = list(refs)
    partial = refs.pop(0) if sends else None
    came = [refs.pop(0) for _ in range(2 if receives else 0)]
    outs = refs[held:]
    kept = [outs.pop(0) for _ in range(2 if receives else 0)]
    sent = [outs.pop(0) for _ in range(2 if sends else 0)]
    own = outs.pop(0) if sends else None
    sems = outs.pop(0)
    at = (place[0] * steps + step) * 2 * count
    slots = [(side, b) for side in range(2) for b in range(count)]
    loads, stores = [], []
    for side, b in slots:
        square = tab[at + side * count + b]
        if sends:
            loads.append(
                pltpu.make_async_copy(partial.at[square], own.at[side, b], sems.at[0, side, b])
            )
            loads[-1].start()
        if receives:
            stores.append(
                pltpu.make_async_copy(came[side].at[b], kept[side].at[square], sems.at[1, side, b])
            )
            stores[-1].start()
    if sends:
        for load, (side, b) in zip(loads, slots):
            load.wait()
            total = own[side, b]
            if receives:
                total = total + came[side][b].astype(F32)
            sent[side][b] = total.astype(BF16)
    for store in stores:
        store.wait()


def hop(table, place, steps, step, count, partial, received, kept, sends, after):
    size = partial.shape[1]
    inside = pl.BlockSpec(memory_space=pltpu.VMEM)
    anywhere = pl.BlockSpec(memory_space=pl.ANY)
    numbers = pl.BlockSpec(memory_space=pltpu.SMEM)
    receives = received is not None
    message = jax.ShapeDtypeStruct((count, size, size), BF16)
    in_specs, operands = [numbers, numbers], [table, place]
    out_specs, out_shape, aliases = [], [], {}
    if sends:
        in_specs += [anywhere]
        operands += [partial]
    if receives:
        aliases = {len(operands) + 2: 0, len(operands) + 3: 1}
        in_specs += [inside, inside, anywhere, anywhere]
        operands += [*received, *kept]
        out_specs += [anywhere, anywhere]
        out_shape += [jax.ShapeDtypeStruct(k.shape, k.dtype) for k in kept]
    in_specs += [anywhere] * len(after)
    operands += after
    scratch = []
    if sends:
        out_specs += [inside, inside]
        out_shape += [message, message]
        scratch = [pltpu.VMEM((2, count, size, size), F32)]
    found = pl.pallas_call(
        functools.partial(
            hop_kernel, receives, sends, (2 if receives else 0) + len(after), count, steps, step
        ),
        in_specs=in_specs,
        out_specs=out_specs,
        out_shape=out_shape,
        scratch_shapes=scratch + [pltpu.SemaphoreType.DMA((2, 2, count))],
        input_output_aliases=aliases,
        compiler_params=params(46 * 1024 * 1024),
        cost_estimate=pl.CostEstimate(
            flops=4 * count * size * size, bytes_accessed=20 * count * size * size, transcendentals=0
        ),
        name="hop",
    )(*operands)
    if receives:
        kept, found = found[:2], found[2:]
    return kept, (found if sends else None)


def column_half(slices, early, z):
    high = lax.div(2 * z, jnp.int32(slices))
    return 1 - high if early else high


def rows_kernel(slices, parts, span, part, local, early, tab, mode, place, *refs):
    n = slices // 2 * parts * 2
    own, right, left = refs[:n], refs[n : 2 * n], refs[2 * n : 3 * n]
    tiles = refs[-1].shape[4]
    out_ref = refs[-1].reshape(span * part * 2 * tiles, LANES)
    z, h = place[0], pl.program_id(0)
    first = column_half(slices, early, z) * (slices // 2)
    has_right, has_left = z > 0, z < slices - 1
    size = span * part

    def total(at):
        r = jnp.where(has_right, right[at][0].astype(F32), 0.0)
        l = jnp.where(has_left, left[at][0].astype(F32), 0.0)
        return own[at][0] + r + l

    for j in range(slices // 2):
        for k in range(parts):
            at = 2 * (j * parts + k)
            kind = mode[((z * parts + h) * slices + first + j) * parts + k]

            def put(ri, value, j=j, k=k):
                for d in range(span):
                    for e in range(span):
                        tile = (d * part * 2 + ri) * tiles + ((j * span + e) * local + k * part) // LANES
                        out_ref[pl.ds(tile, part, stride=2 * tiles), :] = value[
                            d * part : (d + 1) * part, e * part : (e + 1) * part
                        ]

            @pl.when(kind == 0)
            def _():
                put(0, total(at))
                put(1, total(at + 1))

            @pl.when(kind == 1)
            def _():
                put(0, total(at).T)
                put(1, -(total(at + 1).T))

            @pl.when(kind == 2)
            def _():
                direct = total(at)
                mirror = direct.T
                row = lax.broadcasted_iota(jnp.int32, (size, size), 0)
                col = lax.broadcasted_iota(jnp.int32, (size, size), 1)
                put(0, jnp.where(row >= col, direct, mirror))
                put(1, jnp.where(row < col, direct, jnp.where(row == col, 0.0, -mirror)))


def visibility_rows(plan, place, partial, kept, span, part, antennas, out):
    slices, parts = plan.slices, plan.parts
    size = span * part
    local = parts * part
    ids, modes = plan.outputs()
    early = out is None
    per_j = parts * 2
    per_half = slices // 2 * per_j

    def spec(at):
        return pl.BlockSpec(
            (1, size, size),
            lambda h, tab, mode, place: (
                tab[
                    (2 * (place[0] * parts + h) + column_half(slices, early, place[0])) * per_half + at
                ],
                0,
                0,
            ),
        )

    tiles = antennas // 2 // LANES
    again = [] if out is None else [out]
    operands = [partial] * per_half + [kept[0]] * per_half + [kept[1]] * per_half + again
    return pl.pallas_call(
        functools.partial(rows_kernel, slices, parts, span, part, local, early),
        grid_spec=pltpu.PrefetchScalarGridSpec(
            num_scalar_prefetch=3,
            grid=(parts,),
            in_specs=[spec(at) for _ in range(3) for at in range(per_half)]
            + [pl.BlockSpec(memory_space=pl.ANY) for _ in again],
            out_specs=pl.BlockSpec(
                (span, 1, part * 2, 1, tiles, LANES),
                lambda h, tab, mode, place: (0, h, 0, column_half(slices, early, place[0]), 0, 0),
            ),
        ),
        out_shape=jax.ShapeDtypeStruct((span, parts, part * 2, 2, tiles, LANES), F32),
        input_output_aliases={} if out is None else {3 + 3 * per_half: 0},
        compiler_params=params(),
        cost_estimate=pl.CostEstimate(
            flops=span * local * antennas * 4,
            bytes_accessed=span * local * antennas * 12,
            transcendentals=0,
        ),
        name="visibility_rows",
    )(jnp.asarray(ids.reshape(-1)), jnp.asarray(modes.reshape(-1)), place, *operands)


def on_device(voltages, filter_taps, antenna_flags):
    taps, length = filter_taps.shape
    channels, slices = lax.axis_size("chan"), lax.axis_size("tm")
    local = voltages.shape[1]
    samples = voltages.shape[2]
    frames = samples // length
    part = 128
    parts = local // part
    span = channels // slices

    head = taps * length
    halos = []
    for h in range(parts):
        tail = voltages[:, h * part : (h + 1) * part, samples - head :]
        halos.append(lax.ppermute(tail, "tm", [(i, i + 1) for i in range(slices - 1)]))
    weights = filterbank_weights(filter_taps, channels)
    scale = (antenna_flags.astype(F32) / math.sqrt(length)).reshape(1, local)

    plan = Plan(slices, parts, 4)
    table = jnp.asarray(plan.table())
    place = lax.axis_index("tm").astype(jnp.int32).reshape(1)
    weight = 1.0 / (frames * slices)
    antennas = channels * local
    spectra, token = [], weights
    for h in range(parts):
        pieces = 2 if h == 0 else 1
        chunk = frames // pieces
        found = []
        for t in reversed(range(pieces)):
            own, token = filterbank(
                voltages, halos[h], weights, scale, length, channels, part, h, t * chunk, chunk, token
            )
            found.insert(
                0, lax.all_to_all(own, "chan", split_axis=0, concat_axis=0, tiled=True)
            )
        spectra.append(found)

    work = [
        (call, h, k, low, min(low + 2, slices) if call == len(plan.calls) - 1 > 0 else slices)
        for call, (h, k) in enumerate(plan.calls)
        for low in (range(0, slices, 2) if call == len(plan.calls) - 1 > 0 else (0,))
    ]

    def extend(partial, kept, count):
        for _ in range(count):
            call, h, k, low, high = work.pop(0)
            made = correlate(
                partial, plan.total, slices, call, spectra[h], spectra[k], span, weight, h == k,
                low, high,
            )
            partial = made[0]
            if kept is None:
                kept = made[1:]
        return partial, kept

    def needed(step):
        must = sum(1 for item in work if item[0] <= plan.last_call(step))
        soon = any(item[0] <= plan.last_call(step + n) for item in work for n in (1, 2))
        return max(must, 1 if soon and step > 2 else 0)

    partial, kept = extend(None, None, 1)
    arrived, out = {}, None
    early = max(plan.first_ready(), plan.steps - 1)
    holds = []
    for step in range(plan.steps + 2):
        partial, kept = extend(partial, kept, needed(step))
        sends = step < plan.steps
        received = arrived.pop(step - 2, None)
        kept, outgoing = hop(
            table, place, plan.steps + 2, step, plan.count, partial, received, kept, sends, holds
        )
        holds = []
        if sends:
            right = [(p, p + 1) for p in plan.senders(plan.right, step)]
            end = slices - 1
            left = [(end - p, end - p - 1) for p in plan.senders(plan.left, step)]
            arrived[step] = [
                lax.ppermute(outgoing[0], "tm", right),
                lax.ppermute(outgoing[1], "tm", left),
            ]
        if step == early:
            out = visibility_rows(plan, place, partial, kept, span, part, antennas, None)
            holds = [out]
    out = visibility_rows(plan, place, partial, kept, span, part, antennas, out)
    return out.reshape(span * local, 2, 1, antennas)


def solution(mesh):
    placed = (P(None, "chan", "tm"), P(), P("chan"))
    return jax.shard_map(
        on_device,
        mesh=mesh,
        in_specs=placed,
        out_specs=P("tm", None, "chan", None),
        check_vma=False,
    )
```

time: 316 us -> 270 us (0.85)
  Pallas kernels: 160 us -> 126 us
  starting transfers between devices: 107 us -> 121 us
  local copies, waits for them, and re-layouts: 17.5 us -> 3.67 us
  waiting for transfers between devices: 25.2 us -> 13.7 us
    pallas_call x20 -> x22, Pallas kernels: 98.9 us -> 72.3 us  [the longest x17 44.3 us: hop(): pl.pallas_call(functools.partial(hop_kernel, receives, sends, (2 if recei...]
    ppermute x15, starting transfers between devices: 70.2 us -> 85.3 us  [on_device(): lax.ppermute(outgoing[0], 'tm', right)]
    unnamed x24 -> x12, local copies, waits for them, and re-layouts: 10.1 us -> 1.41 us
    ppermute x1 -> x2, waiting for transfers between devices: 6.8 us -> 0.01 us  [on_device(): lax.ppermute(tail, 'tm', [(i, i + 1) for i in range(slices - 1)])]
    pallas_call x4 -> x3, Pallas kernels: 43.8 us -> 38.7 us  [filterbank(): pl.pallas_call(functools.partial(filterbank_kernel, channels, length), gr...]
    all_to_all x4 -> x3, starting transfers between devices: 16.8 us -> 11.6 us  [on_device(): lax.all_to_all(own, 'chan', split_axis=0, concat_axis=0, tiled=True)]
    ppermute x1 -> x2, starting transfers between devices: 3.54 us -> 8.42 us  [on_device(): lax.ppermute(tail, 'tm', [(i, i + 1) for i in range(slices - 1)])]
    ppermute x15, waiting for transfers between devices: 14.3 us -> 9.69 us  [on_device(): lax.ppermute(outgoing[0], 'tm', right)]
  transfers between devices with their start and end apart: 35 -> 35, of which waited for: 16 -> 10; matrix products, arithmetic and copies ran while one was open for 1% -> 0% of each run, Pallas kernels for 41% -> 44%
where the time goes in v2:
time: 270 us; the launch traced here: 266 us
  Pallas kernels  126 us (47%)
  starting transfers between devices  121 us (45%)
  waiting for transfers between devices  13.7 us (5%)
  local copies, waits for them, and re-layouts  3.67 us (1%)
    ppermute x15, starting transfers between devices, on_device(): lax.ppermute(outgoing[0], 'tm', right)  85.3 us
    pallas_call x17, Pallas kernels, hop(): pl.pallas_call(functools.partial(hop_kernel, receives, sends, (2 if recei...  44.3 us
    pallas_call x3, Pallas kernels, filterbank(): pl.pallas_call(functools.partial(filterbank_kernel, channels, length), gr...  38.7 us
    pallas_call x4, Pallas kernels, correlate(): pl.pallas_call(functools.partial(correlate_kernel, len(xs), len(ys), span...  27.7 us
    ppermute x15, starting transfers between devices, on_device(): lax.ppermute(outgoing[1], 'tm', left)  15.6 us
    pallas_call x2, Pallas kernels, visibility_rows(): pl.pallas_call(functools.partial(rows_kernel, slices, parts, span, part,...  15.5 us
    all_to_all x3, starting transfers between devices, on_device(): lax.all_to_all(own, 'chan', split_axis=0, concat_axis=0, tiled=True)  11.6 us
    ppermute x15, waiting for transfers between devices, on_device(): lax.ppermute(outgoing[0], 'tm', right)  9.69 us
  transfers between devices with their start and end apart: 35, of which 10 were waited for; matrix products, arithmetic and copies ran while one was open for 0% of the time, Pallas kernels for 44%

profile of v2, /device:TPU:0, one launch (start us, length us, event | category | flops | bytes accessed | tf_op | source)
XLA Modules:
  0.0 266.3 jit_solution(10101457694363111243)
XLA Ops:
  2.3 4.9 %collective-permute-start.1 = (bf16[2,128,1024]{2,1,0:T(8,128)(2,1)}, bf16[2,128,1024]{2,1,0:T(8,128)(2,1)S(1)}, u32[]{:S(2)}, u32[]{:S(2)}) collective-permute-start(bf16[2,128,1024]{2,1,0:T(8,128)(2,1)} %get-tuple-element.141), channel_id=1, source_target_pairs={{0,1},{1,2},{2,3},{4,5},{5,6},{6,7},{8,9},{9,10},{10,11},{12,13},{... | collective-permute-start | bytes 1572872 | tf_op jit(solution)/shard_map/ppermute | solution.py:532
  9.6 10.5 %filterbank_h0_f256.1 = (bf16[8,2,256,128]{3,2,1,0:T(8,128)(2,1)}, f32[8,128]{1,0:T(8,128)S(1)}) custom-call(bf16[2,256,32768]{2,1,0:T(8,128)(2,1)} %v_ref.5, bf16[2,256,32768]{2,1,0:T(8,128)(2,1)} %v_ref.5, bf16[768,512]{1,0:T(8,128)(2,1)S(1)} %weights.1.w_ref.after_ref, f32[1,256]{1,0:T(1,128)S(1)} %bitcast.3, bf16[768,512]{1,0:T(8,128)(2,1)S(1)} %weights.1.w_ref.after_ref), custom_call_target="tpu_custom_call" | custom-call | flops 6442450944 | bytes 8388608 | tf_op jit(solution)/shard_map/filterbank_h0_f256/pallas_call | solution.py:118
  20.1 3.7 %all-to-all-start.2 = ((bf16[8,2,256,128]{3,2,1,0:T(8,128)(2,1)}), bf16[8,2,256,128]{3,2,1,0:T(8,128)(2,1)S(1)}, u32[]{:S(2)}, u32[]{:S(2)}) async-start(bf16[8,2,256,128]{3,2,1,0:T(8,128)(2,1)} %get-tuple-element.77), calls=%async_computation.2 | async-start | bytes 2097152 | tf_op jit(solution)/shard_map/all_to_all | solution.py:551
  23.8 3.5 %collective-permute-start = (bf16[2,128,1024]{2,1,0:T(8,128)(2,1)}, bf16[2,128,1024]{2,1,0:T(8,128)(2,1)S(1)}, u32[]{:S(2)}, u32[]{:S(2)}) collective-permute-start(bf16[2,128,1024]{2,1,0:T(8,128)(2,1)} %get-tuple-element.142), channel_id=1, source_target_pairs={{0,1},{1,2},{2,3},{4,5},{5,6},{6,7},{8,9},{9,10},{10,11},{12,13},{... | collective-permute-start | bytes 1572872 | tf_op jit(solution)/shard_map/ppermute | solution.py:532
  27.3 10.4 %filterbank_h0_f0.1 = (bf16[8,2,256,128]{3,2,1,0:T(8,128)(2,1)}, f32[8,128]{1,0:T(8,128)S(1)}) custom-call(bf16[2,128,1024]{2,1,0:T(8,128)(2,1)S(1)} %collective-permute-done.1.head_ref, bf16[2,256,32768]{2,1,0:T(8,128)(2,1)} %v_ref.5, bf16[768,512]{1,0:T(8,128)(2,1)S(1)} %weights.1.w_ref.after_ref, f32[1,256]{1,0:T(1,128)S(1)} %bitcast.4, ...), custom_call_target="tpu_custom_call" | custom-call | flops 6442450944 | bytes 8388608 | tf_op jit(solution)/shard_map/filterbank_h0_f0/pallas_call | solution.py:118
  39.2 3.6 %all-to-all-start.1 = ((bf16[8,2,256,128]{3,2,1,0:T(8,128)(2,1)}), bf16[8,2,256,128]{3,2,1,0:T(8,128)(2,1)S(1)}, u32[]{:S(2)}, u32[]{:S(2)}) async-start(bf16[8,2,256,128]{3,2,1,0:T(8,128)(2,1)} %get-tuple-element.76), calls=%async_computation.1 | async-start | bytes 2097152 | tf_op jit(solution)/shard_map/all_to_all | solution.py:551
  42.8 17.8 %filterbank_h1_f0.1 = (bf16[8,2,512,128]{3,2,1,0:T(8,128)(2,1)}, f32[8,128]{1,0:T(8,128)}) custom-call(bf16[2,128,1024]{2,1,0:T(8,128)(2,1)S(1)} %collective-permute-done.head_ref, bf16[2,256,32768]{2,1,0:T(8,128)(2,1)} %v_ref.5, bf16[768,512]{1,0:T(8,128)(2,1)S(1)} %weights.1.w_ref.after_ref, f32[1,256]{1,0:T(1,128)S(1)} %bitcast.5, ...), custom_call_target="tpu_custom_call" | custom-call | flops 12884901888 | bytes 16777216 | tf_op jit(solution)/shard_map/filterbank_h1_f0/pallas_call | solution.py:118
  60.7 4.3 %all-to-all-start = ((bf16[8,2,512,128]{3,2,1,0:T(8,128)(2,1)}), bf16[8,2,512,128]{3,2,1,0:T(8,128)(2,1)}, u32[]{:S(2)}, u32[]{:S(2)}) async-start(bf16[8,2,512,128]{3,2,1,0:T(8,128)(2,1)} %get-tuple-element.75), calls=%async_computation | async-start | bytes 4194304 | tf_op jit(solution)/shard_map/all_to_all | solution.py:551
  65.0 7.9 %correlate.4 = (f32[104,256,256]{2,1,0:T(8,128)}, bf16[104,256,256]{2,1,0:T(8,128)(2,1)}, bf16[104,256,256]{2,1,0:T(8,128)(2,1)}) custom-call(bf16[8,2,256,128]{3,2,1,0:T(8,128)(2,1)S(1)} %all-to-all-done.1.refs_0_.refs_1_, bf16[8,2,256,128]{3,2,1,0:T(8,128)(2,1)} %copy-done.5), custom_call_target="tpu_custom_call" | custom-call | flops 4294967296 | bytes 8388608 | tf_op jit(solution)/shard_map/correlate/pallas_call | solution.py:205
  75.2 3.5 %collective-permute-start.2 = (bf16[4,256,256]{2,1,0:T(8,128)(2,1)S(1)}, bf16[4,256,256]{2,1,0:T(8,128)(2,1)S(1)}, u32[]{:S(2)}, u32[]{:S(2)}) collective-permute-start(bf16[4,256,256]{2,1,0:T(8,128)(2,1)S(1)} %get-tuple-element.79), channel_id=1, source_target_pairs={{0,1},{4,5},{8,9},{12,13},{16,17},{20,21},{24,25},{28,29}} | collective-permute-start | bytes 1572872 | tf_op jit(solution)/shard_map/ppermute | solution.py:595
  79.4 3.2 %hop.19 = (bf16[4,256,256]{2,1,0:T(8,128)(2,1)}, bf16[4,256,256]{2,1,0:T(8,128)(2,1)}) custom-call(s32[544]{0:T(1024)S(1)} %copy-done, s32[1]{0:T(128)} %bitcast.place, f32[104,256,256]{2,1,0:T(8,128)} %get-tuple-element.78.refs_1_.refs_0_), custom_call_target="tpu_custom_call" | custom-call | flops 1048576 | bytes 5242880 | tf_op jit(solution)/shard_map/hop/pallas_call | solution.py:397
  84.7 6.2 %collective-permute-done.2.refs_1_ = bf16[4,256,256]{2,1,0:T(8,128)(2,1)S(1)} collective-permute-done((bf16[4,256,256]{2,1,0:T(8,128)(2,1)S(1)}, bf16[4,256,256]{2,1,0:T(8,128)(2,1)S(1)}, u32[]{:S(2)}, u32[]{:S(2)}) %collective-permute-start.2) | collective-permute-done | bytes 524320 | tf_op jit(solution)/shard_map/ppermute | solution.py:595
  90.9 3.6 %hop.18 = (bf16[104,256,256]{2,1,0:T(8,128)(2,1)}, bf16[104,256,256]{2,1,0:T(8,128)(2,1)}, bf16[4,256,256]{2,1,0:T(8,128)(2,1)}, bf16[4,256,256]{2,1,0:T(8,128)(2,1)}) custom-call(s32[544]{0:T(1024)S(1)} %copy-done, s32[1]{0:T(128)} %bitcast.place, f32[104,256,256]{2,1,0:T(8,128)} %get-tuple-element.78.refs_1_.refs_0_, ...), custom_call_target="tpu_custom_call", output_to_operand_aliasing={{0}: (5, {}), {1}: (6, {})} | custom-call | flops 1048576 | bytes 5242880 | tf_op jit(solution)/shard_map/hop/pallas_call | solution.py:397
  94.5 4.4 %collective-permute-start.4 = (bf16[4,256,256]{2,1,0:T(8,128)(2,1)}, bf16[4,256,256]{2,1,0:T(8,128)(2,1)S(1)}, u32[]{:S(2)}, u32[]{:S(2)}) collective-permute-start(bf16[4,256,256]{2,1,0:T(8,128)(2,1)} %get-tuple-element.83), channel_id=1, source_target_pairs={{0,1},{1,2},{4,5},{5,6},{8,9},{9,10},{12,13},{13,14},{16,17},{17,1... | collective-permute-start | bytes 1572872 | tf_op jit(solution)/shard_map/ppermute | solution.py:595
  99.6 8.2 %correlate.5.refs_3_.refs_0_ = f32[104,256,256]{2,1,0:T(8,128)} custom-call(bf16[8,2,512,128]{3,2,1,0:T(8,128)(2,1)} %all-to-all-done.refs_0_, f32[104,256,256]{2,1,0:T(8,128)} %get-tuple-element.78.refs_1_.refs_0_), custom_call_target="tpu_custom_call", output_to_operand_aliasing={{}: (1, {})} | custom-call | flops 4294967296 | bytes 8388608 | tf_op jit(solution)/shard_map/correlate/pallas_call | solution.py:205
  110.5 4.8 %collective-permute-start.10 = (bf16[4,256,256]{2,1,0:T(8,128)(2,1)S(1)}, bf16[4,256,256]{2,1,0:T(8,128)(2,1)S(1)}, u32[]{:S(2)}, u32[]{:S(2)}) collective-permute-start(bf16[4,256,256]{2,1,0:T(8,128)(2,1)S(1)} %get-tuple-element.93), channel_id=1, source_target_pairs={{0,1},{1,2},{4,5},{5,6},{8,9},{9,10},{12,13},{13,14},{16,17},{17,1... | collective-permute-start | bytes 1572872 | tf_op jit(solution)/shard_map/ppermute | solution.py:595
  115.9 5.8 %correlate.6.refs_3_.refs_0_ = f32[104,256,256]{2,1,0:T(8,128)} custom-call(bf16[8,2,512,128]{3,2,1,0:T(8,128)(2,1)} %all-to-all-done.refs_0_, bf16[8,2,256,128]{3,2,1,0:T(8,128)(2,1)S(1)} %all-to-all-done.1.refs_0_.refs_1_, bf16[8,2,256,128]{3,2,1,0:T(8,128)(2,1)} %copy-done.5, ...), custom_call_target="tpu_custom_call", output_to_operand_aliasing={{}: (3, {})} | custom-call | flops 2147483648 | bytes 4194304 | tf_op jit(solution)/shard_map/correlate/pallas_call | solution.py:205
  124.4 5.1 %collective-permute-start.8 = (bf16[4,256,256]{2,1,0:T(8,128)(2,1)S(1)}, bf16[4,256,256]{2,1,0:T(8,128)(2,1)S(1)}, u32[]{:S(2)}, u32[]{:S(2)}) collective-permute-start(bf16[4,256,256]{2,1,0:T(8,128)(2,1)S(1)} %get-tuple-element.91), channel_id=1, source_target_pairs={{0,1},{1,2},{2,3},{4,5},{5,6},{6,7},{8,9},{9,10},{10,11},{12,13},{... | collective-permute-start | bytes 1572872 | tf_op jit(solution)/shard_map/ppermute | solution.py:595
  131.1 5.8 %correlate.7.refs_0_.refs_1_.refs_2_.refs_3_.refs_4_.refs_5_.refs_6_.refs_7_ = f32[104,256,256]{2,1,0:T(8,128)} custom-call(bf16[8,2,512,128]{3,2,1,0:T(8,128)(2,1)} %all-to-all-done.refs_0_, bf16[8,2,256,128]{3,2,1,0:T(8,128)(2,1)S(1)} %all-to-all-done.1.refs_0_.refs_1_, bf16[8,2,256,128]{3,2,1,0:T(8,128)(2,1)} %copy-done.5, ...), custom_call_target="tpu_custom_call", output_to_operand_aliasing={{}: (3, {})} | custom-call | flops 2147483648 | bytes 4194304 | tf_op jit(solution)/shard_map/correlate/pallas_call | solution.py:205
  139.6 5.2 %collective-permute-start.14 = (bf16[4,256,256]{2,1,0:T(8,128)(2,1)S(1)}, bf16[4,256,256]{2,1,0:T(8,128)(2,1)S(1)}, u32[]{:S(2)}, u32[]{:S(2)}) collective-permute-start(bf16[4,256,256]{2,1,0:T(8,128)(2,1)S(1)} %get-tuple-element.101), channel_id=1, source_target_pairs={{0,1},{1,2},{2,3},{4,5},{5,6},{6,7},{8,9},{9,10},{10,11},{12,13},{... | collective-permute-start | bytes 1572872 | tf_op jit(solution)/shard_map/ppermute | solution.py:595
  148.7 4.6 %collective-permute-start.12 = (bf16[4,256,256]{2,1,0:T(8,128)(2,1)S(1)}, bf16[4,256,256]{2,1,0:T(8,128)(2,1)S(1)}, u32[]{:S(2)}, u32[]{:S(2)}) collective-permute-start(bf16[4,256,256]{2,1,0:T(8,128)(2,1)S(1)} %get-tuple-element.99), channel_id=1, source_target_pairs={{0,1},{1,2},{4,5},{5,6},{8,9},{9,10},{12,13},{13,14},{16,17},{17,1... | collective-permute-start | bytes 1572872 | tf_op jit(solution)/shard_map/ppermute | solution.py:595
  154.0 2.9 %collective-permute-done.14.refs_1_ = bf16[4,256,256]{2,1,0:T(8,128)(2,1)S(1)} collective-permute-done((bf16[4,256,256]{2,1,0:T(8,128)(2,1)S(1)}, bf16[4,256,256]{2,1,0:T(8,128)(2,1)S(1)}, u32[]{:S(2)}, u32[]{:S(2)}) %collective-permute-start.14) | collective-permute-done | bytes 524320 | tf_op jit(solution)/shard_map/ppermute | solution.py:595
  160.5 6.8 %collective-permute-start.18 = (bf16[4,256,256]{2,1,0:T(8,128)(2,1)S(1)}, bf16[4,256,256]{2,1,0:T(8,128)(2,1)S(1)}, u32[]{:S(2)}, u32[]{:S(2)}) collective-permute-start(bf16[4,256,256]{2,1,0:T(8,128)(2,1)S(1)} %get-tuple-element.109), channel_id=1, source_target_pairs={{0,1},{1,2},{2,3},{4,5},{5,6},{6,7},{8,9},{9,10},{10,11},{12,13},{... | collective-permute-start | bytes 1572872 | tf_op jit(solution)/shard_map/ppermute | solution.py:595
  171.4 7.3 %collective-permute-start.16 = (bf16[4,256,256]{2,1,0:T(8,128)(2,1)S(1)}, bf16[4,256,256]{2,1,0:T(8,128)(2,1)S(1)}, u32[]{:S(2)}, u32[]{:S(2)}) collective-permute-start(bf16[4,256,256]{2,1,0:T(8,128)(2,1)S(1)} %get-tuple-element.107), channel_id=1, source_target_pairs={{0,1},{1,2},{2,3},{4,5},{5,6},{6,7},{8,9},{9,10},{10,11},{12,13},{... | collective-permute-start | bytes 1572872 | tf_op jit(solution)/shard_map/ppermute | solution.py:595
  182.9 6.9 %collective-permute-start.22 = (bf16[4,256,256]{2,1,0:T(8,128)(2,1)S(1)}, bf16[4,256,256]{2,1,0:T(8,128)(2,1)S(1)}, u32[]{:S(2)}, u32[]{:S(2)}) collective-permute-start(bf16[4,256,256]{2,1,0:T(8,128)(2,1)S(1)} %get-tuple-element.117), channel_id=1, source_target_pairs={{0,1},{1,2},{4,5},{5,6},{8,9},{9,10},{12,13},{13,14},{16,17},{17,1... | collective-permute-start | bytes 1572872 | tf_op jit(solution)/shard_map/ppermute | solution.py:595
  193.6 7.5 %collective-permute-start.20 = (bf16[4,256,256]{2,1,0:T(8,128)(2,1)S(1)}, bf16[4,256,256]{2,1,0:T(8,128)(2,1)S(1)}, u32[]{:S(2)}, u32[]{:S(2)}) collective-permute-start(bf16[4,256,256]{2,1,0:T(8,128)(2,1)S(1)} %get-tuple-element.115), channel_id=1, source_target_pairs={{0,1},{1,2},{2,3},{4,5},{5,6},{6,7},{8,9},{9,10},{10,11},{12,13},{... | collective-permute-start | bytes 1572872 | tf_op jit(solution)/shard_map/ppermute | solution.py:595
  205.1 7.3 %collective-permute-start.26 = (bf16[4,256,256]{2,1,0:T(8,128)(2,1)S(1)}, bf16[4,256,256]{2,1,0:T(8,128)(2,1)S(1)}, u32[]{:S(2)}, u32[]{:S(2)}) collective-permute-start(bf16[4,256,256]{2,1,0:T(8,128)(2,1)S(1)} %get-tuple-element.125), channel_id=1, source_target_pairs={{0,1},{1,2},{2,3},{4,5},{5,6},{6,7},{8,9},{9,10},{10,11},{12,13},{... | collective-permute-start | bytes 1572872 | tf_op jit(solution)/shard_map/ppermute | solution.py:595
  216.6 6.9 %collective-permute-start.24 = (bf16[4,256,256]{2,1,0:T(8,128)(2,1)S(1)}, bf16[4,256,256]{2,1,0:T(8,128)(2,1)S(1)}, u32[]{:S(2)}, u32[]{:S(2)}) collective-permute-start(bf16[4,256,256]{2,1,0:T(8,128)(2,1)S(1)} %get-tuple-element.123), channel_id=1, source_target_pairs={{0,1},{1,2},{2,3},{4,5},{5,6},{6,7},{8,9},{9,10},{10,11},{12,13},{... | collective-permute-start | bytes 1572872 | tf_op jit(solution)/shard_map/ppermute | solution.py:595
  227.9 6.9 %collective-permute-start.30 = (bf16[4,256,256]{2,1,0:T(8,128)(2,1)S(1)}, bf16[4,256,256]{2,1,0:T(8,128)(2,1)S(1)}, u32[]{:S(2)}, u32[]{:S(2)}) collective-permute-start(bf16[4,256,256]{2,1,0:T(8,128)(2,1)S(1)} %get-tuple-element.133), channel_id=1, source_target_pairs={{0,1},{1,2},{2,3},{4,5},{5,6},{6,7},{8,9},{9,10},{10,11},{12,13},{... | collective-permute-start | bytes 1572872 | tf_op jit(solution)/shard_map/ppermute | solution.py:595
  239.1 6.9 %collective-permute-start.28 = (bf16[4,256,256]{2,1,0:T(8,128)(2,1)S(1)}, bf16[4,256,256]{2,1,0:T(8,128)(2,1)S(1)}, u32[]{:S(2)}, u32[]{:S(2)}) collective-permute-start(bf16[4,256,256]{2,1,0:T(8,128)(2,1)S(1)} %get-tuple-element.131), channel_id=1, source_target_pairs={{0,1},{4,5},{8,9},{12,13},{16,17},{20,21},{24,25},{28,29}} | collective-permute-start | bytes 1572872 | tf_op jit(solution)/shard_map/ppermute | solution.py:595
  248.9 7.5 %visibility_rows.2.refs_4_.refs_24_ = f32[2,2,256,2,8,128]{5,4,3,2,1,0:T(8,128)} custom-call(s32[128]{0:T(128)S(1)} %copy-done.4, s32[64]{0:T(128)S(1)} %copy-done.3, s32[1]{0:T(128)} %bitcast.place, f32[104,256,256]{2,1,0:T(8,128)} %correlate.7.refs_0_.refs_1_.refs_2_.refs_3_.refs_4_.refs_5_.refs_6_.refs_7_, ...), custom_call_target="tpu_custom_call" | custom-call | flops 4194304 | bytes 12582912 | tf_op jit(solution)/shard_map/visibility_rows/pallas_call | solution.py:494
  258.1 8.0 %visibility_rows.3 = f32[2,2,256,2,8,128]{5,4,3,2,1,0:T(8,128)} custom-call(s32[128]{0:T(128)S(1)} %copy-done.4, s32[64]{0:T(128)S(1)} %copy-done.3, s32[1]{0:T(128)} %bitcast.place, f32[104,256,256]{2,1,0:T(8,128)} %correlate.7.refs_0_.refs_1_.refs_2_.refs_3_.refs_4_.refs_5_.refs_6_.refs_7_, ...), custom_call_target="tpu_custom_call", output_to_operand_aliasing={{}: (27, {})} | custom-call | flops 4194304 | bytes 12582912 | tf_op jit(solution)/shard_map/visibility_rows/pallas_call | solution.py:494
  (79 shorter events, 63.6 us)
Async XLA Ops:
  2.3 25.1 %collective-permute-start.1 = (bf16[2,128,1024]{2,1,0:T(8,128)(2,1)}, bf16[2,128,1024]{2,1,0:T(8,128)(2,1)S(1)}, u32[]{:S(2)}, u32[]{:S(2)}) collective-permute-start(bf16[2,128,1024]{2,1,0:T(8,128)(2,1)} %get-tuple-element.141), channel_id=1, source_target_pairs={{0,1},{1,2},{2,3},{4,5},{5,6},{6,7},{8,9},{9,10},{10,11},{12,13},{... | collective-permute-start | bytes 1572872 | tf_op jit(solution)/shard_map/ppermute | solution.py:532
  20.1 19.1 %all-to-all-start.2 = ((bf16[8,2,256,128]{3,2,1,0:T(8,128)(2,1)}), bf16[8,2,256,128]{3,2,1,0:T(8,128)(2,1)S(1)}, u32[]{:S(2)}, u32[]{:S(2)}) async-start(bf16[8,2,256,128]{3,2,1,0:T(8,128)(2,1)} %get-tuple-element.77), calls=%async_computation.2 | async-start | bytes 2097152 | tf_op jit(solution)/shard_map/all_to_all | solution.py:551
  23.8 19.0 %collective-permute-start = (bf16[2,128,1024]{2,1,0:T(8,128)(2,1)}, bf16[2,128,1024]{2,1,0:T(8,128)(2,1)S(1)}, u32[]{:S(2)}, u32[]{:S(2)}) collective-permute-start(bf16[2,128,1024]{2,1,0:T(8,128)(2,1)} %get-tuple-element.142), channel_id=1, source_target_pairs={{0,1},{1,2},{2,3},{4,5},{5,6},{6,7},{8,9},{9,10},{10,11},{12,13},{... | collective-permute-start | bytes 1572872 | tf_op jit(solution)/shard_map/ppermute | solution.py:532
  39.2 21.4 %all-to-all-start.1 = ((bf16[8,2,256,128]{3,2,1,0:T(8,128)(2,1)}), bf16[8,2,256,128]{3,2,1,0:T(8,128)(2,1)S(1)}, u32[]{:S(2)}, u32[]{:S(2)}) async-start(bf16[8,2,256,128]{3,2,1,0:T(8,128)(2,1)} %get-tuple-element.76), calls=%async_computation.1 | async-start | bytes 2097152 | tf_op jit(solution)/shard_map/all_to_all | solution.py:551
  60.7 39.0 %all-to-all-start = ((bf16[8,2,512,128]{3,2,1,0:T(8,128)(2,1)}), bf16[8,2,512,128]{3,2,1,0:T(8,128)(2,1)}, u32[]{:S(2)}, u32[]{:S(2)}) async-start(bf16[8,2,512,128]{3,2,1,0:T(8,128)(2,1)} %get-tuple-element.75), calls=%async_computation | async-start | bytes 4194304 | tf_op jit(solution)/shard_map/all_to_all | solution.py:551
  75.2 15.7 %collective-permute-start.2 = (bf16[4,256,256]{2,1,0:T(8,128)(2,1)S(1)}, bf16[4,256,256]{2,1,0:T(8,128)(2,1)S(1)}, u32[]{:S(2)}, u32[]{:S(2)}) collective-permute-start(bf16[4,256,256]{2,1,0:T(8,128)(2,1)S(1)} %get-tuple-element.79), channel_id=1, source_target_pairs={{0,1},{4,5},{8,9},{12,13},{16,17},{20,21},{24,25},{28,29}} | collective-permute-start | bytes 1572872 | tf_op jit(solution)/shard_map/ppermute | solution.py:595
  82.6 25.2 %collective-permute-start.6 = (bf16[4,256,256]{2,1,0:T(8,128)(2,1)}, bf16[4,256,256]{2,1,0:T(8,128)(2,1)S(1)}, u32[]{:S(2)}, u32[]{:S(2)}) collective-permute-start(bf16[4,256,256]{2,1,0:T(8,128)(2,1)} %get-tuple-element.85), channel_id=1, source_target_pairs={{0,1},{4,5},{8,9},{12,13},{16,17},{20,21},{24,25},{28,29}} | collective-permute-start | bytes 1572872 | tf_op jit(solution)/shard_map/ppermute | solution.py:595
  84.0 23.9 %collective-permute-start.7 = (bf16[4,256,256]{2,1,0:T(8,128)(2,1)}, bf16[4,256,256]{2,1,0:T(8,128)(2,1)S(1)}, u32[]{:S(2)}, u32[]{:S(2)}) collective-permute-start(bf16[4,256,256]{2,1,0:T(8,128)(2,1)} %get-tuple-element.86), channel_id=1, source_target_pairs={{3,2},{7,6},{11,10},{15,14},{19,18},{23,22},{27,26},{31,30}} | collective-permute-start | bytes 1572872 | tf_op jit(solution)/shard_map/ppermute | solution.py:596
  94.5 27.3 %collective-permute-start.4 = (bf16[4,256,256]{2,1,0:T(8,128)(2,1)}, bf16[4,256,256]{2,1,0:T(8,128)(2,1)S(1)}, u32[]{:S(2)}, u32[]{:S(2)}) collective-permute-start(bf16[4,256,256]{2,1,0:T(8,128)(2,1)} %get-tuple-element.83), channel_id=1, source_target_pairs={{0,1},{1,2},{4,5},{5,6},{8,9},{9,10},{12,13},{13,14},{16,17},{17,1... | collective-permute-start | bytes 1572872 | tf_op jit(solution)/shard_map/ppermute | solution.py:595
  98.9 22.9 %collective-permute-start.5 = (bf16[4,256,256]{2,1,0:T(8,128)(2,1)}, bf16[4,256,256]{2,1,0:T(8,128)(2,1)S(1)}, u32[]{:S(2)}, u32[]{:S(2)}) collective-permute-start(bf16[4,256,256]{2,1,0:T(8,128)(2,1)} %get-tuple-element.84), channel_id=1, source_target_pairs={{3,2},{2,1},{7,6},{6,5},{11,10},{10,9},{15,14},{14,13},{19,18},{18... | collective-permute-start | bytes 1572872 | tf_op jit(solution)/shard_map/ppermute | solution.py:596
  110.5 26.5 %collective-permute-start.10 = (bf16[4,256,256]{2,1,0:T(8,128)(2,1)S(1)}, bf16[4,256,256]{2,1,0:T(8,128)(2,1)S(1)}, u32[]{:S(2)}, u32[]{:S(2)}) collective-permute-start(bf16[4,256,256]{2,1,0:T(8,128)(2,1)S(1)} %get-tuple-element.93), channel_id=1, source_target_pairs={{0,1},{1,2},{4,5},{5,6},{8,9},{9,10},{12,13},{13,14},{16,17},{17,1... | collective-permute-start | bytes 1572872 | tf_op jit(solution)/shard_map/ppermute | solution.py:595
  115.2 21.7 %collective-permute-start.11 = (bf16[4,256,256]{2,1,0:T(8,128)(2,1)S(1)}, bf16[4,256,256]{2,1,0:T(8,128)(2,1)S(1)}, u32[]{:S(2)}, u32[]{:S(2)}) collective-permute-start(bf16[4,256,256]{2,1,0:T(8,128)(2,1)S(1)} %get-tuple-element.94), channel_id=1, source_target_pairs={{3,2},{2,1},{7,6},{6,5},{11,10},{10,9},{15,14},{14,13},{19,18},{18... | collective-permute-start | bytes 1572872 | tf_op jit(solution)/shard_map/ppermute | solution.py:596
  124.4 21.6 %collective-permute-start.8 = (bf16[4,256,256]{2,1,0:T(8,128)(2,1)S(1)}, bf16[4,256,256]{2,1,0:T(8,128)(2,1)S(1)}, u32[]{:S(2)}, u32[]{:S(2)}) collective-permute-start(bf16[4,256,256]{2,1,0:T(8,128)(2,1)S(1)} %get-tuple-element.91), channel_id=1, source_target_pairs={{0,1},{1,2},{2,3},{4,5},{5,6},{6,7},{8,9},{9,10},{10,11},{12,13},{... | collective-permute-start | bytes 1572872 | tf_op jit(solution)/shard_map/ppermute | solution.py:595
  129.6 16.5 %collective-permute-start.9 = (bf16[4,256,256]{2,1,0:T(8,128)(2,1)S(1)}, bf16[4,256,256]{2,1,0:T(8,128)(2,1)S(1)}, u32[]{:S(2)}, u32[]{:S(2)}) collective-permute-start(bf16[4,256,256]{2,1,0:T(8,128)(2,1)S(1)} %get-tuple-element.92), channel_id=1, source_target_pairs={{3,2},{2,1},{1,0},{7,6},{6,5},{5,4},{11,10},{10,9},{9,8},{15,14},{... | collective-permute-start | bytes 1572872 | tf_op jit(solution)/shard_map/ppermute | solution.py:596
  139.6 17.3 %collective-permute-start.14 = (bf16[4,256,256]{2,1,0:T(8,128)(2,1)S(1)}, bf16[4,256,256]{2,1,0:T(8,128)(2,1)S(1)}, u32[]{:S(2)}, u32[]{:S(2)}) collective-permute-start(bf16[4,256,256]{2,1,0:T(8,128)(2,1)S(1)} %get-tuple-element.101), channel_id=1, source_target_pairs={{0,1},{1,2},{2,3},{4,5},{5,6},{6,7},{8,9},{9,10},{10,11},{12,13},{... | collective-permute-start | bytes 1572872 | tf_op jit(solution)/shard_map/ppermute | solution.py:595
  144.8 13.1 %collective-permute-start.15 = (bf16[4,256,256]{2,1,0:T(8,128)(2,1)S(1)}, bf16[4,256,256]{2,1,0:T(8,128)(2,1)S(1)}, u32[]{:S(2)}, u32[]{:S(2)}) collective-permute-start(bf16[4,256,256]{2,1,0:T(8,128)(2,1)S(1)} %get-tuple-element.102), channel_id=1, source_target_pairs={{3,2},{2,1},{1,0},{7,6},{6,5},{5,4},{11,10},{10,9},{9,8},{15,14},{... | collective-permute-start | bytes 1572872 | tf_op jit(solution)/shard_map/ppermute | solution.py:596
  148.7 19.9 %collective-permute-start.12 = (bf16[4,256,256]{2,1,0:T(8,128)(2,1)S(1)}, bf16[4,256,256]{2,1,0:T(8,128)(2,1)S(1)}, u32[]{:S(2)}, u32[]{:S(2)}) collective-permute-start(bf16[4,256,256]{2,1,0:T(8,128)(2,1)S(1)} %get-tuple-element.99), channel_id=1, source_target_pairs={{0,1},{1,2},{4,5},{5,6},{8,9},{9,10},{12,13},{13,14},{16,17},{17,1... | collective-permute-start | bytes 1572872 | tf_op jit(solution)/shard_map/ppermute | solution.py:595
  153.3 15.4 %collective-permute-start.13 = (bf16[4,256,256]{2,1,0:T(8,128)(2,1)S(1)}, bf16[4,256,256]{2,1,0:T(8,128)(2,1)S(1)}, u32[]{:S(2)}, u32[]{:S(2)}) collective-permute-start(bf16[4,256,256]{2,1,0:T(8,128)(2,1)S(1)} %get-tuple-element.100), channel_id=1, source_target_pairs={{3,2},{2,1},{7,6},{6,5},{11,10},{10,9},{15,14},{14,13},{19,18},{18... | collective-permute-start | bytes 1572872 | tf_op jit(solution)/shard_map/ppermute | solution.py:596
  160.5 19.4 %collective-permute-start.18 = (bf16[4,256,256]{2,1,0:T(8,128)(2,1)S(1)}, bf16[4,256,256]{2,1,0:T(8,128)(2,1)S(1)}, u32[]{:S(2)}, u32[]{:S(2)}) collective-permute-start(bf16[4,256,256]{2,1,0:T(8,128)(2,1)S(1)} %get-tuple-element.109), channel_id=1, source_target_pairs={{0,1},{1,2},{2,3},{4,5},{5,6},{6,7},{8,9},{9,10},{10,11},{12,13},{... | collective-permute-start | bytes 1572872 | tf_op jit(solution)/shard_map/ppermute | solution.py:595
  167.4 12.9 %collective-permute-start.19 = (bf16[4,256,256]{2,1,0:T(8,128)(2,1)S(1)}, bf16[4,256,256]{2,1,0:T(8,128)(2,1)S(1)}, u32[]{:S(2)}, u32[]{:S(2)}) collective-permute-start(bf16[4,256,256]{2,1,0:T(8,128)(2,1)S(1)} %get-tuple-element.110), channel_id=1, source_target_pairs={{3,2},{2,1},{1,0},{7,6},{6,5},{5,4},{11,10},{10,9},{9,8},{15,14},{... | collective-permute-start | bytes 1572872 | tf_op jit(solution)/shard_map/ppermute | solution.py:596
  171.4 19.6 %collective-permute-start.16 = (bf16[4,256,256]{2,1,0:T(8,128)(2,1)S(1)}, bf16[4,256,256]{2,1,0:T(8,128)(2,1)S(1)}, u32[]{:S(2)}, u32[]{:S(2)}) collective-permute-start(bf16[4,256,256]{2,1,0:T(8,128)(2,1)S(1)} %get-tuple-element.107), channel_id=1, source_target_pairs={{0,1},{1,2},{2,3},{4,5},{5,6},{6,7},{8,9},{9,10},{10,11},{12,13},{... | collective-permute-start | bytes 1572872 | tf_op jit(solution)/shard_map/ppermute | solution.py:595
  178.6 12.3 %collective-permute-start.17 = (bf16[4,256,256]{2,1,0:T(8,128)(2,1)S(1)}, bf16[4,256,256]{2,1,0:T(8,128)(2,1)S(1)}, u32[]{:S(2)}, u32[]{:S(2)}) collective-permute-start(bf16[4,256,256]{2,1,0:T(8,128)(2,1)S(1)} %get-tuple-element.108), channel_id=1, source_target_pairs={{3,2},{2,1},{1,0},{7,6},{6,5},{5,4},{11,10},{10,9},{9,8},{15,14},{... | collective-permute-start | bytes 1572872 | tf_op jit(solution)/shard_map/ppermute | solution.py:596
  182.9 19.4 %collective-permute-start.22 = (bf16[4,256,256]{2,1,0:T(8,128)(2,1)S(1)}, bf16[4,256,256]{2,1,0:T(8,128)(2,1)S(1)}, u32[]{:S(2)}, u32[]{:S(2)}) collective-permute-start(bf16[4,256,256]{2,1,0:T(8,128)(2,1)S(1)} %get-tuple-element.117), channel_id=1, source_target_pairs={{0,1},{1,2},{4,5},{5,6},{8,9},{9,10},{12,13},{13,14},{16,17},{17,1... | collective-permute-start | bytes 1572872 | tf_op jit(solution)/shard_map/ppermute | solution.py:595
  189.8 12.5 %collective-permute-start.23 = (bf16[4,256,256]{2,1,0:T(8,128)(2,1)S(1)}, bf16[4,256,256]{2,1,0:T(8,128)(2,1)S(1)}, u32[]{:S(2)}, u32[]{:S(2)}) collective-permute-start(bf16[4,256,256]{2,1,0:T(8,128)(2,1)S(1)} %get-tuple-element.118), channel_id=1, source_target_pairs={{3,2},{2,1},{7,6},{6,5},{11,10},{10,9},{15,14},{14,13},{19,18},{18... | collective-permute-start | bytes 1572872 | tf_op jit(solution)/shard_map/ppermute | solution.py:596
  193.6 20.0 %collective-permute-start.20 = (bf16[4,256,256]{2,1,0:T(8,128)(2,1)S(1)}, bf16[4,256,256]{2,1,0:T(8,128)(2,1)S(1)}, u32[]{:S(2)}, u32[]{:S(2)}) collective-permute-start(bf16[4,256,256]{2,1,0:T(8,128)(2,1)S(1)} %get-tuple-element.115), channel_id=1, source_target_pairs={{0,1},{1,2},{2,3},{4,5},{5,6},{6,7},{8,9},{9,10},{10,11},{12,13},{... | collective-permute-start | bytes 1572872 | tf_op jit(solution)/shard_map/ppermute | solution.py:595
  201.1 12.9 %collective-permute-start.21 = (bf16[4,256,256]{2,1,0:T(8,128)(2,1)S(1)}, bf16[4,256,256]{2,1,0:T(8,128)(2,1)S(1)}, u32[]{:S(2)}, u32[]{:S(2)}) collective-permute-start(bf16[4,256,256]{2,1,0:T(8,128)(2,1)S(1)} %get-tuple-element.116), channel_id=1, source_target_pairs={{3,2},{2,1},{1,0},{7,6},{6,5},{5,4},{11,10},{10,9},{9,8},{15,14},{... | collective-permute-start | bytes 1572872 | tf_op jit(solution)/shard_map/ppermute | solution.py:596
  205.1 19.8 %collective-permute-start.26 = (bf16[4,256,256]{2,1,0:T(8,128)(2,1)S(1)}, bf16[4,256,256]{2,1,0:T(8,128)(2,1)S(1)}, u32[]{:S(2)}, u32[]{:S(2)}) collective-permute-start(bf16[4,256,256]{2,1,0:T(8,128)(2,1)S(1)} %get-tuple-element.125), channel_id=1, source_target_pairs={{0,1},{1,2},{2,3},{4,5},{5,6},{6,7},{8,9},{9,10},{10,11},{12,13},{... | collective-permute-start | bytes 1572872 | tf_op jit(solution)/shard_map/ppermute | solution.py:595
  212.3 12.9 %collective-permute-start.27 = (bf16[4,256,256]{2,1,0:T(8,128)(2,1)S(1)}, bf16[4,256,256]{2,1,0:T(8,128)(2,1)S(1)}, u32[]{:S(2)}, u32[]{:S(2)}) collective-permute-start(bf16[4,256,256]{2,1,0:T(8,128)(2,1)S(1)} %get-tuple-element.126), channel_id=1, source_target_pairs={{3,2},{2,1},{1,0},{7,6},{6,5},{5,4},{11,10},{10,9},{9,8},{15,14},{... | collective-permute-start | bytes 1572872 | tf_op jit(solution)/shard_map/ppermute | solution.py:596
  216.6 19.4 %collective-permute-start.24 = (bf16[4,256,256]{2,1,0:T(8,128)(2,1)S(1)}, bf16[4,256,256]{2,1,0:T(8,128)(2,1)S(1)}, u32[]{:S(2)}, u32[]{:S(2)}) collective-permute-start(bf16[4,256,256]{2,1,0:T(8,128)(2,1)S(1)} %get-tuple-element.123), channel_id=1, source_target_pairs={{0,1},{1,2},{2,3},{4,5},{5,6},{6,7},{8,9},{9,10},{10,11},{12,13},{... | collective-permute-start | bytes 1572872 | tf_op jit(solution)/shard_map/ppermute | solution.py:595
  223.6 12.9 %collective-permute-start.25 = (bf16[4,256,256]{2,1,0:T(8,128)(2,1)S(1)}, bf16[4,256,256]{2,1,0:T(8,128)(2,1)S(1)}, u32[]{:S(2)}, u32[]{:S(2)}) collective-permute-start(bf16[4,256,256]{2,1,0:T(8,128)(2,1)S(1)} %get-tuple-element.124), channel_id=1, source_target_pairs={{3,2},{2,1},{1,0},{7,6},{6,5},{5,4},{11,10},{10,9},{9,8},{15,14},{... | collective-permute-start | bytes 1572872 | tf_op jit(solution)/shard_map/ppermute | solution.py:596
  227.9 19.2 %collective-permute-start.30 = (bf16[4,256,256]{2,1,0:T(8,128)(2,1)S(1)}, bf16[4,256,256]{2,1,0:T(8,128)(2,1)S(1)}, u32[]{:S(2)}, u32[]{:S(2)}) collective-permute-start(bf16[4,256,256]{2,1,0:T(8,128)(2,1)S(1)} %get-tuple-element.133), channel_id=1, source_target_pairs={{0,1},{1,2},{2,3},{4,5},{5,6},{6,7},{8,9},{9,10},{10,11},{12,13},{... | collective-permute-start | bytes 1572872 | tf_op jit(solution)/shard_map/ppermute | solution.py:595
  239.1 17.2 %collective-permute-start.28 = (bf16[4,256,256]{2,1,0:T(8,128)(2,1)S(1)}, bf16[4,256,256]{2,1,0:T(8,128)(2,1)S(1)}, u32[]{:S(2)}, u32[]{:S(2)}) collective-permute-start(bf16[4,256,256]{2,1,0:T(8,128)(2,1)S(1)} %get-tuple-element.131), channel_id=1, source_target_pairs={{0,1},{4,5},{8,9},{12,13},{16,17},{20,21},{24,25},{28,29}} | collective-permute-start | bytes 1572872 | tf_op jit(solution)/shard_map/ppermute | solution.py:595
  (9 other events, 73.4 us)

commit v3 on v2

--- a/solution.py
+++ b/solution.py
@@ -12,6 +12,7 @@
 F32, BF16 = jnp.float32, jnp.bfloat16
 GROUP = 8
 LANES = 128
+FRAMES_PER_STEP = 128
 VMEM_LIMIT = 52 * 1024 * 1024
 
 
@@ -60,7 +61,7 @@
     )(filter_taps, jnp.asarray(trig.astype(np.float32)))
 
 
-def filterbank_kernel(channels, length, head_ref, v_ref, w_ref, s_ref, after_ref, out_ref, token_ref, carry):
+def filterbank_kernel(channels, length, head_ref, v_ref, w_ref, s_ref, after_ref, out_ref, token_ref, carry, found):
     del after_ref, token_ref
     step = pl.program_id(0)
     _, part, lanes = v_ref.shape
@@ -68,7 +69,7 @@
     half = channels * GROUP
     rows = 2 * half
     blocks = w_ref.shape[0] // (2 * rows)
-    scale = s_ref[...]
+    scale = s_ref[...].astype(F32) / math.sqrt(length)
 
     def advance(ref, at):
         x = ref[:, :, at * size : (at + 1) * size].reshape(2 * part, size)
@@ -89,24 +90,23 @@
         for b in range(head_ref.shape[2] // size):
             advance(head_ref, b)
 
-    def one(b):
+    for b in range(lanes // size):
         done = advance(v_ref, b)
         cos, sin = done[:half], done[half:]
-        real = (cos[:, :part] + sin[:, part:]) * scale
-        imag = (cos[:, part:] - sin[:, :part]) * scale
-        return real, imag
-
-    for b in range(0, lanes // size, 2):
-        first, second = one(b), one(b + 1)
+        both = (
+            (cos[:, :part] + sin[:, part:]) * scale,
+            (cos[:, part:] - sin[:, :part]) * scale,
+        )
         for c in range(channels):
-            take = slice(c * GROUP, (c + 1) * GROUP)
             for ri in range(2):
-                both = jnp.concatenate([first[ri][take], second[ri][take]], axis=0)
-                out_ref[c, ri, b * GROUP : (b + 2) * GROUP, :] = both.astype(BF16)
+                found[c, ri, b * GROUP : (b + 1) * GROUP, :] = both[ri][c * GROUP : (c + 1) * GROUP]
+    for c in range(channels):
+        for ri in range(2):
+            out_ref[c, ri] = found[c, ri].T.astype(BF16)
 
 
 def filterbank(voltages, halo, weights, scale, length, channels, part, h, start, frames, after):
-    block = min(frames, 64)
+    block = min(frames, FRAMES_PER_STEP)
     lanes = block * length
     head = halo.shape[2]
     first = start * length
@@ -126,14 +126,17 @@
             pl.BlockSpec(memory_space=pl.ANY),
         ],
         out_specs=[
-            pl.BlockSpec((channels, 2, block, part), lambda s: (0, 0, s, 0)),
+            pl.BlockSpec((channels, 2, part, block), lambda s: (0, 0, 0, s)),
             pl.BlockSpec(memory_space=pl.ANY),
         ],
         out_shape=[
-            jax.ShapeDtypeStruct((channels, 2, frames, part), BF16),
+            jax.ShapeDtypeStruct((channels, 2, part, frames), BF16),
             jax.ShapeDtypeStruct((8, LANES), F32),
         ],
-        scratch_shapes=[pltpu.VMEM((blocks, 2 * channels * GROUP, 2 * part), F32)],
+        scratch_shapes=[
+            pltpu.VMEM((blocks, 2 * channels * GROUP, 2 * part), F32),
+            pltpu.VMEM((channels, 2, block, part), F32),
+        ],
         compiler_params=params(),
         cost_estimate=pl.CostEstimate(
             flops=2 * weights.size * 2 * part * frames // GROUP,
@@ -144,79 +147,78 @@
     )(before, voltages, weights, scale, after)
 
 
-def correlate_kernel(nx, ny, span, weight, fresh, same, low, *refs):
-    xs = refs[:nx]
-    ys = xs if same else refs[nx : nx + ny]
-    at = nx if same else nx + ny
-    out_ref = refs[at] if fresh else refs[at + 1]
+def correlate_kernel(times, weight, fresh, same, low, first, *refs):
+    xs, ys = refs[:times[0]], refs[times[0] : sum(times)]
+    out_ref = refs[sum(times)] if fresh else refs[sum(times) + 1]
     i = pl.program_id(0) + low
-    part = xs[0].shape[3]
+    span, _, part, _ = xs[0].shape
     size = span * part
-    count = ys[0].shape[0] // span
-
-    def side(some, first, many, ri):
-        wide = [
-            jnp.concatenate([ref[first + d, ri] for d in range(many)], axis=1) for ref in some
-        ]
-        return wide[0] if len(wide) == 1 else jnp.concatenate(wide, axis=0)
-
-    real, imag = side(xs, i * span, span, 0).T, side(xs, i * span, span, 1).T
-    on_real = jnp.concatenate([real, imag], axis=0)
-    on_imag = jnp.concatenate([imag, -real], axis=0)
-    group = 2 if count % 2 == 0 else 1
-
-    def columns_from(first):
-        both = jnp.dot(on_real, side(ys, first * span, group * span, 0), preferred_element_type=F32)
-        both = both + jnp.dot(
-            on_imag, side(ys, first * span, group * span, 1), preferred_element_type=F32
-        )
-        both = both * weight
-        for n in range(group):
-            columns = slice(n * size, (n + 1) * size)
-            out_ref[2 * (first + n)] = both[:size, columns]
-            out_ref[2 * (first + n) + 1] = both[size:, columns]
-            if same:
-
-                @pl.when(i == first + n)
-                def _():
-                    row = lax.broadcasted_iota(jnp.int32, (size, size), 0)
-                    col = lax.broadcasted_iota(jnp.int32, (size, size), 1)
-                    out_ref[2 * (first + n)] = jnp.where(
-                        row >= col, both[:size, columns], both[size:, columns]
-                    )
-
-    for first in range(0, count, group):
-        if same and first > 0:
-            pl.when(i >= first)(functools.partial(columns_from, first))
-        else:
-            columns_from(first)
-
-
-def correlate(partial, total, slices, call, xs, ys, span, weight, same, low, high):
-    size = span * xs[0].shape[3]
-    frames = sum(x.shape[2] for x in xs)
-    spectra = xs if same else xs + ys
-    whole = [pl.BlockSpec(a.shape, lambda i: (0, 0, 0, 0)) for a in spectra]
-    out_block = pl.BlockSpec((2 * slices, size, size), lambda i: (call * slices + low + i, 0, 0))
+    group = ys[0].shape[0] // span
+
+    def side(some, ri):
+        wide = [jnp.concatenate([ref[d, ri] for d in range(ref.shape[0])], axis=0) for ref in some]
+        return wide[0] if len(wide) == 1 else jnp.concatenate(wide, axis=1)
+
+    real, imag = side(xs, 0), side(xs, 1)
+    turned = jnp.concatenate(
+        [jnp.concatenate([real, imag], axis=0), jnp.concatenate([imag, -real], axis=0)], axis=1
+    )
+    both = lax.dot_general(
+        turned,
+        jnp.concatenate([side(ys, 0), side(ys, 1)], axis=1),
+        (((1,), (1,)), ((), ())),
+        preferred_element_type=F32,
+    )
+    both = both * weight
+    for n in range(group):
+        columns = slice(n * size, (n + 1) * size)
+        out_ref[2 * n] = both[:size, columns]
+        out_ref[2 * n + 1] = both[size:, columns]
+        if same:
+
+            @pl.when(i == first + n)
+            def _():
+                row = lax.broadcasted_iota(jnp.int32, (size, size), 0)
+                col = lax.broadcasted_iota(jnp.int32, (size, size), 1)
+                out_ref[2 * n] = jnp.where(row >= col, both[:size, columns], both[size:, columns])
+
+
+def correlate(partial, total, slices, call, xs, ys, span, weight, same, which):
+    part = xs[0].shape[2]
+    size = span * part
+    frames = sum(x.shape[3] for x in xs)
+    group = slices // 2
+    low = which * group if same else 0
+    rows = [
+        pl.BlockSpec((span, 2, part, x.shape[3]), lambda i: (low + i, 0, 0, 0)) for x in xs
+    ]
+    columns = [
+        pl.BlockSpec((group * span, 2, part, y.shape[3]), lambda i: (which, 0, 0, 0)) for y in ys
+    ]
+    out_block = pl.BlockSpec(
+        (2 * group, size, size), lambda i: (2 * (call * slices + low + i) + which, 0, 0)
+    )
     shape = jax.ShapeDtypeStruct((total, size, size), F32)
     store = jax.ShapeDtypeStruct((total, size, size), BF16)
     fresh = partial is None
     anywhere = pl.BlockSpec(memory_space=pl.ANY)
     return pl.pallas_call(
-        functools.partial(correlate_kernel, len(xs), len(ys), span, weight, fresh, same, low),
-        grid=(high - low,),
-        in_specs=whole + ([] if fresh else [anywhere]),
+        functools.partial(
+            correlate_kernel, (len(xs), len(ys)), weight, fresh, same, low, which * group
+        ),
+        grid=(slices - low,),
+        in_specs=rows + columns + ([] if fresh else [anywhere]),
         out_specs=[out_block, anywhere, anywhere] if fresh else [out_block],
         out_shape=[shape, store, store] if fresh else [shape],
-        input_output_aliases={} if fresh else {len(whole): 0},
+        input_output_aliases={} if fresh else {len(xs) + len(ys): 0},
         compiler_params=params(),
         cost_estimate=pl.CostEstimate(
-            flops=8 * (high - low) * slices * size * size * frames,
-            bytes_accessed=8 * (high - low) * slices * size * size,
+            flops=8 * (slices - low) * group * size * size * frames,
+            bytes_accessed=8 * (slices - low) * group * size * size,
             transcendentals=0,
         ),
         name="correlate",
-    )(*spectra, *([] if fresh else [partial]))
+    )(*xs, *ys, *([] if fresh else [partial]))
 
 
 class Plan:
@@ -252,15 +254,16 @@
             if far:
                 late = self.late(i, j) and self.late(j, i)
                 for square in sorted(set(self.squares(h, i, k, j))):
-                    (queues[self.call_of(h, k)] if far > 1 else last).append((-far, late, square))
+                    entry = (-far, late, self.work_of(h, k, j), square)
+                    (queues[self.calls.index((h, k))] if far > 1 else last).append(entry)
         if self.slices == 2:
             queues, last = [last], []
         found = []
         for queue in [sorted(q) for q in queues] + [sorted(last)]:
             for at in range(0, len(queue), self.count):
                 some = queue[at : at + self.count]
-                ids = [square for _, _, square in some]
-                found.append((ids, max(-far for far, _, _ in some)))
+                ids = [entry[-1] for entry in some]
+                found.append((ids, max(-entry[0] for entry in some)))
         return found
 
     def late(self, z, j):
@@ -302,19 +305,19 @@
                             rows[z, step, side * self.count + b] = square
         return rows.reshape(-1)
 
-    def call_of(self, h, k):
-        return self.calls.index((h, k))
-
-    def last_call(self, step):
+    def work_of(self, h, k, j):
+        return 2 * self.calls.index((h, k)) + 2 * j // self.slices
+
+    def last_work(self, step):
         need = 0
         for messages in (self.right, self.left):
             for place in range(self.slices):
                 k = step - 2 * place
                 if 0 <= k < len(messages):
                     for square in messages[k][0]:
-                        for (h, i, c, j), at in self.pair_at.items():
+                        for (h, _, c, j), at in self.pair_at.items():
                             if at == square // 2:
-                                need = max(need, self.call_of(h, c))
+                                need = max(need, self.work_of(h, c, j))
         return need
 
     def outputs(self):
@@ -531,7 +534,7 @@
         tail = voltages[:, h * part : (h + 1) * part, samples - head :]
         halos.append(lax.ppermute(tail, "tm", [(i, i + 1) for i in range(slices - 1)]))
     weights = filterbank_weights(filter_taps, channels)
-    scale = (antenna_flags.astype(F32) / math.sqrt(length)).reshape(1, local)
+    scale = antenna_flags.reshape(1, local)
 
     plan = Plan(slices, parts, 4)
     table = jnp.asarray(plan.table())
@@ -552,30 +555,28 @@
             )
         spectra.append(found)
 
-    work = [
-        (call, h, k, low, min(low + 2, slices) if call == len(plan.calls) - 1 > 0 else slices)
-        for call, (h, k) in enumerate(plan.calls)
-        for low in (range(0, slices, 2) if call == len(plan.calls) - 1 > 0 else (0,))
-    ]
+    done = []
 
     def extend(partial, kept, count):
         for _ in range(count):
-            call, h, k, low, high = work.pop(0)
+            call, which = len(done) // 2, len(done) % 2
+            h, k = plan.calls[call]
             made = correlate(
-                partial, plan.total, slices, call, spectra[h], spectra[k], span, weight, h == k,
-                low, high,
+                partial, plan.total, slices, call, spectra[h], spectra[k], span, weight, h == k, which
             )
             partial = made[0]
             if kept is None:
                 kept = made[1:]
+            done.append(call)
         return partial, kept
 
     def needed(step):
-        must = sum(1 for item in work if item[0] <= plan.last_call(step))
-        soon = any(item[0] <= plan.last_call(step + n) for item in work for n in (1, 2))
-        return max(must, 1 if soon and step > 2 else 0)
-
-    partial, kept = extend(None, None, 1)
+        must = max(0, plan.last_work(step) + 1 - len(done))
+        soon = len(done) <= plan.last_work(step + 1)
+        early = soon and (len(done) < 2 or step > 3)
+        return max(must, 1 if early else 0)
+
+    partial, kept = None, None
     arrived, out = {}, None
     early = max(plan.first_ready(), plan.steps - 1)
     holds = []

time: 270 us -> 267 us (0.989)
  Pallas kernels: 126 us -> 132 us
  waiting for transfers between devices: 13.7 us -> 8.89 us
  starting transfers between devices: 121 us -> 118 us
    pallas_call x4 -> x6, Pallas kernels: 27.7 us -> 32.1 us  [correlate(): pl.pallas_call(functools.partial(correlate_kernel, (len(xs), len(ys)), we...]
    ppermute x15, starting transfers between devices: 85.3 us -> 82.6 us  [on_device(): lax.ppermute(outgoing[0], 'tm', right)]
  transfers between devices with their start and end apart: 35 -> 35, of which waited for: 10 -> 13; matrix products, arithmetic and copies ran while one was open for 0% -> 0% of each run, Pallas kernels for 44% -> 46%
where the time goes in v3:
time: 267 us; the launch traced here: 265 us
  Pallas kernels  132 us (49%)
  starting transfers between devices  118 us (44%)
  waiting for transfers between devices  8.89 us (3%)
  local copies, waits for them, and re-layouts  4.35 us (2%)
    ppermute x15, starting transfers between devices, on_device(): lax.ppermute(outgoing[0], 'tm', right)  82.6 us
    pallas_call x17, Pallas kernels, hop(): pl.pallas_call(functools.partial(hop_kernel, receives, sends, (2 if recei...  44.2 us
    pallas_call x3, Pallas kernels, filterbank(): pl.pallas_call(functools.partial(filterbank_kernel, channels, length), gr...  40.2 us
    pallas_call x6, Pallas kernels, correlate(): pl.pallas_call(functools.partial(correlate_kernel, (len(xs), len(ys)), we...  32.1 us
    ppermute x15, starting transfers between devices, on_device(): lax.ppermute(outgoing[1], 'tm', left)  15.6 us
    pallas_call x2, Pallas kernels, visibility_rows(): pl.pallas_call(functools.partial(rows_kernel, slices, parts, span, part,...  15.6 us
    all_to_all x3, starting transfers between devices, on_device(): lax.all_to_all(own, 'chan', split_axis=0, concat_axis=0, tiled=True)  11.6 us
    ppermute x2, starting transfers between devices, on_device(): lax.ppermute(tail, 'tm', [(i, i + 1) for i in range(slices - 1)])  8.41 us
  transfers between devices with their start and end apart: 35, of which 13 were waited for; matrix products, arithmetic and copies ran while one was open for 0% of the time, Pallas kernels for 46%

profile of v3, /device:TPU:0, one launch (start us, length us, event | category | flops | bytes accessed | tf_op | source)
XLA Modules:
  0.0 264.7 jit_solution(4618165531928408350)
XLA Ops:
  2.3 4.9 %collective-permute-start.1 = (bf16[2,128,1024]{2,1,0:T(8,128)(2,1)}, bf16[2,128,1024]{2,1,0:T(8,128)(2,1)S(1)}, u32[]{:S(2)}, u32[]{:S(2)}) collective-permute-start(bf16[2,128,1024]{2,1,0:T(8,128)(2,1)} %get-tuple-element.141), channel_id=1, source_target_pairs={{0,1},{1,2},{2,3},{4,5},{5,6},{6,7},{8,9},{9,10},{10,11},{12,13},{... | collective-permute-start | bytes 1572872 | tf_op jit(solution)/shard_map/ppermute | solution.py:535
  9.6 11.0 %filterbank_h0_f256.1 = (bf16[8,2,128,256]{3,2,1,0:T(8,128)(2,1)}, f32[8,128]{1,0:T(8,128)S(1)}) custom-call(bf16[2,256,32768]{2,1,0:T(8,128)(2,1)} %v_ref.5, bf16[2,256,32768]{2,1,0:T(8,128)(2,1)} %v_ref.5, bf16[768,512]{1,0:T(8,128)(2,1)S(1)} %weights.1.w_ref.after_ref, s32[1,256]{1,0:T(1,128)S(1)} %bitcast.3, bf16[768,512]{1,0:T(8,128)(2,1)S(1)} %weights.1.w_ref.after_ref), custom_call_target="tpu_custom_call" | custom-call | flops 6442450944 | bytes 8388608 | tf_op jit(solution)/shard_map/filterbank_h0_f256/pallas_call | solution.py:118
  20.6 3.7 %all-to-all-start.2 = ((bf16[8,2,128,256]{3,2,1,0:T(8,128)(2,1)}), bf16[8,2,128,256]{3,2,1,0:T(8,128)(2,1)S(1)}, u32[]{:S(2)}, u32[]{:S(2)}) async-start(bf16[8,2,128,256]{3,2,1,0:T(8,128)(2,1)} %get-tuple-element.77), calls=%async_computation.2 | async-start | bytes 2097152 | tf_op jit(solution)/shard_map/all_to_all | solution.py:554
  24.4 3.5 %collective-permute-start = (bf16[2,128,1024]{2,1,0:T(8,128)(2,1)}, bf16[2,128,1024]{2,1,0:T(8,128)(2,1)S(1)}, u32[]{:S(2)}, u32[]{:S(2)}) collective-permute-start(bf16[2,128,1024]{2,1,0:T(8,128)(2,1)} %get-tuple-element.142), channel_id=1, source_target_pairs={{0,1},{1,2},{2,3},{4,5},{5,6},{6,7},{8,9},{9,10},{10,11},{12,13},{... | collective-permute-start | bytes 1572872 | tf_op jit(solution)/shard_map/ppermute | solution.py:535
  27.9 11.0 %filterbank_h0_f0.1 = (bf16[8,2,128,256]{3,2,1,0:T(8,128)(2,1)}, f32[8,128]{1,0:T(8,128)S(1)}) custom-call(bf16[2,128,1024]{2,1,0:T(8,128)(2,1)S(1)} %collective-permute-done.1.head_ref, bf16[2,256,32768]{2,1,0:T(8,128)(2,1)} %v_ref.5, bf16[768,512]{1,0:T(8,128)(2,1)S(1)} %weights.1.w_ref.after_ref, s32[1,256]{1,0:T(1,128)S(1)} %bitcast.4, ...), custom_call_target="tpu_custom_call" | custom-call | flops 6442450944 | bytes 8388608 | tf_op jit(solution)/shard_map/filterbank_h0_f0/pallas_call | solution.py:118
  39.8 3.6 %all-to-all-start.1 = ((bf16[8,2,128,256]{3,2,1,0:T(8,128)(2,1)}), bf16[8,2,128,256]{3,2,1,0:T(8,128)(2,1)S(1)}, u32[]{:S(2)}, u32[]{:S(2)}) async-start(bf16[8,2,128,256]{3,2,1,0:T(8,128)(2,1)} %get-tuple-element.76), calls=%async_computation.1 | async-start | bytes 2097152 | tf_op jit(solution)/shard_map/all_to_all | solution.py:554
  43.4 18.3 %filterbank_h1_f0.1 = (bf16[8,2,128,512]{3,2,1,0:T(8,128)(2,1)}, f32[8,128]{1,0:T(8,128)}) custom-call(bf16[2,128,1024]{2,1,0:T(8,128)(2,1)S(1)} %collective-permute-done.head_ref, bf16[2,256,32768]{2,1,0:T(8,128)(2,1)} %v_ref.5, bf16[768,512]{1,0:T(8,128)(2,1)S(1)} %weights.1.w_ref.after_ref, s32[1,256]{1,0:T(1,128)S(1)} %bitcast.5, ...), custom_call_target="tpu_custom_call" | custom-call | flops 12884901888 | bytes 16777216 | tf_op jit(solution)/shard_map/filterbank_h1_f0/pallas_call | solution.py:118
  61.6 4.3 %all-to-all-start = ((bf16[8,2,128,512]{3,2,1,0:T(8,128)(2,1)}), bf16[8,2,128,512]{3,2,1,0:T(8,128)(2,1)}, u32[]{:S(2)}, u32[]{:S(2)}) async-start(bf16[8,2,128,512]{3,2,1,0:T(8,128)(2,1)} %get-tuple-element.75), calls=%async_computation | async-start | bytes 4194304 | tf_op jit(solution)/shard_map/all_to_all | solution.py:554
  66.0 5.9 %correlate.6 = (f32[104,256,256]{2,1,0:T(8,128)}, bf16[104,256,256]{2,1,0:T(8,128)(2,1)}, bf16[104,256,256]{2,1,0:T(8,128)(2,1)}) custom-call(bf16[8,2,128,256]{3,2,1,0:T(8,128)(2,1)S(1)} %all-to-all-done.1.refs_0_.refs_2_.refs_1_, bf16[8,2,128,256]{3,2,1,0:T(8,128)(2,1)} %copy-done.7, bf16[8,2,128,256]{3,2,1,0:T(8,128)(2,1)S(1)} %all-to-all-done.1.refs_0_.refs_2_.refs_1_, ...), custom_call_target="tpu_custom_call" | custom-call | flops 2147483648 | bytes 4194304 | tf_op jit(solution)/shard_map/correlate/pallas_call | solution.py:205
  74.2 3.5 %collective-permute-start.2 = (bf16[4,256,256]{2,1,0:T(8,128)(2,1)S(1)}, bf16[4,256,256]{2,1,0:T(8,128)(2,1)S(1)}, u32[]{:S(2)}, u32[]{:S(2)}) collective-permute-start(bf16[4,256,256]{2,1,0:T(8,128)(2,1)S(1)} %get-tuple-element.79), channel_id=1, source_target_pairs={{0,1},{4,5},{8,9},{12,13},{16,17},{20,21},{24,25},{28,29}} | collective-permute-start | bytes 1572872 | tf_op jit(solution)/shard_map/ppermute | solution.py:596
  78.3 3.9 %correlate.7.refs_2_.refs_0_ = f32[104,256,256]{2,1,0:T(8,128)} custom-call(bf16[8,2,128,256]{3,2,1,0:T(8,128)(2,1)S(1)} %all-to-all-done.1.refs_0_.refs_2_.refs_1_, bf16[8,2,128,256]{3,2,1,0:T(8,128)(2,1)} %copy-done.7, bf16[8,2,128,256]{3,2,1,0:T(8,128)(2,1)S(1)} %all-to-all-done.1.refs_0_.refs_2_.refs_1_, ...), custom_call_target="tpu_custom_call", output_to_operand_aliasing={{}: (4, {})} | custom-call | flops 1073741824 | bytes 2097152 | tf_op jit(solution)/shard_map/correlate/pallas_call | solution.py:205
  82.2 3.3 %hop.19 = (bf16[4,256,256]{2,1,0:T(8,128)(2,1)}, bf16[4,256,256]{2,1,0:T(8,128)(2,1)}) custom-call(s32[544]{0:T(1024)S(1)} %copy-done, s32[1]{0:T(128)} %bitcast.place, f32[104,256,256]{2,1,0:T(8,128)} %correlate.7.refs_2_.refs_0_), custom_call_target="tpu_custom_call" | custom-call | flops 1048576 | bytes 5242880 | tf_op jit(solution)/shard_map/hop/pallas_call | solution.py:400
  89.9 3.6 %hop.18 = (bf16[104,256,256]{2,1,0:T(8,128)(2,1)}, bf16[104,256,256]{2,1,0:T(8,128)(2,1)}, bf16[4,256,256]{2,1,0:T(8,128)(2,1)}, bf16[4,256,256]{2,1,0:T(8,128)(2,1)}) custom-call(s32[544]{0:T(1024)S(1)} %copy-done, s32[1]{0:T(128)} %bitcast.place, f32[104,256,256]{2,1,0:T(8,128)} %correlate.7.refs_2_.refs_0_, ...), custom_call_target="tpu_custom_call", output_to_operand_aliasing={{0}: (5, {}), {1}: (6, {})} | custom-call | flops 1048576 | bytes 5242880 | tf_op jit(solution)/shard_map/hop/pallas_call | solution.py:400
  93.5 4.4 %collective-permute-start.4 = (bf16[4,256,256]{2,1,0:T(8,128)(2,1)}, bf16[4,256,256]{2,1,0:T(8,128)(2,1)S(1)}, u32[]{:S(2)}, u32[]{:S(2)}) collective-permute-start(bf16[4,256,256]{2,1,0:T(8,128)(2,1)} %get-tuple-element.83), channel_id=1, source_target_pairs={{0,1},{1,2},{4,5},{5,6},{8,9},{9,10},{12,13},{13,14},{16,17},{17,1... | collective-permute-start | bytes 1572872 | tf_op jit(solution)/shard_map/ppermute | solution.py:596
  98.6 6.3 %correlate.8.refs_2_.refs_0_ = f32[104,256,256]{2,1,0:T(8,128)} custom-call(bf16[8,2,128,512]{3,2,1,0:T(8,128)(2,1)} %all-to-all-done.refs_0_.refs_1_, bf16[8,2,128,512]{3,2,1,0:T(8,128)(2,1)} %all-to-all-done.refs_0_.refs_1_, f32[104,256,256]{2,1,0:T(8,128)} %correlate.7.refs_2_.refs_0_), custom_call_target="tpu_custom_call", output_to_operand_aliasing={{}: (2, {})} | custom-call | flops 2147483648 | bytes 4194304 | tf_op jit(solution)/shard_map/correlate/pallas_call | solution.py:205
  107.6 4.8 %collective-permute-start.10 = (bf16[4,256,256]{2,1,0:T(8,128)(2,1)S(1)}, bf16[4,256,256]{2,1,0:T(8,128)(2,1)S(1)}, u32[]{:S(2)}, u32[]{:S(2)}) collective-permute-start(bf16[4,256,256]{2,1,0:T(8,128)(2,1)S(1)} %get-tuple-element.93), channel_id=1, source_target_pairs={{0,1},{1,2},{4,5},{5,6},{8,9},{9,10},{12,13},{13,14},{16,17},{17,1... | collective-permute-start | bytes 1572872 | tf_op jit(solution)/shard_map/ppermute | solution.py:596
  113.1 4.1 %correlate.9.refs_3_.refs_0_ = f32[104,256,256]{2,1,0:T(8,128)} custom-call(bf16[8,2,128,512]{3,2,1,0:T(8,128)(2,1)} %all-to-all-done.refs_0_.refs_1_, bf16[8,2,128,512]{3,2,1,0:T(8,128)(2,1)} %all-to-all-done.refs_0_.refs_1_, f32[104,256,256]{2,1,0:T(8,128)} %correlate.8.refs_2_.refs_0_), custom_call_target="tpu_custom_call", output_to_operand_aliasing={{}: (2, {})} | custom-call | flops 1073741824 | bytes 2097152 | tf_op jit(solution)/shard_map/correlate/pallas_call | solution.py:205
  119.9 5.1 %collective-permute-start.8 = (bf16[4,256,256]{2,1,0:T(8,128)(2,1)S(1)}, bf16[4,256,256]{2,1,0:T(8,128)(2,1)S(1)}, u32[]{:S(2)}, u32[]{:S(2)}) collective-permute-start(bf16[4,256,256]{2,1,0:T(8,128)(2,1)S(1)} %get-tuple-element.91), channel_id=1, source_target_pairs={{0,1},{1,2},{2,3},{4,5},{5,6},{6,7},{8,9},{9,10},{10,11},{12,13},{... | collective-permute-start | bytes 1572872 | tf_op jit(solution)/shard_map/ppermute | solution.py:596
  126.4 5.9 %correlate.10.refs_3_.refs_0_ = f32[104,256,256]{2,1,0:T(8,128)} custom-call(bf16[8,2,128,512]{3,2,1,0:T(8,128)(2,1)} %all-to-all-done.refs_0_.refs_1_, bf16[8,2,128,256]{3,2,1,0:T(8,128)(2,1)S(1)} %all-to-all-done.1.refs_0_.refs_2_.refs_1_, bf16[8,2,128,256]{3,2,1,0:T(8,128)(2,1)} %copy-done.7, ...), custom_call_target="tpu_custom_call", output_to_operand_aliasing={{}: (3, {})} | custom-call | flops 2147483648 | bytes 4194304 | tf_op jit(solution)/shard_map/correlate/pallas_call | solution.py:205
  134.9 5.2 %collective-permute-start.14 = (bf16[4,256,256]{2,1,0:T(8,128)(2,1)S(1)}, bf16[4,256,256]{2,1,0:T(8,128)(2,1)S(1)}, u32[]{:S(2)}, u32[]{:S(2)}) collective-permute-start(bf16[4,256,256]{2,1,0:T(8,128)(2,1)S(1)} %get-tuple-element.101), channel_id=1, source_target_pairs={{0,1},{1,2},{2,3},{4,5},{5,6},{6,7},{8,9},{9,10},{10,11},{12,13},{... | collective-permute-start | bytes 1572872 | tf_op jit(solution)/shard_map/ppermute | solution.py:596
  141.4 6.0 %correlate.11.refs_0_.refs_1_.refs_2_.refs_3_.refs_4_.refs_5_.refs_6_.refs_7_ = f32[104,256,256]{2,1,0:T(8,128)} custom-call(bf16[8,2,128,512]{3,2,1,0:T(8,128)(2,1)} %all-to-all-done.refs_0_.refs_1_, bf16[8,2,128,256]{3,2,1,0:T(8,128)(2,1)S(1)} %all-to-all-done.1.refs_0_.refs_2_.refs_1_, ...), custom_call_target="tpu_custom_call", output_to_operand_aliasing={{}: (3, {})} | custom-call | flops 2147483648 | bytes 4194304 | tf_op jit(solution)/shard_map/correlate/pallas_call | solution.py:205
  150.1 4.6 %collective-permute-start.12 = (bf16[4,256,256]{2,1,0:T(8,128)(2,1)S(1)}, bf16[4,256,256]{2,1,0:T(8,128)(2,1)S(1)}, u32[]{:S(2)}, u32[]{:S(2)}) collective-permute-start(bf16[4,256,256]{2,1,0:T(8,128)(2,1)S(1)} %get-tuple-element.99), channel_id=1, source_target_pairs={{0,1},{1,2},{4,5},{5,6},{8,9},{9,10},{12,13},{13,14},{16,17},{17,1... | collective-permute-start | bytes 1572872 | tf_op jit(solution)/shard_map/ppermute | solution.py:596
  158.0 4.5 %collective-permute-start.18 = (bf16[4,256,256]{2,1,0:T(8,128)(2,1)S(1)}, bf16[4,256,256]{2,1,0:T(8,128)(2,1)S(1)}, u32[]{:S(2)}, u32[]{:S(2)}) collective-permute-start(bf16[4,256,256]{2,1,0:T(8,128)(2,1)S(1)} %get-tuple-element.109), channel_id=1, source_target_pairs={{0,1},{1,2},{2,3},{4,5},{5,6},{6,7},{8,9},{9,10},{10,11},{12,13},{... | collective-permute-start | bytes 1572872 | tf_op jit(solution)/shard_map/ppermute | solution.py:596
  169.6 7.1 %collective-permute-start.16 = (bf16[4,256,256]{2,1,0:T(8,128)(2,1)S(1)}, bf16[4,256,256]{2,1,0:T(8,128)(2,1)S(1)}, u32[]{:S(2)}, u32[]{:S(2)}) collective-permute-start(bf16[4,256,256]{2,1,0:T(8,128)(2,1)S(1)} %get-tuple-element.107), channel_id=1, source_target_pairs={{0,1},{1,2},{2,3},{4,5},{5,6},{6,7},{8,9},{9,10},{10,11},{12,13},{... | collective-permute-start | bytes 1572872 | tf_op jit(solution)/shard_map/ppermute | solution.py:596
  180.9 7.1 %collective-permute-start.22 = (bf16[4,256,256]{2,1,0:T(8,128)(2,1)S(1)}, bf16[4,256,256]{2,1,0:T(8,128)(2,1)S(1)}, u32[]{:S(2)}, u32[]{:S(2)}) collective-permute-start(bf16[4,256,256]{2,1,0:T(8,128)(2,1)S(1)} %get-tuple-element.117), channel_id=1, source_target_pairs={{0,1},{1,2},{4,5},{5,6},{8,9},{9,10},{12,13},{13,14},{16,17},{17,1... | collective-permute-start | bytes 1572872 | tf_op jit(solution)/shard_map/ppermute | solution.py:596
  192.0 7.2 %collective-permute-start.20 = (bf16[4,256,256]{2,1,0:T(8,128)(2,1)S(1)}, bf16[4,256,256]{2,1,0:T(8,128)(2,1)S(1)}, u32[]{:S(2)}, u32[]{:S(2)}) collective-permute-start(bf16[4,256,256]{2,1,0:T(8,128)(2,1)S(1)} %get-tuple-element.115), channel_id=1, source_target_pairs={{0,1},{1,2},{2,3},{4,5},{5,6},{6,7},{8,9},{9,10},{10,11},{12,13},{... | collective-permute-start | bytes 1572872 | tf_op jit(solution)/shard_map/ppermute | solution.py:596
  203.2 7.2 %collective-permute-start.26 = (bf16[4,256,256]{2,1,0:T(8,128)(2,1)S(1)}, bf16[4,256,256]{2,1,0:T(8,128)(2,1)S(1)}, u32[]{:S(2)}, u32[]{:S(2)}) collective-permute-start(bf16[4,256,256]{2,1,0:T(8,128)(2,1)S(1)} %get-tuple-element.125), channel_id=1, source_target_pairs={{0,1},{1,2},{2,3},{4,5},{5,6},{6,7},{8,9},{9,10},{10,11},{12,13},{... | collective-permute-start | bytes 1572872 | tf_op jit(solution)/shard_map/ppermute | solution.py:596
  214.7 6.9 %collective-permute-start.24 = (bf16[4,256,256]{2,1,0:T(8,128)(2,1)S(1)}, bf16[4,256,256]{2,1,0:T(8,128)(2,1)S(1)}, u32[]{:S(2)}, u32[]{:S(2)}) collective-permute-start(bf16[4,256,256]{2,1,0:T(8,128)(2,1)S(1)} %get-tuple-element.123), channel_id=1, source_target_pairs={{0,1},{1,2},{2,3},{4,5},{5,6},{6,7},{8,9},{9,10},{10,11},{12,13},{... | collective-permute-start | bytes 1572872 | tf_op jit(solution)/shard_map/ppermute | solution.py:596
  226.0 6.9 %collective-permute-start.30 = (bf16[4,256,256]{2,1,0:T(8,128)(2,1)S(1)}, bf16[4,256,256]{2,1,0:T(8,128)(2,1)S(1)}, u32[]{:S(2)}, u32[]{:S(2)}) collective-permute-start(bf16[4,256,256]{2,1,0:T(8,128)(2,1)S(1)} %get-tuple-element.133), channel_id=1, source_target_pairs={{0,1},{1,2},{2,3},{4,5},{5,6},{6,7},{8,9},{9,10},{10,11},{12,13},{... | collective-permute-start | bytes 1572872 | tf_op jit(solution)/shard_map/ppermute | solution.py:596
  237.2 6.9 %collective-permute-start.28 = (bf16[4,256,256]{2,1,0:T(8,128)(2,1)S(1)}, bf16[4,256,256]{2,1,0:T(8,128)(2,1)S(1)}, u32[]{:S(2)}, u32[]{:S(2)}) collective-permute-start(bf16[4,256,256]{2,1,0:T(8,128)(2,1)S(1)} %get-tuple-element.131), channel_id=1, source_target_pairs={{0,1},{4,5},{8,9},{12,13},{16,17},{20,21},{24,25},{28,29}} | collective-permute-start | bytes 1572872 | tf_op jit(solution)/shard_map/ppermute | solution.py:596
  247.2 7.5 %visibility_rows.2.refs_4_.refs_24_ = f32[2,2,256,2,8,128]{5,4,3,2,1,0:T(8,128)} custom-call(s32[128]{0:T(128)S(1)} %copy-done.6, s32[64]{0:T(128)S(1)} %copy-done.5, s32[1]{0:T(128)} %bitcast.place, f32[104,256,256]{2,1,0:T(8,128)} %correlate.11.refs_0_.refs_1_.refs_2_.refs_3_.refs_4_.refs_5_.refs_6_.refs_7_, ...), custom_call_target="tpu_custom_call" | custom-call | flops 4194304 | bytes 12582912 | tf_op jit(solution)/shard_map/visibility_rows/pallas_call | solution.py:497
  256.4 8.1 %visibility_rows.3 = f32[2,2,256,2,8,128]{5,4,3,2,1,0:T(8,128)} custom-call(s32[128]{0:T(128)S(1)} %copy-done.6, s32[64]{0:T(128)S(1)} %copy-done.5, s32[1]{0:T(128)} %bitcast.place, f32[104,256,256]{2,1,0:T(8,128)} %correlate.11.refs_0_.refs_1_.refs_2_.refs_3_.refs_4_.refs_5_.refs_6_.refs_7_, ...), custom_call_target="tpu_custom_call", output_to_operand_aliasing={{}: (27, {})} | custom-call | flops 4194304 | bytes 12582912 | tf_op jit(solution)/shard_map/visibility_rows/pallas_call | solution.py:497
  (84 shorter events, 67.8 us)
Async XLA Ops:
  2.3 25.6 %collective-permute-start.1 = (bf16[2,128,1024]{2,1,0:T(8,128)(2,1)}, bf16[2,128,1024]{2,1,0:T(8,128)(2,1)S(1)}, u32[]{:S(2)}, u32[]{:S(2)}) collective-permute-start(bf16[2,128,1024]{2,1,0:T(8,128)(2,1)} %get-tuple-element.141), channel_id=1, source_target_pairs={{0,1},{1,2},{2,3},{4,5},{5,6},{6,7},{8,9},{9,10},{10,11},{12,13},{... | collective-permute-start | bytes 1572872 | tf_op jit(solution)/shard_map/ppermute | solution.py:535
  20.6 19.1 %all-to-all-start.2 = ((bf16[8,2,128,256]{3,2,1,0:T(8,128)(2,1)}), bf16[8,2,128,256]{3,2,1,0:T(8,128)(2,1)S(1)}, u32[]{:S(2)}, u32[]{:S(2)}) async-start(bf16[8,2,128,256]{3,2,1,0:T(8,128)(2,1)} %get-tuple-element.77), calls=%async_computation.2 | async-start | bytes 2097152 | tf_op jit(solution)/shard_map/all_to_all | solution.py:554
  24.4 19.0 %collective-permute-start = (bf16[2,128,1024]{2,1,0:T(8,128)(2,1)}, bf16[2,128,1024]{2,1,0:T(8,128)(2,1)S(1)}, u32[]{:S(2)}, u32[]{:S(2)}) collective-permute-start(bf16[2,128,1024]{2,1,0:T(8,128)(2,1)} %get-tuple-element.142), channel_id=1, source_target_pairs={{0,1},{1,2},{2,3},{4,5},{5,6},{6,7},{8,9},{9,10},{10,11},{12,13},{... | collective-permute-start | bytes 1572872 | tf_op jit(solution)/shard_map/ppermute | solution.py:535
  39.8 21.9 %all-to-all-start.1 = ((bf16[8,2,128,256]{3,2,1,0:T(8,128)(2,1)}), bf16[8,2,128,256]{3,2,1,0:T(8,128)(2,1)S(1)}, u32[]{:S(2)}, u32[]{:S(2)}) async-start(bf16[8,2,128,256]{3,2,1,0:T(8,128)(2,1)} %get-tuple-element.76), calls=%async_computation.1 | async-start | bytes 2097152 | tf_op jit(solution)/shard_map/all_to_all | solution.py:554
  61.6 37.0 %all-to-all-start = ((bf16[8,2,128,512]{3,2,1,0:T(8,128)(2,1)}), bf16[8,2,128,512]{3,2,1,0:T(8,128)(2,1)}, u32[]{:S(2)}, u32[]{:S(2)}) async-start(bf16[8,2,128,512]{3,2,1,0:T(8,128)(2,1)} %get-tuple-element.75), calls=%async_computation | async-start | bytes 4194304 | tf_op jit(solution)/shard_map/all_to_all | solution.py:554
  74.2 15.7 %collective-permute-start.2 = (bf16[4,256,256]{2,1,0:T(8,128)(2,1)S(1)}, bf16[4,256,256]{2,1,0:T(8,128)(2,1)S(1)}, u32[]{:S(2)}, u32[]{:S(2)}) collective-permute-start(bf16[4,256,256]{2,1,0:T(8,128)(2,1)S(1)} %get-tuple-element.79), channel_id=1, source_target_pairs={{0,1},{4,5},{8,9},{12,13},{16,17},{20,21},{24,25},{28,29}} | collective-permute-start | bytes 1572872 | tf_op jit(solution)/shard_map/ppermute | solution.py:596
  85.5 19.5 %collective-permute-start.6 = (bf16[4,256,256]{2,1,0:T(8,128)(2,1)}, bf16[4,256,256]{2,1,0:T(8,128)(2,1)S(1)}, u32[]{:S(2)}, u32[]{:S(2)}) collective-permute-start(bf16[4,256,256]{2,1,0:T(8,128)(2,1)} %get-tuple-element.85), channel_id=1, source_target_pairs={{0,1},{4,5},{8,9},{12,13},{16,17},{20,21},{24,25},{28,29}} | collective-permute-start | bytes 1572872 | tf_op jit(solution)/shard_map/ppermute | solution.py:596
  86.8 18.1 %collective-permute-start.7 = (bf16[4,256,256]{2,1,0:T(8,128)(2,1)}, bf16[4,256,256]{2,1,0:T(8,128)(2,1)S(1)}, u32[]{:S(2)}, u32[]{:S(2)}) collective-permute-start(bf16[4,256,256]{2,1,0:T(8,128)(2,1)} %get-tuple-element.86), channel_id=1, source_target_pairs={{3,2},{7,6},{11,10},{15,14},{19,18},{23,22},{27,26},{31,30}} | collective-permute-start | bytes 1572872 | tf_op jit(solution)/shard_map/ppermute | solution.py:597
  93.5 23.8 %collective-permute-start.4 = (bf16[4,256,256]{2,1,0:T(8,128)(2,1)}, bf16[4,256,256]{2,1,0:T(8,128)(2,1)S(1)}, u32[]{:S(2)}, u32[]{:S(2)}) collective-permute-start(bf16[4,256,256]{2,1,0:T(8,128)(2,1)} %get-tuple-element.83), channel_id=1, source_target_pairs={{0,1},{1,2},{4,5},{5,6},{8,9},{9,10},{12,13},{13,14},{16,17},{17,1... | collective-permute-start | bytes 1572872 | tf_op jit(solution)/shard_map/ppermute | solution.py:596
  97.9 19.4 %collective-permute-start.5 = (bf16[4,256,256]{2,1,0:T(8,128)(2,1)}, bf16[4,256,256]{2,1,0:T(8,128)(2,1)S(1)}, u32[]{:S(2)}, u32[]{:S(2)}) collective-permute-start(bf16[4,256,256]{2,1,0:T(8,128)(2,1)} %get-tuple-element.84), channel_id=1, source_target_pairs={{3,2},{2,1},{7,6},{6,5},{11,10},{10,9},{15,14},{14,13},{19,18},{18... | collective-permute-start | bytes 1572872 | tf_op jit(solution)/shard_map/ppermute | solution.py:597
  107.6 24.7 %collective-permute-start.10 = (bf16[4,256,256]{2,1,0:T(8,128)(2,1)S(1)}, bf16[4,256,256]{2,1,0:T(8,128)(2,1)S(1)}, u32[]{:S(2)}, u32[]{:S(2)}) collective-permute-start(bf16[4,256,256]{2,1,0:T(8,128)(2,1)S(1)} %get-tuple-element.93), channel_id=1, source_target_pairs={{0,1},{1,2},{4,5},{5,6},{8,9},{9,10},{12,13},{13,14},{16,17},{17,1... | collective-permute-start | bytes 1572872 | tf_op jit(solution)/shard_map/ppermute | solution.py:596
  112.4 19.9 %collective-permute-start.11 = (bf16[4,256,256]{2,1,0:T(8,128)(2,1)S(1)}, bf16[4,256,256]{2,1,0:T(8,128)(2,1)S(1)}, u32[]{:S(2)}, u32[]{:S(2)}) collective-permute-start(bf16[4,256,256]{2,1,0:T(8,128)(2,1)S(1)} %get-tuple-element.94), channel_id=1, source_target_pairs={{3,2},{2,1},{7,6},{6,5},{11,10},{10,9},{15,14},{14,13},{19,18},{18... | collective-permute-start | bytes 1572872 | tf_op jit(solution)/shard_map/ppermute | solution.py:597
  119.9 27.5 %collective-permute-start.8 = (bf16[4,256,256]{2,1,0:T(8,128)(2,1)S(1)}, bf16[4,256,256]{2,1,0:T(8,128)(2,1)S(1)}, u32[]{:S(2)}, u32[]{:S(2)}) collective-permute-start(bf16[4,256,256]{2,1,0:T(8,128)(2,1)S(1)} %get-tuple-element.91), channel_id=1, source_target_pairs={{0,1},{1,2},{2,3},{4,5},{5,6},{6,7},{8,9},{9,10},{10,11},{12,13},{... | collective-permute-start | bytes 1572872 | tf_op jit(solution)/shard_map/ppermute | solution.py:596
  125.1 22.4 %collective-permute-start.9 = (bf16[4,256,256]{2,1,0:T(8,128)(2,1)S(1)}, bf16[4,256,256]{2,1,0:T(8,128)(2,1)S(1)}, u32[]{:S(2)}, u32[]{:S(2)}) collective-permute-start(bf16[4,256,256]{2,1,0:T(8,128)(2,1)S(1)} %get-tuple-element.92), channel_id=1, source_target_pairs={{3,2},{2,1},{1,0},{7,6},{6,5},{5,4},{11,10},{10,9},{9,8},{15,14},{... | collective-permute-start | bytes 1572872 | tf_op jit(solution)/shard_map/ppermute | solution.py:597
  134.9 20.4 %collective-permute-start.14 = (bf16[4,256,256]{2,1,0:T(8,128)(2,1)S(1)}, bf16[4,256,256]{2,1,0:T(8,128)(2,1)S(1)}, u32[]{:S(2)}, u32[]{:S(2)}) collective-permute-start(bf16[4,256,256]{2,1,0:T(8,128)(2,1)S(1)} %get-tuple-element.101), channel_id=1, source_target_pairs={{0,1},{1,2},{2,3},{4,5},{5,6},{6,7},{8,9},{9,10},{10,11},{12,13},{... | collective-permute-start | bytes 1572872 | tf_op jit(solution)/shard_map/ppermute | solution.py:596
  140.1 15.2 %collective-permute-start.15 = (bf16[4,256,256]{2,1,0:T(8,128)(2,1)S(1)}, bf16[4,256,256]{2,1,0:T(8,128)(2,1)S(1)}, u32[]{:S(2)}, u32[]{:S(2)}) collective-permute-start(bf16[4,256,256]{2,1,0:T(8,128)(2,1)S(1)} %get-tuple-element.102), channel_id=1, source_target_pairs={{3,2},{2,1},{1,0},{7,6},{6,5},{5,4},{11,10},{10,9},{9,8},{15,14},{... | collective-permute-start | bytes 1572872 | tf_op jit(solution)/shard_map/ppermute | solution.py:597
  150.1 16.9 %collective-permute-start.12 = (bf16[4,256,256]{2,1,0:T(8,128)(2,1)S(1)}, bf16[4,256,256]{2,1,0:T(8,128)(2,1)S(1)}, u32[]{:S(2)}, u32[]{:S(2)}) collective-permute-start(bf16[4,256,256]{2,1,0:T(8,128)(2,1)S(1)} %get-tuple-element.99), channel_id=1, source_target_pairs={{0,1},{1,2},{4,5},{5,6},{8,9},{9,10},{12,13},{13,14},{16,17},{17,1... | collective-permute-start | bytes 1572872 | tf_op jit(solution)/shard_map/ppermute | solution.py:596
  158.0 20.2 %collective-permute-start.18 = (bf16[4,256,256]{2,1,0:T(8,128)(2,1)S(1)}, bf16[4,256,256]{2,1,0:T(8,128)(2,1)S(1)}, u32[]{:S(2)}, u32[]{:S(2)}) collective-permute-start(bf16[4,256,256]{2,1,0:T(8,128)(2,1)S(1)} %get-tuple-element.109), channel_id=1, source_target_pairs={{0,1},{1,2},{2,3},{4,5},{5,6},{6,7},{8,9},{9,10},{10,11},{12,13},{... | collective-permute-start | bytes 1572872 | tf_op jit(solution)/shard_map/ppermute | solution.py:596
  162.5 15.7 %collective-permute-start.19 = (bf16[4,256,256]{2,1,0:T(8,128)(2,1)S(1)}, bf16[4,256,256]{2,1,0:T(8,128)(2,1)S(1)}, u32[]{:S(2)}, u32[]{:S(2)}) collective-permute-start(bf16[4,256,256]{2,1,0:T(8,128)(2,1)S(1)} %get-tuple-element.110), channel_id=1, source_target_pairs={{3,2},{2,1},{1,0},{7,6},{6,5},{5,4},{11,10},{10,9},{9,8},{15,14},{... | collective-permute-start | bytes 1572872 | tf_op jit(solution)/shard_map/ppermute | solution.py:597
  169.6 19.7 %collective-permute-start.16 = (bf16[4,256,256]{2,1,0:T(8,128)(2,1)S(1)}, bf16[4,256,256]{2,1,0:T(8,128)(2,1)S(1)}, u32[]{:S(2)}, u32[]{:S(2)}) collective-permute-start(bf16[4,256,256]{2,1,0:T(8,128)(2,1)S(1)} %get-tuple-element.107), channel_id=1, source_target_pairs={{0,1},{1,2},{2,3},{4,5},{5,6},{6,7},{8,9},{9,10},{10,11},{12,13},{... | collective-permute-start | bytes 1572872 | tf_op jit(solution)/shard_map/ppermute | solution.py:596
  176.7 12.6 %collective-permute-start.17 = (bf16[4,256,256]{2,1,0:T(8,128)(2,1)S(1)}, bf16[4,256,256]{2,1,0:T(8,128)(2,1)S(1)}, u32[]{:S(2)}, u32[]{:S(2)}) collective-permute-start(bf16[4,256,256]{2,1,0:T(8,128)(2,1)S(1)} %get-tuple-element.108), channel_id=1, source_target_pairs={{3,2},{2,1},{1,0},{7,6},{6,5},{5,4},{11,10},{10,9},{9,8},{15,14},{... | collective-permute-start | bytes 1572872 | tf_op jit(solution)/shard_map/ppermute | solution.py:597
  180.9 19.7 %collective-permute-start.22 = (bf16[4,256,256]{2,1,0:T(8,128)(2,1)S(1)}, bf16[4,256,256]{2,1,0:T(8,128)(2,1)S(1)}, u32[]{:S(2)}, u32[]{:S(2)}) collective-permute-start(bf16[4,256,256]{2,1,0:T(8,128)(2,1)S(1)} %get-tuple-element.117), channel_id=1, source_target_pairs={{0,1},{1,2},{4,5},{5,6},{8,9},{9,10},{12,13},{13,14},{16,17},{17,1... | collective-permute-start | bytes 1572872 | tf_op jit(solution)/shard_map/ppermute | solution.py:596
  187.9 12.6 %collective-permute-start.23 = (bf16[4,256,256]{2,1,0:T(8,128)(2,1)S(1)}, bf16[4,256,256]{2,1,0:T(8,128)(2,1)S(1)}, u32[]{:S(2)}, u32[]{:S(2)}) collective-permute-start(bf16[4,256,256]{2,1,0:T(8,128)(2,1)S(1)} %get-tuple-element.118), channel_id=1, source_target_pairs={{3,2},{2,1},{7,6},{6,5},{11,10},{10,9},{15,14},{14,13},{19,18},{18... | collective-permute-start | bytes 1572872 | tf_op jit(solution)/shard_map/ppermute | solution.py:597
  192.0 19.8 %collective-permute-start.20 = (bf16[4,256,256]{2,1,0:T(8,128)(2,1)S(1)}, bf16[4,256,256]{2,1,0:T(8,128)(2,1)S(1)}, u32[]{:S(2)}, u32[]{:S(2)}) collective-permute-start(bf16[4,256,256]{2,1,0:T(8,128)(2,1)S(1)} %get-tuple-element.115), channel_id=1, source_target_pairs={{0,1},{1,2},{2,3},{4,5},{5,6},{6,7},{8,9},{9,10},{10,11},{12,13},{... | collective-permute-start | bytes 1572872 | tf_op jit(solution)/shard_map/ppermute | solution.py:596
  199.2 12.9 %collective-permute-start.21 = (bf16[4,256,256]{2,1,0:T(8,128)(2,1)S(1)}, bf16[4,256,256]{2,1,0:T(8,128)(2,1)S(1)}, u32[]{:S(2)}, u32[]{:S(2)}) collective-permute-start(bf16[4,256,256]{2,1,0:T(8,128)(2,1)S(1)} %get-tuple-element.116), channel_id=1, source_target_pairs={{3,2},{2,1},{1,0},{7,6},{6,5},{5,4},{11,10},{10,9},{9,8},{15,14},{... | collective-permute-start | bytes 1572872 | tf_op jit(solution)/shard_map/ppermute | solution.py:597
  203.2 19.8 %collective-permute-start.26 = (bf16[4,256,256]{2,1,0:T(8,128)(2,1)S(1)}, bf16[4,256,256]{2,1,0:T(8,128)(2,1)S(1)}, u32[]{:S(2)}, u32[]{:S(2)}) collective-permute-start(bf16[4,256,256]{2,1,0:T(8,128)(2,1)S(1)} %get-tuple-element.125), channel_id=1, source_target_pairs={{0,1},{1,2},{2,3},{4,5},{5,6},{6,7},{8,9},{9,10},{10,11},{12,13},{... | collective-permute-start | bytes 1572872 | tf_op jit(solution)/shard_map/ppermute | solution.py:596
  210.4 12.9 %collective-permute-start.27 = (bf16[4,256,256]{2,1,0:T(8,128)(2,1)S(1)}, bf16[4,256,256]{2,1,0:T(8,128)(2,1)S(1)}, u32[]{:S(2)}, u32[]{:S(2)}) collective-permute-start(bf16[4,256,256]{2,1,0:T(8,128)(2,1)S(1)} %get-tuple-element.126), channel_id=1, source_target_pairs={{3,2},{2,1},{1,0},{7,6},{6,5},{5,4},{11,10},{10,9},{9,8},{15,14},{... | collective-permute-start | bytes 1572872 | tf_op jit(solution)/shard_map/ppermute | solution.py:597
  214.7 19.5 %collective-permute-start.24 = (bf16[4,256,256]{2,1,0:T(8,128)(2,1)S(1)}, bf16[4,256,256]{2,1,0:T(8,128)(2,1)S(1)}, u32[]{:S(2)}, u32[]{:S(2)}) collective-permute-start(bf16[4,256,256]{2,1,0:T(8,128)(2,1)S(1)} %get-tuple-element.123), channel_id=1, source_target_pairs={{0,1},{1,2},{2,3},{4,5},{5,6},{6,7},{8,9},{9,10},{10,11},{12,13},{... | collective-permute-start | bytes 1572872 | tf_op jit(solution)/shard_map/ppermute | solution.py:596
  221.6 12.9 %collective-permute-start.25 = (bf16[4,256,256]{2,1,0:T(8,128)(2,1)S(1)}, bf16[4,256,256]{2,1,0:T(8,128)(2,1)S(1)}, u32[]{:S(2)}, u32[]{:S(2)}) collective-permute-start(bf16[4,256,256]{2,1,0:T(8,128)(2,1)S(1)} %get-tuple-element.124), channel_id=1, source_target_pairs={{3,2},{2,1},{1,0},{7,6},{6,5},{5,4},{11,10},{10,9},{9,8},{15,14},{... | collective-permute-start | bytes 1572872 | tf_op jit(solution)/shard_map/ppermute | solution.py:597
  226.0 19.5 %collective-permute-start.30 = (bf16[4,256,256]{2,1,0:T(8,128)(2,1)S(1)}, bf16[4,256,256]{2,1,0:T(8,128)(2,1)S(1)}, u32[]{:S(2)}, u32[]{:S(2)}) collective-permute-start(bf16[4,256,256]{2,1,0:T(8,128)(2,1)S(1)} %get-tuple-element.133), channel_id=1, source_target_pairs={{0,1},{1,2},{2,3},{4,5},{5,6},{6,7},{8,9},{9,10},{10,11},{12,13},{... | collective-permute-start | bytes 1572872 | tf_op jit(solution)/shard_map/ppermute | solution.py:596
  232.9 12.6 %collective-permute-start.31 = (bf16[4,256,256]{2,1,0:T(8,128)(2,1)S(1)}, bf16[4,256,256]{2,1,0:T(8,128)(2,1)S(1)}, u32[]{:S(2)}, u32[]{:S(2)}) collective-permute-start(bf16[4,256,256]{2,1,0:T(8,128)(2,1)S(1)} %get-tuple-element.134), channel_id=1, source_target_pairs={{3,2},{2,1},{1,0},{7,6},{6,5},{5,4},{11,10},{10,9},{9,8},{15,14},{... | collective-permute-start | bytes 1572872 | tf_op jit(solution)/shard_map/ppermute | solution.py:597
  237.2 17.5 %collective-permute-start.28 = (bf16[4,256,256]{2,1,0:T(8,128)(2,1)S(1)}, bf16[4,256,256]{2,1,0:T(8,128)(2,1)S(1)}, u32[]{:S(2)}, u32[]{:S(2)}) collective-permute-start(bf16[4,256,256]{2,1,0:T(8,128)(2,1)S(1)} %get-tuple-element.131), channel_id=1, source_target_pairs={{0,1},{4,5},{8,9},{12,13},{16,17},{20,21},{24,25},{28,29}} | collective-permute-start | bytes 1572872 | tf_op jit(solution)/shard_map/ppermute | solution.py:596
  (11 other events, 106.5 us)

commit v4 on v3

--- a/solution.py
+++ b/solution.py
@@ -38,11 +38,10 @@
     each = size // LANES
     for t in range(wide.shape[0]):
         full = wide[t]
-        high = full.astype(BF16)
-        low = (full - high.astype(F32)).astype(BF16)
+        high = full.astype(BF16).astype(F32)
         m, lanes = t // each, slice(t % each * LANES, (t % each + 1) * LANES)
-        out_ref[2 * m * n : (2 * m + 1) * n, lanes] = high
-        out_ref[(2 * m + 1) * n : (2 * m + 2) * n, lanes] = low
+        both = jnp.concatenate([high, full - high], axis=0).astype(BF16)
+        out_ref[2 * m * n : 2 * (m + 1) * n, lanes] = both
 
 
 def filterbank_weights(filter_taps, channels):
@@ -50,7 +49,8 @@
     phase = np.arange(length)[None, :] * np.arange(channels)[:, None] % length
     angle = phase * (2.0 * math.pi / length)
     trig = np.stack([np.cos(angle), np.sin(angle)]).reshape(2 * channels, length)
-    rows = 2 * channels * GROUP
+    trig = np.delete(trig, channels, axis=0)
+    rows = trig.shape[0] * GROUP
     blocks = taps // GROUP + 1
     return pl.pallas_call(
         weights_kernel,
@@ -67,7 +67,7 @@
     _, part, lanes = v_ref.shape
     size = GROUP * length
     half = channels * GROUP
-    rows = 2 * half
+    rows = carry.shape[1]
     blocks = w_ref.shape[0] // (2 * rows)
     scale = s_ref[...].astype(F32) / math.sqrt(length)
 
@@ -93,13 +93,14 @@
     for b in range(lanes // size):
         done = advance(v_ref, b)
         cos, sin = done[:half], done[half:]
-        both = (
-            (cos[:, :part] + sin[:, part:]) * scale,
-            (cos[:, part:] - sin[:, :part]) * scale,
-        )
         for c in range(channels):
-            for ri in range(2):
-                found[c, ri, b * GROUP : (b + 1) * GROUP, :] = both[ri][c * GROUP : (c + 1) * GROUP]
+            at = slice(c * GROUP, (c + 1) * GROUP)
+            real, imag = cos[at, :part], cos[at, part:]
+            if c > 0:
+                at = slice((c - 1) * GROUP, c * GROUP)
+                real, imag = real + sin[at, part:], imag - sin[at, :part]
+            found[c, 0, b * GROUP : (b + 1) * GROUP, :] = real * scale
+            found[c, 1, b * GROUP : (b + 1) * GROUP, :] = imag * scale
     for c in range(channels):
         for ri in range(2):
             out_ref[c, ri] = found[c, ri].T.astype(BF16)
@@ -134,7 +135,7 @@
             jax.ShapeDtypeStruct((8, LANES), F32),
         ],
         scratch_shapes=[
-            pltpu.VMEM((blocks, 2 * channels * GROUP, 2 * part), F32),
+            pltpu.VMEM((blocks, (2 * channels - 1) * GROUP, 2 * part), F32),
             pltpu.VMEM((channels, 2, block, part), F32),
         ],
         compiler_params=params(),
@@ -147,40 +148,51 @@
     )(before, voltages, weights, scale, after)
 
 
-def correlate_kernel(times, weight, fresh, same, low, first, *refs):
+def correlate_kernel(times, span, weight, fresh, same, low, first, *refs):
     xs, ys = refs[:times[0]], refs[times[0] : sum(times)]
     out_ref = refs[sum(times)] if fresh else refs[sum(times) + 1]
-    i = pl.program_id(0) + low
-    span, _, part, _ = xs[0].shape
+    part = xs[0].shape[2]
     size = span * part
     group = ys[0].shape[0] // span
-
-    def side(some, ri):
-        wide = [jnp.concatenate([ref[d, ri] for d in range(ref.shape[0])], axis=0) for ref in some]
+    many = xs[0].shape[0] // span
+
+    def side(some, start, count, ri):
+        wide = [
+            jnp.concatenate([ref[start + d, ri] for d in range(count)], axis=0) for ref in some
+        ]
         return wide[0] if len(wide) == 1 else jnp.concatenate(wide, axis=1)
 
-    real, imag = side(xs, 0), side(xs, 1)
+    on_real, on_imag = [], []
+    for n in range(many):
+        real, imag = side(xs, n * span, span, 0), side(xs, n * span, span, 1)
+        on_real += [real, imag]
+        on_imag += [imag, -real]
     turned = jnp.concatenate(
-        [jnp.concatenate([real, imag], axis=0), jnp.concatenate([imag, -real], axis=0)], axis=1
+        [jnp.concatenate(on_real, axis=0), jnp.concatenate(on_imag, axis=0)], axis=1
     )
+    other = [side(ys, 0, group * span, ri) for ri in range(2)]
     both = lax.dot_general(
         turned,
-        jnp.concatenate([side(ys, 0), side(ys, 1)], axis=1),
+        jnp.concatenate(other, axis=1),
         (((1,), (1,)), ((), ())),
         preferred_element_type=F32,
     )
     both = both * weight
-    for n in range(group):
-        columns = slice(n * size, (n + 1) * size)
-        out_ref[2 * n] = both[:size, columns]
-        out_ref[2 * n + 1] = both[size:, columns]
-        if same:
-
-            @pl.when(i == first + n)
-            def _():
-                row = lax.broadcasted_iota(jnp.int32, (size, size), 0)
-                col = lax.broadcasted_iota(jnp.int32, (size, size), 1)
-                out_ref[2 * n] = jnp.where(row >= col, both[:size, columns], both[size:, columns])
+    for m in range(many):
+        i = pl.program_id(0) * many + low + m
+        real = both[2 * m * size : (2 * m + 1) * size]
+        imag = both[(2 * m + 1) * size : (2 * m + 2) * size]
+        for n in range(group):
+            columns = slice(n * size, (n + 1) * size)
+            out_ref[m, 2 * n] = real[:, columns]
+            out_ref[m, 2 * n + 1] = imag[:, columns]
+            if same:
+
+                @pl.when(i == first + n)
+                def _():
+                    row = lax.broadcasted_iota(jnp.int32, (size, size), 0)
+                    col = lax.broadcasted_iota(jnp.int32, (size, size), 1)
+                    out_ref[m, 2 * n] = jnp.where(row >= col, real[:, columns], imag[:, columns])
 
 
 def correlate(partial, total, slices, call, xs, ys, span, weight, same, which):
@@ -189,24 +201,29 @@
     frames = sum(x.shape[3] for x in xs)
     group = slices // 2
     low = which * group if same else 0
+    many = 2 if low % 2 == 0 else 1
     rows = [
-        pl.BlockSpec((span, 2, part, x.shape[3]), lambda i: (low + i, 0, 0, 0)) for x in xs
+        pl.BlockSpec((many * span, 2, part, x.shape[3]), lambda i: (low // many + i, 0, 0, 0))
+        for x in xs
     ]
     columns = [
         pl.BlockSpec((group * span, 2, part, y.shape[3]), lambda i: (which, 0, 0, 0)) for y in ys
     ]
     out_block = pl.BlockSpec(
-        (2 * group, size, size), lambda i: (2 * (call * slices + low + i) + which, 0, 0)
+        (many, 2 * group, size, size), lambda i: ((call * slices + low) // many + i, which, 0, 0)
     )
-    shape = jax.ShapeDtypeStruct((total, size, size), F32)
+    lines = total // (2 * slices)
+    shape = jax.ShapeDtypeStruct((lines, 2 * slices, size, size), F32)
     store = jax.ShapeDtypeStruct((total, size, size), BF16)
     fresh = partial is None
+    if not fresh:
+        partial = partial.reshape(shape.shape)
     anywhere = pl.BlockSpec(memory_space=pl.ANY)
-    return pl.pallas_call(
+    made = pl.pallas_call(
         functools.partial(
-            correlate_kernel, (len(xs), len(ys)), weight, fresh, same, low, which * group
+            correlate_kernel, (len(xs), len(ys)), span, weight, fresh, same, low, which * group
         ),
-        grid=(slices - low,),
+        grid=((slices - low) // many,),
         in_specs=rows + columns + ([] if fresh else [anywhere]),
         out_specs=[out_block, anywhere, anywhere] if fresh else [out_block],
         out_shape=[shape, store, store] if fresh else [shape],
@@ -219,6 +236,7 @@
         ),
         name="correlate",
     )(*xs, *ys, *([] if fresh else [partial]))
+    return [made[0].reshape(total, size, size)] + list(made[1:])
 
 
 class Plan:
@@ -235,7 +253,7 @@
                         if k < h or j <= i:
                             self.pair_at[h, i, k, j] = first + i * slices + j
         self.spare = 2 * len(self.calls) * slices * slices
-        self.total = self.spare + 2 * count
+        self.total = self.spare + -(-2 * count // (2 * slices)) * 2 * slices
         self.right = self.messages(lambda i, j: max(i, j))
         self.left = self.messages(lambda i, j: slices - 1 - min(i, j))
         self.steps = 0
@@ -254,6 +272,8 @@
             if far:
                 late = self.late(i, j) and self.late(j, i)
                 for square in sorted(set(self.squares(h, i, k, j))):
+                    if far == 1:
+                        late = self.only_last(h, i, k, j)
                     entry = (-far, late, self.work_of(h, k, j), square)
                     (queues[self.calls.index((h, k))] if far > 1 else last).append(entry)
         if self.slices == 2:
@@ -269,6 +289,11 @@
     def late(self, z, j):
         return (2 * z < self.slices) == (2 * j < self.slices)
 
+    def only_last(self, h, i, k, j):
+        near = (1, self.slices - 2)
+        touched = [part for part, z in ((h, i), (k, j)) if z in near]
+        return all(part == self.parts - 1 for part in touched)
+
     def first_ready(self):
         ready = 0
         ids, _ = self.outputs()
@@ -278,7 +303,8 @@
                     continue
                 for k, (squares, _) in enumerate(messages):
                     for j in range(self.slices):
-                        if not self.late(z, j) and set(ids[z, :, j].ravel()) & set(squares):
+                        parts = self.parts - 1 if self.late(z, j) else self.parts
+                        if set(ids[z, :parts, j].ravel()) & set(squares):
                             ready = max(ready, k + 2 * place)
         return ready
 
@@ -417,9 +443,11 @@
     return kept, (found if sends else None)
 
 
-def column_half(slices, early, z):
+def piece(slices, parts, early, z, step):
     high = lax.div(2 * z, jnp.int32(slices))
-    return 1 - high if early else high
+    if not early:
+        return parts - 1, high
+    return lax.rem(step, jnp.int32(parts)), jnp.where(step < parts, 1 - high, high)
 
 
 def rows_kernel(slices, parts, span, part, local, early, tab, mode, place, *refs):
@@ -427,8 +455,9 @@
     own, right, left = refs[:n], refs[n : 2 * n], refs[2 * n : 3 * n]
     tiles = refs[-1].shape[4]
     out_ref = refs[-1].reshape(span * part * 2 * tiles, LANES)
-    z, h = place[0], pl.program_id(0)
-    first = column_half(slices, early, z) * (slices // 2)
+    z = place[0]
+    h, half = piece(slices, parts, early, z, pl.program_id(0))
+    first = half * (slices // 2)
     has_right, has_left = z > 0, z < slices - 1
     size = span * part
 
@@ -479,16 +508,18 @@
     per_j = parts * 2
     per_half = slices // 2 * per_j
 
+    def start(s, place):
+        h, half = piece(slices, parts, early, place[0], s)
+        return 2 * (place[0] * parts + h) + half
+
+    def out_map(s, tab, mode, place):
+        h, half = piece(slices, parts, early, place[0], s)
+        return 0, h, 0, half, 0, 0
+
     def spec(at):
         return pl.BlockSpec(
             (1, size, size),
-            lambda h, tab, mode, place: (
-                tab[
-                    (2 * (place[0] * parts + h) + column_half(slices, early, place[0])) * per_half + at
-                ],
-                0,
-                0,
-            ),
+            lambda s, tab, mode, place: (tab[start(s, place) * per_half + at], 0, 0),
         )
 
     tiles = antennas // 2 // LANES
@@ -498,12 +529,11 @@
         functools.partial(rows_kernel, slices, parts, span, part, local, early),
         grid_spec=pltpu.PrefetchScalarGridSpec(
             num_scalar_prefetch=3,
-            grid=(parts,),
+            grid=(2 * parts - 1 if early else 1,),
             in_specs=[spec(at) for _ in range(3) for at in range(per_half)]
             + [pl.BlockSpec(memory_space=pl.ANY) for _ in again],
             out_specs=pl.BlockSpec(
-                (span, 1, part * 2, 1, tiles, LANES),
-                lambda h, tab, mode, place: (0, h, 0, column_half(slices, early, place[0]), 0, 0),
+                (span, 1, part * 2, 1, tiles, LANES), out_map
             ),
         ),
         out_shape=jax.ShapeDtypeStruct((span, parts, part * 2, 2, tiles, LANES), F32),

time: 267 us -> 264 us (0.989)
  transfers between devices with their start and end apart: 35 -> 35, of which waited for: 13 -> 13; matrix products, arithmetic and copies ran while one was open for 0% -> 0% of each run, Pallas kernels for 46% -> 47%
where the time goes in v4:
time: 264 us; the launch traced here: 262 us
  Pallas kernels  130 us (49%)
  starting transfers between devices  118 us (45%)
  waiting for transfers between devices  9.02 us (3%)
  local copies, waits for them, and re-layouts  4.35 us (2%)
    ppermute x15, starting transfers between devices, on_device(): lax.ppermute(outgoing[0], 'tm', right)  82.7 us
    pallas_call x17, Pallas kernels, hop(): pl.pallas_call(functools.partial(hop_kernel, receives, sends, (2 if recei...  44.2 us
    pallas_call x3, Pallas kernels, filterbank(): pl.pallas_call(functools.partial(filterbank_kernel, channels, length), gr...  39.3 us
    pallas_call x6, Pallas kernels, correlate(): pl.pallas_call(functools.partial(correlate_kernel, (len(xs), len(ys)), sp...  30.2 us
    ppermute x15, starting transfers between devices, on_device(): lax.ppermute(outgoing[1], 'tm', left)  15.6 us
    pallas_call x2, Pallas kernels, visibility_rows(): pl.pallas_call(functools.partial(rows_kernel, slices, parts, span, part,...  15.6 us
    all_to_all x3, starting transfers between devices, on_device(): lax.all_to_all(own, 'chan', split_axis=0, concat_axis=0, tiled=True)  11.6 us
    ppermute x2, starting transfers between devices, on_device(): lax.ppermute(tail, 'tm', [(i, i + 1) for i in range(slices - 1)])  8.41 us
  transfers between devices with their start and end apart: 35, of which 13 were waited for; matrix products, arithmetic and copies ran while one was open for 0% of the time, Pallas kernels for 47%

profile of v4, /device:TPU:0, one launch (start us, length us, event | category | flops | bytes accessed | tf_op | source)
XLA Modules:
  0.0 261.8 jit_solution(9962820736724949011)
XLA Ops:
  2.3 4.9 %collective-permute-start.1 = (bf16[2,128,1024]{2,1,0:T(8,128)(2,1)}, bf16[2,128,1024]{2,1,0:T(8,128)(2,1)S(1)}, u32[]{:S(2)}, u32[]{:S(2)}) collective-permute-start(bf16[2,128,1024]{2,1,0:T(8,128)(2,1)} %get-tuple-element.141), channel_id=1, source_target_pairs={{0,1},{1,2},{2,3},{4,5},{5,6},{6,7},{8,9},{9,10},{10,11},{12,13},{... | collective-permute-start | bytes 1572872 | tf_op jit(solution)/shard_map/ppermute | solution.py:565
  9.6 10.8 %filterbank_h0_f256.1 = (bf16[8,2,128,256]{3,2,1,0:T(8,128)(2,1)}, f32[8,128]{1,0:T(8,128)S(1)}) custom-call(bf16[2,256,32768]{2,1,0:T(8,128)(2,1)} %v_ref.5, bf16[2,256,32768]{2,1,0:T(8,128)(2,1)} %v_ref.5, bf16[720,512]{1,0:T(8,128)(2,1)S(1)} %weights.1.w_ref.after_ref, s32[1,256]{1,0:T(1,128)S(1)} %bitcast.9, bf16[720,512]{1,0:T(8,128)(2,1)S(1)} %weights.1.w_ref.after_ref), custom_call_target="tpu_custom_call" | custom-call | flops 6039797760 | bytes 8388608 | tf_op jit(solution)/shard_map/filterbank_h0_f256/pallas_call | solution.py:119
  20.4 3.7 %all-to-all-start.2 = ((bf16[8,2,128,256]{3,2,1,0:T(8,128)(2,1)}), bf16[8,2,128,256]{3,2,1,0:T(8,128)(2,1)S(1)}, u32[]{:S(2)}, u32[]{:S(2)}) async-start(bf16[8,2,128,256]{3,2,1,0:T(8,128)(2,1)} %get-tuple-element.77), calls=%async_computation.2 | async-start | bytes 2097152 | tf_op jit(solution)/shard_map/all_to_all | solution.py:584
  24.1 3.5 %collective-permute-start = (bf16[2,128,1024]{2,1,0:T(8,128)(2,1)}, bf16[2,128,1024]{2,1,0:T(8,128)(2,1)S(1)}, u32[]{:S(2)}, u32[]{:S(2)}) collective-permute-start(bf16[2,128,1024]{2,1,0:T(8,128)(2,1)} %get-tuple-element.142), channel_id=1, source_target_pairs={{0,1},{1,2},{2,3},{4,5},{5,6},{6,7},{8,9},{9,10},{10,11},{12,13},{... | collective-permute-start | bytes 1572872 | tf_op jit(solution)/shard_map/ppermute | solution.py:565
  27.6 10.7 %filterbank_h0_f0.1 = (bf16[8,2,128,256]{3,2,1,0:T(8,128)(2,1)}, f32[8,128]{1,0:T(8,128)S(1)}) custom-call(bf16[2,128,1024]{2,1,0:T(8,128)(2,1)S(1)} %collective-permute-done.1.head_ref, bf16[2,256,32768]{2,1,0:T(8,128)(2,1)} %v_ref.5, bf16[720,512]{1,0:T(8,128)(2,1)S(1)} %weights.1.w_ref.after_ref, s32[1,256]{1,0:T(1,128)S(1)} %bitcast.10, ...), custom_call_target="tpu_custom_call" | custom-call | flops 6039797760 | bytes 8388608 | tf_op jit(solution)/shard_map/filterbank_h0_f0/pallas_call | solution.py:119
  39.6 3.6 %all-to-all-start.1 = ((bf16[8,2,128,256]{3,2,1,0:T(8,128)(2,1)}), bf16[8,2,128,256]{3,2,1,0:T(8,128)(2,1)S(1)}, u32[]{:S(2)}, u32[]{:S(2)}) async-start(bf16[8,2,128,256]{3,2,1,0:T(8,128)(2,1)} %get-tuple-element.76), calls=%async_computation.1 | async-start | bytes 2097152 | tf_op jit(solution)/shard_map/all_to_all | solution.py:584
  43.2 17.8 %filterbank_h1_f0.1 = (bf16[8,2,128,512]{3,2,1,0:T(8,128)(2,1)}, f32[8,128]{1,0:T(8,128)}) custom-call(bf16[2,128,1024]{2,1,0:T(8,128)(2,1)S(1)} %collective-permute-done.head_ref, bf16[2,256,32768]{2,1,0:T(8,128)(2,1)} %v_ref.5, bf16[720,512]{1,0:T(8,128)(2,1)S(1)} %weights.1.w_ref.after_ref, s32[1,256]{1,0:T(1,128)S(1)} %bitcast.11, ...), custom_call_target="tpu_custom_call" | custom-call | flops 12079595520 | bytes 16777216 | tf_op jit(solution)/shard_map/filterbank_h1_f0/pallas_call | solution.py:119
  60.9 4.3 %all-to-all-start = ((bf16[8,2,128,512]{3,2,1,0:T(8,128)(2,1)}), bf16[8,2,128,512]{3,2,1,0:T(8,128)(2,1)}, u32[]{:S(2)}, u32[]{:S(2)}) async-start(bf16[8,2,128,512]{3,2,1,0:T(8,128)(2,1)} %get-tuple-element.75), calls=%async_computation | async-start | bytes 4194304 | tf_op jit(solution)/shard_map/all_to_all | solution.py:584
  65.3 5.4 %correlate.6 = (f32[13,8,256,256]{3,2,1,0:T(8,128)}, bf16[104,256,256]{2,1,0:T(8,128)(2,1)}, bf16[104,256,256]{2,1,0:T(8,128)(2,1)}) custom-call(bf16[8,2,128,256]{3,2,1,0:T(8,128)(2,1)S(1)} %all-to-all-done.1.refs_0_.refs_2_.refs_1_, bf16[8,2,128,256]{3,2,1,0:T(8,128)(2,1)} %copy-done.7, ...), custom_call_target="tpu_custom_call" | custom-call | flops 2147483648 | bytes 4194304 | tf_op jit(solution)/shard_map/correlate/pallas_call | solution.py:222
  73.0 3.5 %collective-permute-start.2 = (bf16[4,256,256]{2,1,0:T(8,128)(2,1)S(1)}, bf16[4,256,256]{2,1,0:T(8,128)(2,1)S(1)}, u32[]{:S(2)}, u32[]{:S(2)}) collective-permute-start(bf16[4,256,256]{2,1,0:T(8,128)(2,1)S(1)} %get-tuple-element.79), channel_id=1, source_target_pairs={{0,1},{4,5},{8,9},{12,13},{16,17},{20,21},{24,25},{28,29}} | collective-permute-start | bytes 1572872 | tf_op jit(solution)/shard_map/ppermute | solution.py:626
  77.3 3.9 %correlate.7.refs_2_ = f32[13,8,256,256]{3,2,1,0:T(8,128)} custom-call(bf16[8,2,128,256]{3,2,1,0:T(8,128)(2,1)S(1)} %all-to-all-done.1.refs_0_.refs_2_.refs_1_, bf16[8,2,128,256]{3,2,1,0:T(8,128)(2,1)} %copy-done.7, bf16[8,2,128,256]{3,2,1,0:T(8,128)(2,1)S(1)} %all-to-all-done.1.refs_0_.refs_2_.refs_1_, ...), custom_call_target="tpu_custom_call", output_to_operand_aliasing={{}: (4, {})} | custom-call | flops 1073741824 | bytes 2097152 | tf_op jit(solution)/shard_map/correlate/pallas_call | solution.py:222
  81.2 3.3 %hop.19 = (bf16[4,256,256]{2,1,0:T(8,128)(2,1)}, bf16[4,256,256]{2,1,0:T(8,128)(2,1)}) custom-call(s32[544]{0:T(1024)S(1)} %copy-done, s32[1]{0:T(128)} %bitcast.place, f32[104,256,256]{2,1,0:T(8,128)} %bitcast.13), custom_call_target="tpu_custom_call" | custom-call | flops 1048576 | bytes 5242880 | tf_op jit(solution)/shard_map/hop/pallas_call | solution.py:426
  88.7 3.6 %hop.18 = (bf16[104,256,256]{2,1,0:T(8,128)(2,1)}, bf16[104,256,256]{2,1,0:T(8,128)(2,1)}, bf16[4,256,256]{2,1,0:T(8,128)(2,1)}, bf16[4,256,256]{2,1,0:T(8,128)(2,1)}) custom-call(s32[544]{0:T(1024)S(1)} %copy-done, s32[1]{0:T(128)} %bitcast.place, f32[104,256,256]{2,1,0:T(8,128)} %bitcast.14, ...), custom_call_target="tpu_custom_call", output_to_operand_aliasing={{0}: (5, {}), {1}: (6, {})} | custom-call | flops 1048576 | bytes 5242880 | tf_op jit(solution)/shard_map/hop/pallas_call | solution.py:426
  92.3 4.4 %collective-permute-start.4 = (bf16[4,256,256]{2,1,0:T(8,128)(2,1)}, bf16[4,256,256]{2,1,0:T(8,128)(2,1)S(1)}, u32[]{:S(2)}, u32[]{:S(2)}) collective-permute-start(bf16[4,256,256]{2,1,0:T(8,128)(2,1)} %get-tuple-element.83), channel_id=1, source_target_pairs={{0,1},{1,2},{4,5},{5,6},{8,9},{9,10},{12,13},{13,14},{16,17},{17,1... | collective-permute-start | bytes 1572872 | tf_op jit(solution)/shard_map/ppermute | solution.py:626
  97.4 6.0 %correlate.8.refs_2_ = f32[13,8,256,256]{3,2,1,0:T(8,128)} custom-call(bf16[8,2,128,512]{3,2,1,0:T(8,128)(2,1)} %all-to-all-done.refs_0_.refs_1_, bf16[8,2,128,512]{3,2,1,0:T(8,128)(2,1)} %all-to-all-done.refs_0_.refs_1_, f32[13,8,256,256]{3,2,1,0:T(8,128)} %correlate.7.refs_2_), custom_call_target="tpu_custom_call", output_to_operand_aliasing={{}: (2, {})} | custom-call | flops 2147483648 | bytes 4194304 | tf_op jit(solution)/shard_map/correlate/pallas_call | solution.py:222
  106.1 4.8 %collective-permute-start.10 = (bf16[4,256,256]{2,1,0:T(8,128)(2,1)S(1)}, bf16[4,256,256]{2,1,0:T(8,128)(2,1)S(1)}, u32[]{:S(2)}, u32[]{:S(2)}) collective-permute-start(bf16[4,256,256]{2,1,0:T(8,128)(2,1)S(1)} %get-tuple-element.93), channel_id=1, source_target_pairs={{0,1},{1,2},{4,5},{5,6},{8,9},{9,10},{12,13},{13,14},{16,17},{17,1... | collective-permute-start | bytes 1572872 | tf_op jit(solution)/shard_map/ppermute | solution.py:626
  111.6 4.3 %correlate.9.refs_3_ = f32[13,8,256,256]{3,2,1,0:T(8,128)} custom-call(bf16[8,2,128,512]{3,2,1,0:T(8,128)(2,1)} %all-to-all-done.refs_0_.refs_1_, bf16[8,2,128,512]{3,2,1,0:T(8,128)(2,1)} %all-to-all-done.refs_0_.refs_1_, f32[13,8,256,256]{3,2,1,0:T(8,128)} %correlate.8.refs_2_), custom_call_target="tpu_custom_call", output_to_operand_aliasing={{}: (2, {})} | custom-call | flops 1073741824 | bytes 2097152 | tf_op jit(solution)/shard_map/correlate/pallas_call | solution.py:222
  118.5 5.1 %collective-permute-start.8 = (bf16[4,256,256]{2,1,0:T(8,128)(2,1)S(1)}, bf16[4,256,256]{2,1,0:T(8,128)(2,1)S(1)}, u32[]{:S(2)}, u32[]{:S(2)}) collective-permute-start(bf16[4,256,256]{2,1,0:T(8,128)(2,1)S(1)} %get-tuple-element.91), channel_id=1, source_target_pairs={{0,1},{1,2},{2,3},{4,5},{5,6},{6,7},{8,9},{9,10},{10,11},{12,13},{... | collective-permute-start | bytes 1572872 | tf_op jit(solution)/shard_map/ppermute | solution.py:626
  124.9 5.3 %correlate.10.refs_3_ = f32[13,8,256,256]{3,2,1,0:T(8,128)} custom-call(bf16[8,2,128,512]{3,2,1,0:T(8,128)(2,1)} %all-to-all-done.refs_0_.refs_1_, bf16[8,2,128,256]{3,2,1,0:T(8,128)(2,1)S(1)} %all-to-all-done.1.refs_0_.refs_2_.refs_1_, bf16[8,2,128,256]{3,2,1,0:T(8,128)(2,1)} %copy-done.7, ...), custom_call_target="tpu_custom_call", output_to_operand_aliasing={{}: (3, {})} | custom-call | flops 2147483648 | bytes 4194304 | tf_op jit(solution)/shard_map/correlate/pallas_call | solution.py:222
  132.9 5.2 %collective-permute-start.14 = (bf16[4,256,256]{2,1,0:T(8,128)(2,1)S(1)}, bf16[4,256,256]{2,1,0:T(8,128)(2,1)S(1)}, u32[]{:S(2)}, u32[]{:S(2)}) collective-permute-start(bf16[4,256,256]{2,1,0:T(8,128)(2,1)S(1)} %get-tuple-element.101), channel_id=1, source_target_pairs={{0,1},{1,2},{2,3},{4,5},{5,6},{6,7},{8,9},{9,10},{10,11},{12,13},{... | collective-permute-start | bytes 1572872 | tf_op jit(solution)/shard_map/ppermute | solution.py:626
  139.4 5.3 %correlate.11 = f32[13,8,256,256]{3,2,1,0:T(8,128)} custom-call(bf16[8,2,128,512]{3,2,1,0:T(8,128)(2,1)} %all-to-all-done.refs_0_.refs_1_, bf16[8,2,128,256]{3,2,1,0:T(8,128)(2,1)S(1)} %all-to-all-done.1.refs_0_.refs_2_.refs_1_, bf16[8,2,128,256]{3,2,1,0:T(8,128)(2,1)} %copy-done.7, ...), custom_call_target="tpu_custom_call", output_to_operand_aliasing={{}: (3, {})} | custom-call | flops 2147483648 | bytes 4194304 | tf_op jit(solution)/shard_map/correlate/pallas_call | solution.py:222
  147.4 4.6 %collective-permute-start.12 = (bf16[4,256,256]{2,1,0:T(8,128)(2,1)S(1)}, bf16[4,256,256]{2,1,0:T(8,128)(2,1)S(1)}, u32[]{:S(2)}, u32[]{:S(2)}) collective-permute-start(bf16[4,256,256]{2,1,0:T(8,128)(2,1)S(1)} %get-tuple-element.99), channel_id=1, source_target_pairs={{0,1},{1,2},{4,5},{5,6},{8,9},{9,10},{12,13},{13,14},{16,17},{17,1... | collective-permute-start | bytes 1572872 | tf_op jit(solution)/shard_map/ppermute | solution.py:626
  155.4 4.5 %collective-permute-start.18 = (bf16[4,256,256]{2,1,0:T(8,128)(2,1)S(1)}, bf16[4,256,256]{2,1,0:T(8,128)(2,1)S(1)}, u32[]{:S(2)}, u32[]{:S(2)}) collective-permute-start(bf16[4,256,256]{2,1,0:T(8,128)(2,1)S(1)} %get-tuple-element.109), channel_id=1, source_target_pairs={{0,1},{1,2},{2,3},{4,5},{5,6},{6,7},{8,9},{9,10},{10,11},{12,13},{... | collective-permute-start | bytes 1572872 | tf_op jit(solution)/shard_map/ppermute | solution.py:626
  166.9 7.1 %collective-permute-start.16 = (bf16[4,256,256]{2,1,0:T(8,128)(2,1)S(1)}, bf16[4,256,256]{2,1,0:T(8,128)(2,1)S(1)}, u32[]{:S(2)}, u32[]{:S(2)}) collective-permute-start(bf16[4,256,256]{2,1,0:T(8,128)(2,1)S(1)} %get-tuple-element.107), channel_id=1, source_target_pairs={{0,1},{1,2},{2,3},{4,5},{5,6},{6,7},{8,9},{9,10},{10,11},{12,13},{... | collective-permute-start | bytes 1572872 | tf_op jit(solution)/shard_map/ppermute | solution.py:626
  178.1 7.1 %collective-permute-start.22 = (bf16[4,256,256]{2,1,0:T(8,128)(2,1)S(1)}, bf16[4,256,256]{2,1,0:T(8,128)(2,1)S(1)}, u32[]{:S(2)}, u32[]{:S(2)}) collective-permute-start(bf16[4,256,256]{2,1,0:T(8,128)(2,1)S(1)} %get-tuple-element.117), channel_id=1, source_target_pairs={{0,1},{1,2},{4,5},{5,6},{8,9},{9,10},{12,13},{13,14},{16,17},{17,1... | collective-permute-start | bytes 1572872 | tf_op jit(solution)/shard_map/ppermute | solution.py:626
  189.3 7.2 %collective-permute-start.20 = (bf16[4,256,256]{2,1,0:T(8,128)(2,1)S(1)}, bf16[4,256,256]{2,1,0:T(8,128)(2,1)S(1)}, u32[]{:S(2)}, u32[]{:S(2)}) collective-permute-start(bf16[4,256,256]{2,1,0:T(8,128)(2,1)S(1)} %get-tuple-element.115), channel_id=1, source_target_pairs={{0,1},{1,2},{2,3},{4,5},{5,6},{6,7},{8,9},{9,10},{10,11},{12,13},{... | collective-permute-start | bytes 1572872 | tf_op jit(solution)/shard_map/ppermute | solution.py:626
  200.5 7.2 %collective-permute-start.26 = (bf16[4,256,256]{2,1,0:T(8,128)(2,1)S(1)}, bf16[4,256,256]{2,1,0:T(8,128)(2,1)S(1)}, u32[]{:S(2)}, u32[]{:S(2)}) collective-permute-start(bf16[4,256,256]{2,1,0:T(8,128)(2,1)S(1)} %get-tuple-element.125), channel_id=1, source_target_pairs={{0,1},{1,2},{2,3},{4,5},{5,6},{6,7},{8,9},{9,10},{10,11},{12,13},{... | collective-permute-start | bytes 1572872 | tf_op jit(solution)/shard_map/ppermute | solution.py:626
  212.0 6.9 %collective-permute-start.24 = (bf16[4,256,256]{2,1,0:T(8,128)(2,1)S(1)}, bf16[4,256,256]{2,1,0:T(8,128)(2,1)S(1)}, u32[]{:S(2)}, u32[]{:S(2)}) collective-permute-start(bf16[4,256,256]{2,1,0:T(8,128)(2,1)S(1)} %get-tuple-element.123), channel_id=1, source_target_pairs={{0,1},{1,2},{2,3},{4,5},{5,6},{6,7},{8,9},{9,10},{10,11},{12,13},{... | collective-permute-start | bytes 1572872 | tf_op jit(solution)/shard_map/ppermute | solution.py:626
  223.3 6.9 %collective-permute-start.30 = (bf16[4,256,256]{2,1,0:T(8,128)(2,1)S(1)}, bf16[4,256,256]{2,1,0:T(8,128)(2,1)S(1)}, u32[]{:S(2)}, u32[]{:S(2)}) collective-permute-start(bf16[4,256,256]{2,1,0:T(8,128)(2,1)S(1)} %get-tuple-element.133), channel_id=1, source_target_pairs={{0,1},{1,2},{2,3},{4,5},{5,6},{6,7},{8,9},{9,10},{10,11},{12,13},{... | collective-permute-start | bytes 1572872 | tf_op jit(solution)/shard_map/ppermute | solution.py:626
  234.5 6.9 %collective-permute-start.28 = (bf16[4,256,256]{2,1,0:T(8,128)(2,1)S(1)}, bf16[4,256,256]{2,1,0:T(8,128)(2,1)S(1)}, u32[]{:S(2)}, u32[]{:S(2)}) collective-permute-start(bf16[4,256,256]{2,1,0:T(8,128)(2,1)S(1)} %get-tuple-element.131), channel_id=1, source_target_pairs={{0,1},{4,5},{8,9},{12,13},{16,17},{20,21},{24,25},{28,29}} | collective-permute-start | bytes 1572872 | tf_op jit(solution)/shard_map/ppermute | solution.py:626
  244.5 10.3 %visibility_rows.2.refs_4_.refs_24_ = f32[2,2,256,2,8,128]{5,4,3,2,1,0:T(8,128)} custom-call(s32[128]{0:T(128)S(1)} %copy-done.6, s32[64]{0:T(128)S(1)} %copy-done.5, s32[1]{0:T(128)} %bitcast.place, f32[104,256,256]{2,1,0:T(8,128)} %bitcast.30, f32[104,256,256]{2,1,0:T(8,128)} %bitcast.28, f32[104,256,256]{2,1,0:T(8,128)} %bitcast.29, ...), custom_call_target="tpu_custom_call" | custom-call | flops 4194304 | bytes 12582912 | tf_op jit(solution)/shard_map/visibility_rows/pallas_call | solution.py:528
  256.5 5.3 %visibility_rows.3 = f32[2,2,256,2,8,128]{5,4,3,2,1,0:T(8,128)} custom-call(s32[128]{0:T(128)S(1)} %copy-done.6, s32[64]{0:T(128)S(1)} %copy-done.5, s32[1]{0:T(128)} %bitcast.place, f32[104,256,256]{2,1,0:T(8,128)} %bitcast.35, f32[104,256,256]{2,1,0:T(8,128)} %bitcast.36, f32[104,256,256]{2,1,0:T(8,128)} %bitcast.37, ...), custom_call_target="tpu_custom_call", output_to_operand_aliasing={{}: (27, {})} | custom-call | flops 4194304 | bytes 12582912 | tf_op jit(solution)/shard_map/visibility_rows/pallas_call | solution.py:528
  (84 shorter events, 67.9 us)
Async XLA Ops:
  2.3 25.3 %collective-permute-start.1 = (bf16[2,128,1024]{2,1,0:T(8,128)(2,1)}, bf16[2,128,1024]{2,1,0:T(8,128)(2,1)S(1)}, u32[]{:S(2)}, u32[]{:S(2)}) collective-permute-start(bf16[2,128,1024]{2,1,0:T(8,128)(2,1)} %get-tuple-element.141), channel_id=1, source_target_pairs={{0,1},{1,2},{2,3},{4,5},{5,6},{6,7},{8,9},{9,10},{10,11},{12,13},{... | collective-permute-start | bytes 1572872 | tf_op jit(solution)/shard_map/ppermute | solution.py:565
  20.4 19.2 %all-to-all-start.2 = ((bf16[8,2,128,256]{3,2,1,0:T(8,128)(2,1)}), bf16[8,2,128,256]{3,2,1,0:T(8,128)(2,1)S(1)}, u32[]{:S(2)}, u32[]{:S(2)}) async-start(bf16[8,2,128,256]{3,2,1,0:T(8,128)(2,1)} %get-tuple-element.77), calls=%async_computation.2 | async-start | bytes 2097152 | tf_op jit(solution)/shard_map/all_to_all | solution.py:584
  24.1 19.0 %collective-permute-start = (bf16[2,128,1024]{2,1,0:T(8,128)(2,1)}, bf16[2,128,1024]{2,1,0:T(8,128)(2,1)S(1)}, u32[]{:S(2)}, u32[]{:S(2)}) collective-permute-start(bf16[2,128,1024]{2,1,0:T(8,128)(2,1)} %get-tuple-element.142), channel_id=1, source_target_pairs={{0,1},{1,2},{2,3},{4,5},{5,6},{6,7},{8,9},{9,10},{10,11},{12,13},{... | collective-permute-start | bytes 1572872 | tf_op jit(solution)/shard_map/ppermute | solution.py:565
  39.6 21.4 %all-to-all-start.1 = ((bf16[8,2,128,256]{3,2,1,0:T(8,128)(2,1)}), bf16[8,2,128,256]{3,2,1,0:T(8,128)(2,1)S(1)}, u32[]{:S(2)}, u32[]{:S(2)}) async-start(bf16[8,2,128,256]{3,2,1,0:T(8,128)(2,1)} %get-tuple-element.76), calls=%async_computation.1 | async-start | bytes 2097152 | tf_op jit(solution)/shard_map/all_to_all | solution.py:584
  60.9 36.5 %all-to-all-start = ((bf16[8,2,128,512]{3,2,1,0:T(8,128)(2,1)}), bf16[8,2,128,512]{3,2,1,0:T(8,128)(2,1)}, u32[]{:S(2)}, u32[]{:S(2)}) async-start(bf16[8,2,128,512]{3,2,1,0:T(8,128)(2,1)} %get-tuple-element.75), calls=%async_computation | async-start | bytes 4194304 | tf_op jit(solution)/shard_map/all_to_all | solution.py:584
  73.0 15.7 %collective-permute-start.2 = (bf16[4,256,256]{2,1,0:T(8,128)(2,1)S(1)}, bf16[4,256,256]{2,1,0:T(8,128)(2,1)S(1)}, u32[]{:S(2)}, u32[]{:S(2)}) collective-permute-start(bf16[4,256,256]{2,1,0:T(8,128)(2,1)S(1)} %get-tuple-element.79), channel_id=1, source_target_pairs={{0,1},{4,5},{8,9},{12,13},{16,17},{20,21},{24,25},{28,29}} | collective-permute-start | bytes 1572872 | tf_op jit(solution)/shard_map/ppermute | solution.py:626
  84.5 18.9 %collective-permute-start.6 = (bf16[4,256,256]{2,1,0:T(8,128)(2,1)}, bf16[4,256,256]{2,1,0:T(8,128)(2,1)S(1)}, u32[]{:S(2)}, u32[]{:S(2)}) collective-permute-start(bf16[4,256,256]{2,1,0:T(8,128)(2,1)} %get-tuple-element.85), channel_id=1, source_target_pairs={{0,1},{4,5},{8,9},{12,13},{16,17},{20,21},{24,25},{28,29}} | collective-permute-start | bytes 1572872 | tf_op jit(solution)/shard_map/ppermute | solution.py:626
  85.8 17.6 %collective-permute-start.7 = (bf16[4,256,256]{2,1,0:T(8,128)(2,1)}, bf16[4,256,256]{2,1,0:T(8,128)(2,1)S(1)}, u32[]{:S(2)}, u32[]{:S(2)}) collective-permute-start(bf16[4,256,256]{2,1,0:T(8,128)(2,1)} %get-tuple-element.86), channel_id=1, source_target_pairs={{3,2},{7,6},{11,10},{15,14},{19,18},{23,22},{27,26},{31,30}} | collective-permute-start | bytes 1572872 | tf_op jit(solution)/shard_map/ppermute | solution.py:627
  92.3 23.5 %collective-permute-start.4 = (bf16[4,256,256]{2,1,0:T(8,128)(2,1)}, bf16[4,256,256]{2,1,0:T(8,128)(2,1)S(1)}, u32[]{:S(2)}, u32[]{:S(2)}) collective-permute-start(bf16[4,256,256]{2,1,0:T(8,128)(2,1)} %get-tuple-element.83), channel_id=1, source_target_pairs={{0,1},{1,2},{4,5},{5,6},{8,9},{9,10},{12,13},{13,14},{16,17},{17,1... | collective-permute-start | bytes 1572872 | tf_op jit(solution)/shard_map/ppermute | solution.py:626
  96.7 19.1 %collective-permute-start.5 = (bf16[4,256,256]{2,1,0:T(8,128)(2,1)}, bf16[4,256,256]{2,1,0:T(8,128)(2,1)S(1)}, u32[]{:S(2)}, u32[]{:S(2)}) collective-permute-start(bf16[4,256,256]{2,1,0:T(8,128)(2,1)} %get-tuple-element.84), channel_id=1, source_target_pairs={{3,2},{2,1},{7,6},{6,5},{11,10},{10,9},{15,14},{14,13},{19,18},{18... | collective-permute-start | bytes 1572872 | tf_op jit(solution)/shard_map/ppermute | solution.py:627
  106.1 24.2 %collective-permute-start.10 = (bf16[4,256,256]{2,1,0:T(8,128)(2,1)S(1)}, bf16[4,256,256]{2,1,0:T(8,128)(2,1)S(1)}, u32[]{:S(2)}, u32[]{:S(2)}) collective-permute-start(bf16[4,256,256]{2,1,0:T(8,128)(2,1)S(1)} %get-tuple-element.93), channel_id=1, source_target_pairs={{0,1},{1,2},{4,5},{5,6},{8,9},{9,10},{12,13},{13,14},{16,17},{17,1... | collective-permute-start | bytes 1572872 | tf_op jit(solution)/shard_map/ppermute | solution.py:626
  110.9 19.4 %collective-permute-start.11 = (bf16[4,256,256]{2,1,0:T(8,128)(2,1)S(1)}, bf16[4,256,256]{2,1,0:T(8,128)(2,1)S(1)}, u32[]{:S(2)}, u32[]{:S(2)}) collective-permute-start(bf16[4,256,256]{2,1,0:T(8,128)(2,1)S(1)} %get-tuple-element.94), channel_id=1, source_target_pairs={{3,2},{2,1},{7,6},{6,5},{11,10},{10,9},{15,14},{14,13},{19,18},{18... | collective-permute-start | bytes 1572872 | tf_op jit(solution)/shard_map/ppermute | solution.py:627
  118.5 26.3 %collective-permute-start.8 = (bf16[4,256,256]{2,1,0:T(8,128)(2,1)S(1)}, bf16[4,256,256]{2,1,0:T(8,128)(2,1)S(1)}, u32[]{:S(2)}, u32[]{:S(2)}) collective-permute-start(bf16[4,256,256]{2,1,0:T(8,128)(2,1)S(1)} %get-tuple-element.91), channel_id=1, source_target_pairs={{0,1},{1,2},{2,3},{4,5},{5,6},{6,7},{8,9},{9,10},{10,11},{12,13},{... | collective-permute-start | bytes 1572872 | tf_op jit(solution)/shard_map/ppermute | solution.py:626
  123.6 21.1 %collective-permute-start.9 = (bf16[4,256,256]{2,1,0:T(8,128)(2,1)S(1)}, bf16[4,256,256]{2,1,0:T(8,128)(2,1)S(1)}, u32[]{:S(2)}, u32[]{:S(2)}) collective-permute-start(bf16[4,256,256]{2,1,0:T(8,128)(2,1)S(1)} %get-tuple-element.92), channel_id=1, source_target_pairs={{3,2},{2,1},{1,0},{7,6},{6,5},{5,4},{11,10},{10,9},{9,8},{15,14},{... | collective-permute-start | bytes 1572872 | tf_op jit(solution)/shard_map/ppermute | solution.py:627
  132.9 19.8 %collective-permute-start.14 = (bf16[4,256,256]{2,1,0:T(8,128)(2,1)S(1)}, bf16[4,256,256]{2,1,0:T(8,128)(2,1)S(1)}, u32[]{:S(2)}, u32[]{:S(2)}) collective-permute-start(bf16[4,256,256]{2,1,0:T(8,128)(2,1)S(1)} %get-tuple-element.101), channel_id=1, source_target_pairs={{0,1},{1,2},{2,3},{4,5},{5,6},{6,7},{8,9},{9,10},{10,11},{12,13},{... | collective-permute-start | bytes 1572872 | tf_op jit(solution)/shard_map/ppermute | solution.py:626
  138.1 14.6 %collective-permute-start.15 = (bf16[4,256,256]{2,1,0:T(8,128)(2,1)S(1)}, bf16[4,256,256]{2,1,0:T(8,128)(2,1)S(1)}, u32[]{:S(2)}, u32[]{:S(2)}) collective-permute-start(bf16[4,256,256]{2,1,0:T(8,128)(2,1)S(1)} %get-tuple-element.102), channel_id=1, source_target_pairs={{3,2},{2,1},{1,0},{7,6},{6,5},{5,4},{11,10},{10,9},{9,8},{15,14},{... | collective-permute-start | bytes 1572872 | tf_op jit(solution)/shard_map/ppermute | solution.py:627
  147.4 16.8 %collective-permute-start.12 = (bf16[4,256,256]{2,1,0:T(8,128)(2,1)S(1)}, bf16[4,256,256]{2,1,0:T(8,128)(2,1)S(1)}, u32[]{:S(2)}, u32[]{:S(2)}) collective-permute-start(bf16[4,256,256]{2,1,0:T(8,128)(2,1)S(1)} %get-tuple-element.99), channel_id=1, source_target_pairs={{0,1},{1,2},{4,5},{5,6},{8,9},{9,10},{12,13},{13,14},{16,17},{17,1... | collective-permute-start | bytes 1572872 | tf_op jit(solution)/shard_map/ppermute | solution.py:626
  155.4 20.1 %collective-permute-start.18 = (bf16[4,256,256]{2,1,0:T(8,128)(2,1)S(1)}, bf16[4,256,256]{2,1,0:T(8,128)(2,1)S(1)}, u32[]{:S(2)}, u32[]{:S(2)}) collective-permute-start(bf16[4,256,256]{2,1,0:T(8,128)(2,1)S(1)} %get-tuple-element.109), channel_id=1, source_target_pairs={{0,1},{1,2},{2,3},{4,5},{5,6},{6,7},{8,9},{9,10},{10,11},{12,13},{... | collective-permute-start | bytes 1572872 | tf_op jit(solution)/shard_map/ppermute | solution.py:626
  159.9 15.6 %collective-permute-start.19 = (bf16[4,256,256]{2,1,0:T(8,128)(2,1)S(1)}, bf16[4,256,256]{2,1,0:T(8,128)(2,1)S(1)}, u32[]{:S(2)}, u32[]{:S(2)}) collective-permute-start(bf16[4,256,256]{2,1,0:T(8,128)(2,1)S(1)} %get-tuple-element.110), channel_id=1, source_target_pairs={{3,2},{2,1},{1,0},{7,6},{6,5},{5,4},{11,10},{10,9},{9,8},{15,14},{... | collective-permute-start | bytes 1572872 | tf_op jit(solution)/shard_map/ppermute | solution.py:627
  166.9 19.7 %collective-permute-start.16 = (bf16[4,256,256]{2,1,0:T(8,128)(2,1)S(1)}, bf16[4,256,256]{2,1,0:T(8,128)(2,1)S(1)}, u32[]{:S(2)}, u32[]{:S(2)}) collective-permute-start(bf16[4,256,256]{2,1,0:T(8,128)(2,1)S(1)} %get-tuple-element.107), channel_id=1, source_target_pairs={{0,1},{1,2},{2,3},{4,5},{5,6},{6,7},{8,9},{9,10},{10,11},{12,13},{... | collective-permute-start | bytes 1572872 | tf_op jit(solution)/shard_map/ppermute | solution.py:626
  174.0 12.6 %collective-permute-start.17 = (bf16[4,256,256]{2,1,0:T(8,128)(2,1)S(1)}, bf16[4,256,256]{2,1,0:T(8,128)(2,1)S(1)}, u32[]{:S(2)}, u32[]{:S(2)}) collective-permute-start(bf16[4,256,256]{2,1,0:T(8,128)(2,1)S(1)} %get-tuple-element.108), channel_id=1, source_target_pairs={{3,2},{2,1},{1,0},{7,6},{6,5},{5,4},{11,10},{10,9},{9,8},{15,14},{... | collective-permute-start | bytes 1572872 | tf_op jit(solution)/shard_map/ppermute | solution.py:627
  178.1 19.7 %collective-permute-start.22 = (bf16[4,256,256]{2,1,0:T(8,128)(2,1)S(1)}, bf16[4,256,256]{2,1,0:T(8,128)(2,1)S(1)}, u32[]{:S(2)}, u32[]{:S(2)}) collective-permute-start(bf16[4,256,256]{2,1,0:T(8,128)(2,1)S(1)} %get-tuple-element.117), channel_id=1, source_target_pairs={{0,1},{1,2},{4,5},{5,6},{8,9},{9,10},{12,13},{13,14},{16,17},{17,1... | collective-permute-start | bytes 1572872 | tf_op jit(solution)/shard_map/ppermute | solution.py:626
  185.2 12.6 %collective-permute-start.23 = (bf16[4,256,256]{2,1,0:T(8,128)(2,1)S(1)}, bf16[4,256,256]{2,1,0:T(8,128)(2,1)S(1)}, u32[]{:S(2)}, u32[]{:S(2)}) collective-permute-start(bf16[4,256,256]{2,1,0:T(8,128)(2,1)S(1)} %get-tuple-element.118), channel_id=1, source_target_pairs={{3,2},{2,1},{7,6},{6,5},{11,10},{10,9},{15,14},{14,13},{19,18},{18... | collective-permute-start | bytes 1572872 | tf_op jit(solution)/shard_map/ppermute | solution.py:627
  189.3 19.8 %collective-permute-start.20 = (bf16[4,256,256]{2,1,0:T(8,128)(2,1)S(1)}, bf16[4,256,256]{2,1,0:T(8,128)(2,1)S(1)}, u32[]{:S(2)}, u32[]{:S(2)}) collective-permute-start(bf16[4,256,256]{2,1,0:T(8,128)(2,1)S(1)} %get-tuple-element.115), channel_id=1, source_target_pairs={{0,1},{1,2},{2,3},{4,5},{5,6},{6,7},{8,9},{9,10},{10,11},{12,13},{... | collective-permute-start | bytes 1572872 | tf_op jit(solution)/shard_map/ppermute | solution.py:626
  196.5 12.9 %collective-permute-start.21 = (bf16[4,256,256]{2,1,0:T(8,128)(2,1)S(1)}, bf16[4,256,256]{2,1,0:T(8,128)(2,1)S(1)}, u32[]{:S(2)}, u32[]{:S(2)}) collective-permute-start(bf16[4,256,256]{2,1,0:T(8,128)(2,1)S(1)} %get-tuple-element.116), channel_id=1, source_target_pairs={{3,2},{2,1},{1,0},{7,6},{6,5},{5,4},{11,10},{10,9},{9,8},{15,14},{... | collective-permute-start | bytes 1572872 | tf_op jit(solution)/shard_map/ppermute | solution.py:627
  200.5 19.8 %collective-permute-start.26 = (bf16[4,256,256]{2,1,0:T(8,128)(2,1)S(1)}, bf16[4,256,256]{2,1,0:T(8,128)(2,1)S(1)}, u32[]{:S(2)}, u32[]{:S(2)}) collective-permute-start(bf16[4,256,256]{2,1,0:T(8,128)(2,1)S(1)} %get-tuple-element.125), channel_id=1, source_target_pairs={{0,1},{1,2},{2,3},{4,5},{5,6},{6,7},{8,9},{9,10},{10,11},{12,13},{... | collective-permute-start | bytes 1572872 | tf_op jit(solution)/shard_map/ppermute | solution.py:626
  207.7 12.9 %collective-permute-start.27 = (bf16[4,256,256]{2,1,0:T(8,128)(2,1)S(1)}, bf16[4,256,256]{2,1,0:T(8,128)(2,1)S(1)}, u32[]{:S(2)}, u32[]{:S(2)}) collective-permute-start(bf16[4,256,256]{2,1,0:T(8,128)(2,1)S(1)} %get-tuple-element.126), channel_id=1, source_target_pairs={{3,2},{2,1},{1,0},{7,6},{6,5},{5,4},{11,10},{10,9},{9,8},{15,14},{... | collective-permute-start | bytes 1572872 | tf_op jit(solution)/shard_map/ppermute | solution.py:627
  212.0 19.5 %collective-permute-start.24 = (bf16[4,256,256]{2,1,0:T(8,128)(2,1)S(1)}, bf16[4,256,256]{2,1,0:T(8,128)(2,1)S(1)}, u32[]{:S(2)}, u32[]{:S(2)}) collective-permute-start(bf16[4,256,256]{2,1,0:T(8,128)(2,1)S(1)} %get-tuple-element.123), channel_id=1, source_target_pairs={{0,1},{1,2},{2,3},{4,5},{5,6},{6,7},{8,9},{9,10},{10,11},{12,13},{... | collective-permute-start | bytes 1572872 | tf_op jit(solution)/shard_map/ppermute | solution.py:626
  218.9 12.9 %collective-permute-start.25 = (bf16[4,256,256]{2,1,0:T(8,128)(2,1)S(1)}, bf16[4,256,256]{2,1,0:T(8,128)(2,1)S(1)}, u32[]{:S(2)}, u32[]{:S(2)}) collective-permute-start(bf16[4,256,256]{2,1,0:T(8,128)(2,1)S(1)} %get-tuple-element.124), channel_id=1, source_target_pairs={{3,2},{2,1},{1,0},{7,6},{6,5},{5,4},{11,10},{10,9},{9,8},{15,14},{... | collective-permute-start | bytes 1572872 | tf_op jit(solution)/shard_map/ppermute | solution.py:627
  223.3 19.5 %collective-permute-start.30 = (bf16[4,256,256]{2,1,0:T(8,128)(2,1)S(1)}, bf16[4,256,256]{2,1,0:T(8,128)(2,1)S(1)}, u32[]{:S(2)}, u32[]{:S(2)}) collective-permute-start(bf16[4,256,256]{2,1,0:T(8,128)(2,1)S(1)} %get-tuple-element.133), channel_id=1, source_target_pairs={{0,1},{1,2},{2,3},{4,5},{5,6},{6,7},{8,9},{9,10},{10,11},{12,13},{... | collective-permute-start | bytes 1572872 | tf_op jit(solution)/shard_map/ppermute | solution.py:626
  234.5 20.3 %collective-permute-start.28 = (bf16[4,256,256]{2,1,0:T(8,128)(2,1)S(1)}, bf16[4,256,256]{2,1,0:T(8,128)(2,1)S(1)}, u32[]{:S(2)}, u32[]{:S(2)}) collective-permute-start(bf16[4,256,256]{2,1,0:T(8,128)(2,1)S(1)} %get-tuple-element.131), channel_id=1, source_target_pairs={{0,1},{4,5},{8,9},{12,13},{16,17},{20,21},{24,25},{28,29}} | collective-permute-start | bytes 1572872 | tf_op jit(solution)/shard_map/ppermute | solution.py:626
  241.4 13.4 %collective-permute-start.29 = (bf16[4,256,256]{2,1,0:T(8,128)(2,1)S(1)}, bf16[4,256,256]{2,1,0:T(8,128)(2,1)S(1)}, u32[]{:S(2)}, u32[]{:S(2)}) collective-permute-start(bf16[4,256,256]{2,1,0:T(8,128)(2,1)S(1)} %get-tuple-element.132), channel_id=1, source_target_pairs={{3,2},{7,6},{11,10},{15,14},{19,18},{23,22},{27,26},{31,30}} | collective-permute-start | bytes 1572872 | tf_op jit(solution)/shard_map/ppermute | solution.py:627
  (11 other events, 107.0 us)

commit v5 on v4

--- a/solution.py
+++ b/solution.py
@@ -195,13 +195,13 @@
                     out_ref[m, 2 * n] = jnp.where(row >= col, real[:, columns], imag[:, columns])
 
 
-def correlate(partial, total, slices, call, xs, ys, span, weight, same, which):
+def correlate(partial, total, slices, call, xs, ys, span, weight, same, which, upper):
     part = xs[0].shape[2]
     size = span * part
     frames = sum(x.shape[3] for x in xs)
     group = slices // 2
-    low = which * group if same else 0
-    many = 2 if low % 2 == 0 else 1
+    low = upper * group
+    many = 1
     rows = [
         pl.BlockSpec((many * span, 2, part, x.shape[3]), lambda i: (low // many + i, 0, 0, 0))
         for x in xs
@@ -223,15 +223,15 @@
         functools.partial(
             correlate_kernel, (len(xs), len(ys)), span, weight, fresh, same, low, which * group
         ),
-        grid=((slices - low) // many,),
+        grid=(group // many,),
         in_specs=rows + columns + ([] if fresh else [anywhere]),
         out_specs=[out_block, anywhere, anywhere] if fresh else [out_block],
         out_shape=[shape, store, store] if fresh else [shape],
         input_output_aliases={} if fresh else {len(xs) + len(ys): 0},
         compiler_params=params(),
         cost_estimate=pl.CostEstimate(
-            flops=8 * (slices - low) * group * size * size * frames,
-            bytes_accessed=8 * (slices - low) * group * size * size,
+            flops=8 * group * group * size * size * frames,
+            bytes_accessed=8 * group * group * size * size,
             transcendentals=0,
         ),
         name="correlate",
@@ -252,6 +252,10 @@
                     for j in range(slices):
                         if k < h or j <= i:
                             self.pair_at[h, i, k, j] = first + i * slices + j
+        self.work = []
+        for call, (h, k) in enumerate(self.calls):
+            quarters = [(0, 1), (0, 0), (1, 1)] if h == k else [(0, 1), (1, 0), (1, 1), (0, 0)]
+            self.work += [(call, which, upper) for which, upper in quarters]
         self.spare = 2 * len(self.calls) * slices * slices
         self.total = self.spare + -(-2 * count // (2 * slices)) * 2 * slices
         self.right = self.messages(lambda i, j: max(i, j))
@@ -274,7 +278,10 @@
                 for square in sorted(set(self.squares(h, i, k, j))):
                     if far == 1:
                         late = self.only_last(h, i, k, j)
-                    entry = (-far, late, self.work_of(h, k, j), square)
+                    order = (-far, late, self.work_of(h, i, k, j))
+                    if far > 1 and h == k:
+                        order = (order[2],) + order[:2]
+                    entry = order + (far, square)
                     (queues[self.calls.index((h, k))] if far > 1 else last).append(entry)
         if self.slices == 2:
             queues, last = [last], []
@@ -283,7 +290,7 @@
             for at in range(0, len(queue), self.count):
                 some = queue[at : at + self.count]
                 ids = [entry[-1] for entry in some]
-                found.append((ids, max(-entry[0] for entry in some)))
+                found.append((ids, max(entry[-2] for entry in some)))
         return found
 
     def late(self, z, j):
@@ -331,8 +338,9 @@
                             rows[z, step, side * self.count + b] = square
         return rows.reshape(-1)
 
-    def work_of(self, h, k, j):
-        return 2 * self.calls.index((h, k)) + 2 * j // self.slices
+    def work_of(self, h, i, k, j):
+        n = self.slices
+        return self.work.index((self.calls.index((h, k)), 2 * j // n, 2 * i // n))
 
     def last_work(self, step):
         need = 0
@@ -341,9 +349,9 @@
                 k = step - 2 * place
                 if 0 <= k < len(messages):
                     for square in messages[k][0]:
-                        for (h, _, c, j), at in self.pair_at.items():
+                        for (h, i, c, j), at in self.pair_at.items():
                             if at == square // 2:
-                                need = max(need, self.work_of(h, c, j))
+                                need = max(need, self.work_of(h, i, c, j))
         return need
 
     def outputs(self):
@@ -589,10 +597,11 @@
 
     def extend(partial, kept, count):
         for _ in range(count):
-            call, which = len(done) // 2, len(done) % 2
+            call, which, upper = plan.work[len(done)]
             h, k = plan.calls[call]
             made = correlate(
-                partial, plan.total, slices, call, spectra[h], spectra[k], span, weight, h == k, which
+                partial, plan.total, slices, call, spectra[h], spectra[k], span, weight, h == k,
+                which, upper,
             )
             partial = made[0]
             if kept is None:
@@ -602,8 +611,8 @@
 
     def needed(step):
         must = max(0, plan.last_work(step) + 1 - len(done))
-        soon = len(done) <= plan.last_work(step + 1)
-        early = soon and (len(done) < 2 or step > 3)
+        soon = len(done) < len(plan.work) and len(done) <= plan.last_work(step + 1)
+        early = soon and step != 0 and (plan.work[len(done)][0] == 0 or step > 3)
         return max(must, 1 if early else 0)
 
     partial, kept = None, None

time: 264 us -> 263 us (level)
  Pallas kernels: 130 us -> 138 us
  starting transfers between devices: 118 us -> 112 us
  waiting for transfers between devices: 9.02 us -> 5.16 us
    pallas_call x6 -> x10, Pallas kernels: 30.2 us -> 38.4 us  [correlate(): pl.pallas_call(functools.partial(correlate_kernel, (len(xs), len(ys)), sp...]
    ppermute x15, starting transfers between devices: 82.7 us -> 76.3 us  [on_device(): lax.ppermute(outgoing[0], 'tm', right)]
    ppermute x15, waiting for transfers between devices: 6.87 us -> 3.01 us  [on_device(): lax.ppermute(outgoing[0], 'tm', right)]
  transfers between devices with their start and end apart: 35 -> 35, of which waited for: 13 -> 10; matrix products, arithmetic and copies ran while one was open for 0% -> 0% of each run, Pallas kernels for 47% -> 50%
where the time goes in v5:
time: 263 us; the launch traced here: 260 us
  Pallas kernels  138 us (52%)
  starting transfers between devices  112 us (43%)
  waiting for transfers between devices  5.16 us (2%)
  local copies, waits for them, and re-layouts  4.35 us (2%)
    ppermute x15, starting transfers between devices, on_device(): lax.ppermute(outgoing[0], 'tm', right)  76.3 us
    pallas_call x17, Pallas kernels, hop(): pl.pallas_call(functools.partial(hop_kernel, receives, sends, (2 if recei...  44.2 us
    pallas_call x3, Pallas kernels, filterbank(): pl.pallas_call(functools.partial(filterbank_kernel, channels, length), gr...  39.3 us
    pallas_call x10, Pallas kernels, correlate(): pl.pallas_call(functools.partial(correlate_kernel, (len(xs), len(ys)), sp...  38.4 us
    ppermute x15, starting transfers between devices, on_device(): lax.ppermute(outgoing[1], 'tm', left)  15.6 us
    pallas_call x2, Pallas kernels, visibility_rows(): pl.pallas_call(functools.partial(rows_kernel, slices, parts, span, part,...  15.6 us
    all_to_all x3, starting transfers between devices, on_device(): lax.all_to_all(own, 'chan', split_axis=0, concat_axis=0, tiled=True)  11.6 us
    ppermute x2, starting transfers between devices, on_device(): lax.ppermute(tail, 'tm', [(i, i + 1) for i in range(slices - 1)])  8.41 us
  transfers between devices with their start and end apart: 35, of which 10 were waited for; matrix products, arithmetic and copies ran while one was open for 0% of the time, Pallas kernels for 50%

profile of v5, /device:TPU:0, one launch (start us, length us, event | category | flops | bytes accessed | tf_op | source)
XLA Modules:
  0.0 259.8 jit_solution(11977812168653595940)
XLA Ops:
  2.3 4.9 %collective-permute-start.1 = (bf16[2,128,1024]{2,1,0:T(8,128)(2,1)}, bf16[2,128,1024]{2,1,0:T(8,128)(2,1)S(1)}, u32[]{:S(2)}, u32[]{:S(2)}) collective-permute-start(bf16[2,128,1024]{2,1,0:T(8,128)(2,1)} %get-tuple-element.141), channel_id=1, source_target_pairs={{0,1},{1,2},{2,3},{4,5},{5,6},{6,7},{8,9},{9,10},{10,11},{12,13},{... | collective-permute-start | bytes 1572872 | tf_op jit(solution)/shard_map/ppermute | solution.py:573
  9.6 10.8 %filterbank_h0_f256.1 = (bf16[8,2,128,256]{3,2,1,0:T(8,128)(2,1)}, f32[8,128]{1,0:T(8,128)S(1)}) custom-call(bf16[2,256,32768]{2,1,0:T(8,128)(2,1)} %v_ref.5, bf16[2,256,32768]{2,1,0:T(8,128)(2,1)} %v_ref.5, bf16[720,512]{1,0:T(8,128)(2,1)S(1)} %weights.1.w_ref.after_ref, s32[1,256]{1,0:T(1,128)S(1)} %bitcast.12, bf16[720,512]{1,0:T(8,128)(2,1)S(1)} %weights.1.w_ref.after_ref), custom_call_target="tpu_custom_call" | custom-call | flops 6039797760 | bytes 8388608 | tf_op jit(solution)/shard_map/filterbank_h0_f256/pallas_call | solution.py:119
  20.4 3.7 %all-to-all-start.2 = ((bf16[8,2,128,256]{3,2,1,0:T(8,128)(2,1)}), bf16[8,2,128,256]{3,2,1,0:T(8,128)(2,1)S(1)}, u32[]{:S(2)}, u32[]{:S(2)}) async-start(bf16[8,2,128,256]{3,2,1,0:T(8,128)(2,1)} %get-tuple-element.77), calls=%async_computation.2 | async-start | bytes 2097152 | tf_op jit(solution)/shard_map/all_to_all | solution.py:592
  27.6 10.7 %filterbank_h0_f0.1 = (bf16[8,2,128,256]{3,2,1,0:T(8,128)(2,1)}, f32[8,128]{1,0:T(8,128)S(1)}) custom-call(bf16[2,128,1024]{2,1,0:T(8,128)(2,1)S(1)} %collective-permute-done.1.head_ref, bf16[2,256,32768]{2,1,0:T(8,128)(2,1)} %v_ref.5, bf16[720,512]{1,0:T(8,128)(2,1)S(1)} %weights.1.w_ref.after_ref, s32[1,256]{1,0:T(1,128)S(1)} %bitcast.13, ...), custom_call_target="tpu_custom_call" | custom-call | flops 6039797760 | bytes 8388608 | tf_op jit(solution)/shard_map/filterbank_h0_f0/pallas_call | solution.py:119
  39.6 3.6 %all-to-all-start.1 = ((bf16[8,2,128,256]{3,2,1,0:T(8,128)(2,1)}), bf16[8,2,128,256]{3,2,1,0:T(8,128)(2,1)S(1)}, u32[]{:S(2)}, u32[]{:S(2)}) async-start(bf16[8,2,128,256]{3,2,1,0:T(8,128)(2,1)} %get-tuple-element.76), calls=%async_computation.1 | async-start | bytes 2097152 | tf_op jit(solution)/shard_map/all_to_all | solution.py:592
  43.2 17.8 %filterbank_h1_f0.1 = (bf16[8,2,128,512]{3,2,1,0:T(8,128)(2,1)}, f32[8,128]{1,0:T(8,128)}) custom-call(bf16[2,128,1024]{2,1,0:T(8,128)(2,1)S(1)} %collective-permute-done.head_ref, bf16[2,256,32768]{2,1,0:T(8,128)(2,1)} %v_ref.5, bf16[720,512]{1,0:T(8,128)(2,1)S(1)} %weights.1.w_ref.after_ref, s32[1,256]{1,0:T(1,128)S(1)} %bitcast.14, ...), custom_call_target="tpu_custom_call" | custom-call | flops 12079595520 | bytes 16777216 | tf_op jit(solution)/shard_map/filterbank_h1_f0/pallas_call | solution.py:119
  60.9 4.3 %all-to-all-start = ((bf16[8,2,128,512]{3,2,1,0:T(8,128)(2,1)}), bf16[8,2,128,512]{3,2,1,0:T(8,128)(2,1)}, u32[]{:S(2)}, u32[]{:S(2)}) async-start(bf16[8,2,128,512]{3,2,1,0:T(8,128)(2,1)} %get-tuple-element.75), calls=%async_computation | async-start | bytes 4194304 | tf_op jit(solution)/shard_map/all_to_all | solution.py:592
  65.3 3.7 %correlate.10 = (f32[13,8,256,256]{3,2,1,0:T(8,128)}, bf16[104,256,256]{2,1,0:T(8,128)(2,1)}, bf16[104,256,256]{2,1,0:T(8,128)(2,1)}) custom-call(bf16[8,2,128,256]{3,2,1,0:T(8,128)(2,1)S(1)} %all-to-all-done.1.refs_0_.refs_2_.refs_1_, bf16[8,2,128,256]{3,2,1,0:T(8,128)(2,1)} %copy-done.7, ...), custom_call_target="tpu_custom_call" | custom-call | flops 1073741824 | bytes 2097152 | tf_op jit(solution)/shard_map/correlate/pallas_call | solution.py:222
  75.6 3.8 %correlate.11.refs_4_ = f32[13,8,256,256]{3,2,1,0:T(8,128)} custom-call(bf16[8,2,128,256]{3,2,1,0:T(8,128)(2,1)S(1)} %all-to-all-done.1.refs_0_.refs_2_.refs_1_, bf16[8,2,128,256]{3,2,1,0:T(8,128)(2,1)} %copy-done.7, bf16[8,2,128,256]{3,2,1,0:T(8,128)(2,1)S(1)} %all-to-all-done.1.refs_0_.refs_2_.refs_1_, ...), custom_call_target="tpu_custom_call", output_to_operand_aliasing={{}: (4, {})} | custom-call | flops 1073741824 | bytes 2097152 | tf_op jit(solution)/shard_map/correlate/pallas_call | solution.py:222
  84.7 3.8 %correlate.12.refs_2_ = f32[13,8,256,256]{3,2,1,0:T(8,128)} custom-call(bf16[8,2,128,256]{3,2,1,0:T(8,128)(2,1)S(1)} %all-to-all-done.1.refs_0_.refs_2_.refs_1_, bf16[8,2,128,256]{3,2,1,0:T(8,128)(2,1)} %copy-done.7, bf16[8,2,128,256]{3,2,1,0:T(8,128)(2,1)S(1)} %all-to-all-done.1.refs_0_.refs_2_.refs_1_, ...), custom_call_target="tpu_custom_call", output_to_operand_aliasing={{}: (4, {})} | custom-call | flops 1073741824 | bytes 2097152 | tf_op jit(solution)/shard_map/correlate/pallas_call | solution.py:222
  88.5 3.6 %hop.18 = (bf16[104,256,256]{2,1,0:T(8,128)(2,1)}, bf16[104,256,256]{2,1,0:T(8,128)(2,1)}, bf16[4,256,256]{2,1,0:T(8,128)(2,1)}, bf16[4,256,256]{2,1,0:T(8,128)(2,1)}) custom-call(s32[544]{0:T(1024)S(1)} %copy-done, s32[1]{0:T(128)} %bitcast.place, f32[104,256,256]{2,1,0:T(8,128)} %bitcast.17, ...), custom_call_target="tpu_custom_call", output_to_operand_aliasing={{0}: (5, {}), {1}: (6, {})} | custom-call | flops 1048576 | bytes 5242880 | tf_op jit(solution)/shard_map/hop/pallas_call | solution.py:434
  95.7 4.0 %correlate.13.refs_2_ = f32[13,8,256,256]{3,2,1,0:T(8,128)} custom-call(bf16[8,2,128,512]{3,2,1,0:T(8,128)(2,1)} %all-to-all-done.refs_0_.refs_1_, bf16[8,2,128,512]{3,2,1,0:T(8,128)(2,1)} %all-to-all-done.refs_0_.refs_1_, f32[13,8,256,256]{3,2,1,0:T(8,128)} %correlate.12.refs_2_), custom_call_target="tpu_custom_call", output_to_operand_aliasing={{}: (2, {})} | custom-call | flops 1073741824 | bytes 2097152 | tf_op jit(solution)/shard_map/correlate/pallas_call | solution.py:222
  102.3 4.8 %collective-permute-start.10 = (bf16[4,256,256]{2,1,0:T(8,128)(2,1)S(1)}, bf16[4,256,256]{2,1,0:T(8,128)(2,1)S(1)}, u32[]{:S(2)}, u32[]{:S(2)}) collective-permute-start(bf16[4,256,256]{2,1,0:T(8,128)(2,1)S(1)} %get-tuple-element.93), channel_id=1, source_target_pairs={{0,1},{1,2},{4,5},{5,6},{8,9},{9,10},{12,13},{13,14},{16,17},{17,1... | collective-permute-start | bytes 1572872 | tf_op jit(solution)/shard_map/ppermute | solution.py:635
  107.8 4.1 %correlate.14.refs_2_ = f32[13,8,256,256]{3,2,1,0:T(8,128)} custom-call(bf16[8,2,128,512]{3,2,1,0:T(8,128)(2,1)} %all-to-all-done.refs_0_.refs_1_, bf16[8,2,128,512]{3,2,1,0:T(8,128)(2,1)} %all-to-all-done.refs_0_.refs_1_, f32[13,8,256,256]{3,2,1,0:T(8,128)} %correlate.13.refs_2_), custom_call_target="tpu_custom_call", output_to_operand_aliasing={{}: (2, {})} | custom-call | flops 1073741824 | bytes 2097152 | tf_op jit(solution)/shard_map/correlate/pallas_call | solution.py:222
  114.6 5.1 %collective-permute-start.8 = (bf16[4,256,256]{2,1,0:T(8,128)(2,1)S(1)}, bf16[4,256,256]{2,1,0:T(8,128)(2,1)S(1)}, u32[]{:S(2)}, u32[]{:S(2)}) collective-permute-start(bf16[4,256,256]{2,1,0:T(8,128)(2,1)S(1)} %get-tuple-element.91), channel_id=1, source_target_pairs={{0,1},{1,2},{2,3},{4,5},{5,6},{6,7},{8,9},{9,10},{10,11},{12,13},{... | collective-permute-start | bytes 1572872 | tf_op jit(solution)/shard_map/ppermute | solution.py:635
  121.0 4.1 %correlate.15.refs_3_ = f32[13,8,256,256]{3,2,1,0:T(8,128)} custom-call(bf16[8,2,128,512]{3,2,1,0:T(8,128)(2,1)} %all-to-all-done.refs_0_.refs_1_, bf16[8,2,128,512]{3,2,1,0:T(8,128)(2,1)} %all-to-all-done.refs_0_.refs_1_, f32[13,8,256,256]{3,2,1,0:T(8,128)} %correlate.14.refs_2_), custom_call_target="tpu_custom_call", output_to_operand_aliasing={{}: (2, {})} | custom-call | flops 1073741824 | bytes 2097152 | tf_op jit(solution)/shard_map/correlate/pallas_call | solution.py:222
  127.8 5.2 %collective-permute-start.14 = (bf16[4,256,256]{2,1,0:T(8,128)(2,1)S(1)}, bf16[4,256,256]{2,1,0:T(8,128)(2,1)S(1)}, u32[]{:S(2)}, u32[]{:S(2)}) collective-permute-start(bf16[4,256,256]{2,1,0:T(8,128)(2,1)S(1)} %get-tuple-element.101), channel_id=1, source_target_pairs={{0,1},{1,2},{4,5},{5,6},{8,9},{9,10},{12,13},{13,14},{16,17},{17,1... | collective-permute-start | bytes 1572872 | tf_op jit(solution)/shard_map/ppermute | solution.py:635
  133.7 3.7 %correlate.16.refs_3_ = f32[13,8,256,256]{3,2,1,0:T(8,128)} custom-call(bf16[8,2,128,512]{3,2,1,0:T(8,128)(2,1)} %all-to-all-done.refs_0_.refs_1_, bf16[8,2,128,256]{3,2,1,0:T(8,128)(2,1)S(1)} %all-to-all-done.1.refs_0_.refs_2_.refs_1_, bf16[8,2,128,256]{3,2,1,0:T(8,128)(2,1)} %copy-done.7, ...), custom_call_target="tpu_custom_call", output_to_operand_aliasing={{}: (3, {})} | custom-call | flops 1073741824 | bytes 2097152 | tf_op jit(solution)/shard_map/correlate/pallas_call | solution.py:222
  140.1 4.5 %collective-permute-start.12 = (bf16[4,256,256]{2,1,0:T(8,128)(2,1)S(1)}, bf16[4,256,256]{2,1,0:T(8,128)(2,1)S(1)}, u32[]{:S(2)}, u32[]{:S(2)}) collective-permute-start(bf16[4,256,256]{2,1,0:T(8,128)(2,1)S(1)} %get-tuple-element.99), channel_id=1, source_target_pairs={{0,1},{1,2},{2,3},{4,5},{5,6},{6,7},{8,9},{9,10},{10,11},{12,13},{... | collective-permute-start | bytes 1572872 | tf_op jit(solution)/shard_map/ppermute | solution.py:635
  145.9 3.7 %correlate.17.refs_3_ = f32[13,8,256,256]{3,2,1,0:T(8,128)} custom-call(bf16[8,2,128,512]{3,2,1,0:T(8,128)(2,1)} %all-to-all-done.refs_0_.refs_1_, bf16[8,2,128,256]{3,2,1,0:T(8,128)(2,1)S(1)} %all-to-all-done.1.refs_0_.refs_2_.refs_1_, bf16[8,2,128,256]{3,2,1,0:T(8,128)(2,1)} %copy-done.7, ...), custom_call_target="tpu_custom_call", output_to_operand_aliasing={{}: (3, {})} | custom-call | flops 1073741824 | bytes 2097152 | tf_op jit(solution)/shard_map/correlate/pallas_call | solution.py:222
  152.3 5.2 %collective-permute-start.18 = (bf16[4,256,256]{2,1,0:T(8,128)(2,1)S(1)}, bf16[4,256,256]{2,1,0:T(8,128)(2,1)S(1)}, u32[]{:S(2)}, u32[]{:S(2)}) collective-permute-start(bf16[4,256,256]{2,1,0:T(8,128)(2,1)S(1)} %get-tuple-element.109), channel_id=1, source_target_pairs={{0,1},{1,2},{2,3},{4,5},{5,6},{6,7},{8,9},{9,10},{10,11},{12,13},{... | collective-permute-start | bytes 1572872 | tf_op jit(solution)/shard_map/ppermute | solution.py:635
  158.8 3.8 %correlate.18.refs_3_ = f32[13,8,256,256]{3,2,1,0:T(8,128)} custom-call(bf16[8,2,128,512]{3,2,1,0:T(8,128)(2,1)} %all-to-all-done.refs_0_.refs_1_, bf16[8,2,128,256]{3,2,1,0:T(8,128)(2,1)S(1)} %all-to-all-done.1.refs_0_.refs_2_.refs_1_, bf16[8,2,128,256]{3,2,1,0:T(8,128)(2,1)} %copy-done.7, ...), custom_call_target="tpu_custom_call", output_to_operand_aliasing={{}: (3, {})} | custom-call | flops 1073741824 | bytes 2097152 | tf_op jit(solution)/shard_map/correlate/pallas_call | solution.py:222
  162.5 3.7 %correlate.19 = f32[13,8,256,256]{3,2,1,0:T(8,128)} custom-call(bf16[8,2,128,512]{3,2,1,0:T(8,128)(2,1)} %all-to-all-done.refs_0_.refs_1_, bf16[8,2,128,256]{3,2,1,0:T(8,128)(2,1)S(1)} %all-to-all-done.1.refs_0_.refs_2_.refs_1_, bf16[8,2,128,256]{3,2,1,0:T(8,128)(2,1)} %copy-done.7, ...), custom_call_target="tpu_custom_call", output_to_operand_aliasing={{}: (3, {})} | custom-call | flops 1073741824 | bytes 2097152 | tf_op jit(solution)/shard_map/correlate/pallas_call | solution.py:222
  168.9 4.6 %collective-permute-start.16 = (bf16[4,256,256]{2,1,0:T(8,128)(2,1)S(1)}, bf16[4,256,256]{2,1,0:T(8,128)(2,1)S(1)}, u32[]{:S(2)}, u32[]{:S(2)}) collective-permute-start(bf16[4,256,256]{2,1,0:T(8,128)(2,1)S(1)} %get-tuple-element.107), channel_id=1, source_target_pairs={{0,1},{1,2},{4,5},{5,6},{8,9},{9,10},{12,13},{13,14},{16,17},{17,1... | collective-permute-start | bytes 1572872 | tf_op jit(solution)/shard_map/ppermute | solution.py:635
  176.9 4.5 %collective-permute-start.22 = (bf16[4,256,256]{2,1,0:T(8,128)(2,1)S(1)}, bf16[4,256,256]{2,1,0:T(8,128)(2,1)S(1)}, u32[]{:S(2)}, u32[]{:S(2)}) collective-permute-start(bf16[4,256,256]{2,1,0:T(8,128)(2,1)S(1)} %get-tuple-element.117), channel_id=1, source_target_pairs={{0,1},{1,2},{2,3},{4,5},{5,6},{6,7},{8,9},{9,10},{10,11},{12,13},{... | collective-permute-start | bytes 1572872 | tf_op jit(solution)/shard_map/ppermute | solution.py:635
  187.3 7.1 %collective-permute-start.20 = (bf16[4,256,256]{2,1,0:T(8,128)(2,1)S(1)}, bf16[4,256,256]{2,1,0:T(8,128)(2,1)S(1)}, u32[]{:S(2)}, u32[]{:S(2)}) collective-permute-start(bf16[4,256,256]{2,1,0:T(8,128)(2,1)S(1)} %get-tuple-element.115), channel_id=1, source_target_pairs={{0,1},{1,2},{2,3},{4,5},{5,6},{6,7},{8,9},{9,10},{10,11},{12,13},{... | collective-permute-start | bytes 1572872 | tf_op jit(solution)/shard_map/ppermute | solution.py:635
  198.7 7.0 %collective-permute-start.26 = (bf16[4,256,256]{2,1,0:T(8,128)(2,1)S(1)}, bf16[4,256,256]{2,1,0:T(8,128)(2,1)S(1)}, u32[]{:S(2)}, u32[]{:S(2)}) collective-permute-start(bf16[4,256,256]{2,1,0:T(8,128)(2,1)S(1)} %get-tuple-element.125), channel_id=1, source_target_pairs={{0,1},{1,2},{2,3},{4,5},{5,6},{6,7},{8,9},{9,10},{10,11},{12,13},{... | collective-permute-start | bytes 1572872 | tf_op jit(solution)/shard_map/ppermute | solution.py:635
  210.0 6.9 %collective-permute-start.24 = (bf16[4,256,256]{2,1,0:T(8,128)(2,1)S(1)}, bf16[4,256,256]{2,1,0:T(8,128)(2,1)S(1)}, u32[]{:S(2)}, u32[]{:S(2)}) collective-permute-start(bf16[4,256,256]{2,1,0:T(8,128)(2,1)S(1)} %get-tuple-element.123), channel_id=1, source_target_pairs={{0,1},{1,2},{2,3},{4,5},{5,6},{6,7},{8,9},{9,10},{10,11},{12,13},{... | collective-permute-start | bytes 1572872 | tf_op jit(solution)/shard_map/ppermute | solution.py:635
  221.2 6.9 %collective-permute-start.30 = (bf16[4,256,256]{2,1,0:T(8,128)(2,1)S(1)}, bf16[4,256,256]{2,1,0:T(8,128)(2,1)S(1)}, u32[]{:S(2)}, u32[]{:S(2)}) collective-permute-start(bf16[4,256,256]{2,1,0:T(8,128)(2,1)S(1)} %get-tuple-element.133), channel_id=1, source_target_pairs={{0,1},{1,2},{2,3},{4,5},{5,6},{6,7},{8,9},{9,10},{10,11},{12,13},{... | collective-permute-start | bytes 1572872 | tf_op jit(solution)/shard_map/ppermute | solution.py:635
  232.4 6.9 %collective-permute-start.28 = (bf16[4,256,256]{2,1,0:T(8,128)(2,1)S(1)}, bf16[4,256,256]{2,1,0:T(8,128)(2,1)S(1)}, u32[]{:S(2)}, u32[]{:S(2)}) collective-permute-start(bf16[4,256,256]{2,1,0:T(8,128)(2,1)S(1)} %get-tuple-element.131), channel_id=1, source_target_pairs={{0,1},{4,5},{8,9},{12,13},{16,17},{20,21},{24,25},{28,29}} | collective-permute-start | bytes 1572872 | tf_op jit(solution)/shard_map/ppermute | solution.py:635
  242.5 10.3 %visibility_rows.2.refs_4_.refs_24_ = f32[2,2,256,2,8,128]{5,4,3,2,1,0:T(8,128)} custom-call(s32[128]{0:T(128)S(1)} %copy-done.6, s32[64]{0:T(128)S(1)} %copy-done.5, s32[1]{0:T(128)} %bitcast.place, f32[104,256,256]{2,1,0:T(8,128)} %bitcast.34, f32[104,256,256]{2,1,0:T(8,128)} %bitcast.31, f32[104,256,256]{2,1,0:T(8,128)} %bitcast.32, ...), custom_call_target="tpu_custom_call" | custom-call | flops 4194304 | bytes 12582912 | tf_op jit(solution)/shard_map/visibility_rows/pallas_call | solution.py:536
  254.4 5.3 %visibility_rows.3 = f32[2,2,256,2,8,128]{5,4,3,2,1,0:T(8,128)} custom-call(s32[128]{0:T(128)S(1)} %copy-done.6, s32[64]{0:T(128)S(1)} %copy-done.5, s32[1]{0:T(128)} %bitcast.place, f32[104,256,256]{2,1,0:T(8,128)} %bitcast.38, f32[104,256,256]{2,1,0:T(8,128)} %bitcast.39, f32[104,256,256]{2,1,0:T(8,128)} %bitcast.40, ...), custom_call_target="tpu_custom_call", output_to_operand_aliasing={{}: (27, {})} | custom-call | flops 4194304 | bytes 12582912 | tf_op jit(solution)/shard_map/visibility_rows/pallas_call | solution.py:536
  (88 shorter events, 77.1 us)
Async XLA Ops:
  2.3 25.3 %collective-permute-start.1 = (bf16[2,128,1024]{2,1,0:T(8,128)(2,1)}, bf16[2,128,1024]{2,1,0:T(8,128)(2,1)S(1)}, u32[]{:S(2)}, u32[]{:S(2)}) collective-permute-start(bf16[2,128,1024]{2,1,0:T(8,128)(2,1)} %get-tuple-element.141), channel_id=1, source_target_pairs={{0,1},{1,2},{2,3},{4,5},{5,6},{6,7},{8,9},{9,10},{10,11},{12,13},{... | collective-permute-start | bytes 1572872 | tf_op jit(solution)/shard_map/ppermute | solution.py:573
  20.4 19.2 %all-to-all-start.2 = ((bf16[8,2,128,256]{3,2,1,0:T(8,128)(2,1)}), bf16[8,2,128,256]{3,2,1,0:T(8,128)(2,1)S(1)}, u32[]{:S(2)}, u32[]{:S(2)}) async-start(bf16[8,2,128,256]{3,2,1,0:T(8,128)(2,1)} %get-tuple-element.77), calls=%async_computation.2 | async-start | bytes 2097152 | tf_op jit(solution)/shard_map/all_to_all | solution.py:592
  24.1 19.0 %collective-permute-start = (bf16[2,128,1024]{2,1,0:T(8,128)(2,1)}, bf16[2,128,1024]{2,1,0:T(8,128)(2,1)S(1)}, u32[]{:S(2)}, u32[]{:S(2)}) collective-permute-start(bf16[2,128,1024]{2,1,0:T(8,128)(2,1)} %get-tuple-element.142), channel_id=1, source_target_pairs={{0,1},{1,2},{2,3},{4,5},{5,6},{6,7},{8,9},{9,10},{10,11},{12,13},{... | collective-permute-start | bytes 1572872 | tf_op jit(solution)/shard_map/ppermute | solution.py:573
  39.6 21.4 %all-to-all-start.1 = ((bf16[8,2,128,256]{3,2,1,0:T(8,128)(2,1)}), bf16[8,2,128,256]{3,2,1,0:T(8,128)(2,1)S(1)}, u32[]{:S(2)}, u32[]{:S(2)}) async-start(bf16[8,2,128,256]{3,2,1,0:T(8,128)(2,1)} %get-tuple-element.76), calls=%async_computation.1 | async-start | bytes 2097152 | tf_op jit(solution)/shard_map/all_to_all | solution.py:592
  60.9 34.8 %all-to-all-start = ((bf16[8,2,128,512]{3,2,1,0:T(8,128)(2,1)}), bf16[8,2,128,512]{3,2,1,0:T(8,128)(2,1)}, u32[]{:S(2)}, u32[]{:S(2)}) async-start(bf16[8,2,128,512]{3,2,1,0:T(8,128)(2,1)} %get-tuple-element.75), calls=%async_computation | async-start | bytes 4194304 | tf_op jit(solution)/shard_map/all_to_all | solution.py:592
  71.2 17.3 %collective-permute-start.2 = (bf16[4,256,256]{2,1,0:T(8,128)(2,1)S(1)}, bf16[4,256,256]{2,1,0:T(8,128)(2,1)S(1)}, u32[]{:S(2)}, u32[]{:S(2)}) collective-permute-start(bf16[4,256,256]{2,1,0:T(8,128)(2,1)S(1)} %get-tuple-element.79), channel_id=1, source_target_pairs={{0,1},{4,5},{8,9},{12,13},{16,17},{20,21},{24,25},{28,29}} | collective-permute-start | bytes 1572872 | tf_op jit(solution)/shard_map/ppermute | solution.py:635
  74.7 13.8 %collective-permute-start.3 = (bf16[4,256,256]{2,1,0:T(8,128)(2,1)S(1)}, bf16[4,256,256]{2,1,0:T(8,128)(2,1)S(1)}, u32[]{:S(2)}, u32[]{:S(2)}) collective-permute-start(bf16[4,256,256]{2,1,0:T(8,128)(2,1)S(1)} %get-tuple-element.80), channel_id=1, source_target_pairs={{3,2},{7,6},{11,10},{15,14},{19,18},{23,22},{27,26},{31,30}} | collective-permute-start | bytes 1572872 | tf_op jit(solution)/shard_map/ppermute | solution.py:636
  82.6 17.0 %collective-permute-start.6 = (bf16[4,256,256]{2,1,0:T(8,128)(2,1)}, bf16[4,256,256]{2,1,0:T(8,128)(2,1)S(1)}, u32[]{:S(2)}, u32[]{:S(2)}) collective-permute-start(bf16[4,256,256]{2,1,0:T(8,128)(2,1)} %get-tuple-element.85), channel_id=1, source_target_pairs={{0,1},{4,5},{8,9},{12,13},{16,17},{20,21},{24,25},{28,29}} | collective-permute-start | bytes 1572872 | tf_op jit(solution)/shard_map/ppermute | solution.py:635
  84.0 15.7 %collective-permute-start.7 = (bf16[4,256,256]{2,1,0:T(8,128)(2,1)}, bf16[4,256,256]{2,1,0:T(8,128)(2,1)S(1)}, u32[]{:S(2)}, u32[]{:S(2)}) collective-permute-start(bf16[4,256,256]{2,1,0:T(8,128)(2,1)} %get-tuple-element.86), channel_id=1, source_target_pairs={{3,2},{7,6},{11,10},{15,14},{19,18},{23,22},{27,26},{31,30}} | collective-permute-start | bytes 1572872 | tf_op jit(solution)/shard_map/ppermute | solution.py:636
  92.1 19.8 %collective-permute-start.4 = (bf16[4,256,256]{2,1,0:T(8,128)(2,1)}, bf16[4,256,256]{2,1,0:T(8,128)(2,1)S(1)}, u32[]{:S(2)}, u32[]{:S(2)}) collective-permute-start(bf16[4,256,256]{2,1,0:T(8,128)(2,1)} %get-tuple-element.83), channel_id=1, source_target_pairs={{0,1},{1,2},{4,5},{5,6},{8,9},{9,10},{12,13},{13,14},{16,17},{17,1... | collective-permute-start | bytes 1572872 | tf_op jit(solution)/shard_map/ppermute | solution.py:635
  95.0 16.9 %collective-permute-start.5 = (bf16[4,256,256]{2,1,0:T(8,128)(2,1)}, bf16[4,256,256]{2,1,0:T(8,128)(2,1)S(1)}, u32[]{:S(2)}, u32[]{:S(2)}) collective-permute-start(bf16[4,256,256]{2,1,0:T(8,128)(2,1)} %get-tuple-element.84), channel_id=1, source_target_pairs={{3,2},{2,1},{7,6},{6,5},{11,10},{10,9},{15,14},{14,13},{19,18},{18... | collective-permute-start | bytes 1572872 | tf_op jit(solution)/shard_map/ppermute | solution.py:636
  102.3 22.8 %collective-permute-start.10 = (bf16[4,256,256]{2,1,0:T(8,128)(2,1)S(1)}, bf16[4,256,256]{2,1,0:T(8,128)(2,1)S(1)}, u32[]{:S(2)}, u32[]{:S(2)}) collective-permute-start(bf16[4,256,256]{2,1,0:T(8,128)(2,1)S(1)} %get-tuple-element.93), channel_id=1, source_target_pairs={{0,1},{1,2},{4,5},{5,6},{8,9},{9,10},{12,13},{13,14},{16,17},{17,1... | collective-permute-start | bytes 1572872 | tf_op jit(solution)/shard_map/ppermute | solution.py:635
  107.1 18.1 %collective-permute-start.11 = (bf16[4,256,256]{2,1,0:T(8,128)(2,1)S(1)}, bf16[4,256,256]{2,1,0:T(8,128)(2,1)S(1)}, u32[]{:S(2)}, u32[]{:S(2)}) collective-permute-start(bf16[4,256,256]{2,1,0:T(8,128)(2,1)S(1)} %get-tuple-element.94), channel_id=1, source_target_pairs={{3,2},{2,1},{7,6},{6,5},{11,10},{10,9},{15,14},{14,13},{19,18},{18... | collective-permute-start | bytes 1572872 | tf_op jit(solution)/shard_map/ppermute | solution.py:636
  114.6 22.9 %collective-permute-start.8 = (bf16[4,256,256]{2,1,0:T(8,128)(2,1)S(1)}, bf16[4,256,256]{2,1,0:T(8,128)(2,1)S(1)}, u32[]{:S(2)}, u32[]{:S(2)}) collective-permute-start(bf16[4,256,256]{2,1,0:T(8,128)(2,1)S(1)} %get-tuple-element.91), channel_id=1, source_target_pairs={{0,1},{1,2},{2,3},{4,5},{5,6},{6,7},{8,9},{9,10},{10,11},{12,13},{... | collective-permute-start | bytes 1572872 | tf_op jit(solution)/shard_map/ppermute | solution.py:635
  119.7 17.7 %collective-permute-start.9 = (bf16[4,256,256]{2,1,0:T(8,128)(2,1)S(1)}, bf16[4,256,256]{2,1,0:T(8,128)(2,1)S(1)}, u32[]{:S(2)}, u32[]{:S(2)}) collective-permute-start(bf16[4,256,256]{2,1,0:T(8,128)(2,1)S(1)} %get-tuple-element.92), channel_id=1, source_target_pairs={{3,2},{2,1},{1,0},{7,6},{6,5},{5,4},{11,10},{10,9},{9,8},{15,14},{... | collective-permute-start | bytes 1572872 | tf_op jit(solution)/shard_map/ppermute | solution.py:636
  127.8 21.8 %collective-permute-start.14 = (bf16[4,256,256]{2,1,0:T(8,128)(2,1)S(1)}, bf16[4,256,256]{2,1,0:T(8,128)(2,1)S(1)}, u32[]{:S(2)}, u32[]{:S(2)}) collective-permute-start(bf16[4,256,256]{2,1,0:T(8,128)(2,1)S(1)} %get-tuple-element.101), channel_id=1, source_target_pairs={{0,1},{1,2},{4,5},{5,6},{8,9},{9,10},{12,13},{13,14},{16,17},{17,1... | collective-permute-start | bytes 1572872 | tf_op jit(solution)/shard_map/ppermute | solution.py:635
  133.0 16.6 %collective-permute-start.15 = (bf16[4,256,256]{2,1,0:T(8,128)(2,1)S(1)}, bf16[4,256,256]{2,1,0:T(8,128)(2,1)S(1)}, u32[]{:S(2)}, u32[]{:S(2)}) collective-permute-start(bf16[4,256,256]{2,1,0:T(8,128)(2,1)S(1)} %get-tuple-element.102), channel_id=1, source_target_pairs={{3,2},{2,1},{7,6},{6,5},{11,10},{10,9},{15,14},{14,13},{19,18},{18... | collective-permute-start | bytes 1572872 | tf_op jit(solution)/shard_map/ppermute | solution.py:636
  140.1 26.1 %collective-permute-start.12 = (bf16[4,256,256]{2,1,0:T(8,128)(2,1)S(1)}, bf16[4,256,256]{2,1,0:T(8,128)(2,1)S(1)}, u32[]{:S(2)}, u32[]{:S(2)}) collective-permute-start(bf16[4,256,256]{2,1,0:T(8,128)(2,1)S(1)} %get-tuple-element.99), channel_id=1, source_target_pairs={{0,1},{1,2},{2,3},{4,5},{5,6},{6,7},{8,9},{9,10},{10,11},{12,13},{... | collective-permute-start | bytes 1572872 | tf_op jit(solution)/shard_map/ppermute | solution.py:635
  144.6 21.6 %collective-permute-start.13 = (bf16[4,256,256]{2,1,0:T(8,128)(2,1)S(1)}, bf16[4,256,256]{2,1,0:T(8,128)(2,1)S(1)}, u32[]{:S(2)}, u32[]{:S(2)}) collective-permute-start(bf16[4,256,256]{2,1,0:T(8,128)(2,1)S(1)} %get-tuple-element.100), channel_id=1, source_target_pairs={{3,2},{2,1},{1,0},{7,6},{6,5},{5,4},{11,10},{10,9},{9,8},{15,14},{... | collective-permute-start | bytes 1572872 | tf_op jit(solution)/shard_map/ppermute | solution.py:636
  152.3 21.9 %collective-permute-start.18 = (bf16[4,256,256]{2,1,0:T(8,128)(2,1)S(1)}, bf16[4,256,256]{2,1,0:T(8,128)(2,1)S(1)}, u32[]{:S(2)}, u32[]{:S(2)}) collective-permute-start(bf16[4,256,256]{2,1,0:T(8,128)(2,1)S(1)} %get-tuple-element.109), channel_id=1, source_target_pairs={{0,1},{1,2},{2,3},{4,5},{5,6},{6,7},{8,9},{9,10},{10,11},{12,13},{... | collective-permute-start | bytes 1572872 | tf_op jit(solution)/shard_map/ppermute | solution.py:635
  157.5 16.7 %collective-permute-start.19 = (bf16[4,256,256]{2,1,0:T(8,128)(2,1)S(1)}, bf16[4,256,256]{2,1,0:T(8,128)(2,1)S(1)}, u32[]{:S(2)}, u32[]{:S(2)}) collective-permute-start(bf16[4,256,256]{2,1,0:T(8,128)(2,1)S(1)} %get-tuple-element.110), channel_id=1, source_target_pairs={{3,2},{2,1},{1,0},{7,6},{6,5},{5,4},{11,10},{10,9},{9,8},{15,14},{... | collective-permute-start | bytes 1572872 | tf_op jit(solution)/shard_map/ppermute | solution.py:636
  168.9 15.7 %collective-permute-start.16 = (bf16[4,256,256]{2,1,0:T(8,128)(2,1)S(1)}, bf16[4,256,256]{2,1,0:T(8,128)(2,1)S(1)}, u32[]{:S(2)}, u32[]{:S(2)}) collective-permute-start(bf16[4,256,256]{2,1,0:T(8,128)(2,1)S(1)} %get-tuple-element.107), channel_id=1, source_target_pairs={{0,1},{1,2},{4,5},{5,6},{8,9},{9,10},{12,13},{13,14},{16,17},{17,1... | collective-permute-start | bytes 1572872 | tf_op jit(solution)/shard_map/ppermute | solution.py:635
  176.9 19.0 %collective-permute-start.22 = (bf16[4,256,256]{2,1,0:T(8,128)(2,1)S(1)}, bf16[4,256,256]{2,1,0:T(8,128)(2,1)S(1)}, u32[]{:S(2)}, u32[]{:S(2)}) collective-permute-start(bf16[4,256,256]{2,1,0:T(8,128)(2,1)S(1)} %get-tuple-element.117), channel_id=1, source_target_pairs={{0,1},{1,2},{2,3},{4,5},{5,6},{6,7},{8,9},{9,10},{10,11},{12,13},{... | collective-permute-start | bytes 1572872 | tf_op jit(solution)/shard_map/ppermute | solution.py:635
  181.4 14.7 %collective-permute-start.23 = (bf16[4,256,256]{2,1,0:T(8,128)(2,1)S(1)}, bf16[4,256,256]{2,1,0:T(8,128)(2,1)S(1)}, u32[]{:S(2)}, u32[]{:S(2)}) collective-permute-start(bf16[4,256,256]{2,1,0:T(8,128)(2,1)S(1)} %get-tuple-element.118), channel_id=1, source_target_pairs={{3,2},{2,1},{1,0},{7,6},{6,5},{5,4},{11,10},{10,9},{9,8},{15,14},{... | collective-permute-start | bytes 1572872 | tf_op jit(solution)/shard_map/ppermute | solution.py:636
  187.3 19.7 %collective-permute-start.20 = (bf16[4,256,256]{2,1,0:T(8,128)(2,1)S(1)}, bf16[4,256,256]{2,1,0:T(8,128)(2,1)S(1)}, u32[]{:S(2)}, u32[]{:S(2)}) collective-permute-start(bf16[4,256,256]{2,1,0:T(8,128)(2,1)S(1)} %get-tuple-element.115), channel_id=1, source_target_pairs={{0,1},{1,2},{2,3},{4,5},{5,6},{6,7},{8,9},{9,10},{10,11},{12,13},{... | collective-permute-start | bytes 1572872 | tf_op jit(solution)/shard_map/ppermute | solution.py:635
  198.7 19.6 %collective-permute-start.26 = (bf16[4,256,256]{2,1,0:T(8,128)(2,1)S(1)}, bf16[4,256,256]{2,1,0:T(8,128)(2,1)S(1)}, u32[]{:S(2)}, u32[]{:S(2)}) collective-permute-start(bf16[4,256,256]{2,1,0:T(8,128)(2,1)S(1)} %get-tuple-element.125), channel_id=1, source_target_pairs={{0,1},{1,2},{2,3},{4,5},{5,6},{6,7},{8,9},{9,10},{10,11},{12,13},{... | collective-permute-start | bytes 1572872 | tf_op jit(solution)/shard_map/ppermute | solution.py:635
  205.6 12.9 %collective-permute-start.27 = (bf16[4,256,256]{2,1,0:T(8,128)(2,1)S(1)}, bf16[4,256,256]{2,1,0:T(8,128)(2,1)S(1)}, u32[]{:S(2)}, u32[]{:S(2)}) collective-permute-start(bf16[4,256,256]{2,1,0:T(8,128)(2,1)S(1)} %get-tuple-element.126), channel_id=1, source_target_pairs={{3,2},{2,1},{1,0},{7,6},{6,5},{5,4},{11,10},{10,9},{9,8},{15,14},{... | collective-permute-start | bytes 1572872 | tf_op jit(solution)/shard_map/ppermute | solution.py:636
  210.0 19.7 %collective-permute-start.24 = (bf16[4,256,256]{2,1,0:T(8,128)(2,1)S(1)}, bf16[4,256,256]{2,1,0:T(8,128)(2,1)S(1)}, u32[]{:S(2)}, u32[]{:S(2)}) collective-permute-start(bf16[4,256,256]{2,1,0:T(8,128)(2,1)S(1)} %get-tuple-element.123), channel_id=1, source_target_pairs={{0,1},{1,2},{2,3},{4,5},{5,6},{6,7},{8,9},{9,10},{10,11},{12,13},{... | collective-permute-start | bytes 1572872 | tf_op jit(solution)/shard_map/ppermute | solution.py:635
  216.9 12.9 %collective-permute-start.25 = (bf16[4,256,256]{2,1,0:T(8,128)(2,1)S(1)}, bf16[4,256,256]{2,1,0:T(8,128)(2,1)S(1)}, u32[]{:S(2)}, u32[]{:S(2)}) collective-permute-start(bf16[4,256,256]{2,1,0:T(8,128)(2,1)S(1)} %get-tuple-element.124), channel_id=1, source_target_pairs={{3,2},{2,1},{1,0},{7,6},{6,5},{5,4},{11,10},{10,9},{9,8},{15,14},{... | collective-permute-start | bytes 1572872 | tf_op jit(solution)/shard_map/ppermute | solution.py:636
  221.2 19.5 %collective-permute-start.30 = (bf16[4,256,256]{2,1,0:T(8,128)(2,1)S(1)}, bf16[4,256,256]{2,1,0:T(8,128)(2,1)S(1)}, u32[]{:S(2)}, u32[]{:S(2)}) collective-permute-start(bf16[4,256,256]{2,1,0:T(8,128)(2,1)S(1)} %get-tuple-element.133), channel_id=1, source_target_pairs={{0,1},{1,2},{2,3},{4,5},{5,6},{6,7},{8,9},{9,10},{10,11},{12,13},{... | collective-permute-start | bytes 1572872 | tf_op jit(solution)/shard_map/ppermute | solution.py:635
  232.4 20.3 %collective-permute-start.28 = (bf16[4,256,256]{2,1,0:T(8,128)(2,1)S(1)}, bf16[4,256,256]{2,1,0:T(8,128)(2,1)S(1)}, u32[]{:S(2)}, u32[]{:S(2)}) collective-permute-start(bf16[4,256,256]{2,1,0:T(8,128)(2,1)S(1)} %get-tuple-element.131), channel_id=1, source_target_pairs={{0,1},{4,5},{8,9},{12,13},{16,17},{20,21},{24,25},{28,29}} | collective-permute-start | bytes 1572872 | tf_op jit(solution)/shard_map/ppermute | solution.py:635
  239.4 13.4 %collective-permute-start.29 = (bf16[4,256,256]{2,1,0:T(8,128)(2,1)S(1)}, bf16[4,256,256]{2,1,0:T(8,128)(2,1)S(1)}, u32[]{:S(2)}, u32[]{:S(2)}) collective-permute-start(bf16[4,256,256]{2,1,0:T(8,128)(2,1)S(1)} %get-tuple-element.132), channel_id=1, source_target_pairs={{3,2},{7,6},{11,10},{15,14},{19,18},{23,22},{27,26},{31,30}} | collective-permute-start | bytes 1572872 | tf_op jit(solution)/shard_map/ppermute | solution.py:636
  (11 other events, 104.9 us)

commit v6 on v5

--- a/solution.py
+++ b/solution.py
@@ -270,6 +270,7 @@
         return (at, at) if (h, i) == (k, j) else (at, at + 1)
 
     def messages(self, reach):
+        slices = self.slices
         queues, last = [[] for _ in self.calls], []
         for (h, i, k, j) in self.pair_at:
             far = reach(i, j)
@@ -281,6 +282,15 @@
                     order = (-far, late, self.work_of(h, i, k, j))
                     if far > 1 and h == k:
                         order = (order[2],) + order[:2]
+                    elif far > 1:
+                        first = self.work_of(self.calls[-1][0], slices - 1, self.calls[-1][1], 0)
+                        if far == slices - 1:
+                            after = late and self.ends_last(h, i, k, j, reach)
+                            order = (2 if late else 0, after, order[2])
+                        elif order[2] == first and not late:
+                            order = (1, False, order[2])
+                        else:
+                            order = (2 + slices - far, late, order[2])
                     entry = order + (far, square)
                     (queues[self.calls.index((h, k))] if far > 1 else last).append(entry)
         if self.slices == 2:
@@ -299,6 +309,11 @@
     def only_last(self, h, i, k, j):
         near = (1, self.slices - 2)
         touched = [part for part, z in ((h, i), (k, j)) if z in near]
+        return all(part == self.parts - 1 for part in touched)
+
+    def ends_last(self, h, i, k, j, reach):
+        end = self.slices - 1 if reach(self.slices - 1, 0) > reach(0, 0) else 0
+        touched = [part for part, z in ((h, i), (k, j)) if z == end]
         return all(part == self.parts - 1 for part in touched)
 
     def first_ready(self):

time: 263 us -> 261 us (level)
  starting transfers between devices: 112 us -> 105 us
  waiting for transfers between devices: 5.16 us -> 10.4 us
    ppermute x15, waiting for transfers between devices: 0.92 us -> 9.1 us  [on_device(): lax.ppermute(outgoing[1], 'tm', left)]
    ppermute x15, starting transfers between devices: 76.3 us -> 69.8 us  [on_device(): lax.ppermute(outgoing[0], 'tm', right)]
    ppermute x15, waiting for transfers between devices: 3.01 us -> 0.04 us  [on_device(): lax.ppermute(outgoing[0], 'tm', right)]
  transfers between devices with their start and end apart: 35 -> 35, of which waited for: 10 -> 5; matrix products, arithmetic and copies ran while one was open for 0% -> 0% of each run, Pallas kernels for 50% -> 51%
where the time goes in v6:
time: 261 us; the launch traced here: 259 us
  Pallas kernels  138 us (53%)
  starting transfers between devices  105 us (40%)
  waiting for transfers between devices  10.4 us (4%)
  local copies, waits for them, and re-layouts  4.35 us (2%)
    ppermute x15, starting transfers between devices, on_device(): lax.ppermute(outgoing[0], 'tm', right)  69.8 us
    pallas_call x17, Pallas kernels, hop(): pl.pallas_call(functools.partial(hop_kernel, receives, sends, (2 if recei...  44.3 us
    pallas_call x3, Pallas kernels, filterbank(): pl.pallas_call(functools.partial(filterbank_kernel, channels, length), gr...  39.3 us
    pallas_call x10, Pallas kernels, correlate(): pl.pallas_call(functools.partial(correlate_kernel, (len(xs), len(ys)), sp...  38.4 us
    ppermute x15, starting transfers between devices, on_device(): lax.ppermute(outgoing[1], 'tm', left)  15.6 us
    pallas_call x2, Pallas kernels, visibility_rows(): pl.pallas_call(functools.partial(rows_kernel, slices, parts, span, part,...  15.6 us
    all_to_all x3, starting transfers between devices, on_device(): lax.all_to_all(own, 'chan', split_axis=0, concat_axis=0, tiled=True)  11.6 us
    ppermute x15, waiting for transfers between devices, on_device(): lax.ppermute(outgoing[1], 'tm', left)  9.1 us
  transfers between devices with their start and end apart: 35, of which 5 were waited for; matrix products, arithmetic and copies ran while one was open for 0% of the time, Pallas kernels for 51%

profile of v6, /device:TPU:0, one launch (start us, length us, event | category | flops | bytes accessed | tf_op | source)
XLA Modules:
  0.0 258.6 jit_solution(16195511852630571023)
XLA Ops:
  2.3 4.9 %collective-permute-start.1 = (bf16[2,128,1024]{2,1,0:T(8,128)(2,1)}, bf16[2,128,1024]{2,1,0:T(8,128)(2,1)S(1)}, u32[]{:S(2)}, u32[]{:S(2)}) collective-permute-start(bf16[2,128,1024]{2,1,0:T(8,128)(2,1)} %get-tuple-element.141), channel_id=1, source_target_pairs={{0,1},{1,2},{2,3},{4,5},{5,6},{6,7},{8,9},{9,10},{10,11},{12,13},{... | collective-permute-start | bytes 1572872 | tf_op jit(solution)/shard_map/ppermute | solution.py:588
  9.6 10.8 %filterbank_h0_f256.1 = (bf16[8,2,128,256]{3,2,1,0:T(8,128)(2,1)}, f32[8,128]{1,0:T(8,128)S(1)}) custom-call(bf16[2,256,32768]{2,1,0:T(8,128)(2,1)} %v_ref.5, bf16[2,256,32768]{2,1,0:T(8,128)(2,1)} %v_ref.5, bf16[720,512]{1,0:T(8,128)(2,1)S(1)} %weights.1.w_ref.after_ref, s32[1,256]{1,0:T(1,128)S(1)} %bitcast.13, bf16[720,512]{1,0:T(8,128)(2,1)S(1)} %weights.1.w_ref.after_ref), custom_call_target="tpu_custom_call" | custom-call | flops 6039797760 | bytes 8388608 | tf_op jit(solution)/shard_map/filterbank_h0_f256/pallas_call | solution.py:119
  20.4 3.7 %all-to-all-start.2 = ((bf16[8,2,128,256]{3,2,1,0:T(8,128)(2,1)}), bf16[8,2,128,256]{3,2,1,0:T(8,128)(2,1)S(1)}, u32[]{:S(2)}, u32[]{:S(2)}) async-start(bf16[8,2,128,256]{3,2,1,0:T(8,128)(2,1)} %get-tuple-element.77), calls=%async_computation.2 | async-start | bytes 2097152 | tf_op jit(solution)/shard_map/all_to_all | solution.py:607
  27.6 10.7 %filterbank_h0_f0.1 = (bf16[8,2,128,256]{3,2,1,0:T(8,128)(2,1)}, f32[8,128]{1,0:T(8,128)S(1)}) custom-call(bf16[2,128,1024]{2,1,0:T(8,128)(2,1)S(1)} %collective-permute-done.1.head_ref, bf16[2,256,32768]{2,1,0:T(8,128)(2,1)} %v_ref.5, bf16[720,512]{1,0:T(8,128)(2,1)S(1)} %weights.1.w_ref.after_ref, s32[1,256]{1,0:T(1,128)S(1)} %bitcast.14, ...), custom_call_target="tpu_custom_call" | custom-call | flops 6039797760 | bytes 8388608 | tf_op jit(solution)/shard_map/filterbank_h0_f0/pallas_call | solution.py:119
  43.2 17.8 %filterbank_h1_f0.1 = (bf16[8,2,128,512]{3,2,1,0:T(8,128)(2,1)}, f32[8,128]{1,0:T(8,128)}) custom-call(bf16[2,128,1024]{2,1,0:T(8,128)(2,1)S(1)} %collective-permute-done.head_ref, bf16[2,256,32768]{2,1,0:T(8,128)(2,1)} %v_ref.5, bf16[720,512]{1,0:T(8,128)(2,1)S(1)} %weights.1.w_ref.after_ref, s32[1,256]{1,0:T(1,128)S(1)} %bitcast.15, ...), custom_call_target="tpu_custom_call" | custom-call | flops 12079595520 | bytes 16777216 | tf_op jit(solution)/shard_map/filterbank_h1_f0/pallas_call | solution.py:119
  60.9 4.3 %all-to-all-start = ((bf16[8,2,128,512]{3,2,1,0:T(8,128)(2,1)}), bf16[8,2,128,512]{3,2,1,0:T(8,128)(2,1)}, u32[]{:S(2)}, u32[]{:S(2)}) async-start(bf16[8,2,128,512]{3,2,1,0:T(8,128)(2,1)} %get-tuple-element.75), calls=%async_computation | async-start | bytes 4194304 | tf_op jit(solution)/shard_map/all_to_all | solution.py:607
  65.3 3.7 %correlate.10 = (f32[13,8,256,256]{3,2,1,0:T(8,128)}, bf16[104,256,256]{2,1,0:T(8,128)(2,1)}, bf16[104,256,256]{2,1,0:T(8,128)(2,1)}) custom-call(bf16[8,2,128,256]{3,2,1,0:T(8,128)(2,1)S(1)} %all-to-all-done.1.refs_0_.refs_2_.refs_1_, bf16[8,2,128,256]{3,2,1,0:T(8,128)(2,1)} %copy-done.7, ...), custom_call_target="tpu_custom_call" | custom-call | flops 1073741824 | bytes 2097152 | tf_op jit(solution)/shard_map/correlate/pallas_call | solution.py:222
  75.6 3.8 %correlate.11.refs_4_ = f32[13,8,256,256]{3,2,1,0:T(8,128)} custom-call(bf16[8,2,128,256]{3,2,1,0:T(8,128)(2,1)S(1)} %all-to-all-done.1.refs_0_.refs_2_.refs_1_, bf16[8,2,128,256]{3,2,1,0:T(8,128)(2,1)} %copy-done.7, bf16[8,2,128,256]{3,2,1,0:T(8,128)(2,1)S(1)} %all-to-all-done.1.refs_0_.refs_2_.refs_1_, ...), custom_call_target="tpu_custom_call", output_to_operand_aliasing={{}: (4, {})} | custom-call | flops 1073741824 | bytes 2097152 | tf_op jit(solution)/shard_map/correlate/pallas_call | solution.py:222
  84.7 3.8 %correlate.12.refs_2_ = f32[13,8,256,256]{3,2,1,0:T(8,128)} custom-call(bf16[8,2,128,256]{3,2,1,0:T(8,128)(2,1)S(1)} %all-to-all-done.1.refs_0_.refs_2_.refs_1_, bf16[8,2,128,256]{3,2,1,0:T(8,128)(2,1)} %copy-done.7, bf16[8,2,128,256]{3,2,1,0:T(8,128)(2,1)S(1)} %all-to-all-done.1.refs_0_.refs_2_.refs_1_, ...), custom_call_target="tpu_custom_call", output_to_operand_aliasing={{}: (4, {})} | custom-call | flops 1073741824 | bytes 2097152 | tf_op jit(solution)/shard_map/correlate/pallas_call | solution.py:222
  88.5 3.6 %hop.18 = (bf16[104,256,256]{2,1,0:T(8,128)(2,1)}, bf16[104,256,256]{2,1,0:T(8,128)(2,1)}, bf16[4,256,256]{2,1,0:T(8,128)(2,1)}, bf16[4,256,256]{2,1,0:T(8,128)(2,1)}) custom-call(s32[544]{0:T(1024)S(1)} %copy-done, s32[1]{0:T(128)} %bitcast.place, f32[104,256,256]{2,1,0:T(8,128)} %bitcast.18, ...), custom_call_target="tpu_custom_call", output_to_operand_aliasing={{0}: (5, {}), {1}: (6, {})} | custom-call | flops 1048576 | bytes 5242880 | tf_op jit(solution)/shard_map/hop/pallas_call | solution.py:449
  95.7 4.0 %correlate.13.refs_2_ = f32[13,8,256,256]{3,2,1,0:T(8,128)} custom-call(bf16[8,2,128,512]{3,2,1,0:T(8,128)(2,1)} %all-to-all-done.refs_0_.refs_1_, bf16[8,2,128,512]{3,2,1,0:T(8,128)(2,1)} %all-to-all-done.refs_0_.refs_1_, f32[13,8,256,256]{3,2,1,0:T(8,128)} %correlate.12.refs_2_), custom_call_target="tpu_custom_call", output_to_operand_aliasing={{}: (2, {})} | custom-call | flops 1073741824 | bytes 2097152 | tf_op jit(solution)/shard_map/correlate/pallas_call | solution.py:222
  102.3 4.8 %collective-permute-start.10 = (bf16[4,256,256]{2,1,0:T(8,128)(2,1)S(1)}, bf16[4,256,256]{2,1,0:T(8,128)(2,1)S(1)}, u32[]{:S(2)}, u32[]{:S(2)}) collective-permute-start(bf16[4,256,256]{2,1,0:T(8,128)(2,1)S(1)} %get-tuple-element.93), channel_id=1, source_target_pairs={{0,1},{1,2},{4,5},{5,6},{8,9},{9,10},{12,13},{13,14},{16,17},{17,1... | collective-permute-start | bytes 1572872 | tf_op jit(solution)/shard_map/ppermute | solution.py:650
  107.8 4.1 %correlate.14.refs_2_ = f32[13,8,256,256]{3,2,1,0:T(8,128)} custom-call(bf16[8,2,128,512]{3,2,1,0:T(8,128)(2,1)} %all-to-all-done.refs_0_.refs_1_, bf16[8,2,128,512]{3,2,1,0:T(8,128)(2,1)} %all-to-all-done.refs_0_.refs_1_, f32[13,8,256,256]{3,2,1,0:T(8,128)} %correlate.13.refs_2_), custom_call_target="tpu_custom_call", output_to_operand_aliasing={{}: (2, {})} | custom-call | flops 1073741824 | bytes 2097152 | tf_op jit(solution)/shard_map/correlate/pallas_call | solution.py:222
  114.6 5.1 %collective-permute-start.8 = (bf16[4,256,256]{2,1,0:T(8,128)(2,1)S(1)}, bf16[4,256,256]{2,1,0:T(8,128)(2,1)S(1)}, u32[]{:S(2)}, u32[]{:S(2)}) collective-permute-start(bf16[4,256,256]{2,1,0:T(8,128)(2,1)S(1)} %get-tuple-element.91), channel_id=1, source_target_pairs={{0,1},{1,2},{2,3},{4,5},{5,6},{6,7},{8,9},{9,10},{10,11},{12,13},{... | collective-permute-start | bytes 1572872 | tf_op jit(solution)/shard_map/ppermute | solution.py:650
  121.0 4.1 %correlate.15.refs_3_ = f32[13,8,256,256]{3,2,1,0:T(8,128)} custom-call(bf16[8,2,128,512]{3,2,1,0:T(8,128)(2,1)} %all-to-all-done.refs_0_.refs_1_, bf16[8,2,128,512]{3,2,1,0:T(8,128)(2,1)} %all-to-all-done.refs_0_.refs_1_, f32[13,8,256,256]{3,2,1,0:T(8,128)} %correlate.14.refs_2_), custom_call_target="tpu_custom_call", output_to_operand_aliasing={{}: (2, {})} | custom-call | flops 1073741824 | bytes 2097152 | tf_op jit(solution)/shard_map/correlate/pallas_call | solution.py:222
  127.8 5.2 %collective-permute-start.14 = (bf16[4,256,256]{2,1,0:T(8,128)(2,1)S(1)}, bf16[4,256,256]{2,1,0:T(8,128)(2,1)S(1)}, u32[]{:S(2)}, u32[]{:S(2)}) collective-permute-start(bf16[4,256,256]{2,1,0:T(8,128)(2,1)S(1)} %get-tuple-element.101), channel_id=1, source_target_pairs={{0,1},{1,2},{4,5},{5,6},{8,9},{9,10},{12,13},{13,14},{16,17},{17,1... | collective-permute-start | bytes 1572872 | tf_op jit(solution)/shard_map/ppermute | solution.py:650
  133.7 3.7 %correlate.16.refs_3_ = f32[13,8,256,256]{3,2,1,0:T(8,128)} custom-call(bf16[8,2,128,512]{3,2,1,0:T(8,128)(2,1)} %all-to-all-done.refs_0_.refs_1_, bf16[8,2,128,256]{3,2,1,0:T(8,128)(2,1)S(1)} %all-to-all-done.1.refs_0_.refs_2_.refs_1_, bf16[8,2,128,256]{3,2,1,0:T(8,128)(2,1)} %copy-done.7, ...), custom_call_target="tpu_custom_call", output_to_operand_aliasing={{}: (3, {})} | custom-call | flops 1073741824 | bytes 2097152 | tf_op jit(solution)/shard_map/correlate/pallas_call | solution.py:222
  140.1 4.5 %collective-permute-start.12 = (bf16[4,256,256]{2,1,0:T(8,128)(2,1)S(1)}, bf16[4,256,256]{2,1,0:T(8,128)(2,1)S(1)}, u32[]{:S(2)}, u32[]{:S(2)}) collective-permute-start(bf16[4,256,256]{2,1,0:T(8,128)(2,1)S(1)} %get-tuple-element.99), channel_id=1, source_target_pairs={{0,1},{1,2},{2,3},{4,5},{5,6},{6,7},{8,9},{9,10},{10,11},{12,13},{... | collective-permute-start | bytes 1572872 | tf_op jit(solution)/shard_map/ppermute | solution.py:650
  145.9 3.7 %correlate.17.refs_3_ = f32[13,8,256,256]{3,2,1,0:T(8,128)} custom-call(bf16[8,2,128,512]{3,2,1,0:T(8,128)(2,1)} %all-to-all-done.refs_0_.refs_1_, bf16[8,2,128,256]{3,2,1,0:T(8,128)(2,1)S(1)} %all-to-all-done.1.refs_0_.refs_2_.refs_1_, bf16[8,2,128,256]{3,2,1,0:T(8,128)(2,1)} %copy-done.7, ...), custom_call_target="tpu_custom_call", output_to_operand_aliasing={{}: (3, {})} | custom-call | flops 1073741824 | bytes 2097152 | tf_op jit(solution)/shard_map/correlate/pallas_call | solution.py:222
  152.3 5.2 %collective-permute-start.18 = (bf16[4,256,256]{2,1,0:T(8,128)(2,1)S(1)}, bf16[4,256,256]{2,1,0:T(8,128)(2,1)S(1)}, u32[]{:S(2)}, u32[]{:S(2)}) collective-permute-start(bf16[4,256,256]{2,1,0:T(8,128)(2,1)S(1)} %get-tuple-element.109), channel_id=1, source_target_pairs={{0,1},{1,2},{2,3},{4,5},{5,6},{6,7},{8,9},{9,10},{10,11},{12,13},{... | collective-permute-start | bytes 1572872 | tf_op jit(solution)/shard_map/ppermute | solution.py:650
  158.8 3.8 %correlate.18.refs_3_ = f32[13,8,256,256]{3,2,1,0:T(8,128)} custom-call(bf16[8,2,128,512]{3,2,1,0:T(8,128)(2,1)} %all-to-all-done.refs_0_.refs_1_, bf16[8,2,128,256]{3,2,1,0:T(8,128)(2,1)S(1)} %all-to-all-done.1.refs_0_.refs_2_.refs_1_, bf16[8,2,128,256]{3,2,1,0:T(8,128)(2,1)} %copy-done.7, ...), custom_call_target="tpu_custom_call", output_to_operand_aliasing={{}: (3, {})} | custom-call | flops 1073741824 | bytes 2097152 | tf_op jit(solution)/shard_map/correlate/pallas_call | solution.py:222
  165.2 4.6 %collective-permute-start.16 = (bf16[4,256,256]{2,1,0:T(8,128)(2,1)S(1)}, bf16[4,256,256]{2,1,0:T(8,128)(2,1)S(1)}, u32[]{:S(2)}, u32[]{:S(2)}) collective-permute-start(bf16[4,256,256]{2,1,0:T(8,128)(2,1)S(1)} %get-tuple-element.107), channel_id=1, source_target_pairs={{0,1},{1,2},{4,5},{5,6},{8,9},{9,10},{12,13},{13,14},{16,17},{17,1... | collective-permute-start | bytes 1572872 | tf_op jit(solution)/shard_map/ppermute | solution.py:650
  170.5 3.7 %correlate.19 = f32[13,8,256,256]{3,2,1,0:T(8,128)} custom-call(bf16[8,2,128,512]{3,2,1,0:T(8,128)(2,1)} %all-to-all-done.refs_0_.refs_1_, bf16[8,2,128,256]{3,2,1,0:T(8,128)(2,1)S(1)} %all-to-all-done.1.refs_0_.refs_2_.refs_1_, bf16[8,2,128,256]{3,2,1,0:T(8,128)(2,1)} %copy-done.7, ...), custom_call_target="tpu_custom_call", output_to_operand_aliasing={{}: (3, {})} | custom-call | flops 1073741824 | bytes 2097152 | tf_op jit(solution)/shard_map/correlate/pallas_call | solution.py:222
  176.9 4.5 %collective-permute-start.22 = (bf16[4,256,256]{2,1,0:T(8,128)(2,1)S(1)}, bf16[4,256,256]{2,1,0:T(8,128)(2,1)S(1)}, u32[]{:S(2)}, u32[]{:S(2)}) collective-permute-start(bf16[4,256,256]{2,1,0:T(8,128)(2,1)S(1)} %get-tuple-element.117), channel_id=1, source_target_pairs={{0,1},{1,2},{2,3},{4,5},{5,6},{6,7},{8,9},{9,10},{10,11},{12,13},{... | collective-permute-start | bytes 1572872 | tf_op jit(solution)/shard_map/ppermute | solution.py:650
  185.3 5.2 %collective-permute-start.20 = (bf16[4,256,256]{2,1,0:T(8,128)(2,1)S(1)}, bf16[4,256,256]{2,1,0:T(8,128)(2,1)S(1)}, u32[]{:S(2)}, u32[]{:S(2)}) collective-permute-start(bf16[4,256,256]{2,1,0:T(8,128)(2,1)S(1)} %get-tuple-element.115), channel_id=1, source_target_pairs={{0,1},{1,2},{2,3},{4,5},{5,6},{6,7},{8,9},{9,10},{10,11},{12,13},{... | collective-permute-start | bytes 1572872 | tf_op jit(solution)/shard_map/ppermute | solution.py:650
  191.8 4.5 %collective-permute-done.23.refs_2_ = bf16[4,256,256]{2,1,0:T(8,128)(2,1)S(1)} collective-permute-done((bf16[4,256,256]{2,1,0:T(8,128)(2,1)S(1)}, bf16[4,256,256]{2,1,0:T(8,128)(2,1)S(1)}, u32[]{:S(2)}, u32[]{:S(2)}) %collective-permute-start.23) | collective-permute-done | bytes 524320 | tf_op jit(solution)/shard_map/ppermute | solution.py:651
  199.0 4.3 %collective-permute-start.26 = (bf16[4,256,256]{2,1,0:T(8,128)(2,1)S(1)}, bf16[4,256,256]{2,1,0:T(8,128)(2,1)S(1)}, u32[]{:S(2)}, u32[]{:S(2)}) collective-permute-start(bf16[4,256,256]{2,1,0:T(8,128)(2,1)S(1)} %get-tuple-element.125), channel_id=1, source_target_pairs={{0,1},{1,2},{2,3},{4,5},{5,6},{6,7},{8,9},{9,10},{10,11},{12,13},{... | collective-permute-start | bytes 1572872 | tf_op jit(solution)/shard_map/ppermute | solution.py:650
  210.3 4.3 %collective-permute-start.24 = (bf16[4,256,256]{2,1,0:T(8,128)(2,1)S(1)}, bf16[4,256,256]{2,1,0:T(8,128)(2,1)S(1)}, u32[]{:S(2)}, u32[]{:S(2)}) collective-permute-start(bf16[4,256,256]{2,1,0:T(8,128)(2,1)S(1)} %get-tuple-element.123), channel_id=1, source_target_pairs={{0,1},{1,2},{4,5},{5,6},{8,9},{9,10},{12,13},{13,14},{16,17},{17,1... | collective-permute-start | bytes 1572872 | tf_op jit(solution)/shard_map/ppermute | solution.py:650
  218.2 7.6 %collective-permute-start.30 = (bf16[4,256,256]{2,1,0:T(8,128)(2,1)S(1)}, bf16[4,256,256]{2,1,0:T(8,128)(2,1)S(1)}, u32[]{:S(2)}, u32[]{:S(2)}) collective-permute-start(bf16[4,256,256]{2,1,0:T(8,128)(2,1)S(1)} %get-tuple-element.133), channel_id=1, source_target_pairs={{0,1},{1,2},{2,3},{4,5},{5,6},{6,7},{8,9},{9,10},{10,11},{12,13},{... | collective-permute-start | bytes 1572872 | tf_op jit(solution)/shard_map/ppermute | solution.py:650
  230.0 7.0 %collective-permute-start.28 = (bf16[4,256,256]{2,1,0:T(8,128)(2,1)S(1)}, bf16[4,256,256]{2,1,0:T(8,128)(2,1)S(1)}, u32[]{:S(2)}, u32[]{:S(2)}) collective-permute-start(bf16[4,256,256]{2,1,0:T(8,128)(2,1)S(1)} %get-tuple-element.131), channel_id=1, source_target_pairs={{0,1},{2,3},{4,5},{6,7},{8,9},{10,11},{12,13},{14,15},{16,17},{18,... | collective-permute-start | bytes 1572872 | tf_op jit(solution)/shard_map/ppermute | solution.py:650
  241.3 10.3 %visibility_rows.2.refs_4_.refs_24_ = f32[2,2,256,2,8,128]{5,4,3,2,1,0:T(8,128)} custom-call(s32[128]{0:T(128)S(1)} %copy-done.6, s32[64]{0:T(128)S(1)} %copy-done.5, s32[1]{0:T(128)} %bitcast.place, f32[104,256,256]{2,1,0:T(8,128)} %bitcast.31, f32[104,256,256]{2,1,0:T(8,128)} %bitcast.32, f32[104,256,256]{2,1,0:T(8,128)} %bitcast.33, ...), custom_call_target="tpu_custom_call" | custom-call | flops 4194304 | bytes 12582912 | tf_op jit(solution)/shard_map/visibility_rows/pallas_call | solution.py:551
  253.3 5.3 %visibility_rows.3 = f32[2,2,256,2,8,128]{5,4,3,2,1,0:T(8,128)} custom-call(s32[128]{0:T(128)S(1)} %copy-done.6, s32[64]{0:T(128)S(1)} %copy-done.5, s32[1]{0:T(128)} %bitcast.place, f32[104,256,256]{2,1,0:T(8,128)} %bitcast.39, f32[104,256,256]{2,1,0:T(8,128)} %bitcast.40, f32[104,256,256]{2,1,0:T(8,128)} %bitcast.41, ...), custom_call_target="tpu_custom_call", output_to_operand_aliasing={{}: (27, {})} | custom-call | flops 4194304 | bytes 12582912 | tf_op jit(solution)/shard_map/visibility_rows/pallas_call | solution.py:551
  (88 shorter events, 81.4 us)
Async XLA Ops:
  2.3 25.3 %collective-permute-start.1 = (bf16[2,128,1024]{2,1,0:T(8,128)(2,1)}, bf16[2,128,1024]{2,1,0:T(8,128)(2,1)S(1)}, u32[]{:S(2)}, u32[]{:S(2)}) collective-permute-start(bf16[2,128,1024]{2,1,0:T(8,128)(2,1)} %get-tuple-element.141), channel_id=1, source_target_pairs={{0,1},{1,2},{2,3},{4,5},{5,6},{6,7},{8,9},{9,10},{10,11},{12,13},{... | collective-permute-start | bytes 1572872 | tf_op jit(solution)/shard_map/ppermute | solution.py:588
  20.4 19.2 %all-to-all-start.2 = ((bf16[8,2,128,256]{3,2,1,0:T(8,128)(2,1)}), bf16[8,2,128,256]{3,2,1,0:T(8,128)(2,1)S(1)}, u32[]{:S(2)}, u32[]{:S(2)}) async-start(bf16[8,2,128,256]{3,2,1,0:T(8,128)(2,1)} %get-tuple-element.77), calls=%async_computation.2 | async-start | bytes 2097152 | tf_op jit(solution)/shard_map/all_to_all | solution.py:607
  24.1 19.0 %collective-permute-start = (bf16[2,128,1024]{2,1,0:T(8,128)(2,1)}, bf16[2,128,1024]{2,1,0:T(8,128)(2,1)S(1)}, u32[]{:S(2)}, u32[]{:S(2)}) collective-permute-start(bf16[2,128,1024]{2,1,0:T(8,128)(2,1)} %get-tuple-element.142), channel_id=1, source_target_pairs={{0,1},{1,2},{2,3},{4,5},{5,6},{6,7},{8,9},{9,10},{10,11},{12,13},{... | collective-permute-start | bytes 1572872 | tf_op jit(solution)/shard_map/ppermute | solution.py:588
  39.6 21.4 %all-to-all-start.1 = ((bf16[8,2,128,256]{3,2,1,0:T(8,128)(2,1)}), bf16[8,2,128,256]{3,2,1,0:T(8,128)(2,1)S(1)}, u32[]{:S(2)}, u32[]{:S(2)}) async-start(bf16[8,2,128,256]{3,2,1,0:T(8,128)(2,1)} %get-tuple-element.76), calls=%async_computation.1 | async-start | bytes 2097152 | tf_op jit(solution)/shard_map/all_to_all | solution.py:607
  60.9 34.8 %all-to-all-start = ((bf16[8,2,128,512]{3,2,1,0:T(8,128)(2,1)}), bf16[8,2,128,512]{3,2,1,0:T(8,128)(2,1)}, u32[]{:S(2)}, u32[]{:S(2)}) async-start(bf16[8,2,128,512]{3,2,1,0:T(8,128)(2,1)} %get-tuple-element.75), calls=%async_computation | async-start | bytes 4194304 | tf_op jit(solution)/shard_map/all_to_all | solution.py:607
  71.2 17.3 %collective-permute-start.2 = (bf16[4,256,256]{2,1,0:T(8,128)(2,1)S(1)}, bf16[4,256,256]{2,1,0:T(8,128)(2,1)S(1)}, u32[]{:S(2)}, u32[]{:S(2)}) collective-permute-start(bf16[4,256,256]{2,1,0:T(8,128)(2,1)S(1)} %get-tuple-element.79), channel_id=1, source_target_pairs={{0,1},{4,5},{8,9},{12,13},{16,17},{20,21},{24,25},{28,29}} | collective-permute-start | bytes 1572872 | tf_op jit(solution)/shard_map/ppermute | solution.py:650
  74.7 13.8 %collective-permute-start.3 = (bf16[4,256,256]{2,1,0:T(8,128)(2,1)S(1)}, bf16[4,256,256]{2,1,0:T(8,128)(2,1)S(1)}, u32[]{:S(2)}, u32[]{:S(2)}) collective-permute-start(bf16[4,256,256]{2,1,0:T(8,128)(2,1)S(1)} %get-tuple-element.80), channel_id=1, source_target_pairs={{3,2},{7,6},{11,10},{15,14},{19,18},{23,22},{27,26},{31,30}} | collective-permute-start | bytes 1572872 | tf_op jit(solution)/shard_map/ppermute | solution.py:651
  82.6 17.0 %collective-permute-start.6 = (bf16[4,256,256]{2,1,0:T(8,128)(2,1)}, bf16[4,256,256]{2,1,0:T(8,128)(2,1)S(1)}, u32[]{:S(2)}, u32[]{:S(2)}) collective-permute-start(bf16[4,256,256]{2,1,0:T(8,128)(2,1)} %get-tuple-element.85), channel_id=1, source_target_pairs={{0,1},{4,5},{8,9},{12,13},{16,17},{20,21},{24,25},{28,29}} | collective-permute-start | bytes 1572872 | tf_op jit(solution)/shard_map/ppermute | solution.py:650
  84.0 15.7 %collective-permute-start.7 = (bf16[4,256,256]{2,1,0:T(8,128)(2,1)}, bf16[4,256,256]{2,1,0:T(8,128)(2,1)S(1)}, u32[]{:S(2)}, u32[]{:S(2)}) collective-permute-start(bf16[4,256,256]{2,1,0:T(8,128)(2,1)} %get-tuple-element.86), channel_id=1, source_target_pairs={{3,2},{7,6},{11,10},{15,14},{19,18},{23,22},{27,26},{31,30}} | collective-permute-start | bytes 1572872 | tf_op jit(solution)/shard_map/ppermute | solution.py:651
  92.1 19.8 %collective-permute-start.4 = (bf16[4,256,256]{2,1,0:T(8,128)(2,1)}, bf16[4,256,256]{2,1,0:T(8,128)(2,1)S(1)}, u32[]{:S(2)}, u32[]{:S(2)}) collective-permute-start(bf16[4,256,256]{2,1,0:T(8,128)(2,1)} %get-tuple-element.83), channel_id=1, source_target_pairs={{0,1},{1,2},{4,5},{5,6},{8,9},{9,10},{12,13},{13,14},{16,17},{17,1... | collective-permute-start | bytes 1572872 | tf_op jit(solution)/shard_map/ppermute | solution.py:650
  95.0 16.9 %collective-permute-start.5 = (bf16[4,256,256]{2,1,0:T(8,128)(2,1)}, bf16[4,256,256]{2,1,0:T(8,128)(2,1)S(1)}, u32[]{:S(2)}, u32[]{:S(2)}) collective-permute-start(bf16[4,256,256]{2,1,0:T(8,128)(2,1)} %get-tuple-element.84), channel_id=1, source_target_pairs={{3,2},{2,1},{7,6},{6,5},{11,10},{10,9},{15,14},{14,13},{19,18},{18... | collective-permute-start | bytes 1572872 | tf_op jit(solution)/shard_map/ppermute | solution.py:651
  102.3 22.8 %collective-permute-start.10 = (bf16[4,256,256]{2,1,0:T(8,128)(2,1)S(1)}, bf16[4,256,256]{2,1,0:T(8,128)(2,1)S(1)}, u32[]{:S(2)}, u32[]{:S(2)}) collective-permute-start(bf16[4,256,256]{2,1,0:T(8,128)(2,1)S(1)} %get-tuple-element.93), channel_id=1, source_target_pairs={{0,1},{1,2},{4,5},{5,6},{8,9},{9,10},{12,13},{13,14},{16,17},{17,1... | collective-permute-start | bytes 1572872 | tf_op jit(solution)/shard_map/ppermute | solution.py:650
  107.1 18.1 %collective-permute-start.11 = (bf16[4,256,256]{2,1,0:T(8,128)(2,1)S(1)}, bf16[4,256,256]{2,1,0:T(8,128)(2,1)S(1)}, u32[]{:S(2)}, u32[]{:S(2)}) collective-permute-start(bf16[4,256,256]{2,1,0:T(8,128)(2,1)S(1)} %get-tuple-element.94), channel_id=1, source_target_pairs={{3,2},{2,1},{7,6},{6,5},{11,10},{10,9},{15,14},{14,13},{19,18},{18... | collective-permute-start | bytes 1572872 | tf_op jit(solution)/shard_map/ppermute | solution.py:651
  114.6 22.9 %collective-permute-start.8 = (bf16[4,256,256]{2,1,0:T(8,128)(2,1)S(1)}, bf16[4,256,256]{2,1,0:T(8,128)(2,1)S(1)}, u32[]{:S(2)}, u32[]{:S(2)}) collective-permute-start(bf16[4,256,256]{2,1,0:T(8,128)(2,1)S(1)} %get-tuple-element.91), channel_id=1, source_target_pairs={{0,1},{1,2},{2,3},{4,5},{5,6},{6,7},{8,9},{9,10},{10,11},{12,13},{... | collective-permute-start | bytes 1572872 | tf_op jit(solution)/shard_map/ppermute | solution.py:650
  119.7 17.7 %collective-permute-start.9 = (bf16[4,256,256]{2,1,0:T(8,128)(2,1)S(1)}, bf16[4,256,256]{2,1,0:T(8,128)(2,1)S(1)}, u32[]{:S(2)}, u32[]{:S(2)}) collective-permute-start(bf16[4,256,256]{2,1,0:T(8,128)(2,1)S(1)} %get-tuple-element.92), channel_id=1, source_target_pairs={{3,2},{2,1},{1,0},{7,6},{6,5},{5,4},{11,10},{10,9},{9,8},{15,14},{... | collective-permute-start | bytes 1572872 | tf_op jit(solution)/shard_map/ppermute | solution.py:651
  127.8 21.8 %collective-permute-start.14 = (bf16[4,256,256]{2,1,0:T(8,128)(2,1)S(1)}, bf16[4,256,256]{2,1,0:T(8,128)(2,1)S(1)}, u32[]{:S(2)}, u32[]{:S(2)}) collective-permute-start(bf16[4,256,256]{2,1,0:T(8,128)(2,1)S(1)} %get-tuple-element.101), channel_id=1, source_target_pairs={{0,1},{1,2},{4,5},{5,6},{8,9},{9,10},{12,13},{13,14},{16,17},{17,1... | collective-permute-start | bytes 1572872 | tf_op jit(solution)/shard_map/ppermute | solution.py:650
  133.0 16.6 %collective-permute-start.15 = (bf16[4,256,256]{2,1,0:T(8,128)(2,1)S(1)}, bf16[4,256,256]{2,1,0:T(8,128)(2,1)S(1)}, u32[]{:S(2)}, u32[]{:S(2)}) collective-permute-start(bf16[4,256,256]{2,1,0:T(8,128)(2,1)S(1)} %get-tuple-element.102), channel_id=1, source_target_pairs={{3,2},{2,1},{7,6},{6,5},{11,10},{10,9},{15,14},{14,13},{19,18},{18... | collective-permute-start | bytes 1572872 | tf_op jit(solution)/shard_map/ppermute | solution.py:651
  140.1 22.4 %collective-permute-start.12 = (bf16[4,256,256]{2,1,0:T(8,128)(2,1)S(1)}, bf16[4,256,256]{2,1,0:T(8,128)(2,1)S(1)}, u32[]{:S(2)}, u32[]{:S(2)}) collective-permute-start(bf16[4,256,256]{2,1,0:T(8,128)(2,1)S(1)} %get-tuple-element.99), channel_id=1, source_target_pairs={{0,1},{1,2},{2,3},{4,5},{5,6},{6,7},{8,9},{9,10},{10,11},{12,13},{... | collective-permute-start | bytes 1572872 | tf_op jit(solution)/shard_map/ppermute | solution.py:650
  144.6 17.9 %collective-permute-start.13 = (bf16[4,256,256]{2,1,0:T(8,128)(2,1)S(1)}, bf16[4,256,256]{2,1,0:T(8,128)(2,1)S(1)}, u32[]{:S(2)}, u32[]{:S(2)}) collective-permute-start(bf16[4,256,256]{2,1,0:T(8,128)(2,1)S(1)} %get-tuple-element.100), channel_id=1, source_target_pairs={{3,2},{2,1},{1,0},{7,6},{6,5},{5,4},{11,10},{10,9},{9,8},{15,14},{... | collective-permute-start | bytes 1572872 | tf_op jit(solution)/shard_map/ppermute | solution.py:651
  152.3 21.9 %collective-permute-start.18 = (bf16[4,256,256]{2,1,0:T(8,128)(2,1)S(1)}, bf16[4,256,256]{2,1,0:T(8,128)(2,1)S(1)}, u32[]{:S(2)}, u32[]{:S(2)}) collective-permute-start(bf16[4,256,256]{2,1,0:T(8,128)(2,1)S(1)} %get-tuple-element.109), channel_id=1, source_target_pairs={{0,1},{1,2},{2,3},{4,5},{5,6},{6,7},{8,9},{9,10},{10,11},{12,13},{... | collective-permute-start | bytes 1572872 | tf_op jit(solution)/shard_map/ppermute | solution.py:650
  157.5 16.7 %collective-permute-start.19 = (bf16[4,256,256]{2,1,0:T(8,128)(2,1)S(1)}, bf16[4,256,256]{2,1,0:T(8,128)(2,1)S(1)}, u32[]{:S(2)}, u32[]{:S(2)}) collective-permute-start(bf16[4,256,256]{2,1,0:T(8,128)(2,1)S(1)} %get-tuple-element.110), channel_id=1, source_target_pairs={{3,2},{2,1},{1,0},{7,6},{6,5},{5,4},{11,10},{10,9},{9,8},{15,14},{... | collective-permute-start | bytes 1572872 | tf_op jit(solution)/shard_map/ppermute | solution.py:651
  165.2 17.5 %collective-permute-start.16 = (bf16[4,256,256]{2,1,0:T(8,128)(2,1)S(1)}, bf16[4,256,256]{2,1,0:T(8,128)(2,1)S(1)}, u32[]{:S(2)}, u32[]{:S(2)}) collective-permute-start(bf16[4,256,256]{2,1,0:T(8,128)(2,1)S(1)} %get-tuple-element.107), channel_id=1, source_target_pairs={{0,1},{1,2},{4,5},{5,6},{8,9},{9,10},{12,13},{13,14},{16,17},{17,1... | collective-permute-start | bytes 1572872 | tf_op jit(solution)/shard_map/ppermute | solution.py:650
  176.9 15.0 %collective-permute-start.22 = (bf16[4,256,256]{2,1,0:T(8,128)(2,1)S(1)}, bf16[4,256,256]{2,1,0:T(8,128)(2,1)S(1)}, u32[]{:S(2)}, u32[]{:S(2)}) collective-permute-start(bf16[4,256,256]{2,1,0:T(8,128)(2,1)S(1)} %get-tuple-element.117), channel_id=1, source_target_pairs={{0,1},{1,2},{2,3},{4,5},{5,6},{6,7},{8,9},{9,10},{10,11},{12,13},{... | collective-permute-start | bytes 1572872 | tf_op jit(solution)/shard_map/ppermute | solution.py:650
  181.4 15.0 %collective-permute-start.23 = (bf16[4,256,256]{2,1,0:T(8,128)(2,1)S(1)}, bf16[4,256,256]{2,1,0:T(8,128)(2,1)S(1)}, u32[]{:S(2)}, u32[]{:S(2)}) collective-permute-start(bf16[4,256,256]{2,1,0:T(8,128)(2,1)S(1)} %get-tuple-element.118), channel_id=1, source_target_pairs={{3,2},{2,1},{1,0},{7,6},{6,5},{5,4},{11,10},{10,9},{9,8},{15,14},{... | collective-permute-start | bytes 1572872 | tf_op jit(solution)/shard_map/ppermute | solution.py:651
  185.3 19.2 %collective-permute-start.20 = (bf16[4,256,256]{2,1,0:T(8,128)(2,1)S(1)}, bf16[4,256,256]{2,1,0:T(8,128)(2,1)S(1)}, u32[]{:S(2)}, u32[]{:S(2)}) collective-permute-start(bf16[4,256,256]{2,1,0:T(8,128)(2,1)S(1)} %get-tuple-element.115), channel_id=1, source_target_pairs={{0,1},{1,2},{2,3},{4,5},{5,6},{6,7},{8,9},{9,10},{10,11},{12,13},{... | collective-permute-start | bytes 1572872 | tf_op jit(solution)/shard_map/ppermute | solution.py:650
  190.5 17.1 %collective-permute-start.21 = (bf16[4,256,256]{2,1,0:T(8,128)(2,1)S(1)}, bf16[4,256,256]{2,1,0:T(8,128)(2,1)S(1)}, u32[]{:S(2)}, u32[]{:S(2)}) collective-permute-start(bf16[4,256,256]{2,1,0:T(8,128)(2,1)S(1)} %get-tuple-element.116), channel_id=1, source_target_pairs={{3,2},{2,1},{1,0},{7,6},{6,5},{5,4},{11,10},{10,9},{9,8},{15,14},{... | collective-permute-start | bytes 1572872 | tf_op jit(solution)/shard_map/ppermute | solution.py:651
  199.0 16.2 %collective-permute-start.26 = (bf16[4,256,256]{2,1,0:T(8,128)(2,1)S(1)}, bf16[4,256,256]{2,1,0:T(8,128)(2,1)S(1)}, u32[]{:S(2)}, u32[]{:S(2)}) collective-permute-start(bf16[4,256,256]{2,1,0:T(8,128)(2,1)S(1)} %get-tuple-element.125), channel_id=1, source_target_pairs={{0,1},{1,2},{2,3},{4,5},{5,6},{6,7},{8,9},{9,10},{10,11},{12,13},{... | collective-permute-start | bytes 1572872 | tf_op jit(solution)/shard_map/ppermute | solution.py:650
  210.3 17.0 %collective-permute-start.24 = (bf16[4,256,256]{2,1,0:T(8,128)(2,1)S(1)}, bf16[4,256,256]{2,1,0:T(8,128)(2,1)S(1)}, u32[]{:S(2)}, u32[]{:S(2)}) collective-permute-start(bf16[4,256,256]{2,1,0:T(8,128)(2,1)S(1)} %get-tuple-element.123), channel_id=1, source_target_pairs={{0,1},{1,2},{4,5},{5,6},{8,9},{9,10},{12,13},{13,14},{16,17},{17,1... | collective-permute-start | bytes 1572872 | tf_op jit(solution)/shard_map/ppermute | solution.py:650
  218.2 20.1 %collective-permute-start.30 = (bf16[4,256,256]{2,1,0:T(8,128)(2,1)S(1)}, bf16[4,256,256]{2,1,0:T(8,128)(2,1)S(1)}, u32[]{:S(2)}, u32[]{:S(2)}) collective-permute-start(bf16[4,256,256]{2,1,0:T(8,128)(2,1)S(1)} %get-tuple-element.133), channel_id=1, source_target_pairs={{0,1},{1,2},{2,3},{4,5},{5,6},{6,7},{8,9},{9,10},{10,11},{12,13},{... | collective-permute-start | bytes 1572872 | tf_op jit(solution)/shard_map/ppermute | solution.py:650
  225.8 13.8 %collective-permute-start.31 = (bf16[4,256,256]{2,1,0:T(8,128)(2,1)S(1)}, bf16[4,256,256]{2,1,0:T(8,128)(2,1)S(1)}, u32[]{:S(2)}, u32[]{:S(2)}) collective-permute-start(bf16[4,256,256]{2,1,0:T(8,128)(2,1)S(1)} %get-tuple-element.134), channel_id=1, source_target_pairs={{3,2},{2,1},{1,0},{7,6},{6,5},{5,4},{11,10},{10,9},{9,8},{15,14},{... | collective-permute-start | bytes 1572872 | tf_op jit(solution)/shard_map/ppermute | solution.py:651
  230.0 21.6 %collective-permute-start.28 = (bf16[4,256,256]{2,1,0:T(8,128)(2,1)S(1)}, bf16[4,256,256]{2,1,0:T(8,128)(2,1)S(1)}, u32[]{:S(2)}, u32[]{:S(2)}) collective-permute-start(bf16[4,256,256]{2,1,0:T(8,128)(2,1)S(1)} %get-tuple-element.131), channel_id=1, source_target_pairs={{0,1},{2,3},{4,5},{6,7},{8,9},{10,11},{12,13},{14,15},{16,17},{18,... | collective-permute-start | bytes 1572872 | tf_op jit(solution)/shard_map/ppermute | solution.py:650
  237.0 14.6 %collective-permute-start.29 = (bf16[4,256,256]{2,1,0:T(8,128)(2,1)S(1)}, bf16[4,256,256]{2,1,0:T(8,128)(2,1)S(1)}, u32[]{:S(2)}, u32[]{:S(2)}) collective-permute-start(bf16[4,256,256]{2,1,0:T(8,128)(2,1)S(1)} %get-tuple-element.132), channel_id=1, source_target_pairs={{3,2},{1,0},{7,6},{5,4},{11,10},{9,8},{15,14},{13,12},{19,18},{17,... | collective-permute-start | bytes 1572872 | tf_op jit(solution)/shard_map/ppermute | solution.py:651
  (11 other events, 106.1 us)

commit v7 on v6

--- a/solution.py
+++ b/solution.py
@@ -177,7 +177,7 @@
         (((1,), (1,)), ((), ())),
         preferred_element_type=F32,
     )
-    both = both * weight
+    both = (both * weight).astype(BF16)
     for m in range(many):
         i = pl.program_id(0) * many + low + m
         real = both[2 * m * size : (2 * m + 1) * size]
@@ -213,7 +213,7 @@
         (many, 2 * group, size, size), lambda i: ((call * slices + low) // many + i, which, 0, 0)
     )
     lines = total // (2 * slices)
-    shape = jax.ShapeDtypeStruct((lines, 2 * slices, size, size), F32)
+    shape = jax.ShapeDtypeStruct((lines, 2 * slices, size, size), BF16)
     store = jax.ShapeDtypeStruct((total, size, size), BF16)
     fresh = partial is None
     if not fresh:
@@ -415,8 +415,8 @@
             load.wait()
             total = own[side, b]
             if receives:
-                total = total + came[side][b].astype(F32)
-            sent[side][b] = total.astype(BF16)
+                total = (total.astype(F32) + came[side][b].astype(F32)).astype(BF16)
+            sent[side][b] = total
     for store in stores:
         store.wait()
 
@@ -445,7 +445,7 @@
     if sends:
         out_specs += [inside, inside]
         out_shape += [message, message]
-        scratch = [pltpu.VMEM((2, count, size, size), F32)]
+        scratch = [pltpu.VMEM((2, count, size, size), BF16)]
     found = pl.pallas_call(
         functools.partial(
             hop_kernel, receives, sends, (2 if receives else 0) + len(after), count, steps, step
@@ -487,7 +487,7 @@
     def total(at):
         r = jnp.where(has_right, right[at][0].astype(F32), 0.0)
         l = jnp.where(has_left, left[at][0].astype(F32), 0.0)
-        return own[at][0] + r + l
+        return own[at][0].astype(F32) + r + l
 
     for j in range(slices // 2):
         for k in range(parts):

time: 261 us -> 257 us (0.985)
  Pallas kernels: 138 us -> 132 us
    ppermute x15, waiting for transfers between devices: 0.04 us -> 3.7 us  [on_device(): lax.ppermute(outgoing[0], 'tm', right)]
    pallas_call x17, Pallas kernels: 44.3 us -> 41.2 us  [hop(): pl.pallas_call(functools.partial(hop_kernel, receives, sends, (2 if recei...]
  transfers between devices with their start and end apart: 35 -> 35, of which waited for: 5 -> 9; matrix products, arithmetic and copies ran while one was open for 0% -> 0% of each run, Pallas kernels for 51% -> 49%
where the time goes in v7:
time: 257 us; the launch traced here: 255 us
  Pallas kernels  132 us (51%)
  starting transfers between devices  106 us (41%)
  waiting for transfers between devices  12.2 us (5%)
  local copies, waits for them, and re-layouts  4.35 us (2%)
    ppermute x15, starting transfers between devices, on_device(): lax.ppermute(outgoing[0], 'tm', right)  70.5 us
    pallas_call x17, Pallas kernels, hop(): pl.pallas_call(functools.partial(hop_kernel, receives, sends, (2 if recei...  41.2 us
    pallas_call x3, Pallas kernels, filterbank(): pl.pallas_call(functools.partial(filterbank_kernel, channels, length), gr...  39.3 us
    pallas_call x10, Pallas kernels, correlate(): pl.pallas_call(functools.partial(correlate_kernel, (len(xs), len(ys)), sp...  36.5 us
    ppermute x15, starting transfers between devices, on_device(): lax.ppermute(outgoing[1], 'tm', left)  15.4 us
    pallas_call x2, Pallas kernels, visibility_rows(): pl.pallas_call(functools.partial(rows_kernel, slices, parts, span, part,...  14.6 us
    all_to_all x3, starting transfers between devices, on_device(): lax.all_to_all(own, 'chan', split_axis=0, concat_axis=0, tiled=True)  11.7 us
    ppermute x2, starting transfers between devices, on_device(): lax.ppermute(tail, 'tm', [(i, i + 1) for i in range(slices - 1)])  8.41 us
  transfers between devices with their start and end apart: 35, of which 9 were waited for; matrix products, arithmetic and copies ran while one was open for 0% of the time, Pallas kernels for 49%

profile of v7, /device:TPU:0, one launch (start us, length us, event | category | flops | bytes accessed | tf_op | source)
XLA Modules:
  0.0 254.9 jit_solution(1814497000885763252)
XLA Ops:
  2.3 4.9 %collective-permute-start.1 = (bf16[2,128,1024]{2,1,0:T(8,128)(2,1)}, bf16[2,128,1024]{2,1,0:T(8,128)(2,1)S(1)}, u32[]{:S(2)}, u32[]{:S(2)}) collective-permute-start(bf16[2,128,1024]{2,1,0:T(8,128)(2,1)} %get-tuple-element.141), channel_id=1, source_target_pairs={{0,1},{1,2},{2,3},{4,5},{5,6},{6,7},{8,9},{9,10},{10,11},{12,13},{... | collective-permute-start | bytes 1572872 | tf_op jit(solution)/shard_map/ppermute | solution.py:588
  9.6 10.8 %filterbank_h0_f256.1 = (bf16[8,2,128,256]{3,2,1,0:T(8,128)(2,1)}, f32[8,128]{1,0:T(8,128)S(1)}) custom-call(bf16[2,256,32768]{2,1,0:T(8,128)(2,1)} %v_ref.5, bf16[2,256,32768]{2,1,0:T(8,128)(2,1)} %v_ref.5, bf16[720,512]{1,0:T(8,128)(2,1)S(1)} %weights.1.w_ref.after_ref, s32[1,256]{1,0:T(1,128)S(1)} %bitcast.13, bf16[720,512]{1,0:T(8,128)(2,1)S(1)} %weights.1.w_ref.after_ref), custom_call_target="tpu_custom_call" | custom-call | flops 6039797760 | bytes 8388608 | tf_op jit(solution)/shard_map/filterbank_h0_f256/pallas_call | solution.py:119
  20.4 3.7 %all-to-all-start.2 = ((bf16[8,2,128,256]{3,2,1,0:T(8,128)(2,1)}), bf16[8,2,128,256]{3,2,1,0:T(8,128)(2,1)S(1)}, u32[]{:S(2)}, u32[]{:S(2)}) async-start(bf16[8,2,128,256]{3,2,1,0:T(8,128)(2,1)} %get-tuple-element.77), calls=%async_computation.2 | async-start | bytes 2097152 | tf_op jit(solution)/shard_map/all_to_all | solution.py:607
  27.6 10.7 %filterbank_h0_f0.1 = (bf16[8,2,128,256]{3,2,1,0:T(8,128)(2,1)}, f32[8,128]{1,0:T(8,128)S(1)}) custom-call(bf16[2,128,1024]{2,1,0:T(8,128)(2,1)S(1)} %collective-permute-done.1.head_ref, bf16[2,256,32768]{2,1,0:T(8,128)(2,1)} %v_ref.5, bf16[720,512]{1,0:T(8,128)(2,1)S(1)} %weights.1.w_ref.after_ref, s32[1,256]{1,0:T(1,128)S(1)} %bitcast.14, ...), custom_call_target="tpu_custom_call" | custom-call | flops 6039797760 | bytes 8388608 | tf_op jit(solution)/shard_map/filterbank_h0_f0/pallas_call | solution.py:119
  39.6 3.6 %all-to-all-start.1 = ((bf16[8,2,128,256]{3,2,1,0:T(8,128)(2,1)}), bf16[8,2,128,256]{3,2,1,0:T(8,128)(2,1)S(1)}, u32[]{:S(2)}, u32[]{:S(2)}) async-start(bf16[8,2,128,256]{3,2,1,0:T(8,128)(2,1)} %get-tuple-element.76), calls=%async_computation.1 | async-start | bytes 2097152 | tf_op jit(solution)/shard_map/all_to_all | solution.py:607
  43.2 17.8 %filterbank_h1_f0.1 = (bf16[8,2,128,512]{3,2,1,0:T(8,128)(2,1)}, f32[8,128]{1,0:T(8,128)}) custom-call(bf16[2,128,1024]{2,1,0:T(8,128)(2,1)S(1)} %collective-permute-done.head_ref, bf16[2,256,32768]{2,1,0:T(8,128)(2,1)} %v_ref.5, bf16[720,512]{1,0:T(8,128)(2,1)S(1)} %weights.1.w_ref.after_ref, s32[1,256]{1,0:T(1,128)S(1)} %bitcast.15, ...), custom_call_target="tpu_custom_call" | custom-call | flops 12079595520 | bytes 16777216 | tf_op jit(solution)/shard_map/filterbank_h1_f0/pallas_call | solution.py:119
  60.9 4.4 %all-to-all-start = ((bf16[8,2,128,512]{3,2,1,0:T(8,128)(2,1)}), bf16[8,2,128,512]{3,2,1,0:T(8,128)(2,1)}, u32[]{:S(2)}, u32[]{:S(2)}) async-start(bf16[8,2,128,512]{3,2,1,0:T(8,128)(2,1)} %get-tuple-element.75), calls=%async_computation | async-start | bytes 4194304 | tf_op jit(solution)/shard_map/all_to_all | solution.py:607
  65.3 3.5 %correlate.10 = (bf16[13,8,256,256]{3,2,1,0:T(8,128)(2,1)}, bf16[104,256,256]{2,1,0:T(8,128)(2,1)}, bf16[104,256,256]{2,1,0:T(8,128)(2,1)}) custom-call(bf16[8,2,128,256]{3,2,1,0:T(8,128)(2,1)S(1)} %all-to-all-done.1.refs_0_.refs_2_.refs_1_, bf16[8,2,128,256]{3,2,1,0:T(8,128)(2,1)} %copy-done.7, ...), custom_call_target="tpu_custom_call" | custom-call | flops 1073741824 | bytes 2097152 | tf_op jit(solution)/shard_map/correlate/pallas_call | solution.py:222
  75.0 3.6 %correlate.11.refs_4_ = bf16[13,8,256,256]{3,2,1,0:T(8,128)(2,1)} custom-call(bf16[8,2,128,256]{3,2,1,0:T(8,128)(2,1)S(1)} %all-to-all-done.1.refs_0_.refs_2_.refs_1_, bf16[8,2,128,256]{3,2,1,0:T(8,128)(2,1)} %copy-done.7, bf16[8,2,128,256]{3,2,1,0:T(8,128)(2,1)S(1)} %all-to-all-done.1.refs_0_.refs_2_.refs_1_, ...), custom_call_target="tpu_custom_call", output_to_operand_aliasing={{}: (4, {})} | custom-call | flops 1073741824 | bytes 2097152 | tf_op jit(solution)/shard_map/correlate/pallas_call | solution.py:222
  83.8 3.6 %correlate.12.refs_2_ = bf16[13,8,256,256]{3,2,1,0:T(8,128)(2,1)} custom-call(bf16[8,2,128,256]{3,2,1,0:T(8,128)(2,1)S(1)} %all-to-all-done.1.refs_0_.refs_2_.refs_1_, bf16[8,2,128,256]{3,2,1,0:T(8,128)(2,1)} %copy-done.7, bf16[8,2,128,256]{3,2,1,0:T(8,128)(2,1)S(1)} %all-to-all-done.1.refs_0_.refs_2_.refs_1_, ...), custom_call_target="tpu_custom_call", output_to_operand_aliasing={{}: (4, {})} | custom-call | flops 1073741824 | bytes 2097152 | tf_op jit(solution)/shard_map/correlate/pallas_call | solution.py:222
  90.8 3.6 %collective-permute-start.4 = (bf16[4,256,256]{2,1,0:T(8,128)(2,1)}, bf16[4,256,256]{2,1,0:T(8,128)(2,1)S(1)}, u32[]{:S(2)}, u32[]{:S(2)}) collective-permute-start(bf16[4,256,256]{2,1,0:T(8,128)(2,1)} %get-tuple-element.83), channel_id=1, source_target_pairs={{0,1},{1,2},{4,5},{5,6},{8,9},{9,10},{12,13},{13,14},{16,17},{17,1... | collective-permute-start | bytes 1572872 | tf_op jit(solution)/shard_map/ppermute | solution.py:650
  95.1 3.8 %correlate.13.refs_2_ = bf16[13,8,256,256]{3,2,1,0:T(8,128)(2,1)} custom-call(bf16[8,2,128,512]{3,2,1,0:T(8,128)(2,1)} %all-to-all-done.refs_0_.refs_1_, bf16[8,2,128,512]{3,2,1,0:T(8,128)(2,1)} %all-to-all-done.refs_0_.refs_1_, bf16[13,8,256,256]{3,2,1,0:T(8,128)(2,1)} %correlate.12.refs_2_), custom_call_target="tpu_custom_call", output_to_operand_aliasing={{}: (2, {})} | custom-call | flops 1073741824 | bytes 2097152 | tf_op jit(solution)/shard_map/correlate/pallas_call | solution.py:222
  101.4 4.8 %collective-permute-start.10 = (bf16[4,256,256]{2,1,0:T(8,128)(2,1)S(1)}, bf16[4,256,256]{2,1,0:T(8,128)(2,1)S(1)}, u32[]{:S(2)}, u32[]{:S(2)}) collective-permute-start(bf16[4,256,256]{2,1,0:T(8,128)(2,1)S(1)} %get-tuple-element.93), channel_id=1, source_target_pairs={{0,1},{1,2},{4,5},{5,6},{8,9},{9,10},{12,13},{13,14},{16,17},{17,1... | collective-permute-start | bytes 1572872 | tf_op jit(solution)/shard_map/ppermute | solution.py:650
  106.8 4.0 %correlate.14.refs_2_ = bf16[13,8,256,256]{3,2,1,0:T(8,128)(2,1)} custom-call(bf16[8,2,128,512]{3,2,1,0:T(8,128)(2,1)} %all-to-all-done.refs_0_.refs_1_, bf16[8,2,128,512]{3,2,1,0:T(8,128)(2,1)} %all-to-all-done.refs_0_.refs_1_, bf16[13,8,256,256]{3,2,1,0:T(8,128)(2,1)} %correlate.13.refs_2_), custom_call_target="tpu_custom_call", output_to_operand_aliasing={{}: (2, {})} | custom-call | flops 1073741824 | bytes 2097152 | tf_op jit(solution)/shard_map/correlate/pallas_call | solution.py:222
  113.3 5.2 %collective-permute-start.8 = (bf16[4,256,256]{2,1,0:T(8,128)(2,1)S(1)}, bf16[4,256,256]{2,1,0:T(8,128)(2,1)S(1)}, u32[]{:S(2)}, u32[]{:S(2)}) collective-permute-start(bf16[4,256,256]{2,1,0:T(8,128)(2,1)S(1)} %get-tuple-element.91), channel_id=1, source_target_pairs={{0,1},{1,2},{2,3},{4,5},{5,6},{6,7},{8,9},{9,10},{10,11},{12,13},{... | collective-permute-start | bytes 1572872 | tf_op jit(solution)/shard_map/ppermute | solution.py:650
  119.7 3.9 %correlate.15.refs_3_ = bf16[13,8,256,256]{3,2,1,0:T(8,128)(2,1)} custom-call(bf16[8,2,128,512]{3,2,1,0:T(8,128)(2,1)} %all-to-all-done.refs_0_.refs_1_, bf16[8,2,128,512]{3,2,1,0:T(8,128)(2,1)} %all-to-all-done.refs_0_.refs_1_, bf16[13,8,256,256]{3,2,1,0:T(8,128)(2,1)} %correlate.14.refs_2_), custom_call_target="tpu_custom_call", output_to_operand_aliasing={{}: (2, {})} | custom-call | flops 1073741824 | bytes 2097152 | tf_op jit(solution)/shard_map/correlate/pallas_call | solution.py:222
  126.1 5.2 %collective-permute-start.14 = (bf16[4,256,256]{2,1,0:T(8,128)(2,1)S(1)}, bf16[4,256,256]{2,1,0:T(8,128)(2,1)S(1)}, u32[]{:S(2)}, u32[]{:S(2)}) collective-permute-start(bf16[4,256,256]{2,1,0:T(8,128)(2,1)S(1)} %get-tuple-element.101), channel_id=1, source_target_pairs={{0,1},{1,2},{4,5},{5,6},{8,9},{9,10},{12,13},{13,14},{16,17},{17,1... | collective-permute-start | bytes 1572872 | tf_op jit(solution)/shard_map/ppermute | solution.py:650
  132.0 3.6 %correlate.16.refs_3_ = bf16[13,8,256,256]{3,2,1,0:T(8,128)(2,1)} custom-call(bf16[8,2,128,512]{3,2,1,0:T(8,128)(2,1)} %all-to-all-done.refs_0_.refs_1_, bf16[8,2,128,256]{3,2,1,0:T(8,128)(2,1)S(1)} %all-to-all-done.1.refs_0_.refs_2_.refs_1_, bf16[8,2,128,256]{3,2,1,0:T(8,128)(2,1)} %copy-done.7, ...), custom_call_target="tpu_custom_call", output_to_operand_aliasing={{}: (3, {})} | custom-call | flops 1073741824 | bytes 2097152 | tf_op jit(solution)/shard_map/correlate/pallas_call | solution.py:222
  138.0 4.5 %collective-permute-start.12 = (bf16[4,256,256]{2,1,0:T(8,128)(2,1)S(1)}, bf16[4,256,256]{2,1,0:T(8,128)(2,1)S(1)}, u32[]{:S(2)}, u32[]{:S(2)}) collective-permute-start(bf16[4,256,256]{2,1,0:T(8,128)(2,1)S(1)} %get-tuple-element.99), channel_id=1, source_target_pairs={{0,1},{1,2},{2,3},{4,5},{5,6},{6,7},{8,9},{9,10},{10,11},{12,13},{... | collective-permute-start | bytes 1572872 | tf_op jit(solution)/shard_map/ppermute | solution.py:650
  143.8 3.5 %correlate.17.refs_3_ = bf16[13,8,256,256]{3,2,1,0:T(8,128)(2,1)} custom-call(bf16[8,2,128,512]{3,2,1,0:T(8,128)(2,1)} %all-to-all-done.refs_0_.refs_1_, bf16[8,2,128,256]{3,2,1,0:T(8,128)(2,1)S(1)} %all-to-all-done.1.refs_0_.refs_2_.refs_1_, bf16[8,2,128,256]{3,2,1,0:T(8,128)(2,1)} %copy-done.7, ...), custom_call_target="tpu_custom_call", output_to_operand_aliasing={{}: (3, {})} | custom-call | flops 1073741824 | bytes 2097152 | tf_op jit(solution)/shard_map/correlate/pallas_call | solution.py:222
  149.8 5.2 %collective-permute-start.18 = (bf16[4,256,256]{2,1,0:T(8,128)(2,1)S(1)}, bf16[4,256,256]{2,1,0:T(8,128)(2,1)S(1)}, u32[]{:S(2)}, u32[]{:S(2)}) collective-permute-start(bf16[4,256,256]{2,1,0:T(8,128)(2,1)S(1)} %get-tuple-element.109), channel_id=1, source_target_pairs={{0,1},{1,2},{2,3},{4,5},{5,6},{6,7},{8,9},{9,10},{10,11},{12,13},{... | collective-permute-start | bytes 1572872 | tf_op jit(solution)/shard_map/ppermute | solution.py:650
  156.3 3.5 %correlate.18.refs_3_ = bf16[13,8,256,256]{3,2,1,0:T(8,128)(2,1)} custom-call(bf16[8,2,128,512]{3,2,1,0:T(8,128)(2,1)} %all-to-all-done.refs_0_.refs_1_, bf16[8,2,128,256]{3,2,1,0:T(8,128)(2,1)S(1)} %all-to-all-done.1.refs_0_.refs_2_.refs_1_, bf16[8,2,128,256]{3,2,1,0:T(8,128)(2,1)} %copy-done.7, ...), custom_call_target="tpu_custom_call", output_to_operand_aliasing={{}: (3, {})} | custom-call | flops 1073741824 | bytes 2097152 | tf_op jit(solution)/shard_map/correlate/pallas_call | solution.py:222
  162.3 4.6 %collective-permute-start.16 = (bf16[4,256,256]{2,1,0:T(8,128)(2,1)S(1)}, bf16[4,256,256]{2,1,0:T(8,128)(2,1)S(1)}, u32[]{:S(2)}, u32[]{:S(2)}) collective-permute-start(bf16[4,256,256]{2,1,0:T(8,128)(2,1)S(1)} %get-tuple-element.107), channel_id=1, source_target_pairs={{0,1},{1,2},{4,5},{5,6},{8,9},{9,10},{12,13},{13,14},{16,17},{17,1... | collective-permute-start | bytes 1572872 | tf_op jit(solution)/shard_map/ppermute | solution.py:650
  167.6 3.5 %correlate.19 = bf16[13,8,256,256]{3,2,1,0:T(8,128)(2,1)} custom-call(bf16[8,2,128,512]{3,2,1,0:T(8,128)(2,1)} %all-to-all-done.refs_0_.refs_1_, bf16[8,2,128,256]{3,2,1,0:T(8,128)(2,1)S(1)} %all-to-all-done.1.refs_0_.refs_2_.refs_1_, bf16[8,2,128,256]{3,2,1,0:T(8,128)(2,1)} %copy-done.7, ...), custom_call_target="tpu_custom_call", output_to_operand_aliasing={{}: (3, {})} | custom-call | flops 1073741824 | bytes 2097152 | tf_op jit(solution)/shard_map/correlate/pallas_call | solution.py:222
  173.6 4.5 %collective-permute-start.22 = (bf16[4,256,256]{2,1,0:T(8,128)(2,1)S(1)}, bf16[4,256,256]{2,1,0:T(8,128)(2,1)S(1)}, u32[]{:S(2)}, u32[]{:S(2)}) collective-permute-start(bf16[4,256,256]{2,1,0:T(8,128)(2,1)S(1)} %get-tuple-element.117), channel_id=1, source_target_pairs={{0,1},{1,2},{2,3},{4,5},{5,6},{6,7},{8,9},{9,10},{10,11},{12,13},{... | collective-permute-start | bytes 1572872 | tf_op jit(solution)/shard_map/ppermute | solution.py:650
  181.9 5.2 %collective-permute-start.20 = (bf16[4,256,256]{2,1,0:T(8,128)(2,1)S(1)}, bf16[4,256,256]{2,1,0:T(8,128)(2,1)S(1)}, u32[]{:S(2)}, u32[]{:S(2)}) collective-permute-start(bf16[4,256,256]{2,1,0:T(8,128)(2,1)S(1)} %get-tuple-element.115), channel_id=1, source_target_pairs={{0,1},{1,2},{2,3},{4,5},{5,6},{6,7},{8,9},{9,10},{10,11},{12,13},{... | collective-permute-start | bytes 1572872 | tf_op jit(solution)/shard_map/ppermute | solution.py:650
  195.8 4.3 %collective-permute-start.26 = (bf16[4,256,256]{2,1,0:T(8,128)(2,1)S(1)}, bf16[4,256,256]{2,1,0:T(8,128)(2,1)S(1)}, u32[]{:S(2)}, u32[]{:S(2)}) collective-permute-start(bf16[4,256,256]{2,1,0:T(8,128)(2,1)S(1)} %get-tuple-element.125), channel_id=1, source_target_pairs={{0,1},{1,2},{2,3},{4,5},{5,6},{6,7},{8,9},{9,10},{10,11},{12,13},{... | collective-permute-start | bytes 1572872 | tf_op jit(solution)/shard_map/ppermute | solution.py:650
  207.0 4.3 %collective-permute-start.24 = (bf16[4,256,256]{2,1,0:T(8,128)(2,1)S(1)}, bf16[4,256,256]{2,1,0:T(8,128)(2,1)S(1)}, u32[]{:S(2)}, u32[]{:S(2)}) collective-permute-start(bf16[4,256,256]{2,1,0:T(8,128)(2,1)S(1)} %get-tuple-element.123), channel_id=1, source_target_pairs={{0,1},{1,2},{4,5},{5,6},{8,9},{9,10},{12,13},{13,14},{16,17},{17,1... | collective-permute-start | bytes 1572872 | tf_op jit(solution)/shard_map/ppermute | solution.py:650
  215.4 7.2 %collective-permute-start.30 = (bf16[4,256,256]{2,1,0:T(8,128)(2,1)S(1)}, bf16[4,256,256]{2,1,0:T(8,128)(2,1)S(1)}, u32[]{:S(2)}, u32[]{:S(2)}) collective-permute-start(bf16[4,256,256]{2,1,0:T(8,128)(2,1)S(1)} %get-tuple-element.133), channel_id=1, source_target_pairs={{0,1},{1,2},{2,3},{4,5},{5,6},{6,7},{8,9},{9,10},{10,11},{12,13},{... | collective-permute-start | bytes 1572872 | tf_op jit(solution)/shard_map/ppermute | solution.py:650
  226.6 7.2 %collective-permute-start.28 = (bf16[4,256,256]{2,1,0:T(8,128)(2,1)S(1)}, bf16[4,256,256]{2,1,0:T(8,128)(2,1)S(1)}, u32[]{:S(2)}, u32[]{:S(2)}) collective-permute-start(bf16[4,256,256]{2,1,0:T(8,128)(2,1)S(1)} %get-tuple-element.131), channel_id=1, source_target_pairs={{0,1},{2,3},{4,5},{6,7},{8,9},{10,11},{12,13},{14,15},{16,17},{18,... | collective-permute-start | bytes 1572872 | tf_op jit(solution)/shard_map/ppermute | solution.py:650
  238.6 9.5 %visibility_rows.2.refs_4_.refs_24_ = f32[2,2,256,2,8,128]{5,4,3,2,1,0:T(8,128)} custom-call(s32[128]{0:T(128)S(1)} %copy-done.6, s32[64]{0:T(128)S(1)} %copy-done.5, s32[1]{0:T(128)} %bitcast.place, bf16[104,256,256]{2,1,0:T(8,128)(2,1)} %bitcast.31, bf16[104,256,256]{2,1,0:T(8,128)(2,1)} %bitcast.32, bf16[104,256,256]{2,1,0:T(8,128)(2,1)} %bitcast.33, ...), custom_call_target="tpu_custom_call" | custom-call | flops 4194304 | bytes 12582912 | tf_op jit(solution)/shard_map/visibility_rows/pallas_call | solution.py:551
  249.8 5.0 %visibility_rows.3 = f32[2,2,256,2,8,128]{5,4,3,2,1,0:T(8,128)} custom-call(s32[128]{0:T(128)S(1)} %copy-done.6, s32[64]{0:T(128)S(1)} %copy-done.5, s32[1]{0:T(128)} %bitcast.place, bf16[104,256,256]{2,1,0:T(8,128)(2,1)} %bitcast.39, bf16[104,256,256]{2,1,0:T(8,128)(2,1)} %bitcast.40, ...), custom_call_target="tpu_custom_call", output_to_operand_aliasing={{}: (27, {})} | custom-call | flops 4194304 | bytes 12582912 | tf_op jit(solution)/shard_map/visibility_rows/pallas_call | solution.py:551
  (88 shorter events, 81.9 us)
Async XLA Ops:
  2.3 25.3 %collective-permute-start.1 = (bf16[2,128,1024]{2,1,0:T(8,128)(2,1)}, bf16[2,128,1024]{2,1,0:T(8,128)(2,1)S(1)}, u32[]{:S(2)}, u32[]{:S(2)}) collective-permute-start(bf16[2,128,1024]{2,1,0:T(8,128)(2,1)} %get-tuple-element.141), channel_id=1, source_target_pairs={{0,1},{1,2},{2,3},{4,5},{5,6},{6,7},{8,9},{9,10},{10,11},{12,13},{... | collective-permute-start | bytes 1572872 | tf_op jit(solution)/shard_map/ppermute | solution.py:588
  20.4 19.2 %all-to-all-start.2 = ((bf16[8,2,128,256]{3,2,1,0:T(8,128)(2,1)}), bf16[8,2,128,256]{3,2,1,0:T(8,128)(2,1)S(1)}, u32[]{:S(2)}, u32[]{:S(2)}) async-start(bf16[8,2,128,256]{3,2,1,0:T(8,128)(2,1)} %get-tuple-element.77), calls=%async_computation.2 | async-start | bytes 2097152 | tf_op jit(solution)/shard_map/all_to_all | solution.py:607
  24.1 19.0 %collective-permute-start = (bf16[2,128,1024]{2,1,0:T(8,128)(2,1)}, bf16[2,128,1024]{2,1,0:T(8,128)(2,1)S(1)}, u32[]{:S(2)}, u32[]{:S(2)}) collective-permute-start(bf16[2,128,1024]{2,1,0:T(8,128)(2,1)} %get-tuple-element.142), channel_id=1, source_target_pairs={{0,1},{1,2},{2,3},{4,5},{5,6},{6,7},{8,9},{9,10},{10,11},{12,13},{... | collective-permute-start | bytes 1572872 | tf_op jit(solution)/shard_map/ppermute | solution.py:588
  39.6 21.4 %all-to-all-start.1 = ((bf16[8,2,128,256]{3,2,1,0:T(8,128)(2,1)}), bf16[8,2,128,256]{3,2,1,0:T(8,128)(2,1)S(1)}, u32[]{:S(2)}, u32[]{:S(2)}) async-start(bf16[8,2,128,256]{3,2,1,0:T(8,128)(2,1)} %get-tuple-element.76), calls=%async_computation.1 | async-start | bytes 2097152 | tf_op jit(solution)/shard_map/all_to_all | solution.py:607
  60.9 34.2 %all-to-all-start = ((bf16[8,2,128,512]{3,2,1,0:T(8,128)(2,1)}), bf16[8,2,128,512]{3,2,1,0:T(8,128)(2,1)}, u32[]{:S(2)}, u32[]{:S(2)}) async-start(bf16[8,2,128,512]{3,2,1,0:T(8,128)(2,1)} %get-tuple-element.75), calls=%async_computation | async-start | bytes 4194304 | tf_op jit(solution)/shard_map/all_to_all | solution.py:607
  70.8 16.5 %collective-permute-start.2 = (bf16[4,256,256]{2,1,0:T(8,128)(2,1)S(1)}, bf16[4,256,256]{2,1,0:T(8,128)(2,1)S(1)}, u32[]{:S(2)}, u32[]{:S(2)}) collective-permute-start(bf16[4,256,256]{2,1,0:T(8,128)(2,1)S(1)} %get-tuple-element.79), channel_id=1, source_target_pairs={{0,1},{4,5},{8,9},{12,13},{16,17},{20,21},{24,25},{28,29}} | collective-permute-start | bytes 1572872 | tf_op jit(solution)/shard_map/ppermute | solution.py:650
  74.3 13.0 %collective-permute-start.3 = (bf16[4,256,256]{2,1,0:T(8,128)(2,1)S(1)}, bf16[4,256,256]{2,1,0:T(8,128)(2,1)S(1)}, u32[]{:S(2)}, u32[]{:S(2)}) collective-permute-start(bf16[4,256,256]{2,1,0:T(8,128)(2,1)S(1)} %get-tuple-element.80), channel_id=1, source_target_pairs={{3,2},{7,6},{11,10},{15,14},{19,18},{23,22},{27,26},{31,30}} | collective-permute-start | bytes 1572872 | tf_op jit(solution)/shard_map/ppermute | solution.py:651
  81.6 17.3 %collective-permute-start.6 = (bf16[4,256,256]{2,1,0:T(8,128)(2,1)}, bf16[4,256,256]{2,1,0:T(8,128)(2,1)S(1)}, u32[]{:S(2)}, u32[]{:S(2)}) collective-permute-start(bf16[4,256,256]{2,1,0:T(8,128)(2,1)} %get-tuple-element.85), channel_id=1, source_target_pairs={{0,1},{4,5},{8,9},{12,13},{16,17},{20,21},{24,25},{28,29}} | collective-permute-start | bytes 1572872 | tf_op jit(solution)/shard_map/ppermute | solution.py:650
  83.1 15.8 %collective-permute-start.7 = (bf16[4,256,256]{2,1,0:T(8,128)(2,1)}, bf16[4,256,256]{2,1,0:T(8,128)(2,1)S(1)}, u32[]{:S(2)}, u32[]{:S(2)}) collective-permute-start(bf16[4,256,256]{2,1,0:T(8,128)(2,1)} %get-tuple-element.86), channel_id=1, source_target_pairs={{3,2},{7,6},{11,10},{15,14},{19,18},{23,22},{27,26},{31,30}} | collective-permute-start | bytes 1572872 | tf_op jit(solution)/shard_map/ppermute | solution.py:651
  90.8 20.0 %collective-permute-start.4 = (bf16[4,256,256]{2,1,0:T(8,128)(2,1)}, bf16[4,256,256]{2,1,0:T(8,128)(2,1)S(1)}, u32[]{:S(2)}, u32[]{:S(2)}) collective-permute-start(bf16[4,256,256]{2,1,0:T(8,128)(2,1)} %get-tuple-element.83), channel_id=1, source_target_pairs={{0,1},{1,2},{4,5},{5,6},{8,9},{9,10},{12,13},{13,14},{16,17},{17,1... | collective-permute-start | bytes 1572872 | tf_op jit(solution)/shard_map/ppermute | solution.py:650
  94.4 16.4 %collective-permute-start.5 = (bf16[4,256,256]{2,1,0:T(8,128)(2,1)}, bf16[4,256,256]{2,1,0:T(8,128)(2,1)S(1)}, u32[]{:S(2)}, u32[]{:S(2)}) collective-permute-start(bf16[4,256,256]{2,1,0:T(8,128)(2,1)} %get-tuple-element.84), channel_id=1, source_target_pairs={{3,2},{2,1},{7,6},{6,5},{11,10},{10,9},{15,14},{14,13},{19,18},{18... | collective-permute-start | bytes 1572872 | tf_op jit(solution)/shard_map/ppermute | solution.py:651
  101.4 22.3 %collective-permute-start.10 = (bf16[4,256,256]{2,1,0:T(8,128)(2,1)S(1)}, bf16[4,256,256]{2,1,0:T(8,128)(2,1)S(1)}, u32[]{:S(2)}, u32[]{:S(2)}) collective-permute-start(bf16[4,256,256]{2,1,0:T(8,128)(2,1)S(1)} %get-tuple-element.93), channel_id=1, source_target_pairs={{0,1},{1,2},{4,5},{5,6},{8,9},{9,10},{12,13},{13,14},{16,17},{17,1... | collective-permute-start | bytes 1572872 | tf_op jit(solution)/shard_map/ppermute | solution.py:650
  106.1 17.5 %collective-permute-start.11 = (bf16[4,256,256]{2,1,0:T(8,128)(2,1)S(1)}, bf16[4,256,256]{2,1,0:T(8,128)(2,1)S(1)}, u32[]{:S(2)}, u32[]{:S(2)}) collective-permute-start(bf16[4,256,256]{2,1,0:T(8,128)(2,1)S(1)} %get-tuple-element.94), channel_id=1, source_target_pairs={{3,2},{2,1},{7,6},{6,5},{11,10},{10,9},{15,14},{14,13},{19,18},{18... | collective-permute-start | bytes 1572872 | tf_op jit(solution)/shard_map/ppermute | solution.py:651
  113.3 22.3 %collective-permute-start.8 = (bf16[4,256,256]{2,1,0:T(8,128)(2,1)S(1)}, bf16[4,256,256]{2,1,0:T(8,128)(2,1)S(1)}, u32[]{:S(2)}, u32[]{:S(2)}) collective-permute-start(bf16[4,256,256]{2,1,0:T(8,128)(2,1)S(1)} %get-tuple-element.91), channel_id=1, source_target_pairs={{0,1},{1,2},{2,3},{4,5},{5,6},{6,7},{8,9},{9,10},{10,11},{12,13},{... | collective-permute-start | bytes 1572872 | tf_op jit(solution)/shard_map/ppermute | solution.py:650
  118.4 17.1 %collective-permute-start.9 = (bf16[4,256,256]{2,1,0:T(8,128)(2,1)S(1)}, bf16[4,256,256]{2,1,0:T(8,128)(2,1)S(1)}, u32[]{:S(2)}, u32[]{:S(2)}) collective-permute-start(bf16[4,256,256]{2,1,0:T(8,128)(2,1)S(1)} %get-tuple-element.92), channel_id=1, source_target_pairs={{3,2},{2,1},{1,0},{7,6},{6,5},{5,4},{11,10},{10,9},{9,8},{15,14},{... | collective-permute-start | bytes 1572872 | tf_op jit(solution)/shard_map/ppermute | solution.py:651
  126.1 21.3 %collective-permute-start.14 = (bf16[4,256,256]{2,1,0:T(8,128)(2,1)S(1)}, bf16[4,256,256]{2,1,0:T(8,128)(2,1)S(1)}, u32[]{:S(2)}, u32[]{:S(2)}) collective-permute-start(bf16[4,256,256]{2,1,0:T(8,128)(2,1)S(1)} %get-tuple-element.101), channel_id=1, source_target_pairs={{0,1},{1,2},{4,5},{5,6},{8,9},{9,10},{12,13},{13,14},{16,17},{17,1... | collective-permute-start | bytes 1572872 | tf_op jit(solution)/shard_map/ppermute | solution.py:650
  131.3 16.1 %collective-permute-start.15 = (bf16[4,256,256]{2,1,0:T(8,128)(2,1)S(1)}, bf16[4,256,256]{2,1,0:T(8,128)(2,1)S(1)}, u32[]{:S(2)}, u32[]{:S(2)}) collective-permute-start(bf16[4,256,256]{2,1,0:T(8,128)(2,1)S(1)} %get-tuple-element.102), channel_id=1, source_target_pairs={{3,2},{2,1},{7,6},{6,5},{11,10},{10,9},{15,14},{14,13},{19,18},{18... | collective-permute-start | bytes 1572872 | tf_op jit(solution)/shard_map/ppermute | solution.py:651
  138.0 21.8 %collective-permute-start.12 = (bf16[4,256,256]{2,1,0:T(8,128)(2,1)S(1)}, bf16[4,256,256]{2,1,0:T(8,128)(2,1)S(1)}, u32[]{:S(2)}, u32[]{:S(2)}) collective-permute-start(bf16[4,256,256]{2,1,0:T(8,128)(2,1)S(1)} %get-tuple-element.99), channel_id=1, source_target_pairs={{0,1},{1,2},{2,3},{4,5},{5,6},{6,7},{8,9},{9,10},{10,11},{12,13},{... | collective-permute-start | bytes 1572872 | tf_op jit(solution)/shard_map/ppermute | solution.py:650
  142.5 17.3 %collective-permute-start.13 = (bf16[4,256,256]{2,1,0:T(8,128)(2,1)S(1)}, bf16[4,256,256]{2,1,0:T(8,128)(2,1)S(1)}, u32[]{:S(2)}, u32[]{:S(2)}) collective-permute-start(bf16[4,256,256]{2,1,0:T(8,128)(2,1)S(1)} %get-tuple-element.100), channel_id=1, source_target_pairs={{3,2},{2,1},{1,0},{7,6},{6,5},{5,4},{11,10},{10,9},{9,8},{15,14},{... | collective-permute-start | bytes 1572872 | tf_op jit(solution)/shard_map/ppermute | solution.py:651
  149.8 21.3 %collective-permute-start.18 = (bf16[4,256,256]{2,1,0:T(8,128)(2,1)S(1)}, bf16[4,256,256]{2,1,0:T(8,128)(2,1)S(1)}, u32[]{:S(2)}, u32[]{:S(2)}) collective-permute-start(bf16[4,256,256]{2,1,0:T(8,128)(2,1)S(1)} %get-tuple-element.109), channel_id=1, source_target_pairs={{0,1},{1,2},{2,3},{4,5},{5,6},{6,7},{8,9},{9,10},{10,11},{12,13},{... | collective-permute-start | bytes 1572872 | tf_op jit(solution)/shard_map/ppermute | solution.py:650
  155.0 16.1 %collective-permute-start.19 = (bf16[4,256,256]{2,1,0:T(8,128)(2,1)S(1)}, bf16[4,256,256]{2,1,0:T(8,128)(2,1)S(1)}, u32[]{:S(2)}, u32[]{:S(2)}) collective-permute-start(bf16[4,256,256]{2,1,0:T(8,128)(2,1)S(1)} %get-tuple-element.110), channel_id=1, source_target_pairs={{3,2},{2,1},{1,0},{7,6},{6,5},{5,4},{11,10},{10,9},{9,8},{15,14},{... | collective-permute-start | bytes 1572872 | tf_op jit(solution)/shard_map/ppermute | solution.py:651
  162.3 17.1 %collective-permute-start.16 = (bf16[4,256,256]{2,1,0:T(8,128)(2,1)S(1)}, bf16[4,256,256]{2,1,0:T(8,128)(2,1)S(1)}, u32[]{:S(2)}, u32[]{:S(2)}) collective-permute-start(bf16[4,256,256]{2,1,0:T(8,128)(2,1)S(1)} %get-tuple-element.107), channel_id=1, source_target_pairs={{0,1},{1,2},{4,5},{5,6},{8,9},{9,10},{12,13},{13,14},{16,17},{17,1... | collective-permute-start | bytes 1572872 | tf_op jit(solution)/shard_map/ppermute | solution.py:650
  173.6 16.8 %collective-permute-start.22 = (bf16[4,256,256]{2,1,0:T(8,128)(2,1)S(1)}, bf16[4,256,256]{2,1,0:T(8,128)(2,1)S(1)}, u32[]{:S(2)}, u32[]{:S(2)}) collective-permute-start(bf16[4,256,256]{2,1,0:T(8,128)(2,1)S(1)} %get-tuple-element.117), channel_id=1, source_target_pairs={{0,1},{1,2},{2,3},{4,5},{5,6},{6,7},{8,9},{9,10},{10,11},{12,13},{... | collective-permute-start | bytes 1572872 | tf_op jit(solution)/shard_map/ppermute | solution.py:650
  178.1 15.2 %collective-permute-start.23 = (bf16[4,256,256]{2,1,0:T(8,128)(2,1)S(1)}, bf16[4,256,256]{2,1,0:T(8,128)(2,1)S(1)}, u32[]{:S(2)}, u32[]{:S(2)}) collective-permute-start(bf16[4,256,256]{2,1,0:T(8,128)(2,1)S(1)} %get-tuple-element.118), channel_id=1, source_target_pairs={{3,2},{2,1},{1,0},{7,6},{6,5},{5,4},{11,10},{10,9},{9,8},{15,14},{... | collective-permute-start | bytes 1572872 | tf_op jit(solution)/shard_map/ppermute | solution.py:651
  181.9 19.8 %collective-permute-start.20 = (bf16[4,256,256]{2,1,0:T(8,128)(2,1)S(1)}, bf16[4,256,256]{2,1,0:T(8,128)(2,1)S(1)}, u32[]{:S(2)}, u32[]{:S(2)}) collective-permute-start(bf16[4,256,256]{2,1,0:T(8,128)(2,1)S(1)} %get-tuple-element.115), channel_id=1, source_target_pairs={{0,1},{1,2},{2,3},{4,5},{5,6},{6,7},{8,9},{9,10},{10,11},{12,13},{... | collective-permute-start | bytes 1572872 | tf_op jit(solution)/shard_map/ppermute | solution.py:650
  187.1 17.5 %collective-permute-start.21 = (bf16[4,256,256]{2,1,0:T(8,128)(2,1)S(1)}, bf16[4,256,256]{2,1,0:T(8,128)(2,1)S(1)}, u32[]{:S(2)}, u32[]{:S(2)}) collective-permute-start(bf16[4,256,256]{2,1,0:T(8,128)(2,1)S(1)} %get-tuple-element.116), channel_id=1, source_target_pairs={{3,2},{2,1},{1,0},{7,6},{6,5},{5,4},{11,10},{10,9},{9,8},{15,14},{... | collective-permute-start | bytes 1572872 | tf_op jit(solution)/shard_map/ppermute | solution.py:651
  195.8 17.1 %collective-permute-start.26 = (bf16[4,256,256]{2,1,0:T(8,128)(2,1)S(1)}, bf16[4,256,256]{2,1,0:T(8,128)(2,1)S(1)}, u32[]{:S(2)}, u32[]{:S(2)}) collective-permute-start(bf16[4,256,256]{2,1,0:T(8,128)(2,1)S(1)} %get-tuple-element.125), channel_id=1, source_target_pairs={{0,1},{1,2},{2,3},{4,5},{5,6},{6,7},{8,9},{9,10},{10,11},{12,13},{... | collective-permute-start | bytes 1572872 | tf_op jit(solution)/shard_map/ppermute | solution.py:650
  207.0 17.1 %collective-permute-start.24 = (bf16[4,256,256]{2,1,0:T(8,128)(2,1)S(1)}, bf16[4,256,256]{2,1,0:T(8,128)(2,1)S(1)}, u32[]{:S(2)}, u32[]{:S(2)}) collective-permute-start(bf16[4,256,256]{2,1,0:T(8,128)(2,1)S(1)} %get-tuple-element.123), channel_id=1, source_target_pairs={{0,1},{1,2},{4,5},{5,6},{8,9},{9,10},{12,13},{13,14},{16,17},{17,1... | collective-permute-start | bytes 1572872 | tf_op jit(solution)/shard_map/ppermute | solution.py:650
  215.4 20.0 %collective-permute-start.30 = (bf16[4,256,256]{2,1,0:T(8,128)(2,1)S(1)}, bf16[4,256,256]{2,1,0:T(8,128)(2,1)S(1)}, u32[]{:S(2)}, u32[]{:S(2)}) collective-permute-start(bf16[4,256,256]{2,1,0:T(8,128)(2,1)S(1)} %get-tuple-element.133), channel_id=1, source_target_pairs={{0,1},{1,2},{2,3},{4,5},{5,6},{6,7},{8,9},{9,10},{10,11},{12,13},{... | collective-permute-start | bytes 1572872 | tf_op jit(solution)/shard_map/ppermute | solution.py:650
  222.5 14.3 %collective-permute-start.31 = (bf16[4,256,256]{2,1,0:T(8,128)(2,1)S(1)}, bf16[4,256,256]{2,1,0:T(8,128)(2,1)S(1)}, u32[]{:S(2)}, u32[]{:S(2)}) collective-permute-start(bf16[4,256,256]{2,1,0:T(8,128)(2,1)S(1)} %get-tuple-element.134), channel_id=1, source_target_pairs={{3,2},{2,1},{1,0},{7,6},{6,5},{5,4},{11,10},{10,9},{9,8},{15,14},{... | collective-permute-start | bytes 1572872 | tf_op jit(solution)/shard_map/ppermute | solution.py:651
  226.6 21.5 %collective-permute-start.28 = (bf16[4,256,256]{2,1,0:T(8,128)(2,1)S(1)}, bf16[4,256,256]{2,1,0:T(8,128)(2,1)S(1)}, u32[]{:S(2)}, u32[]{:S(2)}) collective-permute-start(bf16[4,256,256]{2,1,0:T(8,128)(2,1)S(1)} %get-tuple-element.131), channel_id=1, source_target_pairs={{0,1},{2,3},{4,5},{6,7},{8,9},{10,11},{12,13},{14,15},{16,17},{18,... | collective-permute-start | bytes 1572872 | tf_op jit(solution)/shard_map/ppermute | solution.py:650
  233.8 14.3 %collective-permute-start.29 = (bf16[4,256,256]{2,1,0:T(8,128)(2,1)S(1)}, bf16[4,256,256]{2,1,0:T(8,128)(2,1)S(1)}, u32[]{:S(2)}, u32[]{:S(2)}) collective-permute-start(bf16[4,256,256]{2,1,0:T(8,128)(2,1)S(1)} %get-tuple-element.132), channel_id=1, source_target_pairs={{3,2},{1,0},{7,6},{5,4},{11,10},{9,8},{15,14},{13,12},{19,18},{17,... | collective-permute-start | bytes 1572872 | tf_op jit(solution)/shard_map/ppermute | solution.py:651
  (11 other events, 106.3 us)

commit v8 on v7

--- a/solution.py
+++ b/solution.py
@@ -13,7 +13,7 @@
 GROUP = 8
 LANES = 128
 FRAMES_PER_STEP = 128
-VMEM_LIMIT = 52 * 1024 * 1024
+VMEM_LIMIT = 46 * 1024 * 1024
 
 
 def params(limit=VMEM_LIMIT):

time: 257 us -> 255 us (level)
  Pallas kernels: 132 us -> 119 us
  local copies, waits for them, and re-layouts: 4.35 us -> 8.89 us
  starting transfers between devices: 106 us -> 110 us
    pallas_call x10, Pallas kernels: 36.5 us -> 23.7 us  [correlate(): pl.pallas_call(functools.partial(correlate_kernel, (len(xs), len(ys)), sp...]
    ppermute x15, waiting for transfers between devices: 3.7 us -> 12.2 us  [on_device(): lax.ppermute(outgoing[0], 'tm', right)]
    ppermute x15, waiting for transfers between devices: 7.27 us -> 1.03 us  [on_device(): lax.ppermute(outgoing[1], 'tm', left)]
    unnamed x16 -> x26, local copies, waits for them, and re-layouts: 2.09 us -> 6.61 us
    ppermute x15, starting transfers between devices: 70.5 us -> 73.7 us  [on_device(): lax.ppermute(outgoing[0], 'tm', right)]
  transfers between devices with their start and end apart: 35 -> 35, of which waited for: 9 -> 11; matrix products, arithmetic and copies ran while one was open for 0% -> 0% of each run, Pallas kernels for 49% -> 44%
where the time goes in v8:
time: 255 us; the launch traced here: 253 us
  Pallas kernels  119 us (47%)
  starting transfers between devices  110 us (43%)
  waiting for transfers between devices  14.1 us (6%)
  local copies, waits for them, and re-layouts  8.89 us (3%)
    ppermute x15, starting transfers between devices, on_device(): lax.ppermute(outgoing[0], 'tm', right)  73.7 us
    pallas_call x17, Pallas kernels, hop(): pl.pallas_call(functools.partial(hop_kernel, receives, sends, (2 if recei...  42.2 us
    pallas_call x3, Pallas kernels, filterbank(): pl.pallas_call(functools.partial(filterbank_kernel, channels, length), gr...  38.1 us
    pallas_call x10, Pallas kernels, correlate(): pl.pallas_call(functools.partial(correlate_kernel, (len(xs), len(ys)), sp...  23.7 us
    ppermute x15, starting transfers between devices, on_device(): lax.ppermute(outgoing[1], 'tm', left)  16.9 us
    pallas_call x2, Pallas kernels, visibility_rows(): pl.pallas_call(functools.partial(rows_kernel, slices, parts, span, part,...  14.6 us
    ppermute x15, waiting for transfers between devices, on_device(): lax.ppermute(outgoing[0], 'tm', right)  12.2 us
    all_to_all x3, starting transfers between devices, on_device(): lax.all_to_all(own, 'chan', split_axis=0, concat_axis=0, tiled=True)  11.4 us
  transfers between devices with their start and end apart: 35, of which 11 were waited for; matrix products, arithmetic and copies ran while one was open for 0% of the time, Pallas kernels for 44%

profile of v8, /device:TPU:0, one launch (start us, length us, event | category | flops | bytes accessed | tf_op | source)
XLA Modules:
  0.0 252.8 jit_solution(14398273615783402405)
XLA Ops:
  2.3 4.9 %collective-permute-start.1 = (bf16[2,128,1024]{2,1,0:T(8,128)(2,1)}, bf16[2,128,1024]{2,1,0:T(8,128)(2,1)S(1)}, u32[]{:S(2)}, u32[]{:S(2)}) collective-permute-start(bf16[2,128,1024]{2,1,0:T(8,128)(2,1)} %get-tuple-element.141), channel_id=1, source_target_pairs={{0,1},{1,2},{2,3},{4,5},{5,6},{6,7},{8,9},{9,10},{10,11},{12,13},{... | collective-permute-start | bytes 1572872 | tf_op jit(solution)/shard_map/ppermute | solution.py:588
  9.6 10.8 %filterbank_h0_f256.1 = (bf16[8,2,128,256]{3,2,1,0:T(8,128)(2,1)}, f32[8,128]{1,0:T(8,128)S(1)}) custom-call(bf16[2,256,32768]{2,1,0:T(8,128)(2,1)} %v_ref.5, bf16[2,256,32768]{2,1,0:T(8,128)(2,1)} %v_ref.5, bf16[720,512]{1,0:T(8,128)(2,1)S(1)} %weights.1.w_ref.after_ref, s32[1,256]{1,0:T(1,128)S(1)} %bitcast.13, bf16[720,512]{1,0:T(8,128)(2,1)S(1)} %weights.1.w_ref.after_ref), custom_call_target="tpu_custom_call" | custom-call | flops 6039797760 | bytes 8388608 | tf_op jit(solution)/shard_map/filterbank_h0_f256/pallas_call | solution.py:119
  20.4 3.7 %all-to-all-start.2 = ((bf16[8,2,128,256]{3,2,1,0:T(8,128)(2,1)}), bf16[8,2,128,256]{3,2,1,0:T(8,128)(2,1)S(1)}, u32[]{:S(2)}, u32[]{:S(2)}) async-start(bf16[8,2,128,256]{3,2,1,0:T(8,128)(2,1)} %get-tuple-element.77), calls=%async_computation.2 | async-start | bytes 2097152 | tf_op jit(solution)/shard_map/all_to_all | solution.py:607
  24.2 3.5 %collective-permute-start = (bf16[2,128,1024]{2,1,0:T(8,128)(2,1)}, bf16[2,128,1024]{2,1,0:T(8,128)(2,1)S(1)}, u32[]{:S(2)}, u32[]{:S(2)}) collective-permute-start(bf16[2,128,1024]{2,1,0:T(8,128)(2,1)} %get-tuple-element.142), channel_id=1, source_target_pairs={{0,1},{1,2},{2,3},{4,5},{5,6},{6,7},{8,9},{9,10},{10,11},{12,13},{... | collective-permute-start | bytes 1572872 | tf_op jit(solution)/shard_map/ppermute | solution.py:588
  27.7 10.0 %filterbank_h0_f0.1 = (bf16[8,2,128,256]{3,2,1,0:T(8,128)(2,1)S(1)}, f32[8,128]{1,0:T(8,128)S(1)}) custom-call(bf16[2,128,1024]{2,1,0:T(8,128)(2,1)S(1)} %collective-permute-done.1.head_ref, bf16[2,256,32768]{2,1,0:T(8,128)(2,1)} %v_ref.5, bf16[720,512]{1,0:T(8,128)(2,1)S(1)} %weights.1.w_ref.after_ref, s32[1,256]{1,0:T(1,128)S(1)} %bitcast.14, ...), custom_call_target="tpu_custom_call" | custom-call | flops 6039797760 | bytes 8388608 | tf_op jit(solution)/shard_map/filterbank_h0_f0/pallas_call | solution.py:119
  39.6 3.6 %all-to-all-start.1 = ((bf16[8,2,128,256]{3,2,1,0:T(8,128)(2,1)}), bf16[8,2,128,256]{3,2,1,0:T(8,128)(2,1)S(1)}, u32[]{:S(2)}, u32[]{:S(2)}) async-start(bf16[8,2,128,256]{3,2,1,0:T(8,128)(2,1)} %copy-done.6), calls=%async_computation.1 | async-start | bytes 2097152 | tf_op jit(solution)/shard_map/all_to_all | solution.py:607
  43.2 17.3 %filterbank_h1_f0.1 = (bf16[8,2,128,512]{3,2,1,0:T(8,128)(2,1)S(1)}, f32[8,128]{1,0:T(8,128)}) custom-call(bf16[2,128,1024]{2,1,0:T(8,128)(2,1)S(1)} %collective-permute-done.head_ref, bf16[2,256,32768]{2,1,0:T(8,128)(2,1)} %v_ref.5, bf16[720,512]{1,0:T(8,128)(2,1)S(1)} %weights.1.w_ref.after_ref, s32[1,256]{1,0:T(1,128)S(1)} %bitcast.15, ...), custom_call_target="tpu_custom_call" | custom-call | flops 12079595520 | bytes 16777216 | tf_op jit(solution)/shard_map/filterbank_h1_f0/pallas_call | solution.py:119
  62.7 4.1 %all-to-all-start = ((bf16[8,2,128,512]{3,2,1,0:T(8,128)(2,1)}), bf16[8,2,128,512]{3,2,1,0:T(8,128)(2,1)S(1)}, u32[]{:S(2)}, u32[]{:S(2)}) async-start(bf16[8,2,128,512]{3,2,1,0:T(8,128)(2,1)} %copy-done.4), calls=%async_computation | async-start | bytes 4194304 | tf_op jit(solution)/shard_map/all_to_all | solution.py:607
  72.5 3.5 %collective-permute-start.2 = (bf16[4,256,256]{2,1,0:T(8,128)(2,1)S(1)}, bf16[4,256,256]{2,1,0:T(8,128)(2,1)S(1)}, u32[]{:S(2)}, u32[]{:S(2)}) collective-permute-start(bf16[4,256,256]{2,1,0:T(8,128)(2,1)S(1)} %get-tuple-element.79), channel_id=1, source_target_pairs={{0,1},{4,5},{8,9},{12,13},{16,17},{20,21},{24,25},{28,29}} | collective-permute-start | bytes 1572872 | tf_op jit(solution)/shard_map/ppermute | solution.py:650
  79.3 3.0 %hop.19 = (bf16[4,256,256]{2,1,0:T(8,128)(2,1)}, bf16[4,256,256]{2,1,0:T(8,128)(2,1)}) custom-call(s32[544]{0:T(1024)S(1)} %copy-done.5, s32[1]{0:T(128)} %bitcast.place, bf16[104,256,256]{2,1,0:T(8,128)(2,1)} %bitcast.17), custom_call_target="tpu_custom_call" | custom-call | flops 1048576 | bytes 5242880 | tf_op jit(solution)/shard_map/hop/pallas_call | solution.py:449
  88.2 3.5 %hop.18 = (bf16[104,256,256]{2,1,0:T(8,128)(2,1)}, bf16[104,256,256]{2,1,0:T(8,128)(2,1)}, bf16[4,256,256]{2,1,0:T(8,128)(2,1)}, bf16[4,256,256]{2,1,0:T(8,128)(2,1)}) custom-call(s32[544]{0:T(1024)S(1)} %copy-done.5, s32[1]{0:T(128)} %bitcast.place, bf16[104,256,256]{2,1,0:T(8,128)(2,1)} %bitcast.18, ...), custom_call_target="tpu_custom_call", output_to_operand_aliasing={{0}: (5, {}), {1}: (6, {})} | custom-call | flops 1048576 | bytes 5242880 | tf_op jit(solution)/shard_map/hop/pallas_call | solution.py:449
  91.6 5.2 %collective-permute-start.4 = (bf16[4,256,256]{2,1,0:T(8,128)(2,1)}, bf16[4,256,256]{2,1,0:T(8,128)(2,1)}, u32[]{:S(2)}, u32[]{:S(2)}) collective-permute-start(bf16[4,256,256]{2,1,0:T(8,128)(2,1)} %get-tuple-element.83), channel_id=1, source_target_pairs={{0,1},{1,2},{4,5},{5,6},{8,9},{9,10},{12,13},{13,14},{16,17},{17,1... | collective-permute-start | bytes 1572872 | tf_op jit(solution)/shard_map/ppermute | solution.py:650
  100.7 3.0 %hop.20 = (bf16[104,256,256]{2,1,0:T(8,128)(2,1)}, bf16[104,256,256]{2,1,0:T(8,128)(2,1)}, bf16[4,256,256]{2,1,0:T(8,128)(2,1)S(1)}, bf16[4,256,256]{2,1,0:T(8,128)(2,1)S(1)}) custom-call(s32[544]{0:T(1024)S(1)} %copy-done.5, s32[1]{0:T(128)} %bitcast.place, bf16[104,256,256]{2,1,0:T(8,128)(2,1)} %bitcast.19, ...), custom_call_target="tpu_custom_call", output_to_operand_aliasing={{0}: (5, {}), {1}: (6, {})} | custom-call | flops 1048576 | bytes 5242880 | tf_op jit(solution)/shard_map/hop/pallas_call | solution.py:449
  103.7 3.3 %collective-permute-start.10 = (bf16[4,256,256]{2,1,0:T(8,128)(2,1)S(1)}, bf16[4,256,256]{2,1,0:T(8,128)(2,1)S(1)}, u32[]{:S(2)}, u32[]{:S(2)}) collective-permute-start(bf16[4,256,256]{2,1,0:T(8,128)(2,1)S(1)} %get-tuple-element.93), channel_id=1, source_target_pairs={{0,1},{1,2},{4,5},{5,6},{8,9},{9,10},{12,13},{13,14},{16,17},{17,1... | collective-permute-start | bytes 1572872 | tf_op jit(solution)/shard_map/ppermute | solution.py:650
  110.7 3.0 %hop.21 = (bf16[104,256,256]{2,1,0:T(8,128)(2,1)}, bf16[104,256,256]{2,1,0:T(8,128)(2,1)}, bf16[4,256,256]{2,1,0:T(8,128)(2,1)S(1)}, bf16[4,256,256]{2,1,0:T(8,128)(2,1)S(1)}) custom-call(s32[544]{0:T(1024)S(1)} %copy-done.5, s32[1]{0:T(128)} %bitcast.place, bf16[104,256,256]{2,1,0:T(8,128)(2,1)} %bitcast.20, ...), custom_call_target="tpu_custom_call", output_to_operand_aliasing={{0}: (5, {}), {1}: (6, {})} | custom-call | flops 1048576 | bytes 5242880 | tf_op jit(solution)/shard_map/hop/pallas_call | solution.py:449
  113.8 5.0 %collective-permute-start.8 = (bf16[4,256,256]{2,1,0:T(8,128)(2,1)S(1)}, bf16[4,256,256]{2,1,0:T(8,128)(2,1)S(1)}, u32[]{:S(2)}, u32[]{:S(2)}) collective-permute-start(bf16[4,256,256]{2,1,0:T(8,128)(2,1)S(1)} %get-tuple-element.91), channel_id=1, source_target_pairs={{0,1},{1,2},{2,3},{4,5},{5,6},{6,7},{8,9},{9,10},{10,11},{12,13},{... | collective-permute-start | bytes 1572872 | tf_op jit(solution)/shard_map/ppermute | solution.py:650
  124.9 4.7 %collective-permute-start.14 = (bf16[4,256,256]{2,1,0:T(8,128)(2,1)S(1)}, bf16[4,256,256]{2,1,0:T(8,128)(2,1)S(1)}, u32[]{:S(2)}, u32[]{:S(2)}) collective-permute-start(bf16[4,256,256]{2,1,0:T(8,128)(2,1)S(1)} %get-tuple-element.101), channel_id=1, source_target_pairs={{0,1},{1,2},{4,5},{5,6},{8,9},{9,10},{12,13},{13,14},{16,17},{17,1... | collective-permute-start | bytes 1572872 | tf_op jit(solution)/shard_map/ppermute | solution.py:650
  133.5 2.4 hop.23
  135.9 5.4 %collective-permute-start.12 = (bf16[4,256,256]{2,1,0:T(8,128)(2,1)S(1)}, bf16[4,256,256]{2,1,0:T(8,128)(2,1)S(1)}, u32[]{:S(2)}, u32[]{:S(2)}) collective-permute-start(bf16[4,256,256]{2,1,0:T(8,128)(2,1)S(1)} %get-tuple-element.99), channel_id=1, source_target_pairs={{0,1},{1,2},{2,3},{4,5},{5,6},{6,7},{8,9},{9,10},{10,11},{12,13},{... | collective-permute-start | bytes 1572872 | tf_op jit(solution)/shard_map/ppermute | solution.py:650
  147.4 5.1 %collective-permute-start.18 = (bf16[4,256,256]{2,1,0:T(8,128)(2,1)S(1)}, bf16[4,256,256]{2,1,0:T(8,128)(2,1)S(1)}, u32[]{:S(2)}, u32[]{:S(2)}) collective-permute-start(bf16[4,256,256]{2,1,0:T(8,128)(2,1)S(1)} %get-tuple-element.109), channel_id=1, source_target_pairs={{0,1},{1,2},{2,3},{4,5},{5,6},{6,7},{8,9},{9,10},{10,11},{12,13},{... | collective-permute-start | bytes 1572872 | tf_op jit(solution)/shard_map/ppermute | solution.py:650
  156.1 2.4 hop.25
  158.5 5.2 %collective-permute-start.16 = (bf16[4,256,256]{2,1,0:T(8,128)(2,1)S(1)}, bf16[4,256,256]{2,1,0:T(8,128)(2,1)S(1)}, u32[]{:S(2)}, u32[]{:S(2)}) collective-permute-start(bf16[4,256,256]{2,1,0:T(8,128)(2,1)S(1)} %get-tuple-element.107), channel_id=1, source_target_pairs={{0,1},{1,2},{4,5},{5,6},{8,9},{9,10},{12,13},{13,14},{16,17},{17,1... | collective-permute-start | bytes 1572872 | tf_op jit(solution)/shard_map/ppermute | solution.py:650
  169.2 5.7 %collective-permute-start.22 = (bf16[4,256,256]{2,1,0:T(8,128)(2,1)S(1)}, bf16[4,256,256]{2,1,0:T(8,128)(2,1)S(1)}, u32[]{:S(2)}, u32[]{:S(2)}) collective-permute-start(bf16[4,256,256]{2,1,0:T(8,128)(2,1)S(1)} %get-tuple-element.117), channel_id=1, source_target_pairs={{0,1},{1,2},{2,3},{4,5},{5,6},{6,7},{8,9},{9,10},{10,11},{12,13},{... | collective-permute-start | bytes 1572872 | tf_op jit(solution)/shard_map/ppermute | solution.py:650
  180.5 5.7 %collective-permute-start.20 = (bf16[4,256,256]{2,1,0:T(8,128)(2,1)S(1)}, bf16[4,256,256]{2,1,0:T(8,128)(2,1)S(1)}, u32[]{:S(2)}, u32[]{:S(2)}) collective-permute-start(bf16[4,256,256]{2,1,0:T(8,128)(2,1)S(1)} %get-tuple-element.115), channel_id=1, source_target_pairs={{0,1},{1,2},{2,3},{4,5},{5,6},{6,7},{8,9},{9,10},{10,11},{12,13},{... | collective-permute-start | bytes 1572872 | tf_op jit(solution)/shard_map/ppermute | solution.py:650
  189.3 2.4 hop.28
  191.7 5.7 %collective-permute-start.26 = (bf16[4,256,256]{2,1,0:T(8,128)(2,1)S(1)}, bf16[4,256,256]{2,1,0:T(8,128)(2,1)S(1)}, u32[]{:S(2)}, u32[]{:S(2)}) collective-permute-start(bf16[4,256,256]{2,1,0:T(8,128)(2,1)S(1)} %get-tuple-element.125), channel_id=1, source_target_pairs={{0,1},{1,2},{2,3},{4,5},{5,6},{6,7},{8,9},{9,10},{10,11},{12,13},{... | collective-permute-start | bytes 1572872 | tf_op jit(solution)/shard_map/ppermute | solution.py:650
  202.9 5.7 %collective-permute-start.24 = (bf16[4,256,256]{2,1,0:T(8,128)(2,1)S(1)}, bf16[4,256,256]{2,1,0:T(8,128)(2,1)S(1)}, u32[]{:S(2)}, u32[]{:S(2)}) collective-permute-start(bf16[4,256,256]{2,1,0:T(8,128)(2,1)S(1)} %get-tuple-element.123), channel_id=1, source_target_pairs={{0,1},{1,2},{4,5},{5,6},{8,9},{9,10},{12,13},{13,14},{16,17},{17,1... | collective-permute-start | bytes 1572872 | tf_op jit(solution)/shard_map/ppermute | solution.py:650
  211.7 2.4 hop.30
  214.2 5.9 %collective-permute-start.30 = (bf16[4,256,256]{2,1,0:T(8,128)(2,1)S(1)}, bf16[4,256,256]{2,1,0:T(8,128)(2,1)S(1)}, u32[]{:S(2)}, u32[]{:S(2)}) collective-permute-start(bf16[4,256,256]{2,1,0:T(8,128)(2,1)S(1)} %get-tuple-element.133), channel_id=1, source_target_pairs={{0,1},{1,2},{2,3},{4,5},{5,6},{6,7},{8,9},{9,10},{10,11},{12,13},{... | collective-permute-start | bytes 1572872 | tf_op jit(solution)/shard_map/ppermute | solution.py:650
  225.4 5.5 %collective-permute-start.28 = (bf16[4,256,256]{2,1,0:T(8,128)(2,1)S(1)}, bf16[4,256,256]{2,1,0:T(8,128)(2,1)S(1)}, u32[]{:S(2)}, u32[]{:S(2)}) collective-permute-start(bf16[4,256,256]{2,1,0:T(8,128)(2,1)S(1)} %get-tuple-element.131), channel_id=1, source_target_pairs={{0,1},{2,3},{4,5},{6,7},{8,9},{10,11},{12,13},{14,15},{16,17},{18,... | collective-permute-start | bytes 1572872 | tf_op jit(solution)/shard_map/ppermute | solution.py:650
  236.5 9.5 %visibility_rows.2.refs_4_.refs_24_ = f32[2,2,256,2,8,128]{5,4,3,2,1,0:T(8,128)} custom-call(s32[128]{0:T(128)S(1)} %copy-done.12, s32[64]{0:T(128)S(1)} %copy-done.11, s32[1]{0:T(128)} %bitcast.place, bf16[104,256,256]{2,1,0:T(8,128)(2,1)} %bitcast.31, bf16[104,256,256]{2,1,0:T(8,128)(2,1)} %bitcast.32, bf16[104,256,256]{2,1,0:T(8,128)(2,1)} %bitcast.33, ...), custom_call_target="tpu_custom_call" | custom-call | flops 4194304 | bytes 12582912 | tf_op jit(solution)/shard_map/visibility_rows/pallas_call | solution.py:551
  247.8 5.0 %visibility_rows.3 = f32[2,2,256,2,8,128]{5,4,3,2,1,0:T(8,128)} custom-call(s32[128]{0:T(128)S(1)} %copy-done.12, s32[64]{0:T(128)S(1)} %copy-done.11, s32[1]{0:T(128)} %bitcast.place, bf16[104,256,256]{2,1,0:T(8,128)(2,1)} %bitcast.39, bf16[104,256,256]{2,1,0:T(8,128)(2,1)} %bitcast.40, ...), custom_call_target="tpu_custom_call", output_to_operand_aliasing={{}: (27, {})} | custom-call | flops 4194304 | bytes 12582912 | tf_op jit(solution)/shard_map/visibility_rows/pallas_call | solution.py:551
  (98 shorter events, 85.9 us)
Async XLA Ops:
  2.3 25.4 %collective-permute-start.1 = (bf16[2,128,1024]{2,1,0:T(8,128)(2,1)}, bf16[2,128,1024]{2,1,0:T(8,128)(2,1)S(1)}, u32[]{:S(2)}, u32[]{:S(2)}) collective-permute-start(bf16[2,128,1024]{2,1,0:T(8,128)(2,1)} %get-tuple-element.141), channel_id=1, source_target_pairs={{0,1},{1,2},{2,3},{4,5},{5,6},{6,7},{8,9},{9,10},{10,11},{12,13},{... | collective-permute-start | bytes 1572872 | tf_op jit(solution)/shard_map/ppermute | solution.py:588
  20.4 19.1 %all-to-all-start.2 = ((bf16[8,2,128,256]{3,2,1,0:T(8,128)(2,1)}), bf16[8,2,128,256]{3,2,1,0:T(8,128)(2,1)S(1)}, u32[]{:S(2)}, u32[]{:S(2)}) async-start(bf16[8,2,128,256]{3,2,1,0:T(8,128)(2,1)} %get-tuple-element.77), calls=%async_computation.2 | async-start | bytes 2097152 | tf_op jit(solution)/shard_map/all_to_all | solution.py:607
  24.2 19.0 %collective-permute-start = (bf16[2,128,1024]{2,1,0:T(8,128)(2,1)}, bf16[2,128,1024]{2,1,0:T(8,128)(2,1)S(1)}, u32[]{:S(2)}, u32[]{:S(2)}) collective-permute-start(bf16[2,128,1024]{2,1,0:T(8,128)(2,1)} %get-tuple-element.142), channel_id=1, source_target_pairs={{0,1},{1,2},{2,3},{4,5},{5,6},{6,7},{8,9},{9,10},{10,11},{12,13},{... | collective-permute-start | bytes 1572872 | tf_op jit(solution)/shard_map/ppermute | solution.py:588
  39.6 22.2 %all-to-all-start.1 = ((bf16[8,2,128,256]{3,2,1,0:T(8,128)(2,1)}), bf16[8,2,128,256]{3,2,1,0:T(8,128)(2,1)S(1)}, u32[]{:S(2)}, u32[]{:S(2)}) async-start(bf16[8,2,128,256]{3,2,1,0:T(8,128)(2,1)} %copy-done.6), calls=%async_computation.1 | async-start | bytes 2097152 | tf_op jit(solution)/shard_map/all_to_all | solution.py:607
  62.7 35.5 %all-to-all-start = ((bf16[8,2,128,512]{3,2,1,0:T(8,128)(2,1)}), bf16[8,2,128,512]{3,2,1,0:T(8,128)(2,1)S(1)}, u32[]{:S(2)}, u32[]{:S(2)}) async-start(bf16[8,2,128,512]{3,2,1,0:T(8,128)(2,1)} %copy-done.4), calls=%async_computation | async-start | bytes 4194304 | tf_op jit(solution)/shard_map/all_to_all | solution.py:607
  72.5 15.7 %collective-permute-start.2 = (bf16[4,256,256]{2,1,0:T(8,128)(2,1)S(1)}, bf16[4,256,256]{2,1,0:T(8,128)(2,1)S(1)}, u32[]{:S(2)}, u32[]{:S(2)}) collective-permute-start(bf16[4,256,256]{2,1,0:T(8,128)(2,1)S(1)} %get-tuple-element.79), channel_id=1, source_target_pairs={{0,1},{4,5},{8,9},{12,13},{16,17},{20,21},{24,25},{28,29}} | collective-permute-start | bytes 1572872 | tf_op jit(solution)/shard_map/ppermute | solution.py:650
  82.3 18.4 %collective-permute-start.6 = (bf16[4,256,256]{2,1,0:T(8,128)(2,1)}, bf16[4,256,256]{2,1,0:T(8,128)(2,1)}, u32[]{:S(2)}, u32[]{:S(2)}) collective-permute-start(bf16[4,256,256]{2,1,0:T(8,128)(2,1)} %get-tuple-element.85), channel_id=1, source_target_pairs={{0,1},{4,5},{8,9},{12,13},{16,17},{20,21},{24,25},{28,29}} | collective-permute-start | bytes 1572872 | tf_op jit(solution)/shard_map/ppermute | solution.py:650
  84.3 16.3 %collective-permute-start.7 = (bf16[4,256,256]{2,1,0:T(8,128)(2,1)}, bf16[4,256,256]{2,1,0:T(8,128)(2,1)}, u32[]{:S(2)}, u32[]{:S(2)}) collective-permute-start(bf16[4,256,256]{2,1,0:T(8,128)(2,1)} %get-tuple-element.86), channel_id=1, source_target_pairs={{3,2},{7,6},{11,10},{15,14},{19,18},{23,22},{27,26},{31,30}} | collective-permute-start | bytes 1572872 | tf_op jit(solution)/shard_map/ppermute | solution.py:651
  91.6 19.1 %collective-permute-start.4 = (bf16[4,256,256]{2,1,0:T(8,128)(2,1)}, bf16[4,256,256]{2,1,0:T(8,128)(2,1)}, u32[]{:S(2)}, u32[]{:S(2)}) collective-permute-start(bf16[4,256,256]{2,1,0:T(8,128)(2,1)} %get-tuple-element.83), channel_id=1, source_target_pairs={{0,1},{1,2},{4,5},{5,6},{8,9},{9,10},{12,13},{13,14},{16,17},{17,1... | collective-permute-start | bytes 1572872 | tf_op jit(solution)/shard_map/ppermute | solution.py:650
  103.7 18.8 %collective-permute-start.10 = (bf16[4,256,256]{2,1,0:T(8,128)(2,1)S(1)}, bf16[4,256,256]{2,1,0:T(8,128)(2,1)S(1)}, u32[]{:S(2)}, u32[]{:S(2)}) collective-permute-start(bf16[4,256,256]{2,1,0:T(8,128)(2,1)S(1)} %get-tuple-element.93), channel_id=1, source_target_pairs={{0,1},{1,2},{4,5},{5,6},{8,9},{9,10},{12,13},{13,14},{16,17},{17,1... | collective-permute-start | bytes 1572872 | tf_op jit(solution)/shard_map/ppermute | solution.py:650
  107.0 15.5 %collective-permute-start.11 = (bf16[4,256,256]{2,1,0:T(8,128)(2,1)S(1)}, bf16[4,256,256]{2,1,0:T(8,128)(2,1)S(1)}, u32[]{:S(2)}, u32[]{:S(2)}) collective-permute-start(bf16[4,256,256]{2,1,0:T(8,128)(2,1)S(1)} %get-tuple-element.94), channel_id=1, source_target_pairs={{3,2},{2,1},{7,6},{6,5},{11,10},{10,9},{15,14},{14,13},{19,18},{18... | collective-permute-start | bytes 1572872 | tf_op jit(solution)/shard_map/ppermute | solution.py:651
  113.8 19.3 %collective-permute-start.8 = (bf16[4,256,256]{2,1,0:T(8,128)(2,1)S(1)}, bf16[4,256,256]{2,1,0:T(8,128)(2,1)S(1)}, u32[]{:S(2)}, u32[]{:S(2)}) collective-permute-start(bf16[4,256,256]{2,1,0:T(8,128)(2,1)S(1)} %get-tuple-element.91), channel_id=1, source_target_pairs={{0,1},{1,2},{2,3},{4,5},{5,6},{6,7},{8,9},{9,10},{10,11},{12,13},{... | collective-permute-start | bytes 1572872 | tf_op jit(solution)/shard_map/ppermute | solution.py:650
  118.8 14.7 %collective-permute-start.9 = (bf16[4,256,256]{2,1,0:T(8,128)(2,1)S(1)}, bf16[4,256,256]{2,1,0:T(8,128)(2,1)S(1)}, u32[]{:S(2)}, u32[]{:S(2)}) collective-permute-start(bf16[4,256,256]{2,1,0:T(8,128)(2,1)S(1)} %get-tuple-element.92), channel_id=1, source_target_pairs={{3,2},{2,1},{1,0},{7,6},{6,5},{5,4},{11,10},{10,9},{9,8},{15,14},{... | collective-permute-start | bytes 1572872 | tf_op jit(solution)/shard_map/ppermute | solution.py:651
  124.9 20.0 %collective-permute-start.14 = (bf16[4,256,256]{2,1,0:T(8,128)(2,1)S(1)}, bf16[4,256,256]{2,1,0:T(8,128)(2,1)S(1)}, u32[]{:S(2)}, u32[]{:S(2)}) collective-permute-start(bf16[4,256,256]{2,1,0:T(8,128)(2,1)S(1)} %get-tuple-element.101), channel_id=1, source_target_pairs={{0,1},{1,2},{4,5},{5,6},{8,9},{9,10},{12,13},{13,14},{16,17},{17,1... | collective-permute-start | bytes 1572872 | tf_op jit(solution)/shard_map/ppermute | solution.py:650
  129.6 15.3 %collective-permute-start.15 = (bf16[4,256,256]{2,1,0:T(8,128)(2,1)S(1)}, bf16[4,256,256]{2,1,0:T(8,128)(2,1)S(1)}, u32[]{:S(2)}, u32[]{:S(2)}) collective-permute-start(bf16[4,256,256]{2,1,0:T(8,128)(2,1)S(1)} %get-tuple-element.102), channel_id=1, source_target_pairs={{3,2},{2,1},{7,6},{6,5},{11,10},{10,9},{15,14},{14,13},{19,18},{18... | collective-permute-start | bytes 1572872 | tf_op jit(solution)/shard_map/ppermute | solution.py:651
  135.9 20.1 %collective-permute-start.12 = (bf16[4,256,256]{2,1,0:T(8,128)(2,1)S(1)}, bf16[4,256,256]{2,1,0:T(8,128)(2,1)S(1)}, u32[]{:S(2)}, u32[]{:S(2)}) collective-permute-start(bf16[4,256,256]{2,1,0:T(8,128)(2,1)S(1)} %get-tuple-element.99), channel_id=1, source_target_pairs={{0,1},{1,2},{2,3},{4,5},{5,6},{6,7},{8,9},{9,10},{10,11},{12,13},{... | collective-permute-start | bytes 1572872 | tf_op jit(solution)/shard_map/ppermute | solution.py:650
  141.3 14.8 %collective-permute-start.13 = (bf16[4,256,256]{2,1,0:T(8,128)(2,1)S(1)}, bf16[4,256,256]{2,1,0:T(8,128)(2,1)S(1)}, u32[]{:S(2)}, u32[]{:S(2)}) collective-permute-start(bf16[4,256,256]{2,1,0:T(8,128)(2,1)S(1)} %get-tuple-element.100), channel_id=1, source_target_pairs={{3,2},{2,1},{1,0},{7,6},{6,5},{5,4},{11,10},{10,9},{9,8},{15,14},{... | collective-permute-start | bytes 1572872 | tf_op jit(solution)/shard_map/ppermute | solution.py:651
  147.4 19.4 %collective-permute-start.18 = (bf16[4,256,256]{2,1,0:T(8,128)(2,1)S(1)}, bf16[4,256,256]{2,1,0:T(8,128)(2,1)S(1)}, u32[]{:S(2)}, u32[]{:S(2)}) collective-permute-start(bf16[4,256,256]{2,1,0:T(8,128)(2,1)S(1)} %get-tuple-element.109), channel_id=1, source_target_pairs={{0,1},{1,2},{2,3},{4,5},{5,6},{6,7},{8,9},{9,10},{10,11},{12,13},{... | collective-permute-start | bytes 1572872 | tf_op jit(solution)/shard_map/ppermute | solution.py:650
  152.5 14.3 %collective-permute-start.19 = (bf16[4,256,256]{2,1,0:T(8,128)(2,1)S(1)}, bf16[4,256,256]{2,1,0:T(8,128)(2,1)S(1)}, u32[]{:S(2)}, u32[]{:S(2)}) collective-permute-start(bf16[4,256,256]{2,1,0:T(8,128)(2,1)S(1)} %get-tuple-element.110), channel_id=1, source_target_pairs={{3,2},{2,1},{1,0},{7,6},{6,5},{5,4},{11,10},{10,9},{9,8},{15,14},{... | collective-permute-start | bytes 1572872 | tf_op jit(solution)/shard_map/ppermute | solution.py:651
  158.5 19.5 %collective-permute-start.16 = (bf16[4,256,256]{2,1,0:T(8,128)(2,1)S(1)}, bf16[4,256,256]{2,1,0:T(8,128)(2,1)S(1)}, u32[]{:S(2)}, u32[]{:S(2)}) collective-permute-start(bf16[4,256,256]{2,1,0:T(8,128)(2,1)S(1)} %get-tuple-element.107), channel_id=1, source_target_pairs={{0,1},{1,2},{4,5},{5,6},{8,9},{9,10},{12,13},{13,14},{16,17},{17,1... | collective-permute-start | bytes 1572872 | tf_op jit(solution)/shard_map/ppermute | solution.py:650
  163.7 14.3 %collective-permute-start.17 = (bf16[4,256,256]{2,1,0:T(8,128)(2,1)S(1)}, bf16[4,256,256]{2,1,0:T(8,128)(2,1)S(1)}, u32[]{:S(2)}, u32[]{:S(2)}) collective-permute-start(bf16[4,256,256]{2,1,0:T(8,128)(2,1)S(1)} %get-tuple-element.108), channel_id=1, source_target_pairs={{3,2},{2,1},{7,6},{6,5},{11,10},{10,9},{15,14},{14,13},{19,18},{18... | collective-permute-start | bytes 1572872 | tf_op jit(solution)/shard_map/ppermute | solution.py:651
  169.2 20.0 %collective-permute-start.22 = (bf16[4,256,256]{2,1,0:T(8,128)(2,1)S(1)}, bf16[4,256,256]{2,1,0:T(8,128)(2,1)S(1)}, u32[]{:S(2)}, u32[]{:S(2)}) collective-permute-start(bf16[4,256,256]{2,1,0:T(8,128)(2,1)S(1)} %get-tuple-element.117), channel_id=1, source_target_pairs={{0,1},{1,2},{2,3},{4,5},{5,6},{6,7},{8,9},{9,10},{10,11},{12,13},{... | collective-permute-start | bytes 1572872 | tf_op jit(solution)/shard_map/ppermute | solution.py:650
  174.9 14.3 %collective-permute-start.23 = (bf16[4,256,256]{2,1,0:T(8,128)(2,1)S(1)}, bf16[4,256,256]{2,1,0:T(8,128)(2,1)S(1)}, u32[]{:S(2)}, u32[]{:S(2)}) collective-permute-start(bf16[4,256,256]{2,1,0:T(8,128)(2,1)S(1)} %get-tuple-element.118), channel_id=1, source_target_pairs={{3,2},{2,1},{1,0},{7,6},{6,5},{5,4},{11,10},{10,9},{9,8},{15,14},{... | collective-permute-start | bytes 1572872 | tf_op jit(solution)/shard_map/ppermute | solution.py:651
  180.5 20.0 %collective-permute-start.20 = (bf16[4,256,256]{2,1,0:T(8,128)(2,1)S(1)}, bf16[4,256,256]{2,1,0:T(8,128)(2,1)S(1)}, u32[]{:S(2)}, u32[]{:S(2)}) collective-permute-start(bf16[4,256,256]{2,1,0:T(8,128)(2,1)S(1)} %get-tuple-element.115), channel_id=1, source_target_pairs={{0,1},{1,2},{2,3},{4,5},{5,6},{6,7},{8,9},{9,10},{10,11},{12,13},{... | collective-permute-start | bytes 1572872 | tf_op jit(solution)/shard_map/ppermute | solution.py:650
  186.2 14.3 %collective-permute-start.21 = (bf16[4,256,256]{2,1,0:T(8,128)(2,1)S(1)}, bf16[4,256,256]{2,1,0:T(8,128)(2,1)S(1)}, u32[]{:S(2)}, u32[]{:S(2)}) collective-permute-start(bf16[4,256,256]{2,1,0:T(8,128)(2,1)S(1)} %get-tuple-element.116), channel_id=1, source_target_pairs={{3,2},{2,1},{1,0},{7,6},{6,5},{5,4},{11,10},{10,9},{9,8},{15,14},{... | collective-permute-start | bytes 1572872 | tf_op jit(solution)/shard_map/ppermute | solution.py:651
  191.7 20.0 %collective-permute-start.26 = (bf16[4,256,256]{2,1,0:T(8,128)(2,1)S(1)}, bf16[4,256,256]{2,1,0:T(8,128)(2,1)S(1)}, u32[]{:S(2)}, u32[]{:S(2)}) collective-permute-start(bf16[4,256,256]{2,1,0:T(8,128)(2,1)S(1)} %get-tuple-element.125), channel_id=1, source_target_pairs={{0,1},{1,2},{2,3},{4,5},{5,6},{6,7},{8,9},{9,10},{10,11},{12,13},{... | collective-permute-start | bytes 1572872 | tf_op jit(solution)/shard_map/ppermute | solution.py:650
  202.9 20.0 %collective-permute-start.24 = (bf16[4,256,256]{2,1,0:T(8,128)(2,1)S(1)}, bf16[4,256,256]{2,1,0:T(8,128)(2,1)S(1)}, u32[]{:S(2)}, u32[]{:S(2)}) collective-permute-start(bf16[4,256,256]{2,1,0:T(8,128)(2,1)S(1)} %get-tuple-element.123), channel_id=1, source_target_pairs={{0,1},{1,2},{4,5},{5,6},{8,9},{9,10},{12,13},{13,14},{16,17},{17,1... | collective-permute-start | bytes 1572872 | tf_op jit(solution)/shard_map/ppermute | solution.py:650
  208.7 14.3 %collective-permute-start.25 = (bf16[4,256,256]{2,1,0:T(8,128)(2,1)S(1)}, bf16[4,256,256]{2,1,0:T(8,128)(2,1)S(1)}, u32[]{:S(2)}, u32[]{:S(2)}) collective-permute-start(bf16[4,256,256]{2,1,0:T(8,128)(2,1)S(1)} %get-tuple-element.124), channel_id=1, source_target_pairs={{3,2},{2,1},{7,6},{6,5},{11,10},{10,9},{15,14},{14,13},{19,18},{18... | collective-permute-start | bytes 1572872 | tf_op jit(solution)/shard_map/ppermute | solution.py:651
  214.2 20.0 %collective-permute-start.30 = (bf16[4,256,256]{2,1,0:T(8,128)(2,1)S(1)}, bf16[4,256,256]{2,1,0:T(8,128)(2,1)S(1)}, u32[]{:S(2)}, u32[]{:S(2)}) collective-permute-start(bf16[4,256,256]{2,1,0:T(8,128)(2,1)S(1)} %get-tuple-element.133), channel_id=1, source_target_pairs={{0,1},{1,2},{2,3},{4,5},{5,6},{6,7},{8,9},{9,10},{10,11},{12,13},{... | collective-permute-start | bytes 1572872 | tf_op jit(solution)/shard_map/ppermute | solution.py:650
  220.1 14.7 %collective-permute-start.31 = (bf16[4,256,256]{2,1,0:T(8,128)(2,1)S(1)}, bf16[4,256,256]{2,1,0:T(8,128)(2,1)S(1)}, u32[]{:S(2)}, u32[]{:S(2)}) collective-permute-start(bf16[4,256,256]{2,1,0:T(8,128)(2,1)S(1)} %get-tuple-element.134), channel_id=1, source_target_pairs={{3,2},{2,1},{1,0},{7,6},{6,5},{5,4},{11,10},{10,9},{9,8},{15,14},{... | collective-permute-start | bytes 1572872 | tf_op jit(solution)/shard_map/ppermute | solution.py:651
  225.4 20.7 %collective-permute-start.28 = (bf16[4,256,256]{2,1,0:T(8,128)(2,1)S(1)}, bf16[4,256,256]{2,1,0:T(8,128)(2,1)S(1)}, u32[]{:S(2)}, u32[]{:S(2)}) collective-permute-start(bf16[4,256,256]{2,1,0:T(8,128)(2,1)S(1)} %get-tuple-element.131), channel_id=1, source_target_pairs={{0,1},{2,3},{4,5},{6,7},{8,9},{10,11},{12,13},{14,15},{16,17},{18,... | collective-permute-start | bytes 1572872 | tf_op jit(solution)/shard_map/ppermute | solution.py:650
  230.9 15.2 %collective-permute-start.29 = (bf16[4,256,256]{2,1,0:T(8,128)(2,1)S(1)}, bf16[4,256,256]{2,1,0:T(8,128)(2,1)S(1)}, u32[]{:S(2)}, u32[]{:S(2)}) collective-permute-start(bf16[4,256,256]{2,1,0:T(8,128)(2,1)S(1)} %get-tuple-element.132), channel_id=1, source_target_pairs={{3,2},{1,0},{7,6},{5,4},{11,10},{9,8},{15,14},{13,12},{19,18},{17,... | collective-permute-start | bytes 1572872 | tf_op jit(solution)/shard_map/ppermute | solution.py:651
  (16 other events, 112.4 us)
